TPU v7x, 32 devices: a whole 2x2x4 slice. The times are simulated.
32 devices in a mesh: view: 2 (over core), row: 4 (over y, x), feat: 4 (over z).
Axes of the slice: x: 2, y: 2, z: 4, core: 2. Of those that a mesh axis runs over, the one named last changes fastest.
Arguments:
- views: bfloat16 [2, 12288, 4096], P('view', ('row', 'feat')), may hold values from -8 to 8
- weights: float32 [2, 4096, 256], P('view', ('row', 'feat')), may hold values from -6 to 6
Outputs:
- new_weights: float32 [2, 4096, 256], P('view', ('row', 'feat'))
- projected: bfloat16 [2, 12288, 256], P('view', ('row', 'feat'))
All inputs are finite; a program needn't handle non-finite values.
Results may differ from a plain program's by a relative error of at most 0.012.
Values may be sent and summed in bfloat16 or wider, within the bound.
No kernel may reach another device: no remote copies, remote signals or barrier semaphores. Data moves between devices by JAX's collectives and lax.ppermute only.
A program may use at most 64 MiB of HBM per device.

v0:
```python
import math

import jax
import jax.numpy as jnp
from jax import lax
from jax.sharding import PartitionSpec as P

ITERS = 2


epsilon = 1e-06
step_rate = 0.5


def swapped(block, axis, distance):
    count = lax.axis_size(axis)
    route = []
    for low in range(count):
        high = low | 1 << distance
        if high != low and high < count:
            route += [(low, high), (high, low)]
    return lax.ppermute(block, axis, route)


def on_device(views, weights):
    samples = views[0]
    own_rows = weights[0]
    rows_here = samples.shape[0]
    row_total = rows_here * lax.axis_size("row") * lax.axis_size("feat")
    width_root = math.sqrt(samples.shape[1])
    shown = None
    for sweep in range(ITERS):
        halved = own_rows.astype(jnp.bfloat16)
        whole_dirs = lax.all_gather(halved, ("row", "feat"), axis=0, tiled=True)
        summed_proj = jnp.dot(samples, whole_dirs, preferred_element_type=jnp.float32)
        squares = jnp.sum(summed_proj * summed_proj, axis=0)
        col_sums = lax.psum(squares, ("row", "feat"))
        scaling = lax.rsqrt(col_sums / row_total + epsilon)
        own_proj = (summed_proj * scaling).astype(jnp.bfloat16)
        partner_proj = swapped(own_proj, "view", 0)
        residue = (own_proj.astype(jnp.float32) - partner_proj.astype(jnp.float32)).astype(
            jnp.bfloat16
        )
        grad_share = lax.psum_scatter(
            lax.dot_general(
                samples, residue, (((0,), (0,)), ((), ())), preferred_element_type=jnp.float32
            ),
            ("row", "feat"),
            scatter_dimension=0,
            tiled=True,
        )
        own_rows = width_root * (own_rows * scaling - step_rate * (grad_share / row_total))
        shown = own_proj
    return (own_rows[None], shown[None])


def solution(mesh):
    in_specs = (P("view", ("row", "feat"), None), P("view", ("row", "feat"), None))
    out_specs = (P("view", ("row", "feat"), None), P("view", ("row", "feat"), None))
    return jax.shard_map(
        on_device, mesh=mesh, in_specs=in_specs, out_specs=out_specs, check_vma=False
    )
```

profile of v0, /device:TPU:0, one launch (start us, length us, event | category | flops | bytes accessed | tf_op | source)
XLA Modules:
  0.0 445.6 jit_solution(7726538499044265989)
XLA Ops:
  7.2 0.0 all-gather.3.cloned.1.call-start
  7.2 1.1 copy.4
  8.3 0.7 bitcast_convert_fusion
  9.0 0.0 all-gather.3.cloned.1.call-update
  9.0 0.0 reduce-scatter.3.cloned.1.call-start
  9.0 70.1 %all-gather.3.cloned.1.call-done = bf16[4096,256]{0,1:T(8,128)(2,1)} async-done(((bf16[256,256]{0,1:T(8,128)(2,1)}), bf16[4096,256]{0,1:T(8,128)(2,1)}) %all-gather.3.cloned.1.call-update) | async-done | bytes 2097168 | tf_op jit(solution)/shard_map/all_gather | solution.py:34
  79.1 5.2 %multiply_reduce_fusion.1 = (f32[256]{0:T(256)S(1)}, f32[768,256]{1,0:T(8,128)S(1)}) fusion(bf16[4096,256]{0,1:T(8,128)(2,1)} %all-gather.3.cloned.1.call-done, bf16[1,768,4096]{2,1,0:T(8,128)(2,1)} %param.2), kind=kOutput, calls=%fused_computation.15 | convolution fusion | flops 1611005696 | bytes 9176064 | tf_op jit(solution)/shard_map/dot_general | solution.py:35
  84.4 39.4 %psum.14 = f32[256]{0:T(256)S(1)} all-reduce(f32[256]{0:T(256)S(1)} %get-tuple-element.6), channel_id=1, replica_groups=mesh['view'=2,'row'=4,'feat'=4] {'row','feat'}, use_global_device_ids=true, to_apply=%region_1.0 | all-reduce | flops 256 | bytes 2048 | tf_op jit(solution)/shard_map/psum | solution.py:37
  123.8 0.1 multiply_convert_fusion.1
  123.9 0.1 collective-permute-start
  124.0 1.7 collective-permute-done
  125.7 6.6 %fusion.8 = f32[4096,256]{0,1:T(8,128)} fusion(bf16[1,768,4096]{2,1,0:T(8,128)(2,1)} %param.2, bf16[768,256]{1,0:T(8,128)(2,1)S(1)} %collective-permute-done, bf16[768,256]{1,0:T(8,128)(2,1)S(1)} %multiply_convert_fusion.1), kind=kOutput, calls=%fused_computation.8 | convolution fusion | flops 1611399168 | bytes 11272192 | tf_op jit(solution)/shard_map/dot_general | solution.py:45
  132.2 0.0 reduce-scatter.3.cloned.1.call-update
  132.3 0.0 all-gather.5.cloned.1.call-start
  132.3 92.4 %reduce-scatter.3.cloned.1.call-done = f32[256,256]{0,1:T(8,128)} async-done(((f32[4096,256]{0,1:T(8,128)}), f32[256,256]{0,1:T(8,128)}) %reduce-scatter.3.cloned.1.call-update) | async-done | bytes 262160 | tf_op jit(solution)/shard_map/reduce_scatter | solution.py:44
  224.7 1.7 multiply_convert_fusion.2
  226.4 0.0 all-gather.5.cloned.1.call-update
  226.4 0.0 reduce-scatter.5.cloned.1.call-start
  226.5 64.9 %all-gather.5.cloned.1.call-done = bf16[4096,256]{0,1:T(8,128)(2,1)} async-done(((bf16[256,256]{0,1:T(8,128)(2,1)}), bf16[4096,256]{0,1:T(8,128)(2,1)}) %all-gather.5.cloned.1.call-update) | async-done | bytes 2097168 | tf_op jit(solution)/shard_map/all_gather | solution.py:34
  291.4 5.3 %multiply_reduce_fusion = (f32[256]{0:T(256)S(1)}, f32[256,768]{1,0:T(8,128)S(1)}) fusion(bf16[4096,256]{0,1:T(8,128)(2,1)} %all-gather.5.cloned.1.call-done, bf16[1,768,4096]{2,1,0:T(8,128)(2,1)} %param.2), kind=kOutput, calls=%fused_computation.12 | convolution fusion | flops 1611005696 | bytes 9176064 | tf_op jit(solution)/shard_map/dot_general | solution.py:35
  296.7 39.4 %psum.15 = f32[256]{0:T(256)S(1)} all-reduce(f32[256]{0:T(256)S(1)} %get-tuple-element.8), channel_id=1, replica_groups=mesh['view'=2,'row'=4,'feat'=4] {'row','feat'}, use_global_device_ids=true, to_apply=%region_4.0 | all-reduce | flops 256 | bytes 2048 | tf_op jit(solution)/shard_map/psum | solution.py:37
  336.2 0.1 fusion.19
  336.3 0.1 collective-permute-start.1
  336.4 1.7 collective-permute-done.1
  338.1 6.6 %fusion.11 = f32[4096,256]{0,1:T(8,128)} fusion(bf16[1,768,4096]{2,1,0:T(8,128)(2,1)} %param.2, bf16[768,256]{0,1:T(8,128)(2,1)S(1)} %collective-permute-done.1, f32[256,768]{1,0:T(8,128)S(1)} %get-tuple-element.9, f32[256]{0:T(256)S(1)} %get-tuple-element.5), kind=kOutput, calls=%fused_computation.9 | convolution fusion | flops 1611792384 | bytes 11666432 | tf_op jit(solution)/shard_map/dot_general | solution.py:45
  344.7 0.0 copy-start
  344.7 0.0 reduce-scatter.5.cloned.1.call-update
  344.7 0.1 fusion.18
  344.8 0.9 copy.6
  345.7 91.4 %reduce-scatter.5.cloned.1.call-done = f32[256,256]{0,1:T(8,128)} async-done(((f32[4096,256]{0,1:T(8,128)}), f32[256,256]{0,1:T(8,128)}) %reduce-scatter.5.cloned.1.call-update) | async-done | bytes 262160 | tf_op jit(solution)/shard_map/reduce_scatter | solution.py:44
  437.1 0.0 copy-done
  437.1 1.1 multiply_bitcast_fusion
  438.2 0.8 copy.5
  (2 shorter events, 0.0 us)
Async XLA Ops:
  7.2 72.0 %all-gather.3.cloned.1.call-start = ((), (), s32[]{:S(2)}) async-start(), calls=%async_computation.2 | async-start | bytes 2228224 | tf_op jit(solution)/shard_map/all_gather | solution.py:34
  9.0 215.7 %reduce-scatter.3.cloned.1.call-start = ((), (), s32[]{:S(2)}) async-start(), calls=%async_computation.3 | async-start | bytes 4456448 | tf_op jit(solution)/shard_map/reduce_scatter | solution.py:44
  123.9 1.8 collective-permute-start
  132.3 159.1 %all-gather.5.cloned.1.call-start = ((), (), s32[]{:S(2)}) async-start(), calls=%async_computation.4 | async-start | bytes 2228224 | tf_op jit(solution)/shard_map/all_gather | solution.py:34
  226.4 210.7 %reduce-scatter.5.cloned.1.call-start = ((), (), s32[]{:S(2)}) async-start(), calls=%async_computation.5 | async-start | bytes 4456448 | tf_op jit(solution)/shard_map/reduce_scatter | solution.py:44
  336.3 1.8 collective-permute-start.1
  344.7 92.5 %copy-start = (f32[256,256]{0,1:T(8,128)S(1)}, f32[256,256]{0,1:T(8,128)}, u32[]{:S(2)}) copy-start(f32[256,256]{0,1:T(8,128)} %reduce-scatter.3.cloned.1.call-done) | copy-start | bytes 786436
Sparse Core Ops, SparseCore 0:
  11.3 67.7 all-gather.2
  132.4 92.2 reduce-scatter.2
  228.0 63.3 all-gather.4
  344.8 92.2 reduce-scatter.4
where the time goes:
time: 446 us
  waiting for transfers between devices  322 us (72%)
  blocking collectives  78.8 us (18%)
  matrix products  23.8 us (5%)
  between operations  13.8 us (3%)
    reduce_scatter x2, waiting for transfers between devices, on_device(): lax.psum_scatter(lax.dot_general(samples, residue, (((0,), (0,)), ((), ()...  184 us
    all_gather x2, waiting for transfers between devices, on_device(): whole_dirs = lax.all_gather(halved, ('row', 'feat'), axis=0, tiled=True)  135 us
    psum x2, blocking collectives, on_device(): col_sums = lax.psum(squares, ('row', 'feat'))  78.8 us
    dot_general x2, matrix products, on_device(): lax.dot_general(samples, residue, (((0,), (0,)), ((), ())), preferred_ele...  13.2 us
    dot_general x2, matrix products, on_device(): jnp.dot(samples, whole_dirs, preferred_element_type=jnp.float32)  10.6 us
  transfers between devices with their start and end apart: 6, of which 6 were waited for; matrix products, arithmetic and copies ran while one was open for 0% of the time, Pallas kernels for 0%

commit v1 on v0

v1 whole, which is shorter than its diff:
```python
import math

import jax
import jax.numpy as jnp
from jax import lax
from jax.experimental import pallas as pl
from jax.experimental.pallas import tpu as pltpu
from jax.sharding import PartitionSpec as P

ITERS = 2


epsilon = 1e-06
step_rate = 0.5


def xor_move(block, axis, mask):
    count = lax.axis_size(axis)
    return lax.ppermute(block, axis, [(i, i ^ mask) for i in range(count)])


def after(value, *others):
    return lax.optimization_barrier((value,) + others)[0]


def total(values):
    for axis in ("row", "feat"):
        own = values
        for mask in reversed(range(1, lax.axis_size(axis))):
            values = lax.optimization_barrier(values + xor_move(own, axis, mask))
    return values


def join(*blocks):
    return jnp.concatenate(blocks, axis=0)


def split(pair):
    deep = pair.shape[0] // 2
    return pair[:deep], pair[deep:]


ARRIVALS = (
    ((0, 0), (1, 0), (2, 0), (3, 0), (0, 1), (0, 2)),
    ((0, 3), (3, 2), (1, 1), (1, 2), (2, 1), (2, 2)),
    ((3, 1), (3, 3), (1, 3), (2, 3)),
)


def gather(own):
    b = {(0, 0): own}
    b[0, 2] = xor_move(own, "feat", 2)
    b[0, 1] = xor_move(own, "feat", 1)
    for r in (3, 1, 2):
        b[r, 0] = xor_move(own, "row", r)
    b[3, 2] = xor_move(b[0, 2], "row", 3)
    b[0, 3] = xor_move(b[0, 2], "feat", 1)
    for r in (1, 2):
        b[r, 1], b[r, 2] = split(xor_move(join(b[0, 1], b[0, 2]), "row", r))
    b[3, 1], b[3, 3] = split(xor_move(join(b[3, 0], b[3, 2]), "feat", 1))
    for r in (1, 2):
        b[r, 3] = xor_move(b[0, 3], "row", r)
    return b


def scatter(b):
    def send(axis, mask, *blocks):
        half = [block.astype(jnp.bfloat16) for block in blocks]
        got = xor_move(half[0] if len(half) == 1 else join(*half), axis, mask)
        return [part.astype(jnp.float32) for part in (split(got) if len(half) > 1 else [got])]

    def summed(first, *others):
        return lax.optimization_barrier(sum(others, first).astype(jnp.bfloat16))

    near_across, far_across = send("feat", 1, b[3, 1], b[3, 3])
    (left,), (right,) = send("row", 1, b[1, 3]), send("row", 2, b[2, 3])
    ones, twos = zip(*[send("row", r, b[r, 1], b[r, 2]) for r in (1, 2)])
    far_across = summed(b[3, 2], far_across)
    three = summed(after(b[0, 3], far_across), left, right)
    near_across = summed(after(b[3, 0], three), near_across)
    (far_across,), (three,) = send("row", 3, far_across), send("feat", 1, three)
    two = summed(b[0, 2], *twos, far_across, three)
    one = summed(after(b[0, 1], two), *ones)
    (two,), (near_across,), (one,) = (
        send("feat", 2, two),
        send("row", 3, near_across),
        send("feat", 1, one),
    )
    near = b[0, 0] + send("row", 1, b[1, 0])[0] + send("row", 2, b[2, 0])[0]
    return near + near_across + one + two


def any_mesh(samples, own_rows):
    row_total = samples.shape[0] * lax.axis_size("row") * lax.axis_size("feat")
    width_root = math.sqrt(samples.shape[1])
    for sweep in range(ITERS):
        dirs = lax.all_gather(
            own_rows.astype(jnp.bfloat16), ("row", "feat"), axis=0, tiled=True
        )
        summed_proj = jnp.dot(samples, dirs, preferred_element_type=jnp.float32)
        squares = lax.psum(jnp.sum(summed_proj * summed_proj, axis=0), ("row", "feat"))
        scaling = lax.rsqrt(squares / row_total + epsilon)
        own_proj = (summed_proj * scaling).astype(jnp.bfloat16)
        partner_proj = xor_move(own_proj, "view", 1)
        residue = (own_proj.astype(jnp.float32) - partner_proj.astype(jnp.float32)).astype(
            jnp.bfloat16
        )
        share = lax.dot_general(
            samples, residue, (((0,), (0,)), ((), ())), preferred_element_type=jnp.float32
        )
        share = lax.psum_scatter(share, ("row", "feat"), scatter_dimension=0, tiled=True)
        own_rows = width_root * (own_rows * scaling - step_rate * (share / row_total))
    return (own_rows[None], own_proj[None])


def regroup(samples, depth):
    rows_here = samples.shape[0]
    feats = lax.axis_size("feat")
    count = sum(len(places) for places in ARRIVALS)

    def kernel(samples_ref, *refs):
        outs, done = refs[:-1], refs[-1]
        row_at, feat_at = lax.axis_index("row"), lax.axis_index("feat")
        copies = []
        for out, places in zip(outs, ARRIVALS):
            for i, (r, t) in enumerate(places):
                start = pl.multiple_of(((row_at ^ r) * feats + (feat_at ^ t)) * depth, depth)
                copies.append(
                    pltpu.make_async_copy(
                        samples_ref.at[:, pl.ds(start, depth)],
                        out.at[:, pl.ds(i * depth, depth)],
                        done.at[len(copies)],
                    )
                )
                copies[-1].start()
        for copy in copies:
            copy.wait()

    return pl.pallas_call(
        kernel,
        out_shape=[
            jax.ShapeDtypeStruct((rows_here, len(places) * depth), samples.dtype)
            for places in ARRIVALS
        ],
        in_specs=[pl.BlockSpec(memory_space=pl.ANY)],
        out_specs=[pl.BlockSpec(memory_space=pl.ANY) for places in ARRIVALS],
        scratch_shapes=[pltpu.SemaphoreType.DMA((count,))],
        compiler_params=pltpu.CompilerParams(vmem_limit_bytes=1 << 20),
        cost_estimate=pl.CostEstimate(
            flops=0, bytes_accessed=2 * samples.size * 2, transcendentals=0
        ),
        name="regroup",
    )(samples)


def on_device(views, weights):
    samples = views[0]
    own_rows = weights[0]
    rows_here, width = samples.shape
    depth, pairs = own_rows.shape
    rows, feats = lax.axis_size("row"), lax.axis_size("feat")
    if (rows, feats) != (4, 4) or depth % 128:
        return any_mesh(samples, own_rows)
    row_total = rows_here * rows * feats
    width_root = math.sqrt(width)
    groups = regroup(samples, depth)
    for sweep in range(ITERS):
        dirs = gather(own_rows.astype(jnp.bfloat16))
        summed_proj = 0.0
        for g, places in enumerate(ARRIVALS):
            blocks = lax.optimization_barrier([dirs[p] for p in places])
            part = jnp.dot(
                groups[g], join(*blocks), preferred_element_type=jnp.float32
            )
            summed_proj = lax.optimization_barrier(summed_proj + part) if g < 2 else summed_proj + part
        kept_proj = lax.optimization_barrier(summed_proj.astype(jnp.bfloat16))
        partner_proj = xor_move(kept_proj, "view", 1).astype(jnp.float32)
        squares = jnp.sum(summed_proj * summed_proj, axis=0)
        scaling = lax.rsqrt(total(squares) / row_total + epsilon)
        partner_scaling = xor_move(scaling, "view", 1)
        own_proj = (kept_proj.astype(jnp.float32) * scaling).astype(jnp.bfloat16)
        partner_proj = (partner_proj * partner_scaling).astype(jnp.bfloat16)
        residue = (own_proj.astype(jnp.float32) - partner_proj.astype(jnp.float32)).astype(
            jnp.bfloat16
        )
        shares = {}
        for g in (2, 1, 0):
            share = lax.dot_general(
                groups[g], residue, (((0,), (0,)), ((), ())), preferred_element_type=jnp.float32
            )
            for i, place in enumerate(ARRIVALS[g]):
                shares[place] = share[i * depth : (i + 1) * depth]
        if sweep == ITERS - 1:
            kept_proj, shown_scaling = lax.optimization_barrier((kept_proj, scaling))
            own_proj = (kept_proj.astype(jnp.float32) * shown_scaling).astype(jnp.bfloat16)
        grad = scatter(shares) / row_total
        own_rows = width_root * (own_rows * scaling - step_rate * grad)
    return (own_rows[None], own_proj[None])


def solution(mesh):
    in_specs = (P("view", ("row", "feat"), None), P("view", ("row", "feat"), None))
    out_specs = (P("view", ("row", "feat"), None), P("view", ("row", "feat"), None))
    return jax.shard_map(
        on_device, mesh=mesh, in_specs=in_specs, out_specs=out_specs, check_vma=False
    )
```

time: 446 us -> 145 us (0.33)
  waiting for transfers between devices: 322 us -> 52 us
  blocking collectives: 78.8 us -> 0 us
  starting transfers between devices: 0.31 us -> 73.7 us
  matrix products: 23.8 us -> 9.38 us
  between operations: 13.8 us -> 1.27 us
    reduce_scatter x2 -> x0, waiting for transfers between devices: 184 us -> none  [on_device(): lax.psum_scatter(lax.dot_general(samples, residue, (((0,), (0,)), ((), ()...]
    all_gather x2 -> x0, waiting for transfers between devices: 135 us -> none  [on_device(): whole_dirs = lax.all_gather(halved, ('row', 'feat'), axis=0, tiled=True)]
    psum x2 -> x0, blocking collectives: 78.8 us -> none  [on_device(): col_sums = lax.psum(squares, ('row', 'feat'))]
    ppermute x2 -> x64, starting transfers between devices: 0.14 us -> 73.7 us  [xor_move(): return lax.ppermute(block, axis, [(i, i ^ mask) for i in range(count)])]
    ppermute x2 -> x64, waiting for transfers between devices: 3.42 us -> 52 us  [xor_move(): return lax.ppermute(block, axis, [(i, i ^ mask) for i in range(count)])]
    dot_general x4 -> x12, matrix products: 23.8 us -> 9.38 us  [the longest x6 4.78 us: on_device(): lax.dot_general(groups[g], residue, (((0,), (0,)), ((), ())), preferred_e...]
  transfers between devices with their start and end apart: 6 -> 64, of which waited for: 6 -> 35; matrix products, arithmetic and copies ran while one was open for 0% -> 6% of each run, Pallas kernels for 0% -> 1%
where the time goes in v1:
time: 145 us
  starting transfers between devices  73.7 us (51%)
  waiting for transfers between devices  52 us (36%)
  matrix products  9.38 us (6%)
  local copies, waits for them, and re-layouts  6.22 us (4%)
    ppermute x64, starting transfers between devices, xor_move(): return lax.ppermute(block, axis, [(i, i ^ mask) for i in range(count)])  73.7 us
    ppermute x64, waiting for transfers between devices, xor_move(): return lax.ppermute(block, axis, [(i, i ^ mask) for i in range(count)])  52 us
    unnamed x27, local copies, waits for them, and re-layouts  5.86 us
    dot_general x6, matrix products, on_device(): lax.dot_general(groups[g], residue, (((0,), (0,)), ((), ())), preferred_e...  4.78 us
    dot_general x6, matrix products, on_device(): part = jnp.dot(groups[g], join(*blocks), preferred_element_type=jnp.float32)  4.6 us
  transfers between devices with their start and end apart: 64, of which 35 were waited for; matrix products, arithmetic and copies ran while one was open for 6% of the time, Pallas kernels for 1%

profile of v1, /device:TPU:0, one launch (start us, length us, event | category | flops | bytes accessed | tf_op | source)
XLA Modules:
  0.0 144.8 jit_solution(8278438872693328344)
XLA Ops:
  1.7 3.1 %collective-permute-start.3 = (bf16[256,256]{0,1:T(8,128)(2,1)S(1)}, bf16[256,256]{0,1:T(8,128)(2,1)S(1)}, u32[]{:S(2)}, u32[]{:S(2)}) collective-permute-start(bf16[256,256]{0,1:T(8,128)(2,1)S(1)} %bitcast_convert_fusion), channel_id=1, source_target_pairs={{0,1},{1,0},{2,3},{3,2},{4,5},{5,4},{6,7},{7,6},{8,9},{9,8},{10,11... | collective-permute-start | bytes 393224 | tf_op jit(solution)/shard_map/ppermute | solution.py:19
  4.8 2.6 %collective-permute-start.4 = (bf16[256,256]{0,1:T(8,128)(2,1)S(1)}, bf16[256,256]{0,1:T(8,128)(2,1)S(1)}, u32[]{:S(2)}, u32[]{:S(2)}) collective-permute-start(bf16[256,256]{0,1:T(8,128)(2,1)S(1)} %bitcast_convert_fusion), channel_id=1, source_target_pairs={{0,2},{1,3},{2,0},{3,1},{4,6},{5,7},{6,4},{7,5},{8,10},{9,11},{10,... | collective-permute-start | bytes 393224 | tf_op jit(solution)/shard_map/ppermute | solution.py:19
  7.4 2.4 %collective-permute-start.2 = (bf16[256,256]{0,1:T(8,128)(2,1)S(1)}, bf16[256,256]{0,1:T(8,128)(2,1)S(1)}, u32[]{:S(2)}, u32[]{:S(2)}) collective-permute-start(bf16[256,256]{0,1:T(8,128)(2,1)S(1)} %bitcast_convert_fusion), channel_id=1, source_target_pairs={{0,12},{4,8},{8,4},{12,0},{1,13},{5,9},{9,5},{13,1},{2,14},{6,10},... | collective-permute-start | bytes 393224 | tf_op jit(solution)/shard_map/ppermute | solution.py:19
  10.9 2.8 %copy-done = bf16[1,768,4096]{2,1,0:T(8,128)(2,1)S(1)} copy-done((bf16[1,768,4096]{2,1,0:T(8,128)(2,1)S(1)}, bf16[1,768,4096]{2,1,0:T(8,128)(2,1)}, u32[]{:S(2)}) %copy-start) | copy-done | bytes 6291480
  14.8 1.6 %collective-permute-start.8 = (bf16[512,256]{0,1:T(8,128)(2,1)S(1)}, bf16[512,256]{0,1:T(8,128)(2,1)S(1)}, u32[]{:S(2)}, u32[]{:S(2)}) collective-permute-start(bf16[512,256]{0,1:T(8,128)(2,1)S(1)} %constant_dynamic-update-slice_fusion.6), channel_id=1, source_target_pairs={{0,8},{4,12},{8,0},{12,4},{1,9},{5,13},{9,1},{13,5},{2,10},{6,14},... | collective-permute-start | bytes 786440 | tf_op jit(solution)/shard_map/ppermute | solution.py:19
  16.4 1.5 %collective-permute-start.7 = (bf16[512,256]{0,1:T(8,128)(2,1)S(1)}, bf16[512,256]{0,1:T(8,128)(2,1)S(1)}, u32[]{:S(2)}, u32[]{:S(2)}) collective-permute-start(bf16[512,256]{0,1:T(8,128)(2,1)S(1)} %constant_dynamic-update-slice_fusion.6), channel_id=1, source_target_pairs={{0,4},{4,0},{8,12},{12,8},{1,5},{5,1},{9,13},{13,9},{2,6},{6,2},{1... | collective-permute-start | bytes 786440 | tf_op jit(solution)/shard_map/ppermute | solution.py:19
  19.9 5.7 %collective-permute-done.6 = bf16[256,256]{0,1:T(8,128)(2,1)S(1)} collective-permute-done((bf16[256,256]{0,1:T(8,128)(2,1)S(1)}, bf16[256,256]{0,1:T(8,128)(2,1)S(1)}, u32[]{:S(2)}, u32[]{:S(2)}) %collective-permute-start.6) | collective-permute-done | bytes 131104 | tf_op jit(solution)/shard_map/ppermute | solution.py:19
  26.1 1.5 %collective-permute-start.11 = (bf16[256,256]{0,1:T(8,128)(2,1)S(1)}, bf16[256,256]{0,1:T(8,128)(2,1)S(1)}, u32[]{:S(2)}, u32[]{:S(2)}) collective-permute-start(bf16[256,256]{0,1:T(8,128)(2,1)S(1)} %collective-permute-done.5), channel_id=1, source_target_pairs={{0,8},{4,12},{8,0},{12,4},{1,9},{5,13},{9,1},{13,5},{2,10},{6,14},... | collective-permute-start | bytes 393224 | tf_op jit(solution)/shard_map/ppermute | solution.py:19
  27.6 1.5 %collective-permute-start.10 = (bf16[256,256]{0,1:T(8,128)(2,1)S(1)}, bf16[256,256]{0,1:T(8,128)(2,1)S(1)}, u32[]{:S(2)}, u32[]{:S(2)}) collective-permute-start(bf16[256,256]{0,1:T(8,128)(2,1)S(1)} %collective-permute-done.5), channel_id=1, source_target_pairs={{0,4},{4,0},{8,12},{12,8},{1,5},{5,1},{9,13},{13,9},{2,6},{6,2},{1... | collective-permute-start | bytes 393224 | tf_op jit(solution)/shard_map/ppermute | solution.py:19
  30.1 1.9 %collective-permute-done.9 = bf16[512,256]{0,1:T(8,128)(2,1)S(1)} collective-permute-done((bf16[512,256]{0,1:T(8,128)(2,1)S(1)}, bf16[512,256]{0,1:T(8,128)(2,1)S(1)}, u32[]{:S(2)}, u32[]{:S(2)}) %collective-permute-start.9) | collective-permute-done | bytes 262176 | tf_op jit(solution)/shard_map/ppermute | solution.py:19
  33.4 2.0 %collective-permute-start.12 = (f32[256]{0:T(256)S(1)}, f32[256]{0:T(256)S(1)}, u32[]{:S(2)}, u32[]{:S(2)}) collective-permute-start(f32[256]{0:T(256)S(1)} %get-tuple-element.112), channel_id=1, source_target_pairs={{0,12},{4,8},{8,4},{12,0},{1,13},{5,9},{9,5},{13,1},{2,14},{6,10},... | collective-permute-start | bytes 3080 | tf_op jit(solution)/shard_map/ppermute | solution.py:19
  40.0 1.3 collective-permute-start.15
  41.3 1.7 %collective-permute-start.16 = (f32[256]{0:T(256)S(1)}, f32[256]{0:T(256)S(1)}, u32[]{:S(2)}, u32[]{:S(2)}) collective-permute-start(f32[256]{0:T(256)S(1)} %add.148), channel_id=1, source_target_pairs={{0,2},{1,3},{2,0},{3,1},{4,6},{5,7},{6,4},{7,5},{8,10},{9,11},{10,... | collective-permute-start | bytes 3080 | tf_op jit(solution)/shard_map/ppermute | solution.py:19
  43.0 1.4 collective-permute-start.17
  49.6 1.8 %collective-permute-start.22 = (bf16[512,256]{0,1:T(8,128)(2,1)S(1)}, bf16[512,256]{0,1:T(8,128)(2,1)S(1)}, u32[]{:S(2)}, u32[]{:S(2)}) collective-permute-start(bf16[512,256]{0,1:T(8,128)(2,1)S(1)} %slice.262), channel_id=1, source_target_pairs={{0,1},{1,0},{2,3},{3,2},{4,5},{5,4},{6,7},{7,6},{8,9},{9,8},{10,11... | collective-permute-start | bytes 786440 | tf_op jit(solution)/shard_map/ppermute | solution.py:19
  52.3 1.6 %collective-permute-start.26 = (bf16[512,256]{0,1:T(8,128)(2,1)S(1)}, bf16[512,256]{0,1:T(8,128)(2,1)S(1)}, u32[]{:S(2)}, u32[]{:S(2)}) collective-permute-start(bf16[512,256]{0,1:T(8,128)(2,1)S(1)} %get-tuple-element.110), channel_id=1, source_target_pairs={{0,4},{4,0},{8,12},{12,8},{1,5},{5,1},{9,13},{13,9},{2,6},{6,2},{1... | collective-permute-start | bytes 786440 | tf_op jit(solution)/shard_map/ppermute | solution.py:19
  55.8 1.7 %collective-permute-done.22 = bf16[512,256]{0,1:T(8,128)(2,1)S(1)} collective-permute-done((bf16[512,256]{0,1:T(8,128)(2,1)S(1)}, bf16[512,256]{0,1:T(8,128)(2,1)S(1)}, u32[]{:S(2)}, u32[]{:S(2)}) %collective-permute-start.22) | collective-permute-done | bytes 262176 | tf_op jit(solution)/shard_map/ppermute | solution.py:19
  57.6 2.4 %collective-permute-start.28 = (bf16[256,256]{0,1:T(8,128)(2,1)S(1)}, bf16[256,256]{0,1:T(8,128)(2,1)S(1)}, u32[]{:S(2)}, u32[]{:S(2)}) collective-permute-start(bf16[256,256]{0,1:T(8,128)(2,1)S(1)} %get-tuple-element.100), channel_id=1, source_target_pairs={{0,12},{4,8},{8,4},{12,0},{1,13},{5,9},{9,5},{13,1},{2,14},{6,10},... | collective-permute-start | bytes 393224 | tf_op jit(solution)/shard_map/ppermute | solution.py:19
  60.0 1.4 collective-permute-start.29
  63.1 1.3 collective-permute-done.27
  65.3 1.6 %collective-permute-start.25 = (bf16[256,256]{0,1:T(8,128)(2,1)S(1)}, bf16[256,256]{0,1:T(8,128)(2,1)S(1)}, u32[]{:S(2)}, u32[]{:S(2)}) collective-permute-start(bf16[256,256]{0,1:T(8,128)(2,1)S(1)} %add_convert_fusion.4), channel_id=1, source_target_pairs={{0,12},{4,8},{8,4},{12,0},{1,13},{5,9},{9,5},{13,1},{2,14},{6,10},... | collective-permute-start | bytes 393224 | tf_op jit(solution)/shard_map/ppermute | solution.py:19
  69.1 2.1 %collective-permute-done.25 = bf16[256,256]{0,1:T(8,128)(2,1)S(1)} collective-permute-done((bf16[256,256]{0,1:T(8,128)(2,1)S(1)}, bf16[256,256]{0,1:T(8,128)(2,1)S(1)}, u32[]{:S(2)}, u32[]{:S(2)}) %collective-permute-start.25) | collective-permute-done | bytes 131104 | tf_op jit(solution)/shard_map/ppermute | solution.py:19
  72.2 3.6 %collective-permute-done.31 = bf16[256,256]{0,1:T(8,128)(2,1)S(1)} collective-permute-done((bf16[256,256]{0,1:T(8,128)(2,1)S(1)}, bf16[256,256]{0,1:T(8,128)(2,1)S(1)}, u32[]{:S(2)}, u32[]{:S(2)}) %collective-permute-start.31) | collective-permute-done | bytes 131104 | tf_op jit(solution)/shard_map/ppermute | solution.py:19
  76.1 1.8 %collective-permute-start.36 = (bf16[256,256]{0,1:T(8,128)(2,1)S(1)}, bf16[256,256]{0,1:T(8,128)(2,1)S(1)}, u32[]{:S(2)}, u32[]{:S(2)}) collective-permute-start(bf16[256,256]{0,1:T(8,128)(2,1)S(1)} %get-tuple-element.67), channel_id=1, source_target_pairs={{0,2},{1,3},{2,0},{3,1},{4,6},{5,7},{6,4},{7,5},{8,10},{9,11},{10,... | collective-permute-start | bytes 393224 | tf_op jit(solution)/shard_map/ppermute | solution.py:19
  77.9 1.4 collective-permute-start.34
  79.2 1.3 collective-permute-start.33
  82.5 1.2 collective-permute-start.40
  86.3 1.7 %collective-permute-done.32 = bf16[256,256]{0,1:T(8,128)(2,1)S(1)} collective-permute-done((bf16[256,256]{0,1:T(8,128)(2,1)S(1)}, bf16[256,256]{0,1:T(8,128)(2,1)S(1)}, u32[]{:S(2)}, u32[]{:S(2)}) %collective-permute-start.32) | collective-permute-done | bytes 131104 | tf_op jit(solution)/shard_map/ppermute | solution.py:19
  88.1 1.2 collective-permute-start.38
  90.2 4.3 %collective-permute-done.38 = bf16[256,256]{0,1:T(8,128)(2,1)S(1)} collective-permute-done((bf16[256,256]{0,1:T(8,128)(2,1)S(1)}, bf16[256,256]{0,1:T(8,128)(2,1)S(1)}, u32[]{:S(2)}, u32[]{:S(2)}) %collective-permute-start.38) | collective-permute-done | bytes 131104 | tf_op jit(solution)/shard_map/ppermute | solution.py:19
  96.4 1.5 %collective-permute-start.42 = (bf16[256,256]{0,1:T(8,128)(2,1)S(1)}, bf16[256,256]{0,1:T(8,128)(2,1)S(1)}, u32[]{:S(2)}, u32[]{:S(2)}) collective-permute-start(bf16[256,256]{0,1:T(8,128)(2,1)S(1)} %collective-permute-done.37), channel_id=1, source_target_pairs={{0,4},{4,0},{8,12},{12,8},{1,5},{5,1},{9,13},{13,9},{2,6},{6,2},{1... | collective-permute-start | bytes 393224 | tf_op jit(solution)/shard_map/ppermute | solution.py:19
  98.9 2.0 %collective-permute-done.41 = bf16[512,256]{0,1:T(8,128)(2,1)S(1)} collective-permute-done((bf16[512,256]{0,1:T(8,128)(2,1)S(1)}, bf16[512,256]{0,1:T(8,128)(2,1)S(1)}, u32[]{:S(2)}, u32[]{:S(2)}) %collective-permute-start.41) | collective-permute-done | bytes 262176 | tf_op jit(solution)/shard_map/ppermute | solution.py:19
  102.1 1.6 %collective-permute-start.44 = (f32[256]{0:T(256)S(1)}, f32[256]{0:T(256)S(1)}, u32[]{:S(2)}, u32[]{:S(2)}) collective-permute-start(f32[256]{0:T(256)S(1)} %get-tuple-element.106), channel_id=1, source_target_pairs={{0,12},{4,8},{8,4},{12,0},{1,13},{5,9},{9,5},{13,1},{2,14},{6,10},... | collective-permute-start | bytes 3080 | tf_op jit(solution)/shard_map/ppermute | solution.py:19
  103.7 1.4 collective-permute-start.45
  107.3 1.4 collective-permute-done.46
  108.7 2.0 %collective-permute-start.47 = (f32[256]{0:T(256)S(1)}, f32[256]{0:T(256)S(1)}, u32[]{:S(2)}, u32[]{:S(2)}) collective-permute-start(f32[256]{0:T(256)S(1)} %add.172), channel_id=1, source_target_pairs={{0,3},{1,2},{2,1},{3,0},{4,7},{5,6},{6,5},{7,4},{8,11},{9,10},{10,... | collective-permute-start | bytes 3080 | tf_op jit(solution)/shard_map/ppermute | solution.py:19
  110.7 2.4 %collective-permute-start.49 = (f32[256]{0:T(256)S(1)}, f32[256]{0:T(256)S(1)}, u32[]{:S(2)}, u32[]{:S(2)}) collective-permute-start(f32[256]{0:T(256)S(1)} %add.172), channel_id=1, source_target_pairs={{0,1},{1,0},{2,3},{3,2},{4,5},{5,4},{6,7},{7,6},{8,9},{9,8},{10,11... | collective-permute-start | bytes 3080 | tf_op jit(solution)/shard_map/ppermute | solution.py:19
  118.6 1.2 collective-permute-start.56
  119.8 1.6 %collective-permute-start.54 = (bf16[512,256]{0,1:T(8,128)(2,1)S(1)}, bf16[512,256]{0,1:T(8,128)(2,1)S(1)}, u32[]{:S(2)}, u32[]{:S(2)}) collective-permute-start(bf16[512,256]{0,1:T(8,128)(2,1)S(1)} %slice.287), channel_id=1, source_target_pairs={{0,1},{1,0},{2,3},{3,2},{4,5},{5,4},{6,7},{7,6},{8,9},{9,8},{10,11... | collective-permute-start | bytes 786440 | tf_op jit(solution)/shard_map/ppermute | solution.py:19
  122.2 1.4 collective-permute-start.59
  124.6 3.1 %collective-permute-done.54 = bf16[512,256]{0,1:T(8,128)(2,1)S(1)} collective-permute-done((bf16[512,256]{0,1:T(8,128)(2,1)S(1)}, bf16[512,256]{0,1:T(8,128)(2,1)S(1)}, u32[]{:S(2)}, u32[]{:S(2)}) %collective-permute-start.54) | collective-permute-done | bytes 262176 | tf_op jit(solution)/shard_map/ppermute | solution.py:19
  127.7 1.9 %collective-permute-start.60 = (bf16[256,256]{0,1:T(8,128)(2,1)S(1)}, bf16[256,256]{0,1:T(8,128)(2,1)S(1)}, u32[]{:S(2)}, u32[]{:S(2)}) collective-permute-start(bf16[256,256]{0,1:T(8,128)(2,1)S(1)} %get-tuple-element.95), channel_id=1, source_target_pairs={{0,12},{4,8},{8,4},{12,0},{1,13},{5,9},{9,5},{13,1},{2,14},{6,10},... | collective-permute-start | bytes 393224 | tf_op jit(solution)/shard_map/ppermute | solution.py:19
  129.7 1.5 %collective-permute-start.61 = (bf16[256,256]{0,1:T(8,128)(2,1)S(1)}, bf16[256,256]{0,1:T(8,128)(2,1)S(1)}, u32[]{:S(2)}, u32[]{:S(2)}) collective-permute-start(bf16[256,256]{0,1:T(8,128)(2,1)S(1)} %add_convert_fusion.2), channel_id=1, source_target_pairs={{0,1},{1,0},{2,3},{3,2},{4,5},{5,4},{6,7},{7,6},{8,9},{9,8},{10,11... | collective-permute-start | bytes 393224 | tf_op jit(solution)/shard_map/ppermute | solution.py:19
  131.8 1.3 collective-permute-start.53
  133.1 1.6 %collective-permute-done.61 = bf16[256,256]{0,1:T(8,128)(2,1)S(1)} collective-permute-done((bf16[256,256]{0,1:T(8,128)(2,1)S(1)}, bf16[256,256]{0,1:T(8,128)(2,1)S(1)}, u32[]{:S(2)}, u32[]{:S(2)}) %collective-permute-start.61) | collective-permute-done | bytes 131104 | tf_op jit(solution)/shard_map/ppermute | solution.py:19
  135.1 1.8 %collective-permute-start.63 = (bf16[256,256]{0,1:T(8,128)(2,1)S(1)}, bf16[256,256]{0,1:T(8,128)(2,1)S(1)}, u32[]{:S(2)}, u32[]{:S(2)}) collective-permute-start(bf16[256,256]{0,1:T(8,128)(2,1)S(1)} %get-tuple-element.93), channel_id=1, source_target_pairs={{0,2},{1,3},{2,0},{3,1},{4,6},{5,7},{6,4},{7,5},{8,10},{9,11},{10,... | collective-permute-start | bytes 393224 | tf_op jit(solution)/shard_map/ppermute | solution.py:19
  137.0 1.5 %collective-permute-start.57 = (bf16[256,256]{0,1:T(8,128)(2,1)S(1)}, bf16[256,256]{0,1:T(8,128)(2,1)S(1)}, u32[]{:S(2)}, u32[]{:S(2)}) collective-permute-start(bf16[256,256]{0,1:T(8,128)(2,1)S(1)} %add_convert_fusion.1), channel_id=1, source_target_pairs={{0,12},{4,8},{8,4},{12,0},{1,13},{5,9},{9,5},{13,1},{2,14},{6,10},... | collective-permute-start | bytes 393224 | tf_op jit(solution)/shard_map/ppermute | solution.py:19
  140.3 2.6 %collective-permute-done.57 = bf16[256,256]{0,1:T(8,128)(2,1)S(1)} collective-permute-done((bf16[256,256]{0,1:T(8,128)(2,1)S(1)}, bf16[256,256]{0,1:T(8,128)(2,1)S(1)}, u32[]{:S(2)}, u32[]{:S(2)}) %collective-permute-start.57) | collective-permute-done | bytes 131104 | tf_op jit(solution)/shard_map/ppermute | solution.py:19
  (170 shorter events, 50.2 us)
Async XLA Ops:
  1.7 13.0 %collective-permute-start.3 = (bf16[256,256]{0,1:T(8,128)(2,1)S(1)}, bf16[256,256]{0,1:T(8,128)(2,1)S(1)}, u32[]{:S(2)}, u32[]{:S(2)}) collective-permute-start(bf16[256,256]{0,1:T(8,128)(2,1)S(1)} %bitcast_convert_fusion), channel_id=1, source_target_pairs={{0,1},{1,0},{2,3},{3,2},{4,5},{5,4},{6,7},{7,6},{8,9},{9,8},{10,11... | collective-permute-start | bytes 393224 | tf_op jit(solution)/shard_map/ppermute | solution.py:19
  4.8 10.0 %collective-permute-start.4 = (bf16[256,256]{0,1:T(8,128)(2,1)S(1)}, bf16[256,256]{0,1:T(8,128)(2,1)S(1)}, u32[]{:S(2)}, u32[]{:S(2)}) collective-permute-start(bf16[256,256]{0,1:T(8,128)(2,1)S(1)} %bitcast_convert_fusion), channel_id=1, source_target_pairs={{0,2},{1,3},{2,0},{3,1},{4,6},{5,7},{6,4},{7,5},{8,10},{9,11},{10,... | collective-permute-start | bytes 393224 | tf_op jit(solution)/shard_map/ppermute | solution.py:19
  7.4 10.5 %collective-permute-start.2 = (bf16[256,256]{0,1:T(8,128)(2,1)S(1)}, bf16[256,256]{0,1:T(8,128)(2,1)S(1)}, u32[]{:S(2)}, u32[]{:S(2)}) collective-permute-start(bf16[256,256]{0,1:T(8,128)(2,1)S(1)} %bitcast_convert_fusion), channel_id=1, source_target_pairs={{0,12},{4,8},{8,4},{12,0},{1,13},{5,9},{9,5},{13,1},{2,14},{6,10},... | collective-permute-start | bytes 393224 | tf_op jit(solution)/shard_map/ppermute | solution.py:19
  9.9 8.0 %collective-permute-start.1 = (bf16[256,256]{0,1:T(8,128)(2,1)S(1)}, bf16[256,256]{0,1:T(8,128)(2,1)S(1)}, u32[]{:S(2)}, u32[]{:S(2)}) collective-permute-start(bf16[256,256]{0,1:T(8,128)(2,1)S(1)} %bitcast_convert_fusion), channel_id=1, source_target_pairs={{0,8},{4,12},{8,0},{12,4},{1,9},{5,13},{9,1},{13,5},{2,10},{6,14},... | collective-permute-start | bytes 393224 | tf_op jit(solution)/shard_map/ppermute | solution.py:19
  10.4 7.5 %collective-permute-start = (bf16[256,256]{0,1:T(8,128)(2,1)S(1)}, bf16[256,256]{0,1:T(8,128)(2,1)S(1)}, u32[]{:S(2)}, u32[]{:S(2)}) collective-permute-start(bf16[256,256]{0,1:T(8,128)(2,1)S(1)} %bitcast_convert_fusion), channel_id=1, source_target_pairs={{0,4},{4,0},{8,12},{12,8},{1,5},{5,1},{9,13},{13,9},{2,6},{6,2},{1... | collective-permute-start | bytes 393224 | tf_op jit(solution)/shard_map/ppermute | solution.py:19
  14.8 14.3 %collective-permute-start.8 = (bf16[512,256]{0,1:T(8,128)(2,1)S(1)}, bf16[512,256]{0,1:T(8,128)(2,1)S(1)}, u32[]{:S(2)}, u32[]{:S(2)}) collective-permute-start(bf16[512,256]{0,1:T(8,128)(2,1)S(1)} %constant_dynamic-update-slice_fusion.6), channel_id=1, source_target_pairs={{0,8},{4,12},{8,0},{12,4},{1,9},{5,13},{9,1},{13,5},{2,10},{6,14},... | collective-permute-start | bytes 786440 | tf_op jit(solution)/shard_map/ppermute | solution.py:19
  16.4 12.7 %collective-permute-start.7 = (bf16[512,256]{0,1:T(8,128)(2,1)S(1)}, bf16[512,256]{0,1:T(8,128)(2,1)S(1)}, u32[]{:S(2)}, u32[]{:S(2)}) collective-permute-start(bf16[512,256]{0,1:T(8,128)(2,1)S(1)} %constant_dynamic-update-slice_fusion.6), channel_id=1, source_target_pairs={{0,4},{4,0},{8,12},{12,8},{1,5},{5,1},{9,13},{13,9},{2,6},{6,2},{1... | collective-permute-start | bytes 786440 | tf_op jit(solution)/shard_map/ppermute | solution.py:19
  18.0 7.5 %collective-permute-start.6 = (bf16[256,256]{0,1:T(8,128)(2,1)S(1)}, bf16[256,256]{0,1:T(8,128)(2,1)S(1)}, u32[]{:S(2)}, u32[]{:S(2)}) collective-permute-start(bf16[256,256]{0,1:T(8,128)(2,1)S(1)} %collective-permute-done.4), channel_id=1, source_target_pairs={{0,12},{4,8},{8,4},{12,0},{1,13},{5,9},{9,5},{13,1},{2,14},{6,10},... | collective-permute-start | bytes 393224 | tf_op jit(solution)/shard_map/ppermute | solution.py:19
  18.6 7.5 %collective-permute-start.5 = (bf16[256,256]{0,1:T(8,128)(2,1)S(1)}, bf16[256,256]{0,1:T(8,128)(2,1)S(1)}, u32[]{:S(2)}, u32[]{:S(2)}) collective-permute-start(bf16[256,256]{0,1:T(8,128)(2,1)S(1)} %collective-permute-done.4), channel_id=1, source_target_pairs={{0,1},{1,0},{2,3},{3,2},{4,5},{5,4},{6,7},{7,6},{8,9},{9,8},{10,11... | collective-permute-start | bytes 393224 | tf_op jit(solution)/shard_map/ppermute | solution.py:19
  25.6 6.4 %collective-permute-start.9 = (bf16[512,256]{0,1:T(8,128)(2,1)S(1)}, bf16[512,256]{0,1:T(8,128)(2,1)S(1)}, u32[]{:S(2)}, u32[]{:S(2)}) collective-permute-start(bf16[512,256]{0,1:T(8,128)(2,1)S(1)} %pad_maximum_fusion), channel_id=1, source_target_pairs={{0,1},{1,0},{2,3},{3,2},{4,5},{5,4},{6,7},{7,6},{8,9},{9,8},{10,11... | collective-permute-start | bytes 786440 | tf_op jit(solution)/shard_map/ppermute | solution.py:19
  26.1 5.9 %collective-permute-start.11 = (bf16[256,256]{0,1:T(8,128)(2,1)S(1)}, bf16[256,256]{0,1:T(8,128)(2,1)S(1)}, u32[]{:S(2)}, u32[]{:S(2)}) collective-permute-start(bf16[256,256]{0,1:T(8,128)(2,1)S(1)} %collective-permute-done.5), channel_id=1, source_target_pairs={{0,8},{4,12},{8,0},{12,4},{1,9},{5,13},{9,1},{13,5},{2,10},{6,14},... | collective-permute-start | bytes 393224 | tf_op jit(solution)/shard_map/ppermute | solution.py:19
  33.3 14.5 %collective-permute-start.18 = (bf16[768,256]{0,1:T(8,128)(2,1)S(1)}, bf16[768,256]{0,1:T(8,128)(2,1)S(1)}, u32[]{:S(2)}, u32[]{:S(2)}) collective-permute-start(bf16[768,256]{0,1:T(8,128)(2,1)S(1)} %get-tuple-element.113), channel_id=1, source_target_pairs={{0,16},{16,0},{1,17},{17,1},{2,18},{18,2},{3,19},{19,3},{4,20},{20... | collective-permute-start | bytes 1179656 | tf_op jit(solution)/shard_map/ppermute | solution.py:19
  40.0 5.4 %collective-permute-start.15 = (f32[256]{0:T(256)S(1)}, f32[256]{0:T(256)S(1)}, u32[]{:S(2)}, u32[]{:S(2)}) collective-permute-start(f32[256]{0:T(256)S(1)} %add.148), channel_id=1, source_target_pairs={{0,3},{1,2},{2,1},{3,0},{4,7},{5,6},{6,5},{7,4},{8,11},{9,10},{10,... | collective-permute-start | bytes 3080 | tf_op jit(solution)/shard_map/ppermute | solution.py:19
  48.4 11.5 %collective-permute-start.23 = (bf16[256,256]{0,1:T(8,128)(2,1)S(1)}, bf16[256,256]{0,1:T(8,128)(2,1)S(1)}, u32[]{:S(2)}, u32[]{:S(2)}) collective-permute-start(bf16[256,256]{0,1:T(8,128)(2,1)S(1)} %get-tuple-element.116), channel_id=1, source_target_pairs={{0,4},{4,0},{8,12},{12,8},{1,5},{5,1},{9,13},{13,9},{2,6},{6,2},{1... | collective-permute-start | bytes 393224 | tf_op jit(solution)/shard_map/ppermute | solution.py:19
  49.1 10.9 %collective-permute-start.24 = (bf16[256,256]{0,1:T(8,128)(2,1)S(1)}, bf16[256,256]{0,1:T(8,128)(2,1)S(1)}, u32[]{:S(2)}, u32[]{:S(2)}) collective-permute-start(bf16[256,256]{0,1:T(8,128)(2,1)S(1)} %get-tuple-element.117), channel_id=1, source_target_pairs={{0,8},{4,12},{8,0},{12,4},{1,9},{5,13},{9,1},{13,5},{2,10},{6,14},... | collective-permute-start | bytes 393224 | tf_op jit(solution)/shard_map/ppermute | solution.py:19
  49.6 7.9 %collective-permute-start.22 = (bf16[512,256]{0,1:T(8,128)(2,1)S(1)}, bf16[512,256]{0,1:T(8,128)(2,1)S(1)}, u32[]{:S(2)}, u32[]{:S(2)}) collective-permute-start(bf16[512,256]{0,1:T(8,128)(2,1)S(1)} %slice.262), channel_id=1, source_target_pairs={{0,1},{1,0},{2,3},{3,2},{4,5},{5,4},{6,7},{7,6},{8,9},{9,8},{10,11... | collective-permute-start | bytes 786440 | tf_op jit(solution)/shard_map/ppermute | solution.py:19
  52.3 9.8 %collective-permute-start.26 = (bf16[512,256]{0,1:T(8,128)(2,1)S(1)}, bf16[512,256]{0,1:T(8,128)(2,1)S(1)}, u32[]{:S(2)}, u32[]{:S(2)}) collective-permute-start(bf16[512,256]{0,1:T(8,128)(2,1)S(1)} %get-tuple-element.110), channel_id=1, source_target_pairs={{0,4},{4,0},{8,12},{12,8},{1,5},{5,1},{9,13},{13,9},{2,6},{6,2},{1... | collective-permute-start | bytes 786440 | tf_op jit(solution)/shard_map/ppermute | solution.py:19
  53.9 10.5 %collective-permute-start.27 = (bf16[512,256]{0,1:T(8,128)(2,1)S(1)}, bf16[512,256]{0,1:T(8,128)(2,1)S(1)}, u32[]{:S(2)}, u32[]{:S(2)}) collective-permute-start(bf16[512,256]{0,1:T(8,128)(2,1)S(1)} %get-tuple-element.111), channel_id=1, source_target_pairs={{0,8},{4,12},{8,0},{12,4},{1,9},{5,13},{9,1},{13,5},{2,10},{6,14},... | collective-permute-start | bytes 786440 | tf_op jit(solution)/shard_map/ppermute | solution.py:19
  57.6 7.5 %collective-permute-start.28 = (bf16[256,256]{0,1:T(8,128)(2,1)S(1)}, bf16[256,256]{0,1:T(8,128)(2,1)S(1)}, u32[]{:S(2)}, u32[]{:S(2)}) collective-permute-start(bf16[256,256]{0,1:T(8,128)(2,1)S(1)} %get-tuple-element.100), channel_id=1, source_target_pairs={{0,12},{4,8},{8,4},{12,0},{1,13},{5,9},{9,5},{13,1},{2,14},{6,10},... | collective-permute-start | bytes 393224 | tf_op jit(solution)/shard_map/ppermute | solution.py:19
  61.5 7.7 %collective-permute-start.20 = (bf16[256,256]{0,1:T(8,128)(2,1)S(1)}, bf16[256,256]{0,1:T(8,128)(2,1)S(1)}, u32[]{:S(2)}, u32[]{:S(2)}) collective-permute-start(bf16[256,256]{0,1:T(8,128)(2,1)S(1)} %get-tuple-element.108), channel_id=1, source_target_pairs={{0,4},{4,0},{8,12},{12,8},{1,5},{5,1},{9,13},{13,9},{2,6},{6,2},{1... | collective-permute-start | bytes 393224 | tf_op jit(solution)/shard_map/ppermute | solution.py:19
  62.1 7.1 %collective-permute-start.21 = (bf16[256,256]{0,1:T(8,128)(2,1)S(1)}, bf16[256,256]{0,1:T(8,128)(2,1)S(1)}, u32[]{:S(2)}, u32[]{:S(2)}) collective-permute-start(bf16[256,256]{0,1:T(8,128)(2,1)S(1)} %get-tuple-element.109), channel_id=1, source_target_pairs={{0,8},{4,12},{8,0},{12,4},{1,9},{5,13},{9,1},{13,5},{2,10},{6,14},... | collective-permute-start | bytes 393224 | tf_op jit(solution)/shard_map/ppermute | solution.py:19
  65.3 5.9 %collective-permute-start.25 = (bf16[256,256]{0,1:T(8,128)(2,1)S(1)}, bf16[256,256]{0,1:T(8,128)(2,1)S(1)}, u32[]{:S(2)}, u32[]{:S(2)}) collective-permute-start(bf16[256,256]{0,1:T(8,128)(2,1)S(1)} %add_convert_fusion.4), channel_id=1, source_target_pairs={{0,12},{4,8},{8,4},{12,0},{1,13},{5,9},{9,5},{13,1},{2,14},{6,10},... | collective-permute-start | bytes 393224 | tf_op jit(solution)/shard_map/ppermute | solution.py:19
  66.9 5.3 %collective-permute-start.30 = (bf16[256,256]{0,1:T(8,128)(2,1)S(1)}, bf16[256,256]{0,1:T(8,128)(2,1)S(1)}, u32[]{:S(2)}, u32[]{:S(2)}) collective-permute-start(bf16[256,256]{0,1:T(8,128)(2,1)S(1)} %add_convert_fusion.3), channel_id=1, source_target_pairs={{0,1},{1,0},{2,3},{3,2},{4,5},{5,4},{6,7},{7,6},{8,9},{9,8},{10,11... | collective-permute-start | bytes 393224 | tf_op jit(solution)/shard_map/ppermute | solution.py:19
  68.1 7.8 %collective-permute-start.31 = (bf16[256,256]{0,1:T(8,128)(2,1)S(1)}, bf16[256,256]{0,1:T(8,128)(2,1)S(1)}, u32[]{:S(2)}, u32[]{:S(2)}) collective-permute-start(bf16[256,256]{0,1:T(8,128)(2,1)S(1)} %get-tuple-element.98), channel_id=1, source_target_pairs={{0,2},{1,3},{2,0},{3,1},{4,6},{5,7},{6,4},{7,5},{8,10},{9,11},{10,... | collective-permute-start | bytes 393224 | tf_op jit(solution)/shard_map/ppermute | solution.py:19
  76.0 6.4 %collective-permute-start.35 = (bf16[256,256]{0,1:T(8,128)(2,1)S(1)}, bf16[256,256]{0,1:T(8,128)(2,1)S(1)}, u32[]{:S(2)}, u32[]{:S(2)}) collective-permute-start(bf16[256,256]{0,1:T(8,128)(2,1)S(1)} %get-tuple-element.67), channel_id=1, source_target_pairs={{0,1},{1,0},{2,3},{3,2},{4,5},{5,4},{6,7},{7,6},{8,9},{9,8},{10,11... | collective-permute-start | bytes 393224 | tf_op jit(solution)/shard_map/ppermute | solution.py:19
  76.1 6.4 %collective-permute-start.36 = (bf16[256,256]{0,1:T(8,128)(2,1)S(1)}, bf16[256,256]{0,1:T(8,128)(2,1)S(1)}, u32[]{:S(2)}, u32[]{:S(2)}) collective-permute-start(bf16[256,256]{0,1:T(8,128)(2,1)S(1)} %get-tuple-element.67), channel_id=1, source_target_pairs={{0,2},{1,3},{2,0},{3,1},{4,6},{5,7},{6,4},{7,5},{8,10},{9,11},{10,... | collective-permute-start | bytes 393224 | tf_op jit(solution)/shard_map/ppermute | solution.py:19
  77.9 7.2 %collective-permute-start.34 = (bf16[256,256]{0,1:T(8,128)(2,1)S(1)}, bf16[256,256]{0,1:T(8,128)(2,1)S(1)}, u32[]{:S(2)}, u32[]{:S(2)}) collective-permute-start(bf16[256,256]{0,1:T(8,128)(2,1)S(1)} %get-tuple-element.67), channel_id=1, source_target_pairs={{0,12},{4,8},{8,4},{12,0},{1,13},{5,9},{9,5},{13,1},{2,14},{6,10},... | collective-permute-start | bytes 393224 | tf_op jit(solution)/shard_map/ppermute | solution.py:19
  79.2 7.0 %collective-permute-start.33 = (bf16[256,256]{0,1:T(8,128)(2,1)S(1)}, bf16[256,256]{0,1:T(8,128)(2,1)S(1)}, u32[]{:S(2)}, u32[]{:S(2)}) collective-permute-start(bf16[256,256]{0,1:T(8,128)(2,1)S(1)} %get-tuple-element.67), channel_id=1, source_target_pairs={{0,8},{4,12},{8,0},{12,4},{1,9},{5,13},{9,1},{13,5},{2,10},{6,14},... | collective-permute-start | bytes 393224 | tf_op jit(solution)/shard_map/ppermute | solution.py:19
  80.6 7.4 %collective-permute-start.32 = (bf16[256,256]{0,1:T(8,128)(2,1)S(1)}, bf16[256,256]{0,1:T(8,128)(2,1)S(1)}, u32[]{:S(2)}, u32[]{:S(2)}) collective-permute-start(bf16[256,256]{0,1:T(8,128)(2,1)S(1)} %get-tuple-element.67), channel_id=1, source_target_pairs={{0,4},{4,0},{8,12},{12,8},{1,5},{5,1},{9,13},{13,9},{2,6},{6,2},{1... | collective-permute-start | bytes 393224 | tf_op jit(solution)/shard_map/ppermute | solution.py:19
  82.5 15.4 %collective-permute-start.40 = (bf16[512,256]{0,1:T(8,128)(2,1)S(1)}, bf16[512,256]{0,1:T(8,128)(2,1)S(1)}, u32[]{:S(2)}, u32[]{:S(2)}) collective-permute-start(bf16[512,256]{0,1:T(8,128)(2,1)S(1)} %constant_dynamic-update-slice_fusion.20), channel_id=1, source_target_pairs={{0,8},{4,12},{8,0},{12,4},{1,9},{5,13},{9,1},{13,5},{2,10},{6,14},... | collective-permute-start | bytes 786440 | tf_op jit(solution)/shard_map/ppermute | solution.py:19
  83.7 14.3 %collective-permute-start.39 = (bf16[512,256]{0,1:T(8,128)(2,1)S(1)}, bf16[512,256]{0,1:T(8,128)(2,1)S(1)}, u32[]{:S(2)}, u32[]{:S(2)}) collective-permute-start(bf16[512,256]{0,1:T(8,128)(2,1)S(1)} %constant_dynamic-update-slice_fusion.20), channel_id=1, source_target_pairs={{0,4},{4,0},{8,12},{12,8},{1,5},{5,1},{9,13},{13,9},{2,6},{6,2},{1... | collective-permute-start | bytes 786440 | tf_op jit(solution)/shard_map/ppermute | solution.py:19
  88.1 6.4 %collective-permute-start.38 = (bf16[256,256]{0,1:T(8,128)(2,1)S(1)}, bf16[256,256]{0,1:T(8,128)(2,1)S(1)}, u32[]{:S(2)}, u32[]{:S(2)}) collective-permute-start(bf16[256,256]{0,1:T(8,128)(2,1)S(1)} %collective-permute-done.36), channel_id=1, source_target_pairs={{0,12},{4,8},{8,4},{12,0},{1,13},{5,9},{9,5},{13,1},{2,14},{6,10},... | collective-permute-start | bytes 393224 | tf_op jit(solution)/shard_map/ppermute | solution.py:19
  89.3 6.3 %collective-permute-start.37 = (bf16[256,256]{0,1:T(8,128)(2,1)S(1)}, bf16[256,256]{0,1:T(8,128)(2,1)S(1)}, u32[]{:S(2)}, u32[]{:S(2)}) collective-permute-start(bf16[256,256]{0,1:T(8,128)(2,1)S(1)} %collective-permute-done.36), channel_id=1, source_target_pairs={{0,1},{1,0},{2,3},{3,2},{4,5},{5,4},{6,7},{7,6},{8,9},{9,8},{10,11... | collective-permute-start | bytes 393224 | tf_op jit(solution)/shard_map/ppermute | solution.py:19
  94.5 6.4 %collective-permute-start.41 = (bf16[512,256]{0,1:T(8,128)(2,1)S(1)}, bf16[512,256]{0,1:T(8,128)(2,1)S(1)}, u32[]{:S(2)}, u32[]{:S(2)}) collective-permute-start(bf16[512,256]{0,1:T(8,128)(2,1)S(1)} %pad_maximum_fusion.1), channel_id=1, source_target_pairs={{0,1},{1,0},{2,3},{3,2},{4,5},{5,4},{6,7},{7,6},{8,9},{9,8},{10,11... | collective-permute-start | bytes 786440 | tf_op jit(solution)/shard_map/ppermute | solution.py:19
  95.6 5.3 %collective-permute-start.43 = (bf16[256,256]{0,1:T(8,128)(2,1)S(1)}, bf16[256,256]{0,1:T(8,128)(2,1)S(1)}, u32[]{:S(2)}, u32[]{:S(2)}) collective-permute-start(bf16[256,256]{0,1:T(8,128)(2,1)S(1)} %collective-permute-done.37), channel_id=1, source_target_pairs={{0,8},{4,12},{8,0},{12,4},{1,9},{5,13},{9,1},{13,5},{2,10},{6,14},... | collective-permute-start | bytes 393224 | tf_op jit(solution)/shard_map/ppermute | solution.py:19
  102.0 14.4 %collective-permute-start.50 = (bf16[768,256]{0,1:T(8,128)(2,1)S(1)}, bf16[768,256]{0,1:T(8,128)(2,1)S(1)}, u32[]{:S(2)}, u32[]{:S(2)}) collective-permute-start(bf16[768,256]{0,1:T(8,128)(2,1)S(1)} %get-tuple-element.86), channel_id=1, source_target_pairs={{0,16},{16,0},{1,17},{17,1},{2,18},{18,2},{3,19},{19,3},{4,20},{20... | collective-permute-start | bytes 1179656 | tf_op jit(solution)/shard_map/ppermute | solution.py:19
  108.7 5.4 %collective-permute-start.47 = (f32[256]{0:T(256)S(1)}, f32[256]{0:T(256)S(1)}, u32[]{:S(2)}, u32[]{:S(2)}) collective-permute-start(f32[256]{0:T(256)S(1)} %add.172), channel_id=1, source_target_pairs={{0,3},{1,2},{2,1},{3,0},{4,7},{5,6},{6,5},{7,4},{8,11},{9,10},{10,... | collective-permute-start | bytes 3080 | tf_op jit(solution)/shard_map/ppermute | solution.py:19
  118.1 11.5 %collective-permute-start.55 = (bf16[256,256]{0,1:T(8,128)(2,1)S(1)}, bf16[256,256]{0,1:T(8,128)(2,1)S(1)}, u32[]{:S(2)}, u32[]{:S(2)}) collective-permute-start(bf16[256,256]{0,1:T(8,128)(2,1)S(1)} %get-tuple-element.114), channel_id=1, source_target_pairs={{0,4},{4,0},{8,12},{12,8},{1,5},{5,1},{9,13},{13,9},{2,6},{6,2},{1... | collective-permute-start | bytes 393224 | tf_op jit(solution)/shard_map/ppermute | solution.py:19
  118.6 11.0 %collective-permute-start.56 = (bf16[256,256]{0,1:T(8,128)(2,1)S(1)}, bf16[256,256]{0,1:T(8,128)(2,1)S(1)}, u32[]{:S(2)}, u32[]{:S(2)}) collective-permute-start(bf16[256,256]{0,1:T(8,128)(2,1)S(1)} %get-tuple-element.115), channel_id=1, source_target_pairs={{0,8},{4,12},{8,0},{12,4},{1,9},{5,13},{9,1},{13,5},{2,10},{6,14},... | collective-permute-start | bytes 393224 | tf_op jit(solution)/shard_map/ppermute | solution.py:19
  119.8 7.8 %collective-permute-start.54 = (bf16[512,256]{0,1:T(8,128)(2,1)S(1)}, bf16[512,256]{0,1:T(8,128)(2,1)S(1)}, u32[]{:S(2)}, u32[]{:S(2)}) collective-permute-start(bf16[512,256]{0,1:T(8,128)(2,1)S(1)} %slice.287), channel_id=1, source_target_pairs={{0,1},{1,0},{2,3},{3,2},{4,5},{5,4},{6,7},{7,6},{8,9},{9,8},{10,11... | collective-permute-start | bytes 786440 | tf_op jit(solution)/shard_map/ppermute | solution.py:19
  121.4 10.4 %collective-permute-start.58 = (bf16[512,256]{0,1:T(8,128)(2,1)S(1)}, bf16[512,256]{0,1:T(8,128)(2,1)S(1)}, u32[]{:S(2)}, u32[]{:S(2)}) collective-permute-start(bf16[512,256]{0,1:T(8,128)(2,1)S(1)} %get-tuple-element.104), channel_id=1, source_target_pairs={{0,4},{4,0},{8,12},{12,8},{1,5},{5,1},{9,13},{13,9},{2,6},{6,2},{1... | collective-permute-start | bytes 786440 | tf_op jit(solution)/shard_map/ppermute | solution.py:19
  122.2 10.8 %collective-permute-start.59 = (bf16[512,256]{0,1:T(8,128)(2,1)S(1)}, bf16[512,256]{0,1:T(8,128)(2,1)S(1)}, u32[]{:S(2)}, u32[]{:S(2)}) collective-permute-start(bf16[512,256]{0,1:T(8,128)(2,1)S(1)} %get-tuple-element.105), channel_id=1, source_target_pairs={{0,8},{4,12},{8,0},{12,4},{1,9},{5,13},{9,1},{13,5},{2,10},{6,14},... | collective-permute-start | bytes 786440 | tf_op jit(solution)/shard_map/ppermute | solution.py:19
  127.7 7.3 %collective-permute-start.60 = (bf16[256,256]{0,1:T(8,128)(2,1)S(1)}, bf16[256,256]{0,1:T(8,128)(2,1)S(1)}, u32[]{:S(2)}, u32[]{:S(2)}) collective-permute-start(bf16[256,256]{0,1:T(8,128)(2,1)S(1)} %get-tuple-element.95), channel_id=1, source_target_pairs={{0,12},{4,8},{8,4},{12,0},{1,13},{5,9},{9,5},{13,1},{2,14},{6,10},... | collective-permute-start | bytes 393224 | tf_op jit(solution)/shard_map/ppermute | solution.py:19
  131.2 9.1 %collective-permute-start.52 = (bf16[256,256]{0,1:T(8,128)(2,1)S(1)}, bf16[256,256]{0,1:T(8,128)(2,1)S(1)}, u32[]{:S(2)}, u32[]{:S(2)}) collective-permute-start(bf16[256,256]{0,1:T(8,128)(2,1)S(1)} %get-tuple-element.102), channel_id=1, source_target_pairs={{0,4},{4,0},{8,12},{12,8},{1,5},{5,1},{9,13},{13,9},{2,6},{6,2},{1... | collective-permute-start | bytes 393224 | tf_op jit(solution)/shard_map/ppermute | solution.py:19
  131.8 8.5 %collective-permute-start.53 = (bf16[256,256]{0,1:T(8,128)(2,1)S(1)}, bf16[256,256]{0,1:T(8,128)(2,1)S(1)}, u32[]{:S(2)}, u32[]{:S(2)}) collective-permute-start(bf16[256,256]{0,1:T(8,128)(2,1)S(1)} %get-tuple-element.103), channel_id=1, source_target_pairs={{0,8},{4,12},{8,0},{12,4},{1,9},{5,13},{9,1},{13,5},{2,10},{6,14},... | collective-permute-start | bytes 393224 | tf_op jit(solution)/shard_map/ppermute | solution.py:19
  135.1 8.7 %collective-permute-start.63 = (bf16[256,256]{0,1:T(8,128)(2,1)S(1)}, bf16[256,256]{0,1:T(8,128)(2,1)S(1)}, u32[]{:S(2)}, u32[]{:S(2)}) collective-permute-start(bf16[256,256]{0,1:T(8,128)(2,1)S(1)} %get-tuple-element.93), channel_id=1, source_target_pairs={{0,2},{1,3},{2,0},{3,1},{4,6},{5,7},{6,4},{7,5},{8,10},{9,11},{10,... | collective-permute-start | bytes 393224 | tf_op jit(solution)/shard_map/ppermute | solution.py:19
  137.0 5.9 %collective-permute-start.57 = (bf16[256,256]{0,1:T(8,128)(2,1)S(1)}, bf16[256,256]{0,1:T(8,128)(2,1)S(1)}, u32[]{:S(2)}, u32[]{:S(2)}) collective-permute-start(bf16[256,256]{0,1:T(8,128)(2,1)S(1)} %add_convert_fusion.1), channel_id=1, source_target_pairs={{0,12},{4,8},{8,4},{12,0},{1,13},{5,9},{9,5},{13,1},{2,14},{6,10},... | collective-permute-start | bytes 393224 | tf_op jit(solution)/shard_map/ppermute | solution.py:19
  138.5 5.3 %collective-permute-start.62 = (bf16[256,256]{0,1:T(8,128)(2,1)S(1)}, bf16[256,256]{0,1:T(8,128)(2,1)S(1)}, u32[]{:S(2)}, u32[]{:S(2)}) collective-permute-start(bf16[256,256]{0,1:T(8,128)(2,1)S(1)} %add_convert_fusion), channel_id=1, source_target_pairs={{0,1},{1,0},{2,3},{3,2},{4,5},{5,4},{6,7},{7,6},{8,9},{9,8},{10,11... | collective-permute-start | bytes 393224 | tf_op jit(solution)/shard_map/ppermute | solution.py:19
  (17 other events, 65.5 us)

commit v2 on v1

--- a/solution.py
+++ b/solution.py
@@ -56,7 +56,8 @@
     b[3, 2] = xor_move(b[0, 2], "row", 3)
     b[0, 3] = xor_move(b[0, 2], "feat", 1)
     for r in (1, 2):
-        b[r, 1], b[r, 2] = split(xor_move(join(b[0, 1], b[0, 2]), "row", r))
+        pair = join(after(b[0, 1], b[3, 0]), b[0, 2])
+        b[r, 1], b[r, 2] = split(xor_move(pair, "row", r))
     b[3, 1], b[3, 3] = split(xor_move(join(b[3, 0], b[3, 2]), "feat", 1))
     for r in (1, 2):
         b[r, 3] = xor_move(b[0, 3], "row", r)
@@ -80,13 +81,11 @@
     near_across = summed(after(b[3, 0], three), near_across)
     (far_across,), (three,) = send("row", 3, far_across), send("feat", 1, three)
     two = summed(b[0, 2], *twos, far_across, three)
-    one = summed(after(b[0, 1], two), *ones)
-    (two,), (near_across,), (one,) = (
-        send("feat", 2, two),
-        send("row", 3, near_across),
-        send("feat", 1, one),
-    )
-    near = b[0, 0] + send("row", 1, b[1, 0])[0] + send("row", 2, b[2, 0])[0]
+    (two,), (near_across,) = send("feat", 2, two), send("row", 3, near_across)
+    (one,) = send("feat", 1, summed(after(b[0, 1], near_across), *ones))
+    near = b[0, 0]
+    for r in (1, 2):
+        near = near + send("row", r, after(b[r, 0], ones[0]))[0]
     return near + near_across + one + two
 
 
@@ -142,7 +141,7 @@
             jax.ShapeDtypeStruct((rows_here, len(places) * depth), samples.dtype)
             for places in ARRIVALS
         ],
-        in_specs=[pl.BlockSpec(memory_space=pl.ANY)],
+        in_specs=[pl.BlockSpec(memory_space=pltpu.HBM)],
         out_specs=[pl.BlockSpec(memory_space=pl.ANY) for places in ARRIVALS],
         scratch_shapes=[pltpu.SemaphoreType.DMA((count,))],
         compiler_params=pltpu.CompilerParams(vmem_limit_bytes=1 << 20),

time: 145 us -> 146 us (level)
  transfers between devices with their start and end apart: 64 -> 64, of which waited for: 35 -> 31; matrix products, arithmetic and copies ran while one was open for 6% -> 6% of each run, Pallas kernels for 1% -> 1%
where the time goes in v2:
time: 146 us
  starting transfers between devices  74.1 us (51%)
  waiting for transfers between devices  52.9 us (36%)
  matrix products  9.39 us (6%)
  local copies, waits for them, and re-layouts  6.23 us (4%)
    ppermute x64, starting transfers between devices, xor_move(): return lax.ppermute(block, axis, [(i, i ^ mask) for i in range(count)])  74.1 us
    ppermute x64, waiting for transfers between devices, xor_move(): return lax.ppermute(block, axis, [(i, i ^ mask) for i in range(count)])  52.9 us
    unnamed x27, local copies, waits for them, and re-layouts  5.86 us
    dot_general x6, matrix products, on_device(): lax.dot_general(groups[g], residue, (((0,), (0,)), ((), ())), preferred_e...  4.79 us
    dot_general x6, matrix products, on_device(): part = jnp.dot(groups[g], join(*blocks), preferred_element_type=jnp.float32)  4.6 us
  transfers between devices with their start and end apart: 64, of which 31 were waited for; matrix products, arithmetic and copies ran while one was open for 6% of the time, Pallas kernels for 1%

profile of v2, /device:TPU:0, one launch (start us, length us, event | category | flops | bytes accessed | tf_op | source)
XLA Modules:
  0.0 146.1 jit_solution(16809335618521687055)
XLA Ops:
  1.7 4.0 %collective-permute-start.2 = (bf16[256,256]{0,1:T(8,128)(2,1)S(1)}, bf16[256,256]{0,1:T(8,128)(2,1)S(1)}, u32[]{:S(2)}, u32[]{:S(2)}) collective-permute-start(bf16[256,256]{0,1:T(8,128)(2,1)S(1)} %bitcast_convert_fusion), channel_id=1, source_target_pairs={{0,12},{4,8},{8,4},{12,0},{1,13},{5,9},{9,5},{13,1},{2,14},{6,10},... | collective-permute-start | bytes 393224 | tf_op jit(solution)/shard_map/ppermute | solution.py:19
  5.7 1.6 %collective-permute-start.3 = (bf16[256,256]{0,1:T(8,128)(2,1)S(1)}, bf16[256,256]{0,1:T(8,128)(2,1)S(1)}, u32[]{:S(2)}, u32[]{:S(2)}) collective-permute-start(bf16[256,256]{0,1:T(8,128)(2,1)S(1)} %bitcast_convert_fusion), channel_id=1, source_target_pairs={{0,1},{1,0},{2,3},{3,2},{4,5},{5,4},{6,7},{7,6},{8,9},{9,8},{10,11... | collective-permute-start | bytes 393224 | tf_op jit(solution)/shard_map/ppermute | solution.py:19
  7.3 2.6 %collective-permute-start.4 = (bf16[256,256]{0,1:T(8,128)(2,1)S(1)}, bf16[256,256]{0,1:T(8,128)(2,1)S(1)}, u32[]{:S(2)}, u32[]{:S(2)}) collective-permute-start(bf16[256,256]{0,1:T(8,128)(2,1)S(1)} %bitcast_convert_fusion), channel_id=1, source_target_pairs={{0,2},{1,3},{2,0},{3,1},{4,6},{5,7},{6,4},{7,5},{8,10},{9,11},{10,... | collective-permute-start | bytes 393224 | tf_op jit(solution)/shard_map/ppermute | solution.py:19
  10.9 2.8 %copy-done = bf16[1,768,4096]{2,1,0:T(8,128)(2,1)S(1)} copy-done((bf16[1,768,4096]{2,1,0:T(8,128)(2,1)S(1)}, bf16[1,768,4096]{2,1,0:T(8,128)(2,1)}, u32[]{:S(2)}) %copy-start) | copy-done | bytes 6291480
  16.4 1.5 %collective-permute-start.7 = (bf16[512,256]{0,1:T(8,128)(2,1)S(1)}, bf16[512,256]{0,1:T(8,128)(2,1)S(1)}, u32[]{:S(2)}, u32[]{:S(2)}) collective-permute-start(bf16[512,256]{0,1:T(8,128)(2,1)S(1)} %constant_dynamic-update-slice_fusion.6), channel_id=1, source_target_pairs={{0,4},{4,0},{8,12},{12,8},{1,5},{5,1},{9,13},{13,9},{2,6},{6,2},{1... | collective-permute-start | bytes 786440 | tf_op jit(solution)/shard_map/ppermute | solution.py:19
  18.6 1.2 collective-permute-start.6
  20.6 4.9 %collective-permute-done.6 = bf16[256,256]{0,1:T(8,128)(2,1)S(1)} collective-permute-done((bf16[256,256]{0,1:T(8,128)(2,1)S(1)}, bf16[256,256]{0,1:T(8,128)(2,1)S(1)}, u32[]{:S(2)}, u32[]{:S(2)}) %collective-permute-start.6) | collective-permute-done | bytes 131104 | tf_op jit(solution)/shard_map/ppermute | solution.py:19
  25.6 1.3 collective-permute-start.9
  27.6 1.5 %collective-permute-start.11 = (bf16[256,256]{0,1:T(8,128)(2,1)S(1)}, bf16[256,256]{0,1:T(8,128)(2,1)S(1)}, u32[]{:S(2)}, u32[]{:S(2)}) collective-permute-start(bf16[256,256]{0,1:T(8,128)(2,1)S(1)} %collective-permute-done.5), channel_id=1, source_target_pairs={{0,8},{4,12},{8,0},{12,4},{1,9},{5,13},{9,1},{13,5},{2,10},{6,14},... | collective-permute-start | bytes 393224 | tf_op jit(solution)/shard_map/ppermute | solution.py:19
  30.1 1.9 %collective-permute-done.9 = bf16[512,256]{0,1:T(8,128)(2,1)S(1)} collective-permute-done((bf16[512,256]{0,1:T(8,128)(2,1)S(1)}, bf16[512,256]{0,1:T(8,128)(2,1)S(1)}, u32[]{:S(2)}, u32[]{:S(2)}) %collective-permute-start.9) | collective-permute-done | bytes 262176 | tf_op jit(solution)/shard_map/ppermute | solution.py:19
  33.3 2.1 %collective-permute-start.12 = (f32[256]{0:T(256)S(1)}, f32[256]{0:T(256)S(1)}, u32[]{:S(2)}, u32[]{:S(2)}) collective-permute-start(f32[256]{0:T(256)S(1)} %get-tuple-element.124), channel_id=1, source_target_pairs={{0,12},{4,8},{8,4},{12,0},{1,13},{5,9},{9,5},{13,1},{2,14},{6,10},... | collective-permute-start | bytes 3080 | tf_op jit(solution)/shard_map/ppermute | solution.py:19
  39.7 1.8 %collective-permute-start.15 = (f32[256]{0:T(256)S(1)}, f32[256]{0:T(256)S(1)}, u32[]{:S(2)}, u32[]{:S(2)}) collective-permute-start(f32[256]{0:T(256)S(1)} %add.148), channel_id=1, source_target_pairs={{0,3},{1,2},{2,1},{3,0},{4,7},{5,6},{6,5},{7,4},{8,11},{9,10},{10,... | collective-permute-start | bytes 3080 | tf_op jit(solution)/shard_map/ppermute | solution.py:19
  42.0 2.1 %collective-permute-start.17 = (f32[256]{0:T(256)S(1)}, f32[256]{0:T(256)S(1)}, u32[]{:S(2)}, u32[]{:S(2)}) collective-permute-start(f32[256]{0:T(256)S(1)} %add.148), channel_id=1, source_target_pairs={{0,1},{1,0},{2,3},{3,2},{4,5},{5,4},{6,7},{7,6},{8,9},{9,8},{10,11... | collective-permute-start | bytes 3080 | tf_op jit(solution)/shard_map/ppermute | solution.py:19
  50.0 1.4 collective-permute-start.23
  51.3 1.3 collective-permute-start.24
  52.6 1.4 collective-permute-start.25
  55.5 2.5 %collective-permute-done.23 = bf16[512,256]{0,1:T(8,128)(2,1)S(1)} collective-permute-done((bf16[512,256]{0,1:T(8,128)(2,1)S(1)}, bf16[512,256]{0,1:T(8,128)(2,1)S(1)}, u32[]{:S(2)}, u32[]{:S(2)}) %collective-permute-start.23) | collective-permute-done | bytes 262176 | tf_op jit(solution)/shard_map/ppermute | solution.py:19
  58.1 1.8 %collective-permute-start.29 = (bf16[256,256]{0,1:T(8,128)(2,1)S(1)}, bf16[256,256]{0,1:T(8,128)(2,1)S(1)}, u32[]{:S(2)}, u32[]{:S(2)}) collective-permute-start(bf16[256,256]{0,1:T(8,128)(2,1)S(1)} %get-tuple-element.116), channel_id=1, source_target_pairs={{0,12},{4,8},{8,4},{12,0},{1,13},{5,9},{9,5},{13,1},{2,14},{6,10},... | collective-permute-start | bytes 393224 | tf_op jit(solution)/shard_map/ppermute | solution.py:19
  60.3 1.7 %collective-permute-start.30 = (bf16[256,256]{0,1:T(8,128)(2,1)S(1)}, bf16[256,256]{0,1:T(8,128)(2,1)S(1)}, u32[]{:S(2)}, u32[]{:S(2)}) collective-permute-start(bf16[256,256]{0,1:T(8,128)(2,1)S(1)} %add_convert_fusion.5), channel_id=1, source_target_pairs={{0,1},{1,0},{2,3},{3,2},{4,5},{5,4},{6,7},{7,6},{8,9},{9,8},{10,11... | collective-permute-start | bytes 393224 | tf_op jit(solution)/shard_map/ppermute | solution.py:19
  62.8 1.5 %collective-permute-start.22 = (bf16[256,256]{0,1:T(8,128)(2,1)S(1)}, bf16[256,256]{0,1:T(8,128)(2,1)S(1)}, u32[]{:S(2)}, u32[]{:S(2)}) collective-permute-start(bf16[256,256]{0,1:T(8,128)(2,1)S(1)} %get-tuple-element.72), channel_id=1, source_target_pairs={{0,8},{4,12},{8,0},{12,4},{1,9},{5,13},{9,1},{13,5},{2,10},{6,14},... | collective-permute-start | bytes 393224 | tf_op jit(solution)/shard_map/ppermute | solution.py:19
  64.3 2.9 %collective-permute-done.27 = bf16[512,256]{0,1:T(8,128)(2,1)S(1)} collective-permute-done((bf16[512,256]{0,1:T(8,128)(2,1)S(1)}, bf16[512,256]{0,1:T(8,128)(2,1)S(1)}, u32[]{:S(2)}, u32[]{:S(2)}) %collective-permute-start.27) | collective-permute-done | bytes 262176 | tf_op jit(solution)/shard_map/ppermute | solution.py:19
  67.4 1.5 %collective-permute-start.26 = (bf16[256,256]{0,1:T(8,128)(2,1)S(1)}, bf16[256,256]{0,1:T(8,128)(2,1)S(1)}, u32[]{:S(2)}, u32[]{:S(2)}) collective-permute-start(bf16[256,256]{0,1:T(8,128)(2,1)S(1)} %add_convert_fusion.4), channel_id=1, source_target_pairs={{0,12},{4,8},{8,4},{12,0},{1,13},{5,9},{9,5},{13,1},{2,14},{6,10},... | collective-permute-start | bytes 393224 | tf_op jit(solution)/shard_map/ppermute | solution.py:19
  69.2 1.4 collective-permute-start.31
  70.5 2.8 %collective-permute-done.26 = bf16[256,256]{0,1:T(8,128)(2,1)S(1)} collective-permute-done((bf16[256,256]{0,1:T(8,128)(2,1)S(1)}, bf16[256,256]{0,1:T(8,128)(2,1)S(1)}, u32[]{:S(2)}, u32[]{:S(2)}) %collective-permute-start.26) | collective-permute-done | bytes 131104 | tf_op jit(solution)/shard_map/ppermute | solution.py:19
  73.3 2.7 %collective-permute-done.28 = bf16[256,256]{0,1:T(8,128)(2,1)S(1)} collective-permute-done((bf16[256,256]{0,1:T(8,128)(2,1)S(1)}, bf16[256,256]{0,1:T(8,128)(2,1)S(1)}, u32[]{:S(2)}, u32[]{:S(2)}) %collective-permute-start.28) | collective-permute-done | bytes 131104 | tf_op jit(solution)/shard_map/ppermute | solution.py:19
  76.2 1.3 collective-permute-start.34
  78.7 2.0 %collective-permute-start.36 = (bf16[256,256]{0,1:T(8,128)(2,1)S(1)}, bf16[256,256]{0,1:T(8,128)(2,1)S(1)}, u32[]{:S(2)}, u32[]{:S(2)}) collective-permute-start(bf16[256,256]{0,1:T(8,128)(2,1)S(1)} %get-tuple-element.76), channel_id=1, source_target_pairs={{0,2},{1,3},{2,0},{3,1},{4,6},{5,7},{6,4},{7,5},{8,10},{9,11},{10,... | collective-permute-start | bytes 393224 | tf_op jit(solution)/shard_map/ppermute | solution.py:19
  80.8 1.9 %collective-permute-start.33 = (bf16[256,256]{0,1:T(8,128)(2,1)S(1)}, bf16[256,256]{0,1:T(8,128)(2,1)S(1)}, u32[]{:S(2)}, u32[]{:S(2)}) collective-permute-start(bf16[256,256]{0,1:T(8,128)(2,1)S(1)} %get-tuple-element.76), channel_id=1, source_target_pairs={{0,8},{4,12},{8,0},{12,4},{1,9},{5,13},{9,1},{13,5},{2,10},{6,14},... | collective-permute-start | bytes 393224 | tf_op jit(solution)/shard_map/ppermute | solution.py:19
  82.7 3.2 %collective-permute-done.36 = bf16[256,256]{0,1:T(8,128)(2,1)S(1)} collective-permute-done((bf16[256,256]{0,1:T(8,128)(2,1)S(1)}, bf16[256,256]{0,1:T(8,128)(2,1)S(1)}, u32[]{:S(2)}, u32[]{:S(2)}) %collective-permute-start.36) | collective-permute-done | bytes 131104 | tf_op jit(solution)/shard_map/ppermute | solution.py:19
  88.2 1.5 %collective-permute-start.38 = (bf16[256,256]{0,1:T(8,128)(2,1)S(1)}, bf16[256,256]{0,1:T(8,128)(2,1)S(1)}, u32[]{:S(2)}, u32[]{:S(2)}) collective-permute-start(bf16[256,256]{0,1:T(8,128)(2,1)S(1)} %collective-permute-done.36), channel_id=1, source_target_pairs={{0,12},{4,8},{8,4},{12,0},{1,13},{5,9},{9,5},{13,1},{2,14},{6,10},... | collective-permute-start | bytes 393224 | tf_op jit(solution)/shard_map/ppermute | solution.py:19
  90.6 6.1 %collective-permute-done.38 = bf16[256,256]{0,1:T(8,128)(2,1)S(1)} collective-permute-done((bf16[256,256]{0,1:T(8,128)(2,1)S(1)}, bf16[256,256]{0,1:T(8,128)(2,1)S(1)}, u32[]{:S(2)}, u32[]{:S(2)}) %collective-permute-start.38) | collective-permute-done | bytes 131104 | tf_op jit(solution)/shard_map/ppermute | solution.py:19
  97.2 1.6 %collective-permute-start.43 = (bf16[256,256]{0,1:T(8,128)(2,1)S(1)}, bf16[256,256]{0,1:T(8,128)(2,1)S(1)}, u32[]{:S(2)}, u32[]{:S(2)}) collective-permute-start(bf16[256,256]{0,1:T(8,128)(2,1)S(1)} %collective-permute-done.37), channel_id=1, source_target_pairs={{0,8},{4,12},{8,0},{12,4},{1,9},{5,13},{9,1},{13,5},{2,10},{6,14},... | collective-permute-start | bytes 393224 | tf_op jit(solution)/shard_map/ppermute | solution.py:19
  99.9 3.3 %collective-permute-done.41 = bf16[512,256]{0,1:T(8,128)(2,1)S(1)} collective-permute-done((bf16[512,256]{0,1:T(8,128)(2,1)S(1)}, bf16[512,256]{0,1:T(8,128)(2,1)S(1)}, u32[]{:S(2)}, u32[]{:S(2)}) %collective-permute-start.41) | collective-permute-done | bytes 262176 | tf_op jit(solution)/shard_map/ppermute | solution.py:19
  103.9 1.5 %collective-permute-start.44 = (f32[256]{0:T(256)S(1)}, f32[256]{0:T(256)S(1)}, u32[]{:S(2)}, u32[]{:S(2)}) collective-permute-start(f32[256]{0:T(256)S(1)} %get-tuple-element.120), channel_id=1, source_target_pairs={{0,12},{4,8},{8,4},{12,0},{1,13},{5,9},{9,5},{13,1},{2,14},{6,10},... | collective-permute-start | bytes 3080 | tf_op jit(solution)/shard_map/ppermute | solution.py:19
  106.1 1.4 collective-permute-start.46
  109.7 1.9 %collective-permute-start.47 = (f32[256]{0:T(256)S(1)}, f32[256]{0:T(256)S(1)}, u32[]{:S(2)}, u32[]{:S(2)}) collective-permute-start(f32[256]{0:T(256)S(1)} %add.172), channel_id=1, source_target_pairs={{0,3},{1,2},{2,1},{3,0},{4,7},{5,6},{6,5},{7,4},{8,11},{9,10},{10,... | collective-permute-start | bytes 3080 | tf_op jit(solution)/shard_map/ppermute | solution.py:19
  111.6 1.5 %collective-permute-start.48 = (f32[256]{0:T(256)S(1)}, f32[256]{0:T(256)S(1)}, u32[]{:S(2)}, u32[]{:S(2)}) collective-permute-start(f32[256]{0:T(256)S(1)} %add.172), channel_id=1, source_target_pairs={{0,2},{1,3},{2,0},{3,1},{4,6},{5,7},{6,4},{7,5},{8,10},{9,11},{10,... | collective-permute-start | bytes 3080 | tf_op jit(solution)/shard_map/ppermute | solution.py:19
  119.7 1.4 collective-permute-start.56
  125.6 1.5 %collective-permute-done.55 = bf16[512,256]{0,1:T(8,128)(2,1)S(1)} collective-permute-done((bf16[512,256]{0,1:T(8,128)(2,1)S(1)}, bf16[512,256]{0,1:T(8,128)(2,1)S(1)}, u32[]{:S(2)}, u32[]{:S(2)}) %collective-permute-start.55) | collective-permute-done | bytes 262176 | tf_op jit(solution)/shard_map/ppermute | solution.py:19
  127.1 1.5 %collective-permute-start.61 = (bf16[256,256]{0,1:T(8,128)(2,1)S(1)}, bf16[256,256]{0,1:T(8,128)(2,1)S(1)}, u32[]{:S(2)}, u32[]{:S(2)}) collective-permute-start(bf16[256,256]{0,1:T(8,128)(2,1)S(1)} %get-tuple-element.109), channel_id=1, source_target_pairs={{0,12},{4,8},{8,4},{12,0},{1,13},{5,9},{9,5},{13,1},{2,14},{6,10},... | collective-permute-start | bytes 393224 | tf_op jit(solution)/shard_map/ppermute | solution.py:19
  128.7 1.5 %collective-permute-start.62 = (bf16[256,256]{0,1:T(8,128)(2,1)S(1)}, bf16[256,256]{0,1:T(8,128)(2,1)S(1)}, u32[]{:S(2)}, u32[]{:S(2)}) collective-permute-start(bf16[256,256]{0,1:T(8,128)(2,1)S(1)} %add_convert_fusion.2), channel_id=1, source_target_pairs={{0,1},{1,0},{2,3},{3,2},{4,5},{5,4},{6,7},{7,6},{8,9},{9,8},{10,11... | collective-permute-start | bytes 393224 | tf_op jit(solution)/shard_map/ppermute | solution.py:19
  130.3 1.4 collective-permute-done.52
  131.6 1.6 %collective-permute-start.53 = (bf16[256,256]{0,1:T(8,128)(2,1)S(1)}, bf16[256,256]{0,1:T(8,128)(2,1)S(1)}, u32[]{:S(2)}, u32[]{:S(2)}) collective-permute-start(bf16[256,256]{0,1:T(8,128)(2,1)S(1)} %get-tuple-element.93), channel_id=1, source_target_pairs={{0,4},{4,0},{8,12},{12,8},{1,5},{5,1},{9,13},{13,9},{2,6},{6,2},{1... | collective-permute-start | bytes 393224 | tf_op jit(solution)/shard_map/ppermute | solution.py:19
  133.9 1.6 %collective-permute-done.61 = bf16[256,256]{0,1:T(8,128)(2,1)S(1)} collective-permute-done((bf16[256,256]{0,1:T(8,128)(2,1)S(1)}, bf16[256,256]{0,1:T(8,128)(2,1)S(1)}, u32[]{:S(2)}, u32[]{:S(2)}) %collective-permute-start.61) | collective-permute-done | bytes 131104 | tf_op jit(solution)/shard_map/ppermute | solution.py:19
  135.7 1.4 collective-permute-start.58
  137.8 1.6 %collective-permute-start.63 = (bf16[256,256]{0,1:T(8,128)(2,1)S(1)}, bf16[256,256]{0,1:T(8,128)(2,1)S(1)}, u32[]{:S(2)}, u32[]{:S(2)}) collective-permute-start(bf16[256,256]{0,1:T(8,128)(2,1)S(1)} %get-tuple-element.105), channel_id=1, source_target_pairs={{0,2},{1,3},{2,0},{3,1},{4,6},{5,7},{6,4},{7,5},{8,10},{9,11},{10,... | collective-permute-start | bytes 393224 | tf_op jit(solution)/shard_map/ppermute | solution.py:19
  141.6 1.9 %collective-permute-done.60 = bf16[256,256]{0,1:T(8,128)(2,1)S(1)} collective-permute-done((bf16[256,256]{0,1:T(8,128)(2,1)S(1)}, bf16[256,256]{0,1:T(8,128)(2,1)S(1)}, u32[]{:S(2)}, u32[]{:S(2)}) %collective-permute-start.60) | collective-permute-done | bytes 131104 | tf_op jit(solution)/shard_map/ppermute | solution.py:19
  143.5 1.6 %collective-permute-done.63 = bf16[256,256]{0,1:T(8,128)(2,1)S(1)} collective-permute-done((bf16[256,256]{0,1:T(8,128)(2,1)S(1)}, bf16[256,256]{0,1:T(8,128)(2,1)S(1)}, u32[]{:S(2)}, u32[]{:S(2)}) %collective-permute-start.63) | collective-permute-done | bytes 131104 | tf_op jit(solution)/shard_map/ppermute | solution.py:19
  (170 shorter events, 48.4 us)
Async XLA Ops:
  1.7 13.0 %collective-permute-start.2 = (bf16[256,256]{0,1:T(8,128)(2,1)S(1)}, bf16[256,256]{0,1:T(8,128)(2,1)S(1)}, u32[]{:S(2)}, u32[]{:S(2)}) collective-permute-start(bf16[256,256]{0,1:T(8,128)(2,1)S(1)} %bitcast_convert_fusion), channel_id=1, source_target_pairs={{0,12},{4,8},{8,4},{12,0},{1,13},{5,9},{9,5},{13,1},{2,14},{6,10},... | collective-permute-start | bytes 393224 | tf_op jit(solution)/shard_map/ppermute | solution.py:19
  5.7 9.1 %collective-permute-start.3 = (bf16[256,256]{0,1:T(8,128)(2,1)S(1)}, bf16[256,256]{0,1:T(8,128)(2,1)S(1)}, u32[]{:S(2)}, u32[]{:S(2)}) collective-permute-start(bf16[256,256]{0,1:T(8,128)(2,1)S(1)} %bitcast_convert_fusion), channel_id=1, source_target_pairs={{0,1},{1,0},{2,3},{3,2},{4,5},{5,4},{6,7},{7,6},{8,9},{9,8},{10,11... | collective-permute-start | bytes 393224 | tf_op jit(solution)/shard_map/ppermute | solution.py:19
  7.3 8.4 %collective-permute-start.4 = (bf16[256,256]{0,1:T(8,128)(2,1)S(1)}, bf16[256,256]{0,1:T(8,128)(2,1)S(1)}, u32[]{:S(2)}, u32[]{:S(2)}) collective-permute-start(bf16[256,256]{0,1:T(8,128)(2,1)S(1)} %bitcast_convert_fusion), channel_id=1, source_target_pairs={{0,2},{1,3},{2,0},{3,1},{4,6},{5,7},{6,4},{7,5},{8,10},{9,11},{10,... | collective-permute-start | bytes 393224 | tf_op jit(solution)/shard_map/ppermute | solution.py:19
  9.9 8.0 %collective-permute-start = (bf16[256,256]{0,1:T(8,128)(2,1)S(1)}, bf16[256,256]{0,1:T(8,128)(2,1)S(1)}, u32[]{:S(2)}, u32[]{:S(2)}) collective-permute-start(bf16[256,256]{0,1:T(8,128)(2,1)S(1)} %bitcast_convert_fusion), channel_id=1, source_target_pairs={{0,4},{4,0},{8,12},{12,8},{1,5},{5,1},{9,13},{13,9},{2,6},{6,2},{1... | collective-permute-start | bytes 393224 | tf_op jit(solution)/shard_map/ppermute | solution.py:19
  10.4 7.5 %collective-permute-start.1 = (bf16[256,256]{0,1:T(8,128)(2,1)S(1)}, bf16[256,256]{0,1:T(8,128)(2,1)S(1)}, u32[]{:S(2)}, u32[]{:S(2)}) collective-permute-start(bf16[256,256]{0,1:T(8,128)(2,1)S(1)} %bitcast_convert_fusion), channel_id=1, source_target_pairs={{0,8},{4,12},{8,0},{12,4},{1,9},{5,13},{9,1},{13,5},{2,10},{6,14},... | collective-permute-start | bytes 393224 | tf_op jit(solution)/shard_map/ppermute | solution.py:19
  15.7 13.4 %collective-permute-start.8 = (bf16[512,256]{0,1:T(8,128)(2,1)S(1)}, bf16[512,256]{0,1:T(8,128)(2,1)S(1)}, u32[]{:S(2)}, u32[]{:S(2)}) collective-permute-start(bf16[512,256]{0,1:T(8,128)(2,1)S(1)} %constant_dynamic-update-slice_fusion.6), channel_id=1, source_target_pairs={{0,8},{4,12},{8,0},{12,4},{1,9},{5,13},{9,1},{13,5},{2,10},{6,14},... | collective-permute-start | bytes 786440 | tf_op jit(solution)/shard_map/ppermute | solution.py:19
  16.4 12.7 %collective-permute-start.7 = (bf16[512,256]{0,1:T(8,128)(2,1)S(1)}, bf16[512,256]{0,1:T(8,128)(2,1)S(1)}, u32[]{:S(2)}, u32[]{:S(2)}) collective-permute-start(bf16[512,256]{0,1:T(8,128)(2,1)S(1)} %constant_dynamic-update-slice_fusion.6), channel_id=1, source_target_pairs={{0,4},{4,0},{8,12},{12,8},{1,5},{5,1},{9,13},{13,9},{2,6},{6,2},{1... | collective-permute-start | bytes 786440 | tf_op jit(solution)/shard_map/ppermute | solution.py:19
  18.0 8.8 %collective-permute-start.5 = (bf16[256,256]{0,1:T(8,128)(2,1)S(1)}, bf16[256,256]{0,1:T(8,128)(2,1)S(1)}, u32[]{:S(2)}, u32[]{:S(2)}) collective-permute-start(bf16[256,256]{0,1:T(8,128)(2,1)S(1)} %collective-permute-done.4), channel_id=1, source_target_pairs={{0,1},{1,0},{2,3},{3,2},{4,5},{5,4},{6,7},{7,6},{8,9},{9,8},{10,11... | collective-permute-start | bytes 393224 | tf_op jit(solution)/shard_map/ppermute | solution.py:19
  18.6 7.0 %collective-permute-start.6 = (bf16[256,256]{0,1:T(8,128)(2,1)S(1)}, bf16[256,256]{0,1:T(8,128)(2,1)S(1)}, u32[]{:S(2)}, u32[]{:S(2)}) collective-permute-start(bf16[256,256]{0,1:T(8,128)(2,1)S(1)} %collective-permute-done.4), channel_id=1, source_target_pairs={{0,12},{4,8},{8,4},{12,0},{1,13},{5,9},{9,5},{13,1},{2,14},{6,10},... | collective-permute-start | bytes 393224 | tf_op jit(solution)/shard_map/ppermute | solution.py:19
  25.6 6.4 %collective-permute-start.9 = (bf16[512,256]{0,1:T(8,128)(2,1)S(1)}, bf16[512,256]{0,1:T(8,128)(2,1)S(1)}, u32[]{:S(2)}, u32[]{:S(2)}) collective-permute-start(bf16[512,256]{0,1:T(8,128)(2,1)S(1)} %pad_maximum_fusion), channel_id=1, source_target_pairs={{0,1},{1,0},{2,3},{3,2},{4,5},{5,4},{6,7},{7,6},{8,9},{9,8},{10,11... | collective-permute-start | bytes 786440 | tf_op jit(solution)/shard_map/ppermute | solution.py:19
  33.3 14.0 %collective-permute-start.18 = (bf16[768,256]{0,1:T(8,128)(2,1)S(1)}, bf16[768,256]{0,1:T(8,128)(2,1)S(1)}, u32[]{:S(2)}, u32[]{:S(2)}) collective-permute-start(bf16[768,256]{0,1:T(8,128)(2,1)S(1)} %get-tuple-element.125), channel_id=1, source_target_pairs={{0,16},{16,0},{1,17},{17,1},{2,18},{18,2},{3,19},{19,3},{4,20},{20... | collective-permute-start | bytes 1179656 | tf_op jit(solution)/shard_map/ppermute | solution.py:19
  39.7 5.4 %collective-permute-start.15 = (f32[256]{0:T(256)S(1)}, f32[256]{0:T(256)S(1)}, u32[]{:S(2)}, u32[]{:S(2)}) collective-permute-start(f32[256]{0:T(256)S(1)} %add.148), channel_id=1, source_target_pairs={{0,3},{1,2},{2,1},{3,0},{4,7},{5,6},{6,5},{7,4},{8,11},{9,10},{10,... | collective-permute-start | bytes 3080 | tf_op jit(solution)/shard_map/ppermute | solution.py:19
  48.9 13.1 %collective-permute-start.20 = (bf16[512,256]{0,1:T(8,128)(2,1)S(1)}, bf16[512,256]{0,1:T(8,128)(2,1)S(1)}, u32[]{:S(2)}, u32[]{:S(2)}) collective-permute-start(bf16[512,256]{0,1:T(8,128)(2,1)S(1)} %get-tuple-element.122), channel_id=1, source_target_pairs={{0,4},{4,0},{8,12},{12,8},{1,5},{5,1},{9,13},{13,9},{2,6},{6,2},{1... | collective-permute-start | bytes 786440 | tf_op jit(solution)/shard_map/ppermute | solution.py:19
  50.0 8.1 %collective-permute-start.23 = (bf16[512,256]{0,1:T(8,128)(2,1)S(1)}, bf16[512,256]{0,1:T(8,128)(2,1)S(1)}, u32[]{:S(2)}, u32[]{:S(2)}) collective-permute-start(bf16[512,256]{0,1:T(8,128)(2,1)S(1)} %slice.260), channel_id=1, source_target_pairs={{0,1},{1,0},{2,3},{3,2},{4,5},{5,4},{6,7},{7,6},{8,9},{9,8},{10,11... | collective-permute-start | bytes 786440 | tf_op jit(solution)/shard_map/ppermute | solution.py:19
  51.3 8.9 %collective-permute-start.24 = (bf16[256,256]{0,1:T(8,128)(2,1)S(1)}, bf16[256,256]{0,1:T(8,128)(2,1)S(1)}, u32[]{:S(2)}, u32[]{:S(2)}) collective-permute-start(bf16[256,256]{0,1:T(8,128)(2,1)S(1)} %get-tuple-element.128), channel_id=1, source_target_pairs={{0,4},{4,0},{8,12},{12,8},{1,5},{5,1},{9,13},{13,9},{2,6},{6,2},{1... | collective-permute-start | bytes 393224 | tf_op jit(solution)/shard_map/ppermute | solution.py:19
  52.6 7.6 %collective-permute-start.25 = (bf16[256,256]{0,1:T(8,128)(2,1)S(1)}, bf16[256,256]{0,1:T(8,128)(2,1)S(1)}, u32[]{:S(2)}, u32[]{:S(2)}) collective-permute-start(bf16[256,256]{0,1:T(8,128)(2,1)S(1)} %get-tuple-element.129), channel_id=1, source_target_pairs={{0,8},{4,12},{8,0},{12,4},{1,9},{5,13},{9,1},{13,5},{2,10},{6,14},... | collective-permute-start | bytes 393224 | tf_op jit(solution)/shard_map/ppermute | solution.py:19
  54.0 13.2 %collective-permute-start.27 = (bf16[512,256]{0,1:T(8,128)(2,1)S(1)}, bf16[512,256]{0,1:T(8,128)(2,1)S(1)}, u32[]{:S(2)}, u32[]{:S(2)}) collective-permute-start(bf16[512,256]{0,1:T(8,128)(2,1)S(1)} %get-tuple-element.123), channel_id=1, source_target_pairs={{0,8},{4,12},{8,0},{12,4},{1,9},{5,13},{9,1},{13,5},{2,10},{6,14},... | collective-permute-start | bytes 786440 | tf_op jit(solution)/shard_map/ppermute | solution.py:19
  58.1 9.1 %collective-permute-start.29 = (bf16[256,256]{0,1:T(8,128)(2,1)S(1)}, bf16[256,256]{0,1:T(8,128)(2,1)S(1)}, u32[]{:S(2)}, u32[]{:S(2)}) collective-permute-start(bf16[256,256]{0,1:T(8,128)(2,1)S(1)} %get-tuple-element.116), channel_id=1, source_target_pairs={{0,12},{4,8},{8,4},{12,0},{1,13},{5,9},{9,5},{13,1},{2,14},{6,10},... | collective-permute-start | bytes 393224 | tf_op jit(solution)/shard_map/ppermute | solution.py:19
  60.3 7.0 %collective-permute-start.30 = (bf16[256,256]{0,1:T(8,128)(2,1)S(1)}, bf16[256,256]{0,1:T(8,128)(2,1)S(1)}, u32[]{:S(2)}, u32[]{:S(2)}) collective-permute-start(bf16[256,256]{0,1:T(8,128)(2,1)S(1)} %add_convert_fusion.5), channel_id=1, source_target_pairs={{0,1},{1,0},{2,3},{3,2},{4,5},{5,4},{6,7},{7,6},{8,9},{9,8},{10,11... | collective-permute-start | bytes 393224 | tf_op jit(solution)/shard_map/ppermute | solution.py:19
  62.0 8.5 %collective-permute-start.21 = (bf16[256,256]{0,1:T(8,128)(2,1)S(1)}, bf16[256,256]{0,1:T(8,128)(2,1)S(1)}, u32[]{:S(2)}, u32[]{:S(2)}) collective-permute-start(bf16[256,256]{0,1:T(8,128)(2,1)S(1)} %get-tuple-element.71), channel_id=1, source_target_pairs={{0,4},{4,0},{8,12},{12,8},{1,5},{5,1},{9,13},{13,9},{2,6},{6,2},{1... | collective-permute-start | bytes 393224 | tf_op jit(solution)/shard_map/ppermute | solution.py:19
  62.8 7.8 %collective-permute-start.22 = (bf16[256,256]{0,1:T(8,128)(2,1)S(1)}, bf16[256,256]{0,1:T(8,128)(2,1)S(1)}, u32[]{:S(2)}, u32[]{:S(2)}) collective-permute-start(bf16[256,256]{0,1:T(8,128)(2,1)S(1)} %get-tuple-element.72), channel_id=1, source_target_pairs={{0,8},{4,12},{8,0},{12,4},{1,9},{5,13},{9,1},{13,5},{2,10},{6,14},... | collective-permute-start | bytes 393224 | tf_op jit(solution)/shard_map/ppermute | solution.py:19
  67.4 5.9 %collective-permute-start.26 = (bf16[256,256]{0,1:T(8,128)(2,1)S(1)}, bf16[256,256]{0,1:T(8,128)(2,1)S(1)}, u32[]{:S(2)}, u32[]{:S(2)}) collective-permute-start(bf16[256,256]{0,1:T(8,128)(2,1)S(1)} %add_convert_fusion.4), channel_id=1, source_target_pairs={{0,12},{4,8},{8,4},{12,0},{1,13},{5,9},{9,5},{13,1},{2,14},{6,10},... | collective-permute-start | bytes 393224 | tf_op jit(solution)/shard_map/ppermute | solution.py:19
  69.0 7.1 %collective-permute-start.28 = (bf16[256,256]{0,1:T(8,128)(2,1)S(1)}, bf16[256,256]{0,1:T(8,128)(2,1)S(1)}, u32[]{:S(2)}, u32[]{:S(2)}) collective-permute-start(bf16[256,256]{0,1:T(8,128)(2,1)S(1)} %add_convert_fusion.3), channel_id=1, source_target_pairs={{0,1},{1,0},{2,3},{3,2},{4,5},{5,4},{6,7},{7,6},{8,9},{9,8},{10,11... | collective-permute-start | bytes 393224 | tf_op jit(solution)/shard_map/ppermute | solution.py:19
  69.2 6.8 %collective-permute-start.31 = (bf16[256,256]{0,1:T(8,128)(2,1)S(1)}, bf16[256,256]{0,1:T(8,128)(2,1)S(1)}, u32[]{:S(2)}, u32[]{:S(2)}) collective-permute-start(bf16[256,256]{0,1:T(8,128)(2,1)S(1)} %get-tuple-element.114), channel_id=1, source_target_pairs={{0,2},{1,3},{2,0},{3,1},{4,6},{5,7},{6,4},{7,5},{8,10},{9,11},{10,... | collective-permute-start | bytes 393224 | tf_op jit(solution)/shard_map/ppermute | solution.py:19
  76.2 6.5 %collective-permute-start.34 = (bf16[256,256]{0,1:T(8,128)(2,1)S(1)}, bf16[256,256]{0,1:T(8,128)(2,1)S(1)}, u32[]{:S(2)}, u32[]{:S(2)}) collective-permute-start(bf16[256,256]{0,1:T(8,128)(2,1)S(1)} %get-tuple-element.76), channel_id=1, source_target_pairs={{0,12},{4,8},{8,4},{12,0},{1,13},{5,9},{9,5},{13,1},{2,14},{6,10},... | collective-permute-start | bytes 393224 | tf_op jit(solution)/shard_map/ppermute | solution.py:19
  78.7 7.3 %collective-permute-start.36 = (bf16[256,256]{0,1:T(8,128)(2,1)S(1)}, bf16[256,256]{0,1:T(8,128)(2,1)S(1)}, u32[]{:S(2)}, u32[]{:S(2)}) collective-permute-start(bf16[256,256]{0,1:T(8,128)(2,1)S(1)} %get-tuple-element.76), channel_id=1, source_target_pairs={{0,2},{1,3},{2,0},{3,1},{4,6},{5,7},{6,4},{7,5},{8,10},{9,11},{10,... | collective-permute-start | bytes 393224 | tf_op jit(solution)/shard_map/ppermute | solution.py:19
  80.6 7.4 %collective-permute-start.32 = (bf16[256,256]{0,1:T(8,128)(2,1)S(1)}, bf16[256,256]{0,1:T(8,128)(2,1)S(1)}, u32[]{:S(2)}, u32[]{:S(2)}) collective-permute-start(bf16[256,256]{0,1:T(8,128)(2,1)S(1)} %get-tuple-element.76), channel_id=1, source_target_pairs={{0,4},{4,0},{8,12},{12,8},{1,5},{5,1},{9,13},{13,9},{2,6},{6,2},{1... | collective-permute-start | bytes 393224 | tf_op jit(solution)/shard_map/ppermute | solution.py:19
  80.8 7.3 %collective-permute-start.33 = (bf16[256,256]{0,1:T(8,128)(2,1)S(1)}, bf16[256,256]{0,1:T(8,128)(2,1)S(1)}, u32[]{:S(2)}, u32[]{:S(2)}) collective-permute-start(bf16[256,256]{0,1:T(8,128)(2,1)S(1)} %get-tuple-element.76), channel_id=1, source_target_pairs={{0,8},{4,12},{8,0},{12,4},{1,9},{5,13},{9,1},{13,5},{2,10},{6,14},... | collective-permute-start | bytes 393224 | tf_op jit(solution)/shard_map/ppermute | solution.py:19
  86.0 12.9 %collective-permute-start.40 = (bf16[512,256]{0,1:T(8,128)(2,1)S(1)}, bf16[512,256]{0,1:T(8,128)(2,1)S(1)}, u32[]{:S(2)}, u32[]{:S(2)}) collective-permute-start(bf16[512,256]{0,1:T(8,128)(2,1)S(1)} %constant_dynamic-update-slice_fusion.20), channel_id=1, source_target_pairs={{0,8},{4,12},{8,0},{12,4},{1,9},{5,13},{9,1},{13,5},{2,10},{6,14},... | collective-permute-start | bytes 786440 | tf_op jit(solution)/shard_map/ppermute | solution.py:19
  87.2 11.8 %collective-permute-start.39 = (bf16[512,256]{0,1:T(8,128)(2,1)S(1)}, bf16[512,256]{0,1:T(8,128)(2,1)S(1)}, u32[]{:S(2)}, u32[]{:S(2)}) collective-permute-start(bf16[512,256]{0,1:T(8,128)(2,1)S(1)} %constant_dynamic-update-slice_fusion.20), channel_id=1, source_target_pairs={{0,4},{4,0},{8,12},{12,8},{1,5},{5,1},{9,13},{13,9},{2,6},{6,2},{1... | collective-permute-start | bytes 786440 | tf_op jit(solution)/shard_map/ppermute | solution.py:19
  88.2 8.5 %collective-permute-start.38 = (bf16[256,256]{0,1:T(8,128)(2,1)S(1)}, bf16[256,256]{0,1:T(8,128)(2,1)S(1)}, u32[]{:S(2)}, u32[]{:S(2)}) collective-permute-start(bf16[256,256]{0,1:T(8,128)(2,1)S(1)} %collective-permute-done.36), channel_id=1, source_target_pairs={{0,12},{4,8},{8,4},{12,0},{1,13},{5,9},{9,5},{13,1},{2,14},{6,10},... | collective-permute-start | bytes 393224 | tf_op jit(solution)/shard_map/ppermute | solution.py:19
  89.7 7.1 %collective-permute-start.37 = (bf16[256,256]{0,1:T(8,128)(2,1)S(1)}, bf16[256,256]{0,1:T(8,128)(2,1)S(1)}, u32[]{:S(2)}, u32[]{:S(2)}) collective-permute-start(bf16[256,256]{0,1:T(8,128)(2,1)S(1)} %collective-permute-done.36), channel_id=1, source_target_pairs={{0,1},{1,0},{2,3},{3,2},{4,5},{5,4},{6,7},{7,6},{8,9},{9,8},{10,11... | collective-permute-start | bytes 393224 | tf_op jit(solution)/shard_map/ppermute | solution.py:19
  96.7 6.4 %collective-permute-start.41 = (bf16[512,256]{0,1:T(8,128)(2,1)S(1)}, bf16[512,256]{0,1:T(8,128)(2,1)S(1)}, u32[]{:S(2)}, u32[]{:S(2)}) collective-permute-start(bf16[512,256]{0,1:T(8,128)(2,1)S(1)} %pad_maximum_fusion.1), channel_id=1, source_target_pairs={{0,1},{1,0},{2,3},{3,2},{4,5},{5,4},{6,7},{7,6},{8,9},{9,8},{10,11... | collective-permute-start | bytes 786440 | tf_op jit(solution)/shard_map/ppermute | solution.py:19
  96.8 6.4 %collective-permute-start.42 = (bf16[256,256]{0,1:T(8,128)(2,1)S(1)}, bf16[256,256]{0,1:T(8,128)(2,1)S(1)}, u32[]{:S(2)}, u32[]{:S(2)}) collective-permute-start(bf16[256,256]{0,1:T(8,128)(2,1)S(1)} %collective-permute-done.37), channel_id=1, source_target_pairs={{0,4},{4,0},{8,12},{12,8},{1,5},{5,1},{9,13},{13,9},{2,6},{6,2},{1... | collective-permute-start | bytes 393224 | tf_op jit(solution)/shard_map/ppermute | solution.py:19
  97.2 5.9 %collective-permute-start.43 = (bf16[256,256]{0,1:T(8,128)(2,1)S(1)}, bf16[256,256]{0,1:T(8,128)(2,1)S(1)}, u32[]{:S(2)}, u32[]{:S(2)}) collective-permute-start(bf16[256,256]{0,1:T(8,128)(2,1)S(1)} %collective-permute-done.37), channel_id=1, source_target_pairs={{0,8},{4,12},{8,0},{12,4},{1,9},{5,13},{9,1},{13,5},{2,10},{6,14},... | collective-permute-start | bytes 393224 | tf_op jit(solution)/shard_map/ppermute | solution.py:19
  103.9 14.0 %collective-permute-start.50 = (bf16[768,256]{0,1:T(8,128)(2,1)S(1)}, bf16[768,256]{0,1:T(8,128)(2,1)S(1)}, u32[]{:S(2)}, u32[]{:S(2)}) collective-permute-start(bf16[768,256]{0,1:T(8,128)(2,1)S(1)} %get-tuple-element.98), channel_id=1, source_target_pairs={{0,16},{16,0},{1,17},{17,1},{2,18},{18,2},{3,19},{19,3},{4,20},{20... | collective-permute-start | bytes 1179656 | tf_op jit(solution)/shard_map/ppermute | solution.py:19
  109.7 5.4 %collective-permute-start.47 = (f32[256]{0:T(256)S(1)}, f32[256]{0:T(256)S(1)}, u32[]{:S(2)}, u32[]{:S(2)}) collective-permute-start(f32[256]{0:T(256)S(1)} %add.172), channel_id=1, source_target_pairs={{0,3},{1,2},{2,1},{3,0},{4,7},{5,6},{6,5},{7,4},{8,11},{9,10},{10,... | collective-permute-start | bytes 3080 | tf_op jit(solution)/shard_map/ppermute | solution.py:19
  118.6 8.5 %collective-permute-start.55 = (bf16[512,256]{0,1:T(8,128)(2,1)S(1)}, bf16[512,256]{0,1:T(8,128)(2,1)S(1)}, u32[]{:S(2)}, u32[]{:S(2)}) collective-permute-start(bf16[512,256]{0,1:T(8,128)(2,1)S(1)} %slice.285), channel_id=1, source_target_pairs={{0,1},{1,0},{2,3},{3,2},{4,5},{5,4},{6,7},{7,6},{8,9},{9,8},{10,11... | collective-permute-start | bytes 786440 | tf_op jit(solution)/shard_map/ppermute | solution.py:19
  119.7 9.0 %collective-permute-start.56 = (bf16[256,256]{0,1:T(8,128)(2,1)S(1)}, bf16[256,256]{0,1:T(8,128)(2,1)S(1)}, u32[]{:S(2)}, u32[]{:S(2)}) collective-permute-start(bf16[256,256]{0,1:T(8,128)(2,1)S(1)} %get-tuple-element.126), channel_id=1, source_target_pairs={{0,4},{4,0},{8,12},{12,8},{1,5},{5,1},{9,13},{13,9},{2,6},{6,2},{1... | collective-permute-start | bytes 393224 | tf_op jit(solution)/shard_map/ppermute | solution.py:19
  121.0 7.7 %collective-permute-start.57 = (bf16[256,256]{0,1:T(8,128)(2,1)S(1)}, bf16[256,256]{0,1:T(8,128)(2,1)S(1)}, u32[]{:S(2)}, u32[]{:S(2)}) collective-permute-start(bf16[256,256]{0,1:T(8,128)(2,1)S(1)} %get-tuple-element.127), channel_id=1, source_target_pairs={{0,8},{4,12},{8,0},{12,4},{1,9},{5,13},{9,1},{13,5},{2,10},{6,14},... | collective-permute-start | bytes 393224 | tf_op jit(solution)/shard_map/ppermute | solution.py:19
  123.1 8.5 %collective-permute-start.52 = (bf16[512,256]{0,1:T(8,128)(2,1)S(1)}, bf16[512,256]{0,1:T(8,128)(2,1)S(1)}, u32[]{:S(2)}, u32[]{:S(2)}) collective-permute-start(bf16[512,256]{0,1:T(8,128)(2,1)S(1)} %get-tuple-element.118), channel_id=1, source_target_pairs={{0,4},{4,0},{8,12},{12,8},{1,5},{5,1},{9,13},{13,9},{2,6},{6,2},{1... | collective-permute-start | bytes 786440 | tf_op jit(solution)/shard_map/ppermute | solution.py:19
  124.1 9.9 %collective-permute-start.59 = (bf16[512,256]{0,1:T(8,128)(2,1)S(1)}, bf16[512,256]{0,1:T(8,128)(2,1)S(1)}, u32[]{:S(2)}, u32[]{:S(2)}) collective-permute-start(bf16[512,256]{0,1:T(8,128)(2,1)S(1)} %get-tuple-element.119), channel_id=1, source_target_pairs={{0,8},{4,12},{8,0},{12,4},{1,9},{5,13},{9,1},{13,5},{2,10},{6,14},... | collective-permute-start | bytes 786440 | tf_op jit(solution)/shard_map/ppermute | solution.py:19
  127.1 8.4 %collective-permute-start.61 = (bf16[256,256]{0,1:T(8,128)(2,1)S(1)}, bf16[256,256]{0,1:T(8,128)(2,1)S(1)}, u32[]{:S(2)}, u32[]{:S(2)}) collective-permute-start(bf16[256,256]{0,1:T(8,128)(2,1)S(1)} %get-tuple-element.109), channel_id=1, source_target_pairs={{0,12},{4,8},{8,4},{12,0},{1,13},{5,9},{9,5},{13,1},{2,14},{6,10},... | collective-permute-start | bytes 393224 | tf_op jit(solution)/shard_map/ppermute | solution.py:19
  131.6 8.9 %collective-permute-start.53 = (bf16[256,256]{0,1:T(8,128)(2,1)S(1)}, bf16[256,256]{0,1:T(8,128)(2,1)S(1)}, u32[]{:S(2)}, u32[]{:S(2)}) collective-permute-start(bf16[256,256]{0,1:T(8,128)(2,1)S(1)} %get-tuple-element.93), channel_id=1, source_target_pairs={{0,4},{4,0},{8,12},{12,8},{1,5},{5,1},{9,13},{13,9},{2,6},{6,2},{1... | collective-permute-start | bytes 393224 | tf_op jit(solution)/shard_map/ppermute | solution.py:19
  133.2 7.3 %collective-permute-start.54 = (bf16[256,256]{0,1:T(8,128)(2,1)S(1)}, bf16[256,256]{0,1:T(8,128)(2,1)S(1)}, u32[]{:S(2)}, u32[]{:S(2)}) collective-permute-start(bf16[256,256]{0,1:T(8,128)(2,1)S(1)} %get-tuple-element.94), channel_id=1, source_target_pairs={{0,8},{4,12},{8,0},{12,4},{1,9},{5,13},{9,1},{13,5},{2,10},{6,14},... | collective-permute-start | bytes 393224 | tf_op jit(solution)/shard_map/ppermute | solution.py:19
  135.7 5.9 %collective-permute-start.58 = (bf16[256,256]{0,1:T(8,128)(2,1)S(1)}, bf16[256,256]{0,1:T(8,128)(2,1)S(1)}, u32[]{:S(2)}, u32[]{:S(2)}) collective-permute-start(bf16[256,256]{0,1:T(8,128)(2,1)S(1)} %add_convert_fusion.1), channel_id=1, source_target_pairs={{0,12},{4,8},{8,4},{12,0},{1,13},{5,9},{9,5},{13,1},{2,14},{6,10},... | collective-permute-start | bytes 393224 | tf_op jit(solution)/shard_map/ppermute | solution.py:19
  137.2 6.3 %collective-permute-start.60 = (bf16[256,256]{0,1:T(8,128)(2,1)S(1)}, bf16[256,256]{0,1:T(8,128)(2,1)S(1)}, u32[]{:S(2)}, u32[]{:S(2)}) collective-permute-start(bf16[256,256]{0,1:T(8,128)(2,1)S(1)} %add_convert_fusion), channel_id=1, source_target_pairs={{0,1},{1,0},{2,3},{3,2},{4,5},{5,4},{6,7},{7,6},{8,9},{9,8},{10,11... | collective-permute-start | bytes 393224 | tf_op jit(solution)/shard_map/ppermute | solution.py:19
  137.8 7.3 %collective-permute-start.63 = (bf16[256,256]{0,1:T(8,128)(2,1)S(1)}, bf16[256,256]{0,1:T(8,128)(2,1)S(1)}, u32[]{:S(2)}, u32[]{:S(2)}) collective-permute-start(bf16[256,256]{0,1:T(8,128)(2,1)S(1)} %get-tuple-element.105), channel_id=1, source_target_pairs={{0,2},{1,3},{2,0},{3,1},{4,6},{5,7},{6,4},{7,5},{8,10},{9,11},{10,... | collective-permute-start | bytes 393224 | tf_op jit(solution)/shard_map/ppermute | solution.py:19
  (17 other events, 65.6 us)

commit v3 on v1

--- a/solution.py
+++ b/solution.py
@@ -56,7 +56,8 @@
     b[3, 2] = xor_move(b[0, 2], "row", 3)
     b[0, 3] = xor_move(b[0, 2], "feat", 1)
     for r in (1, 2):
-        b[r, 1], b[r, 2] = split(xor_move(join(b[0, 1], b[0, 2]), "row", r))
+        pair = join(after(b[0, 1], b[0, 2]), b[0, 2])
+        b[r, 1], b[r, 2] = split(xor_move(pair, "row", r))
     b[3, 1], b[3, 3] = split(xor_move(join(b[3, 0], b[3, 2]), "feat", 1))
     for r in (1, 2):
         b[r, 3] = xor_move(b[0, 3], "row", r)
@@ -87,7 +88,7 @@
         send("feat", 1, one),
     )
     near = b[0, 0] + send("row", 1, b[1, 0])[0] + send("row", 2, b[2, 0])[0]
-    return near + near_across + one + two
+    return lax.optimization_barrier(near + two) + near_across + one
 
 
 def any_mesh(samples, own_rows):
@@ -145,7 +146,7 @@
         in_specs=[pl.BlockSpec(memory_space=pl.ANY)],
         out_specs=[pl.BlockSpec(memory_space=pl.ANY) for places in ARRIVALS],
         scratch_shapes=[pltpu.SemaphoreType.DMA((count,))],
-        compiler_params=pltpu.CompilerParams(vmem_limit_bytes=1 << 20),
+        compiler_params=pltpu.CompilerParams(vmem_limit_bytes=44 << 20),
         cost_estimate=pl.CostEstimate(
             flops=0, bytes_accessed=2 * samples.size * 2, transcendentals=0
         ),
@@ -168,7 +169,8 @@
         dirs = gather(own_rows.astype(jnp.bfloat16))
         summed_proj = 0.0
         for g, places in enumerate(ARRIVALS):
-            blocks = lax.optimization_barrier([dirs[p] for p in places])
+            blocks = [dirs[p] for p in places]
+            blocks = lax.optimization_barrier(blocks + [dirs[3, 2]])[: len(places)]
             part = jnp.dot(
                 groups[g], join(*blocks), preferred_element_type=jnp.float32
             )

time: 145 us -> 140 us (0.966)
  waiting for transfers between devices: 52 us -> 43.5 us
  local copies, waits for them, and re-layouts: 6.22 us -> 3.45 us
  starting transfers between devices: 73.7 us -> 76.1 us
  Pallas kernels: 1.06 us -> 3 us
    ppermute x64, waiting for transfers between devices: 52 us -> 43.5 us  [xor_move(): return lax.ppermute(block, axis, [(i, i ^ mask) for i in range(count)])]
    unnamed x27 -> x33, local copies, waits for them, and re-layouts: 5.86 us -> 3.09 us
    ppermute x64, starting transfers between devices: 73.7 us -> 76.1 us  [xor_move(): return lax.ppermute(block, axis, [(i, i ^ mask) for i in range(count)])]
    pallas_call x1, Pallas kernels: 1.06 us -> 3 us  [regroup(): pl.pallas_call(kernel, out_shape=[jax.ShapeDtypeStruct((rows_here, len(pl...]
  transfers between devices with their start and end apart: 64 -> 64, of which waited for: 35 -> 35; matrix products, arithmetic and copies ran while one was open for 6% -> 6% of each run, Pallas kernels for 1% -> 2%
where the time goes in v3:
time: 140 us
  starting transfers between devices  76.1 us (54%)
  waiting for transfers between devices  43.5 us (31%)
  matrix products  10.8 us (8%)
  local copies, waits for them, and re-layouts  3.45 us (2%)
  Pallas kernels  3 us (2%)
  other arithmetic  1.82 us (1%)
    ppermute x64, starting transfers between devices, xor_move(): return lax.ppermute(block, axis, [(i, i ^ mask) for i in range(count)])  76.1 us
    ppermute x64, waiting for transfers between devices, xor_move(): return lax.ppermute(block, axis, [(i, i ^ mask) for i in range(count)])  43.5 us
    dot_general x6, matrix products, on_device(): lax.dot_general(groups[g], residue, (((0,), (0,)), ((), ())), preferred_e...  6.16 us
    dot_general x6, matrix products, on_device(): part = jnp.dot(groups[g], join(*blocks), preferred_element_type=jnp.float32)  4.6 us
    unnamed x33, local copies, waits for them, and re-layouts  3.09 us
    pallas_call x1, Pallas kernels, regroup(): pl.pallas_call(kernel, out_shape=[jax.ShapeDtypeStruct((rows_here, len(pl...  3 us
  transfers between devices with their start and end apart: 64, of which 35 were waited for; matrix products, arithmetic and copies ran while one was open for 6% of the time, Pallas kernels for 2%

profile of v3, /device:TPU:0, one launch (start us, length us, event | category | flops | bytes accessed | tf_op | source)
XLA Modules:
  0.0 139.8 jit_solution(15410687956158330646)
XLA Ops:
  1.7 4.1 %collective-permute-start.4 = (bf16[256,256]{0,1:T(8,128)(2,1)S(1)}, bf16[256,256]{0,1:T(8,128)(2,1)S(1)}, u32[]{:S(2)}, u32[]{:S(2)}) collective-permute-start(bf16[256,256]{0,1:T(8,128)(2,1)S(1)} %bitcast_convert_fusion), channel_id=1, source_target_pairs={{0,2},{1,3},{2,0},{3,1},{4,6},{5,7},{6,4},{7,5},{8,10},{9,11},{10,... | collective-permute-start | bytes 393224 | tf_op jit(solution)/shard_map/ppermute | solution.py:19
  5.8 1.6 %collective-permute-start.3 = (bf16[256,256]{0,1:T(8,128)(2,1)S(1)}, bf16[256,256]{0,1:T(8,128)(2,1)S(1)}, u32[]{:S(2)}, u32[]{:S(2)}) collective-permute-start(bf16[256,256]{0,1:T(8,128)(2,1)S(1)} %bitcast_convert_fusion), channel_id=1, source_target_pairs={{0,1},{1,0},{2,3},{3,2},{4,5},{5,4},{6,7},{7,6},{8,9},{9,8},{10,11... | collective-permute-start | bytes 393224 | tf_op jit(solution)/shard_map/ppermute | solution.py:19
  7.4 2.4 %collective-permute-start.2 = (bf16[256,256]{0,1:T(8,128)(2,1)S(1)}, bf16[256,256]{0,1:T(8,128)(2,1)S(1)}, u32[]{:S(2)}, u32[]{:S(2)}) collective-permute-start(bf16[256,256]{0,1:T(8,128)(2,1)S(1)} %bitcast_convert_fusion), channel_id=1, source_target_pairs={{0,12},{4,8},{8,4},{12,0},{1,13},{5,9},{9,5},{13,1},{2,14},{6,10},... | collective-permute-start | bytes 393224 | tf_op jit(solution)/shard_map/ppermute | solution.py:19
  10.9 3.0 %regroup.1 = (bf16[768,1536]{1,0:T(8,128)(2,1)S(1)}, bf16[768,1536]{1,0:T(8,128)(2,1)S(1)}, bf16[768,1024]{1,0:T(8,128)(2,1)S(1)}) custom-call(bf16[768,4096]{1,0:T(8,128)(2,1)} %bitcast.59), custom_call_target="tpu_custom_call" | custom-call | bytes 12582912 | tf_op jit(solution)/shard_map/regroup/pallas_call | solution.py:140
  14.0 2.5 %collective-permute-start.5 = (bf16[256,256]{0,1:T(8,128)(2,1)S(1)}, bf16[256,256]{0,1:T(8,128)(2,1)S(1)}, u32[]{:S(2)}, u32[]{:S(2)}) collective-permute-start(bf16[256,256]{0,1:T(8,128)(2,1)S(1)} %collective-permute-done.4), channel_id=1, source_target_pairs={{0,12},{4,8},{8,4},{12,0},{1,13},{5,9},{9,5},{13,1},{2,14},{6,10},... | collective-permute-start | bytes 393224 | tf_op jit(solution)/shard_map/ppermute | solution.py:19
  18.1 3.2 %collective-permute-done.5 = bf16[256,256]{0,1:T(8,128)(2,1)S(1)} collective-permute-done((bf16[256,256]{0,1:T(8,128)(2,1)S(1)}, bf16[256,256]{0,1:T(8,128)(2,1)S(1)}, u32[]{:S(2)}, u32[]{:S(2)}) %collective-permute-start.5) | collective-permute-done | bytes 131104 | tf_op jit(solution)/shard_map/ppermute | solution.py:19
  24.0 1.6 %collective-permute-start.11 = (bf16[256,256]{0,1:T(8,128)(2,1)S(1)}, bf16[256,256]{0,1:T(8,128)(2,1)S(1)}, u32[]{:S(2)}, u32[]{:S(2)}) collective-permute-start(bf16[256,256]{0,1:T(8,128)(2,1)S(1)} %collective-permute-done.6), channel_id=1, source_target_pairs={{0,8},{4,12},{8,0},{12,4},{1,9},{5,13},{9,1},{13,5},{2,10},{6,14},... | collective-permute-start | bytes 393224 | tf_op jit(solution)/shard_map/ppermute | solution.py:19
  25.5 1.5 %collective-permute-start.10 = (bf16[256,256]{0,1:T(8,128)(2,1)S(1)}, bf16[256,256]{0,1:T(8,128)(2,1)S(1)}, u32[]{:S(2)}, u32[]{:S(2)}) collective-permute-start(bf16[256,256]{0,1:T(8,128)(2,1)S(1)} %collective-permute-done.6), channel_id=1, source_target_pairs={{0,4},{4,0},{8,12},{12,8},{1,5},{5,1},{9,13},{13,9},{2,6},{6,2},{1... | collective-permute-start | bytes 393224 | tf_op jit(solution)/shard_map/ppermute | solution.py:19
  28.9 1.6 %collective-permute-done.10 = bf16[256,256]{0,1:T(8,128)(2,1)S(1)} collective-permute-done((bf16[256,256]{0,1:T(8,128)(2,1)S(1)}, bf16[256,256]{0,1:T(8,128)(2,1)S(1)}, u32[]{:S(2)}, u32[]{:S(2)}) %collective-permute-start.10) | collective-permute-done | bytes 131104 | tf_op jit(solution)/shard_map/ppermute | solution.py:19
  31.3 1.5 %collective-permute-start.12 = (f32[256]{0:T(256)S(1)}, f32[256]{0:T(256)S(1)}, u32[]{:S(2)}, u32[]{:S(2)}) collective-permute-start(f32[256]{0:T(256)S(1)} %get-tuple-element.116), channel_id=1, source_target_pairs={{0,12},{4,8},{8,4},{12,0},{1,13},{5,9},{9,5},{13,1},{2,14},{6,10},... | collective-permute-start | bytes 3080 | tf_op jit(solution)/shard_map/ppermute | solution.py:19
  32.8 1.5 %collective-permute-start.13 = (f32[256]{0:T(256)S(1)}, f32[256]{0:T(256)S(1)}, u32[]{:S(2)}, u32[]{:S(2)}) collective-permute-start(f32[256]{0:T(256)S(1)} %get-tuple-element.116), channel_id=1, source_target_pairs={{0,8},{4,12},{8,0},{12,4},{1,9},{5,13},{9,1},{13,5},{2,10},{6,14},... | collective-permute-start | bytes 3080 | tf_op jit(solution)/shard_map/ppermute | solution.py:19
  36.3 1.5 %collective-permute-done.14 = f32[256]{0:T(256)S(1)} collective-permute-done((f32[256]{0:T(256)S(1)}, f32[256]{0:T(256)S(1)}, u32[]{:S(2)}, u32[]{:S(2)}) %collective-permute-start.14) | collective-permute-done | bytes 1056 | tf_op jit(solution)/shard_map/ppermute | solution.py:19
  38.4 1.3 collective-permute-start.16
  39.8 2.5 %collective-permute-start.17 = (f32[256]{0:T(256)S(1)}, f32[256]{0:T(256)S(1)}, u32[]{:S(2)}, u32[]{:S(2)}) collective-permute-start(f32[256]{0:T(256)S(1)} %add.148), channel_id=1, source_target_pairs={{0,1},{1,0},{2,3},{3,2},{4,5},{5,4},{6,7},{7,6},{8,9},{9,8},{10,11... | collective-permute-start | bytes 3080 | tf_op jit(solution)/shard_map/ppermute | solution.py:19
  46.8 2.0 %collective-permute-start.24 = (bf16[512,256]{0,1:T(8,128)(2,1)S(1)}, bf16[512,256]{0,1:T(8,128)(2,1)S(1)}, u32[]{:S(2)}, u32[]{:S(2)}) collective-permute-start(bf16[512,256]{0,1:T(8,128)(2,1)S(1)} %slice.265), channel_id=1, source_target_pairs={{0,1},{1,0},{2,3},{3,2},{4,5},{5,4},{6,7},{7,6},{8,9},{9,8},{10,11... | collective-permute-start | bytes 786440 | tf_op jit(solution)/shard_map/ppermute | solution.py:19
  49.7 1.6 %collective-permute-start.22 = (bf16[512,256]{0,1:T(8,128)(2,1)S(1)}, bf16[512,256]{0,1:T(8,128)(2,1)S(1)}, u32[]{:S(2)}, u32[]{:S(2)}) collective-permute-start(bf16[512,256]{0,1:T(8,128)(2,1)S(1)} %get-tuple-element.114), channel_id=1, source_target_pairs={{0,4},{4,0},{8,12},{12,8},{1,5},{5,1},{9,13},{13,9},{2,6},{6,2},{1... | collective-permute-start | bytes 786440 | tf_op jit(solution)/shard_map/ppermute | solution.py:19
  51.3 1.5 %collective-permute-start.23 = (bf16[512,256]{0,1:T(8,128)(2,1)S(1)}, bf16[512,256]{0,1:T(8,128)(2,1)S(1)}, u32[]{:S(2)}, u32[]{:S(2)}) collective-permute-start(bf16[512,256]{0,1:T(8,128)(2,1)S(1)} %get-tuple-element.115), channel_id=1, source_target_pairs={{0,8},{4,12},{8,0},{12,4},{1,9},{5,13},{9,1},{13,5},{2,10},{6,14},... | collective-permute-start | bytes 786440 | tf_op jit(solution)/shard_map/ppermute | solution.py:19
  54.9 2.5 %collective-permute-start.25 = (bf16[256,256]{0,1:T(8,128)(2,1)S(1)}, bf16[256,256]{0,1:T(8,128)(2,1)S(1)}, u32[]{:S(2)}, u32[]{:S(2)}) collective-permute-start(bf16[256,256]{0,1:T(8,128)(2,1)S(1)} %get-tuple-element.104), channel_id=1, source_target_pairs={{0,12},{4,8},{8,4},{12,0},{1,13},{5,9},{9,5},{13,1},{2,14},{6,10},... | collective-permute-start | bytes 393224 | tf_op jit(solution)/shard_map/ppermute | solution.py:19
  57.5 1.8 %collective-permute-start.28 = (bf16[256,256]{0,1:T(8,128)(2,1)S(1)}, bf16[256,256]{0,1:T(8,128)(2,1)S(1)}, u32[]{:S(2)}, u32[]{:S(2)}) collective-permute-start(bf16[256,256]{0,1:T(8,128)(2,1)S(1)} %add_convert_fusion.5), channel_id=1, source_target_pairs={{0,1},{1,0},{2,3},{3,2},{4,5},{5,4},{6,7},{7,6},{8,9},{9,8},{10,11... | collective-permute-start | bytes 393224 | tf_op jit(solution)/shard_map/ppermute | solution.py:19
  60.7 1.9 %collective-permute-done.28 = bf16[256,256]{0,1:T(8,128)(2,1)S(1)} collective-permute-done((bf16[256,256]{0,1:T(8,128)(2,1)S(1)}, bf16[256,256]{0,1:T(8,128)(2,1)S(1)}, u32[]{:S(2)}, u32[]{:S(2)}) %collective-permute-start.28) | collective-permute-done | bytes 131104 | tf_op jit(solution)/shard_map/ppermute | solution.py:19
  63.7 1.8 %collective-permute-start.31 = (bf16[256,256]{0,1:T(8,128)(2,1)S(1)}, bf16[256,256]{0,1:T(8,128)(2,1)S(1)}, u32[]{:S(2)}, u32[]{:S(2)}) collective-permute-start(bf16[256,256]{0,1:T(8,128)(2,1)S(1)} %add_convert_fusion.3), channel_id=1, source_target_pairs={{0,1},{1,0},{2,3},{3,2},{4,5},{5,4},{6,7},{7,6},{8,9},{9,8},{10,11... | collective-permute-start | bytes 393224 | tf_op jit(solution)/shard_map/ppermute | solution.py:19
  65.5 1.4 collective-permute-start.30
  66.9 1.8 %collective-permute-done.29 = bf16[256,256]{0,1:T(8,128)(2,1)S(1)} collective-permute-done((bf16[256,256]{0,1:T(8,128)(2,1)S(1)}, bf16[256,256]{0,1:T(8,128)(2,1)S(1)}, u32[]{:S(2)}, u32[]{:S(2)}) %collective-permute-start.29) | collective-permute-done | bytes 131104 | tf_op jit(solution)/shard_map/ppermute | solution.py:19
  70.0 1.4 collective-permute-done.30
  72.2 2.4 %collective-permute-start.36 = (bf16[256,256]{0,1:T(8,128)(2,1)S(1)}, bf16[256,256]{0,1:T(8,128)(2,1)S(1)}, u32[]{:S(2)}, u32[]{:S(2)}) collective-permute-start(bf16[256,256]{0,1:T(8,128)(2,1)S(1)} %get-tuple-element.70), channel_id=1, source_target_pairs={{0,2},{1,3},{2,0},{3,1},{4,6},{5,7},{6,4},{7,5},{8,10},{9,11},{10,... | collective-permute-start | bytes 393224 | tf_op jit(solution)/shard_map/ppermute | solution.py:19
  74.7 1.8 %collective-permute-start.34 = (bf16[256,256]{0,1:T(8,128)(2,1)S(1)}, bf16[256,256]{0,1:T(8,128)(2,1)S(1)}, u32[]{:S(2)}, u32[]{:S(2)}) collective-permute-start(bf16[256,256]{0,1:T(8,128)(2,1)S(1)} %get-tuple-element.70), channel_id=1, source_target_pairs={{0,12},{4,8},{8,4},{12,0},{1,13},{5,9},{9,5},{13,1},{2,14},{6,10},... | collective-permute-start | bytes 393224 | tf_op jit(solution)/shard_map/ppermute | solution.py:19
  79.3 1.3 collective-permute-done.35
  80.6 1.4 collective-permute-start.37
  82.1 2.1 %collective-permute-start.39 = (bf16[512,256]{0,1:T(8,128)(2,1)S(1)}, bf16[512,256]{0,1:T(8,128)(2,1)S(1)}, u32[]{:S(2)}, u32[]{:S(2)}) collective-permute-start(bf16[512,256]{0,1:T(8,128)(2,1)S(1)} %constant_dynamic-update-slice_fusion.20), channel_id=1, source_target_pairs={{0,4},{4,0},{8,12},{12,8},{1,5},{5,1},{9,13},{13,9},{2,6},{6,2},{1... | collective-permute-start | bytes 786440 | tf_op jit(solution)/shard_map/ppermute | solution.py:19
  85.5 2.5 %collective-permute-done.37 = bf16[256,256]{0,1:T(8,128)(2,1)S(1)} collective-permute-done((bf16[256,256]{0,1:T(8,128)(2,1)S(1)}, bf16[256,256]{0,1:T(8,128)(2,1)S(1)}, u32[]{:S(2)}, u32[]{:S(2)}) %collective-permute-start.37) | collective-permute-done | bytes 131104 | tf_op jit(solution)/shard_map/ppermute | solution.py:19
  90.2 1.5 %collective-permute-start.42 = (bf16[256,256]{0,1:T(8,128)(2,1)S(1)}, bf16[256,256]{0,1:T(8,128)(2,1)S(1)}, u32[]{:S(2)}, u32[]{:S(2)}) collective-permute-start(bf16[256,256]{0,1:T(8,128)(2,1)S(1)} %collective-permute-done.38), channel_id=1, source_target_pairs={{0,4},{4,0},{8,12},{12,8},{1,5},{5,1},{9,13},{13,9},{2,6},{6,2},{1... | collective-permute-start | bytes 393224 | tf_op jit(solution)/shard_map/ppermute | solution.py:19
  92.7 1.7 %collective-permute-done.41 = bf16[512,256]{0,1:T(8,128)(2,1)S(1)} collective-permute-done((bf16[512,256]{0,1:T(8,128)(2,1)S(1)}, bf16[512,256]{0,1:T(8,128)(2,1)S(1)}, u32[]{:S(2)}, u32[]{:S(2)}) %collective-permute-start.41) | collective-permute-done | bytes 262176 | tf_op jit(solution)/shard_map/ppermute | solution.py:19
  96.9 1.9 %collective-permute-start.45 = (f32[256]{0:T(256)S(1)}, f32[256]{0:T(256)S(1)}, u32[]{:S(2)}, u32[]{:S(2)}) collective-permute-start(f32[256]{0:T(256)S(1)} %get-tuple-element.110), channel_id=1, source_target_pairs={{0,8},{4,12},{8,0},{12,4},{1,9},{5,13},{9,1},{13,5},{2,10},{6,14},... | collective-permute-start | bytes 3080 | tf_op jit(solution)/shard_map/ppermute | solution.py:19
  100.5 1.9 %collective-permute-done.46 = f32[256]{0:T(256)S(1)} collective-permute-done((f32[256]{0:T(256)S(1)}, f32[256]{0:T(256)S(1)}, u32[]{:S(2)}, u32[]{:S(2)}) %collective-permute-start.46) | collective-permute-done | bytes 1056 | tf_op jit(solution)/shard_map/ppermute | solution.py:19
  103.1 1.8 %collective-permute-start.48 = (f32[256]{0:T(256)S(1)}, f32[256]{0:T(256)S(1)}, u32[]{:S(2)}, u32[]{:S(2)}) collective-permute-start(f32[256]{0:T(256)S(1)} %add.172), channel_id=1, source_target_pairs={{0,2},{1,3},{2,0},{3,1},{4,6},{5,7},{6,4},{7,5},{8,10},{9,11},{10,... | collective-permute-start | bytes 3080 | tf_op jit(solution)/shard_map/ppermute | solution.py:19
  105.0 1.9 %collective-permute-start.49 = (f32[256]{0:T(256)S(1)}, f32[256]{0:T(256)S(1)}, u32[]{:S(2)}, u32[]{:S(2)}) collective-permute-start(f32[256]{0:T(256)S(1)} %add.172), channel_id=1, source_target_pairs={{0,1},{1,0},{2,3},{3,2},{4,5},{5,4},{6,7},{7,6},{8,9},{9,8},{10,11... | collective-permute-start | bytes 3080 | tf_op jit(solution)/shard_map/ppermute | solution.py:19
  109.8 2.0 %fusion.5 = bf16[1024,256]{0,1:T(8,128)(2,1)S(1)} fusion(bf16[768,1024]{1,0:T(8,128)(2,1)} %copy-done.2, bf16[768,256]{0,1:T(8,128)(2,1)S(1)} %get-tuple-element.90, bf16[768,256]{0,1:T(8,128)(2,1)S(1)} %collective-permute-done.50, f32[256]{0:T(256)S(1)} %collective-permute-done.51, f32[256]{0:T(256)S(1)} %get-tuple-element.91), kind=kOutput, calls=%fused_computation.17 | convolution fusion | flops 404881408 | bytes 2885632 | tf_op jit(solution)/shard_map/dot_general | solution.py:190
  113.6 1.7 %collective-permute-start.59 = (bf16[256,256]{0,1:T(8,128)(2,1)S(1)}, bf16[256,256]{0,1:T(8,128)(2,1)S(1)}, u32[]{:S(2)}, u32[]{:S(2)}) collective-permute-start(bf16[256,256]{0,1:T(8,128)(2,1)S(1)} %get-tuple-element.119), channel_id=1, source_target_pairs={{0,8},{4,12},{8,0},{12,4},{1,9},{5,13},{9,1},{13,5},{2,10},{6,14},... | collective-permute-start | bytes 393224 | tf_op jit(solution)/shard_map/ppermute | solution.py:19
  115.2 1.4 collective-permute-start.56
  116.8 1.9 %collective-permute-start.55 = (bf16[512,256]{0,1:T(8,128)(2,1)S(1)}, bf16[512,256]{0,1:T(8,128)(2,1)S(1)}, u32[]{:S(2)}, u32[]{:S(2)}) collective-permute-start(bf16[512,256]{0,1:T(8,128)(2,1)S(1)} %get-tuple-element.109), channel_id=1, source_target_pairs={{0,8},{4,12},{8,0},{12,4},{1,9},{5,13},{9,1},{13,5},{2,10},{6,14},... | collective-permute-start | bytes 786440 | tf_op jit(solution)/shard_map/ppermute | solution.py:19
  119.7 3.7 %collective-permute-done.56 = bf16[512,256]{0,1:T(8,128)(2,1)S(1)} collective-permute-done((bf16[512,256]{0,1:T(8,128)(2,1)S(1)}, bf16[512,256]{0,1:T(8,128)(2,1)S(1)}, u32[]{:S(2)}, u32[]{:S(2)}) %collective-permute-start.56) | collective-permute-done | bytes 262176 | tf_op jit(solution)/shard_map/ppermute | solution.py:19
  123.4 1.3 collective-permute-start.57
  124.7 1.8 %collective-permute-start.60 = (bf16[256,256]{0,1:T(8,128)(2,1)S(1)}, bf16[256,256]{0,1:T(8,128)(2,1)S(1)}, u32[]{:S(2)}, u32[]{:S(2)}) collective-permute-start(bf16[256,256]{0,1:T(8,128)(2,1)S(1)} %add_convert_fusion.2), channel_id=1, source_target_pairs={{0,1},{1,0},{2,3},{3,2},{4,5},{5,4},{6,7},{7,6},{8,9},{9,8},{10,11... | collective-permute-start | bytes 393224 | tf_op jit(solution)/shard_map/ppermute | solution.py:19
  127.2 1.3 collective-permute-start.53
  128.5 1.2 collective-permute-done.60
  131.7 1.3 collective-permute-start.63
  133.0 1.5 %collective-permute-start.62 = (bf16[256,256]{0,1:T(8,128)(2,1)S(1)}, bf16[256,256]{0,1:T(8,128)(2,1)S(1)}, u32[]{:S(2)}, u32[]{:S(2)}) collective-permute-start(bf16[256,256]{0,1:T(8,128)(2,1)S(1)} %add_convert_fusion.1), channel_id=1, source_target_pairs={{0,12},{4,8},{8,4},{12,0},{1,13},{5,9},{9,5},{13,1},{2,14},{6,10},... | collective-permute-start | bytes 393224 | tf_op jit(solution)/shard_map/ppermute | solution.py:19
  134.5 3.5 %collective-permute-done.61 = bf16[256,256]{0,1:T(8,128)(2,1)S(1)} collective-permute-done((bf16[256,256]{0,1:T(8,128)(2,1)S(1)}, bf16[256,256]{0,1:T(8,128)(2,1)S(1)}, u32[]{:S(2)}, u32[]{:S(2)}) %collective-permute-start.61) | collective-permute-done | bytes 131104 | tf_op jit(solution)/shard_map/ppermute | solution.py:19
  (178 shorter events, 46.1 us)
Async XLA Ops:
  1.7 12.2 %collective-permute-start.4 = (bf16[256,256]{0,1:T(8,128)(2,1)S(1)}, bf16[256,256]{0,1:T(8,128)(2,1)S(1)}, u32[]{:S(2)}, u32[]{:S(2)}) collective-permute-start(bf16[256,256]{0,1:T(8,128)(2,1)S(1)} %bitcast_convert_fusion), channel_id=1, source_target_pairs={{0,2},{1,3},{2,0},{3,1},{4,6},{5,7},{6,4},{7,5},{8,10},{9,11},{10,... | collective-permute-start | bytes 393224 | tf_op jit(solution)/shard_map/ppermute | solution.py:19
  5.8 8.1 %collective-permute-start.3 = (bf16[256,256]{0,1:T(8,128)(2,1)S(1)}, bf16[256,256]{0,1:T(8,128)(2,1)S(1)}, u32[]{:S(2)}, u32[]{:S(2)}) collective-permute-start(bf16[256,256]{0,1:T(8,128)(2,1)S(1)} %bitcast_convert_fusion), channel_id=1, source_target_pairs={{0,1},{1,0},{2,3},{3,2},{4,5},{5,4},{6,7},{7,6},{8,9},{9,8},{10,11... | collective-permute-start | bytes 393224 | tf_op jit(solution)/shard_map/ppermute | solution.py:19
  7.4 9.7 %collective-permute-start.2 = (bf16[256,256]{0,1:T(8,128)(2,1)S(1)}, bf16[256,256]{0,1:T(8,128)(2,1)S(1)}, u32[]{:S(2)}, u32[]{:S(2)}) collective-permute-start(bf16[256,256]{0,1:T(8,128)(2,1)S(1)} %bitcast_convert_fusion), channel_id=1, source_target_pairs={{0,12},{4,8},{8,4},{12,0},{1,13},{5,9},{9,5},{13,1},{2,14},{6,10},... | collective-permute-start | bytes 393224 | tf_op jit(solution)/shard_map/ppermute | solution.py:19
  9.9 7.7 %collective-permute-start.1 = (bf16[256,256]{0,1:T(8,128)(2,1)S(1)}, bf16[256,256]{0,1:T(8,128)(2,1)S(1)}, u32[]{:S(2)}, u32[]{:S(2)}) collective-permute-start(bf16[256,256]{0,1:T(8,128)(2,1)S(1)} %bitcast_convert_fusion), channel_id=1, source_target_pairs={{0,8},{4,12},{8,0},{12,4},{1,9},{5,13},{9,1},{13,5},{2,10},{6,14},... | collective-permute-start | bytes 393224 | tf_op jit(solution)/shard_map/ppermute | solution.py:19
  10.4 7.7 %collective-permute-start = (bf16[256,256]{0,1:T(8,128)(2,1)S(1)}, bf16[256,256]{0,1:T(8,128)(2,1)S(1)}, u32[]{:S(2)}, u32[]{:S(2)}) collective-permute-start(bf16[256,256]{0,1:T(8,128)(2,1)S(1)} %bitcast_convert_fusion), channel_id=1, source_target_pairs={{0,4},{4,0},{8,12},{12,8},{1,5},{5,1},{9,13},{13,9},{2,6},{6,2},{1... | collective-permute-start | bytes 393224 | tf_op jit(solution)/shard_map/ppermute | solution.py:19
  14.0 7.3 %collective-permute-start.5 = (bf16[256,256]{0,1:T(8,128)(2,1)S(1)}, bf16[256,256]{0,1:T(8,128)(2,1)S(1)}, u32[]{:S(2)}, u32[]{:S(2)}) collective-permute-start(bf16[256,256]{0,1:T(8,128)(2,1)S(1)} %collective-permute-done.4), channel_id=1, source_target_pairs={{0,12},{4,8},{8,4},{12,0},{1,13},{5,9},{9,5},{13,1},{2,14},{6,10},... | collective-permute-start | bytes 393224 | tf_op jit(solution)/shard_map/ppermute | solution.py:19
  16.5 10.5 %collective-permute-start.8 = (bf16[512,256]{0,1:T(8,128)(2,1)S(1)}, bf16[512,256]{0,1:T(8,128)(2,1)S(1)}, u32[]{:S(2)}, u32[]{:S(2)}) collective-permute-start(bf16[512,256]{0,1:T(8,128)(2,1)S(1)} %constant_dynamic-update-slice_fusion.6), channel_id=1, source_target_pairs={{0,8},{4,12},{8,0},{12,4},{1,9},{5,13},{9,1},{13,5},{2,10},{6,14},... | collective-permute-start | bytes 786440 | tf_op jit(solution)/shard_map/ppermute | solution.py:19
  17.1 10.0 %collective-permute-start.7 = (bf16[512,256]{0,1:T(8,128)(2,1)S(1)}, bf16[512,256]{0,1:T(8,128)(2,1)S(1)}, u32[]{:S(2)}, u32[]{:S(2)}) collective-permute-start(bf16[512,256]{0,1:T(8,128)(2,1)S(1)} %constant_dynamic-update-slice_fusion.6), channel_id=1, source_target_pairs={{0,4},{4,0},{8,12},{12,8},{1,5},{5,1},{9,13},{13,9},{2,6},{6,2},{1... | collective-permute-start | bytes 786440 | tf_op jit(solution)/shard_map/ppermute | solution.py:19
  17.6 6.4 %collective-permute-start.6 = (bf16[256,256]{0,1:T(8,128)(2,1)S(1)}, bf16[256,256]{0,1:T(8,128)(2,1)S(1)}, u32[]{:S(2)}, u32[]{:S(2)}) collective-permute-start(bf16[256,256]{0,1:T(8,128)(2,1)S(1)} %collective-permute-done.4), channel_id=1, source_target_pairs={{0,1},{1,0},{2,3},{3,2},{4,5},{5,4},{6,7},{7,6},{8,9},{9,8},{10,11... | collective-permute-start | bytes 393224 | tf_op jit(solution)/shard_map/ppermute | solution.py:19
  21.3 6.7 %collective-permute-start.9 = (bf16[512,256]{0,1:T(8,128)(2,1)S(1)}, bf16[512,256]{0,1:T(8,128)(2,1)S(1)}, u32[]{:S(2)}, u32[]{:S(2)}) collective-permute-start(bf16[512,256]{0,1:T(8,128)(2,1)S(1)} %pad_maximum_fusion), channel_id=1, source_target_pairs={{0,1},{1,0},{2,3},{3,2},{4,5},{5,4},{6,7},{7,6},{8,9},{9,8},{10,11... | collective-permute-start | bytes 786440 | tf_op jit(solution)/shard_map/ppermute | solution.py:19
  31.2 13.8 %collective-permute-start.18 = (bf16[768,256]{0,1:T(8,128)(2,1)S(1)}, bf16[768,256]{0,1:T(8,128)(2,1)S(1)}, u32[]{:S(2)}, u32[]{:S(2)}) collective-permute-start(bf16[768,256]{0,1:T(8,128)(2,1)S(1)} %get-tuple-element.117), channel_id=1, source_target_pairs={{0,16},{16,0},{1,17},{17,1},{2,18},{18,2},{3,19},{19,3},{4,20},{20... | collective-permute-start | bytes 1179656 | tf_op jit(solution)/shard_map/ppermute | solution.py:19
  37.9 5.4 %collective-permute-start.15 = (f32[256]{0:T(256)S(1)}, f32[256]{0:T(256)S(1)}, u32[]{:S(2)}, u32[]{:S(2)}) collective-permute-start(f32[256]{0:T(256)S(1)} %add.148), channel_id=1, source_target_pairs={{0,3},{1,2},{2,1},{3,0},{4,7},{5,6},{6,5},{7,4},{8,11},{9,10},{10,... | collective-permute-start | bytes 3080 | tf_op jit(solution)/shard_map/ppermute | solution.py:19
  45.7 11.8 %collective-permute-start.26 = (bf16[256,256]{0,1:T(8,128)(2,1)S(1)}, bf16[256,256]{0,1:T(8,128)(2,1)S(1)}, u32[]{:S(2)}, u32[]{:S(2)}) collective-permute-start(bf16[256,256]{0,1:T(8,128)(2,1)S(1)} %get-tuple-element.120), channel_id=1, source_target_pairs={{0,4},{4,0},{8,12},{12,8},{1,5},{5,1},{9,13},{13,9},{2,6},{6,2},{1... | collective-permute-start | bytes 393224 | tf_op jit(solution)/shard_map/ppermute | solution.py:19
  46.3 11.2 %collective-permute-start.27 = (bf16[256,256]{0,1:T(8,128)(2,1)S(1)}, bf16[256,256]{0,1:T(8,128)(2,1)S(1)}, u32[]{:S(2)}, u32[]{:S(2)}) collective-permute-start(bf16[256,256]{0,1:T(8,128)(2,1)S(1)} %get-tuple-element.121), channel_id=1, source_target_pairs={{0,8},{4,12},{8,0},{12,4},{1,9},{5,13},{9,1},{13,5},{2,10},{6,14},... | collective-permute-start | bytes 393224 | tf_op jit(solution)/shard_map/ppermute | solution.py:19
  46.8 8.1 %collective-permute-start.24 = (bf16[512,256]{0,1:T(8,128)(2,1)S(1)}, bf16[512,256]{0,1:T(8,128)(2,1)S(1)}, u32[]{:S(2)}, u32[]{:S(2)}) collective-permute-start(bf16[512,256]{0,1:T(8,128)(2,1)S(1)} %slice.265), channel_id=1, source_target_pairs={{0,1},{1,0},{2,3},{3,2},{4,5},{5,4},{6,7},{7,6},{8,9},{9,8},{10,11... | collective-permute-start | bytes 786440 | tf_op jit(solution)/shard_map/ppermute | solution.py:19
  49.7 10.3 %collective-permute-start.22 = (bf16[512,256]{0,1:T(8,128)(2,1)S(1)}, bf16[512,256]{0,1:T(8,128)(2,1)S(1)}, u32[]{:S(2)}, u32[]{:S(2)}) collective-permute-start(bf16[512,256]{0,1:T(8,128)(2,1)S(1)} %get-tuple-element.114), channel_id=1, source_target_pairs={{0,4},{4,0},{8,12},{12,8},{1,5},{5,1},{9,13},{13,9},{2,6},{6,2},{1... | collective-permute-start | bytes 786440 | tf_op jit(solution)/shard_map/ppermute | solution.py:19
  51.3 9.4 %collective-permute-start.23 = (bf16[512,256]{0,1:T(8,128)(2,1)S(1)}, bf16[512,256]{0,1:T(8,128)(2,1)S(1)}, u32[]{:S(2)}, u32[]{:S(2)}) collective-permute-start(bf16[512,256]{0,1:T(8,128)(2,1)S(1)} %get-tuple-element.115), channel_id=1, source_target_pairs={{0,8},{4,12},{8,0},{12,4},{1,9},{5,13},{9,1},{13,5},{2,10},{6,14},... | collective-permute-start | bytes 786440 | tf_op jit(solution)/shard_map/ppermute | solution.py:19
  54.9 7.6 %collective-permute-start.25 = (bf16[256,256]{0,1:T(8,128)(2,1)S(1)}, bf16[256,256]{0,1:T(8,128)(2,1)S(1)}, u32[]{:S(2)}, u32[]{:S(2)}) collective-permute-start(bf16[256,256]{0,1:T(8,128)(2,1)S(1)} %get-tuple-element.104), channel_id=1, source_target_pairs={{0,12},{4,8},{8,4},{12,0},{1,13},{5,9},{9,5},{13,1},{2,14},{6,10},... | collective-permute-start | bytes 393224 | tf_op jit(solution)/shard_map/ppermute | solution.py:19
  57.5 5.0 %collective-permute-start.28 = (bf16[256,256]{0,1:T(8,128)(2,1)S(1)}, bf16[256,256]{0,1:T(8,128)(2,1)S(1)}, u32[]{:S(2)}, u32[]{:S(2)}) collective-permute-start(bf16[256,256]{0,1:T(8,128)(2,1)S(1)} %add_convert_fusion.5), channel_id=1, source_target_pairs={{0,1},{1,0},{2,3},{3,2},{4,5},{5,4},{6,7},{7,6},{8,9},{9,8},{10,11... | collective-permute-start | bytes 393224 | tf_op jit(solution)/shard_map/ppermute | solution.py:19
  59.4 7.6 %collective-permute-start.20 = (bf16[256,256]{0,1:T(8,128)(2,1)S(1)}, bf16[256,256]{0,1:T(8,128)(2,1)S(1)}, u32[]{:S(2)}, u32[]{:S(2)}) collective-permute-start(bf16[256,256]{0,1:T(8,128)(2,1)S(1)} %get-tuple-element.112), channel_id=1, source_target_pairs={{0,4},{4,0},{8,12},{12,8},{1,5},{5,1},{9,13},{13,9},{2,6},{6,2},{1... | collective-permute-start | bytes 393224 | tf_op jit(solution)/shard_map/ppermute | solution.py:19
  60.0 7.0 %collective-permute-start.21 = (bf16[256,256]{0,1:T(8,128)(2,1)S(1)}, bf16[256,256]{0,1:T(8,128)(2,1)S(1)}, u32[]{:S(2)}, u32[]{:S(2)}) collective-permute-start(bf16[256,256]{0,1:T(8,128)(2,1)S(1)} %get-tuple-element.113), channel_id=1, source_target_pairs={{0,8},{4,12},{8,0},{12,4},{1,9},{5,13},{9,1},{13,5},{2,10},{6,14},... | collective-permute-start | bytes 393224 | tf_op jit(solution)/shard_map/ppermute | solution.py:19
  62.7 6.0 %collective-permute-start.29 = (bf16[256,256]{0,1:T(8,128)(2,1)S(1)}, bf16[256,256]{0,1:T(8,128)(2,1)S(1)}, u32[]{:S(2)}, u32[]{:S(2)}) collective-permute-start(bf16[256,256]{0,1:T(8,128)(2,1)S(1)} %get-tuple-element.103), channel_id=1, source_target_pairs={{0,2},{1,3},{2,0},{3,1},{4,6},{5,7},{6,4},{7,5},{8,10},{9,11},{10,... | collective-permute-start | bytes 393224 | tf_op jit(solution)/shard_map/ppermute | solution.py:19
  63.7 6.3 %collective-permute-start.31 = (bf16[256,256]{0,1:T(8,128)(2,1)S(1)}, bf16[256,256]{0,1:T(8,128)(2,1)S(1)}, u32[]{:S(2)}, u32[]{:S(2)}) collective-permute-start(bf16[256,256]{0,1:T(8,128)(2,1)S(1)} %add_convert_fusion.3), channel_id=1, source_target_pairs={{0,1},{1,0},{2,3},{3,2},{4,5},{5,4},{6,7},{7,6},{8,9},{9,8},{10,11... | collective-permute-start | bytes 393224 | tf_op jit(solution)/shard_map/ppermute | solution.py:19
  65.5 5.9 %collective-permute-start.30 = (bf16[256,256]{0,1:T(8,128)(2,1)S(1)}, bf16[256,256]{0,1:T(8,128)(2,1)S(1)}, u32[]{:S(2)}, u32[]{:S(2)}) collective-permute-start(bf16[256,256]{0,1:T(8,128)(2,1)S(1)} %add_convert_fusion.4), channel_id=1, source_target_pairs={{0,12},{4,8},{8,4},{12,0},{1,13},{5,9},{9,5},{13,1},{2,14},{6,10},... | collective-permute-start | bytes 393224 | tf_op jit(solution)/shard_map/ppermute | solution.py:19
  72.2 7.1 %collective-permute-start.36 = (bf16[256,256]{0,1:T(8,128)(2,1)S(1)}, bf16[256,256]{0,1:T(8,128)(2,1)S(1)}, u32[]{:S(2)}, u32[]{:S(2)}) collective-permute-start(bf16[256,256]{0,1:T(8,128)(2,1)S(1)} %get-tuple-element.70), channel_id=1, source_target_pairs={{0,2},{1,3},{2,0},{3,1},{4,6},{5,7},{6,4},{7,5},{8,10},{9,11},{10,... | collective-permute-start | bytes 393224 | tf_op jit(solution)/shard_map/ppermute | solution.py:19
  74.6 6.0 %collective-permute-start.35 = (bf16[256,256]{0,1:T(8,128)(2,1)S(1)}, bf16[256,256]{0,1:T(8,128)(2,1)S(1)}, u32[]{:S(2)}, u32[]{:S(2)}) collective-permute-start(bf16[256,256]{0,1:T(8,128)(2,1)S(1)} %get-tuple-element.70), channel_id=1, source_target_pairs={{0,1},{1,0},{2,3},{3,2},{4,5},{5,4},{6,7},{7,6},{8,9},{9,8},{10,11... | collective-permute-start | bytes 393224 | tf_op jit(solution)/shard_map/ppermute | solution.py:19
  74.7 7.5 %collective-permute-start.34 = (bf16[256,256]{0,1:T(8,128)(2,1)S(1)}, bf16[256,256]{0,1:T(8,128)(2,1)S(1)}, u32[]{:S(2)}, u32[]{:S(2)}) collective-permute-start(bf16[256,256]{0,1:T(8,128)(2,1)S(1)} %get-tuple-element.70), channel_id=1, source_target_pairs={{0,12},{4,8},{8,4},{12,0},{1,13},{5,9},{9,5},{13,1},{2,14},{6,10},... | collective-permute-start | bytes 393224 | tf_op jit(solution)/shard_map/ppermute | solution.py:19
  76.5 8.1 %collective-permute-start.33 = (bf16[256,256]{0,1:T(8,128)(2,1)S(1)}, bf16[256,256]{0,1:T(8,128)(2,1)S(1)}, u32[]{:S(2)}, u32[]{:S(2)}) collective-permute-start(bf16[256,256]{0,1:T(8,128)(2,1)S(1)} %get-tuple-element.70), channel_id=1, source_target_pairs={{0,8},{4,12},{8,0},{12,4},{1,9},{5,13},{9,1},{13,5},{2,10},{6,14},... | collective-permute-start | bytes 393224 | tf_op jit(solution)/shard_map/ppermute | solution.py:19
  77.3 8.2 %collective-permute-start.32 = (bf16[256,256]{0,1:T(8,128)(2,1)S(1)}, bf16[256,256]{0,1:T(8,128)(2,1)S(1)}, u32[]{:S(2)}, u32[]{:S(2)}) collective-permute-start(bf16[256,256]{0,1:T(8,128)(2,1)S(1)} %get-tuple-element.70), channel_id=1, source_target_pairs={{0,4},{4,0},{8,12},{12,8},{1,5},{5,1},{9,13},{13,9},{2,6},{6,2},{1... | collective-permute-start | bytes 393224 | tf_op jit(solution)/shard_map/ppermute | solution.py:19
  80.6 7.3 %collective-permute-start.37 = (bf16[256,256]{0,1:T(8,128)(2,1)S(1)}, bf16[256,256]{0,1:T(8,128)(2,1)S(1)}, u32[]{:S(2)}, u32[]{:S(2)}) collective-permute-start(bf16[256,256]{0,1:T(8,128)(2,1)S(1)} %collective-permute-done.36), channel_id=1, source_target_pairs={{0,12},{4,8},{8,4},{12,0},{1,13},{5,9},{9,5},{13,1},{2,14},{6,10},... | collective-permute-start | bytes 393224 | tf_op jit(solution)/shard_map/ppermute | solution.py:19
  82.0 9.7 %collective-permute-start.40 = (bf16[512,256]{0,1:T(8,128)(2,1)S(1)}, bf16[512,256]{0,1:T(8,128)(2,1)S(1)}, u32[]{:S(2)}, u32[]{:S(2)}) collective-permute-start(bf16[512,256]{0,1:T(8,128)(2,1)S(1)} %constant_dynamic-update-slice_fusion.20), channel_id=1, source_target_pairs={{0,8},{4,12},{8,0},{12,4},{1,9},{5,13},{9,1},{13,5},{2,10},{6,14},... | collective-permute-start | bytes 786440 | tf_op jit(solution)/shard_map/ppermute | solution.py:19
  82.1 9.6 %collective-permute-start.39 = (bf16[512,256]{0,1:T(8,128)(2,1)S(1)}, bf16[512,256]{0,1:T(8,128)(2,1)S(1)}, u32[]{:S(2)}, u32[]{:S(2)}) collective-permute-start(bf16[512,256]{0,1:T(8,128)(2,1)S(1)} %constant_dynamic-update-slice_fusion.20), channel_id=1, source_target_pairs={{0,4},{4,0},{8,12},{12,8},{1,5},{5,1},{9,13},{13,9},{2,6},{6,2},{1... | collective-permute-start | bytes 786440 | tf_op jit(solution)/shard_map/ppermute | solution.py:19
  88.0 6.4 %collective-permute-start.41 = (bf16[512,256]{0,1:T(8,128)(2,1)S(1)}, bf16[512,256]{0,1:T(8,128)(2,1)S(1)}, u32[]{:S(2)}, u32[]{:S(2)}) collective-permute-start(bf16[512,256]{0,1:T(8,128)(2,1)S(1)} %pad_maximum_fusion.1), channel_id=1, source_target_pairs={{0,1},{1,0},{2,3},{3,2},{4,5},{5,4},{6,7},{7,6},{8,9},{9,8},{10,11... | collective-permute-start | bytes 786440 | tf_op jit(solution)/shard_map/ppermute | solution.py:19
  89.5 5.0 %collective-permute-start.43 = (bf16[256,256]{0,1:T(8,128)(2,1)S(1)}, bf16[256,256]{0,1:T(8,128)(2,1)S(1)}, u32[]{:S(2)}, u32[]{:S(2)}) collective-permute-start(bf16[256,256]{0,1:T(8,128)(2,1)S(1)} %collective-permute-done.38), channel_id=1, source_target_pairs={{0,8},{4,12},{8,0},{12,4},{1,9},{5,13},{9,1},{13,5},{2,10},{6,14},... | collective-permute-start | bytes 393224 | tf_op jit(solution)/shard_map/ppermute | solution.py:19
  90.2 5.0 %collective-permute-start.42 = (bf16[256,256]{0,1:T(8,128)(2,1)S(1)}, bf16[256,256]{0,1:T(8,128)(2,1)S(1)}, u32[]{:S(2)}, u32[]{:S(2)}) collective-permute-start(bf16[256,256]{0,1:T(8,128)(2,1)S(1)} %collective-permute-done.38), channel_id=1, source_target_pairs={{0,4},{4,0},{8,12},{12,8},{1,5},{5,1},{9,13},{13,9},{2,6},{6,2},{1... | collective-permute-start | bytes 393224 | tf_op jit(solution)/shard_map/ppermute | solution.py:19
  102.5 5.4 %collective-permute-start.47 = (f32[256]{0:T(256)S(1)}, f32[256]{0:T(256)S(1)}, u32[]{:S(2)}, u32[]{:S(2)}) collective-permute-start(f32[256]{0:T(256)S(1)} %add.172), channel_id=1, source_target_pairs={{0,3},{1,2},{2,1},{3,0},{4,7},{5,6},{6,5},{7,4},{8,11},{9,10},{10,... | collective-permute-start | bytes 3080 | tf_op jit(solution)/shard_map/ppermute | solution.py:19
  112.8 11.9 %collective-permute-start.58 = (bf16[256,256]{0,1:T(8,128)(2,1)S(1)}, bf16[256,256]{0,1:T(8,128)(2,1)S(1)}, u32[]{:S(2)}, u32[]{:S(2)}) collective-permute-start(bf16[256,256]{0,1:T(8,128)(2,1)S(1)} %get-tuple-element.118), channel_id=1, source_target_pairs={{0,4},{4,0},{8,12},{12,8},{1,5},{5,1},{9,13},{13,9},{2,6},{6,2},{1... | collective-permute-start | bytes 393224 | tf_op jit(solution)/shard_map/ppermute | solution.py:19
  113.6 11.1 %collective-permute-start.59 = (bf16[256,256]{0,1:T(8,128)(2,1)S(1)}, bf16[256,256]{0,1:T(8,128)(2,1)S(1)}, u32[]{:S(2)}, u32[]{:S(2)}) collective-permute-start(bf16[256,256]{0,1:T(8,128)(2,1)S(1)} %get-tuple-element.119), channel_id=1, source_target_pairs={{0,8},{4,12},{8,0},{12,4},{1,9},{5,13},{9,1},{13,5},{2,10},{6,14},... | collective-permute-start | bytes 393224 | tf_op jit(solution)/shard_map/ppermute | solution.py:19
  115.2 8.1 %collective-permute-start.56 = (bf16[512,256]{0,1:T(8,128)(2,1)S(1)}, bf16[512,256]{0,1:T(8,128)(2,1)S(1)}, u32[]{:S(2)}, u32[]{:S(2)}) collective-permute-start(bf16[512,256]{0,1:T(8,128)(2,1)S(1)} %slice.290), channel_id=1, source_target_pairs={{0,1},{1,0},{2,3},{3,2},{4,5},{5,4},{6,7},{7,6},{8,9},{9,8},{10,11... | collective-permute-start | bytes 786440 | tf_op jit(solution)/shard_map/ppermute | solution.py:19
  116.6 10.6 %collective-permute-start.54 = (bf16[512,256]{0,1:T(8,128)(2,1)S(1)}, bf16[512,256]{0,1:T(8,128)(2,1)S(1)}, u32[]{:S(2)}, u32[]{:S(2)}) collective-permute-start(bf16[512,256]{0,1:T(8,128)(2,1)S(1)} %get-tuple-element.108), channel_id=1, source_target_pairs={{0,4},{4,0},{8,12},{12,8},{1,5},{5,1},{9,13},{13,9},{2,6},{6,2},{1... | collective-permute-start | bytes 786440 | tf_op jit(solution)/shard_map/ppermute | solution.py:19
  116.8 11.7 %collective-permute-start.55 = (bf16[512,256]{0,1:T(8,128)(2,1)S(1)}, bf16[512,256]{0,1:T(8,128)(2,1)S(1)}, u32[]{:S(2)}, u32[]{:S(2)}) collective-permute-start(bf16[512,256]{0,1:T(8,128)(2,1)S(1)} %get-tuple-element.109), channel_id=1, source_target_pairs={{0,8},{4,12},{8,0},{12,4},{1,9},{5,13},{9,1},{13,5},{2,10},{6,14},... | collective-permute-start | bytes 786440 | tf_op jit(solution)/shard_map/ppermute | solution.py:19
  123.4 7.2 %collective-permute-start.57 = (bf16[256,256]{0,1:T(8,128)(2,1)S(1)}, bf16[256,256]{0,1:T(8,128)(2,1)S(1)}, u32[]{:S(2)}, u32[]{:S(2)}) collective-permute-start(bf16[256,256]{0,1:T(8,128)(2,1)S(1)} %get-tuple-element.99), channel_id=1, source_target_pairs={{0,12},{4,8},{8,4},{12,0},{1,13},{5,9},{9,5},{13,1},{2,14},{6,10},... | collective-permute-start | bytes 393224 | tf_op jit(solution)/shard_map/ppermute | solution.py:19
  124.7 5.0 %collective-permute-start.60 = (bf16[256,256]{0,1:T(8,128)(2,1)S(1)}, bf16[256,256]{0,1:T(8,128)(2,1)S(1)}, u32[]{:S(2)}, u32[]{:S(2)}) collective-permute-start(bf16[256,256]{0,1:T(8,128)(2,1)S(1)} %add_convert_fusion.2), channel_id=1, source_target_pairs={{0,1},{1,0},{2,3},{3,2},{4,5},{5,4},{6,7},{7,6},{8,9},{9,8},{10,11... | collective-permute-start | bytes 393224 | tf_op jit(solution)/shard_map/ppermute | solution.py:19
  126.6 7.9 %collective-permute-start.52 = (bf16[256,256]{0,1:T(8,128)(2,1)S(1)}, bf16[256,256]{0,1:T(8,128)(2,1)S(1)}, u32[]{:S(2)}, u32[]{:S(2)}) collective-permute-start(bf16[256,256]{0,1:T(8,128)(2,1)S(1)} %get-tuple-element.106), channel_id=1, source_target_pairs={{0,4},{4,0},{8,12},{12,8},{1,5},{5,1},{9,13},{13,9},{2,6},{6,2},{1... | collective-permute-start | bytes 393224 | tf_op jit(solution)/shard_map/ppermute | solution.py:19
  127.2 7.3 %collective-permute-start.53 = (bf16[256,256]{0,1:T(8,128)(2,1)S(1)}, bf16[256,256]{0,1:T(8,128)(2,1)S(1)}, u32[]{:S(2)}, u32[]{:S(2)}) collective-permute-start(bf16[256,256]{0,1:T(8,128)(2,1)S(1)} %get-tuple-element.107), channel_id=1, source_target_pairs={{0,8},{4,12},{8,0},{12,4},{1,9},{5,13},{9,1},{13,5},{2,10},{6,14},... | collective-permute-start | bytes 393224 | tf_op jit(solution)/shard_map/ppermute | solution.py:19
  130.7 7.3 %collective-permute-start.61 = (bf16[256,256]{0,1:T(8,128)(2,1)S(1)}, bf16[256,256]{0,1:T(8,128)(2,1)S(1)}, u32[]{:S(2)}, u32[]{:S(2)}) collective-permute-start(bf16[256,256]{0,1:T(8,128)(2,1)S(1)} %get-tuple-element.98), channel_id=1, source_target_pairs={{0,2},{1,3},{2,0},{3,1},{4,6},{5,7},{6,4},{7,5},{8,10},{9,11},{10,... | collective-permute-start | bytes 393224 | tf_op jit(solution)/shard_map/ppermute | solution.py:19
  131.7 6.4 %collective-permute-start.63 = (bf16[256,256]{0,1:T(8,128)(2,1)S(1)}, bf16[256,256]{0,1:T(8,128)(2,1)S(1)}, u32[]{:S(2)}, u32[]{:S(2)}) collective-permute-start(bf16[256,256]{0,1:T(8,128)(2,1)S(1)} %add_convert_fusion), channel_id=1, source_target_pairs={{0,1},{1,0},{2,3},{3,2},{4,5},{5,4},{6,7},{7,6},{8,9},{9,8},{10,11... | collective-permute-start | bytes 393224 | tf_op jit(solution)/shard_map/ppermute | solution.py:19
  133.0 5.9 %collective-permute-start.62 = (bf16[256,256]{0,1:T(8,128)(2,1)S(1)}, bf16[256,256]{0,1:T(8,128)(2,1)S(1)}, u32[]{:S(2)}, u32[]{:S(2)}) collective-permute-start(bf16[256,256]{0,1:T(8,128)(2,1)S(1)} %add_convert_fusion.1), channel_id=1, source_target_pairs={{0,12},{4,8},{8,4},{12,0},{1,13},{5,9},{9,5},{13,1},{2,14},{6,10},... | collective-permute-start | bytes 393224 | tf_op jit(solution)/shard_map/ppermute | solution.py:19
  (20 other events, 237.2 us)

commit v4 on v3

--- a/solution.py
+++ b/solution.py
@@ -88,7 +88,8 @@
         send("feat", 1, one),
     )
     near = b[0, 0] + send("row", 1, b[1, 0])[0] + send("row", 2, b[2, 0])[0]
-    return lax.optimization_barrier(near + two) + near_across + one
+    near = lax.optimization_barrier(near + near_across)
+    return lax.optimization_barrier(near + two) + one
 
 
 def any_mesh(samples, own_rows):
@@ -146,7 +147,7 @@
         in_specs=[pl.BlockSpec(memory_space=pl.ANY)],
         out_specs=[pl.BlockSpec(memory_space=pl.ANY) for places in ARRIVALS],
         scratch_shapes=[pltpu.SemaphoreType.DMA((count,))],
-        compiler_params=pltpu.CompilerParams(vmem_limit_bytes=44 << 20),
+        compiler_params=pltpu.CompilerParams(vmem_limit_bytes=42 << 20),
         cost_estimate=pl.CostEstimate(
             flops=0, bytes_accessed=2 * samples.size * 2, transcendentals=0
         ),
@@ -170,7 +171,7 @@
         summed_proj = 0.0
         for g, places in enumerate(ARRIVALS):
             blocks = [dirs[p] for p in places]
-            blocks = lax.optimization_barrier(blocks + [dirs[3, 2]])[: len(places)]
+            blocks = lax.optimization_barrier(blocks + [dirs[3, 2], dirs[0, 3]])[: len(places)]
             part = jnp.dot(
                 groups[g], join(*blocks), preferred_element_type=jnp.float32
             )

time: 140 us -> 146 us (1.043)
  waiting for transfers between devices: 43.5 us -> 46.5 us
  matrix products: 10.8 us -> 13 us
    ppermute x64, waiting for transfers between devices: 43.5 us -> 46.5 us  [xor_move(): return lax.ppermute(block, axis, [(i, i ^ mask) for i in range(count)])]
    dot_general x6, matrix products: 6.16 us -> 8.42 us  [on_device(): lax.dot_general(groups[g], residue, (((0,), (0,)), ((), ())), preferred_e...]
    unnamed x33 -> x31, local copies, waits for them, and re-layouts: 3.09 us -> 4.08 us
  transfers between devices with their start and end apart: 64 -> 64, of which waited for: 35 -> 31; matrix products, arithmetic and copies ran while one was open for 6% -> 8% of each run, Pallas kernels for 2% -> 2%
where the time goes in v4:
time: 146 us; the launch traced here: 145 us
  starting transfers between devices  75.2 us (52%)
  waiting for transfers between devices  46.5 us (32%)
  matrix products  13 us (9%)
  local copies, waits for them, and re-layouts  4.44 us (3%)
  Pallas kernels  3 us (2%)
  other arithmetic  1.95 us (1%)
    ppermute x64, starting transfers between devices, xor_move(): return lax.ppermute(block, axis, [(i, i ^ mask) for i in range(count)])  75.2 us
    ppermute x64, waiting for transfers between devices, xor_move(): return lax.ppermute(block, axis, [(i, i ^ mask) for i in range(count)])  46.5 us
    dot_general x6, matrix products, on_device(): lax.dot_general(groups[g], residue, (((0,), (0,)), ((), ())), preferred_e...  8.42 us
    dot_general x6, matrix products, on_device(): part = jnp.dot(groups[g], join(*blocks), preferred_element_type=jnp.float32)  4.59 us
    unnamed x31, local copies, waits for them, and re-layouts  4.08 us
    pallas_call x1, Pallas kernels, regroup(): pl.pallas_call(kernel, out_shape=[jax.ShapeDtypeStruct((rows_here, len(pl...  3 us
  transfers between devices with their start and end apart: 64, of which 31 were waited for; matrix products, arithmetic and copies ran while one was open for 8% of the time, Pallas kernels for 2%

profile of v4, /device:TPU:0, one launch (start us, length us, event | category | flops | bytes accessed | tf_op | source)
XLA Modules:
  0.0 145.4 jit_solution(8068379356316042784)
XLA Ops:
  1.7 4.1 %collective-permute-start.4 = (bf16[256,256]{0,1:T(8,128)(2,1)S(1)}, bf16[256,256]{0,1:T(8,128)(2,1)S(1)}, u32[]{:S(2)}, u32[]{:S(2)}) collective-permute-start(bf16[256,256]{0,1:T(8,128)(2,1)S(1)} %bitcast_convert_fusion), channel_id=1, source_target_pairs={{0,2},{1,3},{2,0},{3,1},{4,6},{5,7},{6,4},{7,5},{8,10},{9,11},{10,... | collective-permute-start | bytes 393224 | tf_op jit(solution)/shard_map/ppermute | solution.py:19
  5.8 1.6 %collective-permute-start.3 = (bf16[256,256]{0,1:T(8,128)(2,1)S(1)}, bf16[256,256]{0,1:T(8,128)(2,1)S(1)}, u32[]{:S(2)}, u32[]{:S(2)}) collective-permute-start(bf16[256,256]{0,1:T(8,128)(2,1)S(1)} %bitcast_convert_fusion), channel_id=1, source_target_pairs={{0,1},{1,0},{2,3},{3,2},{4,5},{5,4},{6,7},{7,6},{8,9},{9,8},{10,11... | collective-permute-start | bytes 393224 | tf_op jit(solution)/shard_map/ppermute | solution.py:19
  7.4 2.4 %collective-permute-start.2 = (bf16[256,256]{0,1:T(8,128)(2,1)S(1)}, bf16[256,256]{0,1:T(8,128)(2,1)S(1)}, u32[]{:S(2)}, u32[]{:S(2)}) collective-permute-start(bf16[256,256]{0,1:T(8,128)(2,1)S(1)} %bitcast_convert_fusion), channel_id=1, source_target_pairs={{0,12},{4,8},{8,4},{12,0},{1,13},{5,9},{9,5},{13,1},{2,14},{6,10},... | collective-permute-start | bytes 393224 | tf_op jit(solution)/shard_map/ppermute | solution.py:19
  10.9 3.0 %regroup.1 = (bf16[768,1536]{1,0:T(8,128)(2,1)S(1)}, bf16[768,1536]{1,0:T(8,128)(2,1)S(1)}, bf16[768,1024]{1,0:T(8,128)(2,1)S(1)}) custom-call(bf16[768,4096]{1,0:T(8,128)(2,1)} %bitcast.62), custom_call_target="tpu_custom_call" | custom-call | bytes 12582912 | tf_op jit(solution)/shard_map/regroup/pallas_call | solution.py:141
  14.5 2.4 %collective-permute-start.5 = (bf16[256,256]{0,1:T(8,128)(2,1)S(1)}, bf16[256,256]{0,1:T(8,128)(2,1)S(1)}, u32[]{:S(2)}, u32[]{:S(2)}) collective-permute-start(bf16[256,256]{0,1:T(8,128)(2,1)S(1)} %collective-permute-done.4), channel_id=1, source_target_pairs={{0,12},{4,8},{8,4},{12,0},{1,13},{5,9},{9,5},{13,1},{2,14},{6,10},... | collective-permute-start | bytes 393224 | tf_op jit(solution)/shard_map/ppermute | solution.py:19
  19.0 2.8 %collective-permute-done.5 = bf16[256,256]{0,1:T(8,128)(2,1)S(1)} collective-permute-done((bf16[256,256]{0,1:T(8,128)(2,1)S(1)}, bf16[256,256]{0,1:T(8,128)(2,1)S(1)}, u32[]{:S(2)}, u32[]{:S(2)}) %collective-permute-start.5) | collective-permute-done | bytes 131104 | tf_op jit(solution)/shard_map/ppermute | solution.py:19
  21.8 1.6 %collective-permute-start.9 = (bf16[512,256]{0,1:T(8,128)(2,1)S(1)}, bf16[512,256]{0,1:T(8,128)(2,1)S(1)}, u32[]{:S(2)}, u32[]{:S(2)}) collective-permute-start(bf16[512,256]{0,1:T(8,128)(2,1)S(1)} %pad_maximum_fusion), channel_id=1, source_target_pairs={{0,1},{1,0},{2,3},{3,2},{4,5},{5,4},{6,7},{7,6},{8,9},{9,8},{10,11... | collective-permute-start | bytes 786440 | tf_op jit(solution)/shard_map/ppermute | solution.py:19
  24.3 1.6 %collective-permute-start.11 = (bf16[256,256]{0,1:T(8,128)(2,1)S(1)}, bf16[256,256]{0,1:T(8,128)(2,1)S(1)}, u32[]{:S(2)}, u32[]{:S(2)}) collective-permute-start(bf16[256,256]{0,1:T(8,128)(2,1)S(1)} %collective-permute-done.6), channel_id=1, source_target_pairs={{0,8},{4,12},{8,0},{12,4},{1,9},{5,13},{9,1},{13,5},{2,10},{6,14},... | collective-permute-start | bytes 393224 | tf_op jit(solution)/shard_map/ppermute | solution.py:19
  25.9 1.6 %collective-permute-start.10 = (bf16[256,256]{0,1:T(8,128)(2,1)S(1)}, bf16[256,256]{0,1:T(8,128)(2,1)S(1)}, u32[]{:S(2)}, u32[]{:S(2)}) collective-permute-start(bf16[256,256]{0,1:T(8,128)(2,1)S(1)} %collective-permute-done.6), channel_id=1, source_target_pairs={{0,4},{4,0},{8,12},{12,8},{1,5},{5,1},{9,13},{13,9},{2,6},{6,2},{1... | collective-permute-start | bytes 393224 | tf_op jit(solution)/shard_map/ppermute | solution.py:19
  29.3 1.6 %collective-permute-done.10 = bf16[256,256]{0,1:T(8,128)(2,1)S(1)} collective-permute-done((bf16[256,256]{0,1:T(8,128)(2,1)S(1)}, bf16[256,256]{0,1:T(8,128)(2,1)S(1)}, u32[]{:S(2)}, u32[]{:S(2)}) %collective-permute-start.10) | collective-permute-done | bytes 131104 | tf_op jit(solution)/shard_map/ppermute | solution.py:19
  31.7 1.5 %collective-permute-start.12 = (f32[256]{0:T(256)S(1)}, f32[256]{0:T(256)S(1)}, u32[]{:S(2)}, u32[]{:S(2)}) collective-permute-start(f32[256]{0:T(256)S(1)} %get-tuple-element.114), channel_id=1, source_target_pairs={{0,12},{4,8},{8,4},{12,0},{1,13},{5,9},{9,5},{13,1},{2,14},{6,10},... | collective-permute-start | bytes 3080 | tf_op jit(solution)/shard_map/ppermute | solution.py:19
  33.2 1.6 %collective-permute-start.13 = (f32[256]{0:T(256)S(1)}, f32[256]{0:T(256)S(1)}, u32[]{:S(2)}, u32[]{:S(2)}) collective-permute-start(f32[256]{0:T(256)S(1)} %get-tuple-element.114), channel_id=1, source_target_pairs={{0,8},{4,12},{8,0},{12,4},{1,9},{5,13},{9,1},{13,5},{2,10},{6,14},... | collective-permute-start | bytes 3080 | tf_op jit(solution)/shard_map/ppermute | solution.py:19
  36.7 1.6 %collective-permute-done.14 = f32[256]{0:T(256)S(1)} collective-permute-done((f32[256]{0:T(256)S(1)}, f32[256]{0:T(256)S(1)}, u32[]{:S(2)}, u32[]{:S(2)}) %collective-permute-start.14) | collective-permute-done | bytes 1056 | tf_op jit(solution)/shard_map/ppermute | solution.py:19
  38.4 1.6 %collective-permute-start.15 = (f32[256]{0:T(256)S(1)}, f32[256]{0:T(256)S(1)}, u32[]{:S(2)}, u32[]{:S(2)}) collective-permute-start(f32[256]{0:T(256)S(1)} %add.148), channel_id=1, source_target_pairs={{0,3},{1,2},{2,1},{3,0},{4,7},{5,6},{6,5},{7,4},{8,11},{9,10},{10,... | collective-permute-start | bytes 3080 | tf_op jit(solution)/shard_map/ppermute | solution.py:19
  40.2 2.6 %collective-permute-start.17 = (f32[256]{0:T(256)S(1)}, f32[256]{0:T(256)S(1)}, u32[]{:S(2)}, u32[]{:S(2)}) collective-permute-start(f32[256]{0:T(256)S(1)} %add.148), channel_id=1, source_target_pairs={{0,1},{1,0},{2,3},{3,2},{4,5},{5,4},{6,7},{7,6},{8,9},{9,8},{10,11... | collective-permute-start | bytes 3080 | tf_op jit(solution)/shard_map/ppermute | solution.py:19
  47.2 2.0 %collective-permute-start.22 = (bf16[512,256]{0,1:T(8,128)(2,1)S(1)}, bf16[512,256]{0,1:T(8,128)(2,1)S(1)}, u32[]{:S(2)}, u32[]{:S(2)}) collective-permute-start(bf16[512,256]{0,1:T(8,128)(2,1)S(1)} %slice.262), channel_id=1, source_target_pairs={{0,1},{1,0},{2,3},{3,2},{4,5},{5,4},{6,7},{7,6},{8,9},{9,8},{10,11... | collective-permute-start | bytes 786440 | tf_op jit(solution)/shard_map/ppermute | solution.py:19
  50.1 1.6 %collective-permute-start.26 = (bf16[512,256]{0,1:T(8,128)(2,1)S(1)}, bf16[512,256]{0,1:T(8,128)(2,1)S(1)}, u32[]{:S(2)}, u32[]{:S(2)}) collective-permute-start(bf16[512,256]{0,1:T(8,128)(2,1)S(1)} %get-tuple-element.110), channel_id=1, source_target_pairs={{0,4},{4,0},{8,12},{12,8},{1,5},{5,1},{9,13},{13,9},{2,6},{6,2},{1... | collective-permute-start | bytes 786440 | tf_op jit(solution)/shard_map/ppermute | solution.py:19
  51.7 1.6 %collective-permute-start.27 = (bf16[512,256]{0,1:T(8,128)(2,1)S(1)}, bf16[512,256]{0,1:T(8,128)(2,1)S(1)}, u32[]{:S(2)}, u32[]{:S(2)}) collective-permute-start(bf16[512,256]{0,1:T(8,128)(2,1)S(1)} %get-tuple-element.111), channel_id=1, source_target_pairs={{0,8},{4,12},{8,0},{12,4},{1,9},{5,13},{9,1},{13,5},{2,10},{6,14},... | collective-permute-start | bytes 786440 | tf_op jit(solution)/shard_map/ppermute | solution.py:19
  55.3 2.7 %collective-permute-start.28 = (bf16[256,256]{0,1:T(8,128)(2,1)S(1)}, bf16[256,256]{0,1:T(8,128)(2,1)S(1)}, u32[]{:S(2)}, u32[]{:S(2)}) collective-permute-start(bf16[256,256]{0,1:T(8,128)(2,1)S(1)} %get-tuple-element.102), channel_id=1, source_target_pairs={{0,12},{4,8},{8,4},{12,0},{1,13},{5,9},{9,5},{13,1},{2,14},{6,10},... | collective-permute-start | bytes 393224 | tf_op jit(solution)/shard_map/ppermute | solution.py:19
  58.0 1.8 %collective-permute-start.29 = (bf16[256,256]{0,1:T(8,128)(2,1)S(1)}, bf16[256,256]{0,1:T(8,128)(2,1)S(1)}, u32[]{:S(2)}, u32[]{:S(2)}) collective-permute-start(bf16[256,256]{0,1:T(8,128)(2,1)S(1)} %add_convert_fusion.5), channel_id=1, source_target_pairs={{0,1},{1,0},{2,3},{3,2},{4,5},{5,4},{6,7},{7,6},{8,9},{9,8},{10,11... | collective-permute-start | bytes 393224 | tf_op jit(solution)/shard_map/ppermute | solution.py:19
  61.4 1.6 %collective-permute-done.29 = bf16[256,256]{0,1:T(8,128)(2,1)S(1)} collective-permute-done((bf16[256,256]{0,1:T(8,128)(2,1)S(1)}, bf16[256,256]{0,1:T(8,128)(2,1)S(1)}, u32[]{:S(2)}, u32[]{:S(2)}) %collective-permute-start.29) | collective-permute-done | bytes 131104 | tf_op jit(solution)/shard_map/ppermute | solution.py:19
  63.2 1.9 %collective-permute-start.30 = (bf16[256,256]{0,1:T(8,128)(2,1)S(1)}, bf16[256,256]{0,1:T(8,128)(2,1)S(1)}, u32[]{:S(2)}, u32[]{:S(2)}) collective-permute-start(bf16[256,256]{0,1:T(8,128)(2,1)S(1)} %get-tuple-element.100), channel_id=1, source_target_pairs={{0,2},{1,3},{2,0},{3,1},{4,6},{5,7},{6,4},{7,5},{8,10},{9,11},{10,... | collective-permute-start | bytes 393224 | tf_op jit(solution)/shard_map/ppermute | solution.py:19
  65.1 1.4 collective-permute-start.25
  67.6 3.5 %collective-permute-done.25 = bf16[256,256]{0,1:T(8,128)(2,1)S(1)} collective-permute-done((bf16[256,256]{0,1:T(8,128)(2,1)S(1)}, bf16[256,256]{0,1:T(8,128)(2,1)S(1)}, u32[]{:S(2)}, u32[]{:S(2)}) %collective-permute-start.25) | collective-permute-done | bytes 131104 | tf_op jit(solution)/shard_map/ppermute | solution.py:19
  71.2 2.5 %collective-permute-done.31 = bf16[256,256]{0,1:T(8,128)(2,1)S(1)} collective-permute-done((bf16[256,256]{0,1:T(8,128)(2,1)S(1)}, bf16[256,256]{0,1:T(8,128)(2,1)S(1)}, u32[]{:S(2)}, u32[]{:S(2)}) %collective-permute-start.31) | collective-permute-done | bytes 131104 | tf_op jit(solution)/shard_map/ppermute | solution.py:19
  75.0 1.5 %collective-permute-start.34 = (bf16[256,256]{0,1:T(8,128)(2,1)S(1)}, bf16[256,256]{0,1:T(8,128)(2,1)S(1)}, u32[]{:S(2)}, u32[]{:S(2)}) collective-permute-start(bf16[256,256]{0,1:T(8,128)(2,1)S(1)} %multiply_convert_fusion.5), channel_id=1, source_target_pairs={{0,12},{4,8},{8,4},{12,0},{1,13},{5,9},{9,5},{13,1},{2,14},{6,10},... | collective-permute-start | bytes 393224 | tf_op jit(solution)/shard_map/ppermute | solution.py:19
  76.5 1.6 %collective-permute-start.33 = (bf16[256,256]{0,1:T(8,128)(2,1)S(1)}, bf16[256,256]{0,1:T(8,128)(2,1)S(1)}, u32[]{:S(2)}, u32[]{:S(2)}) collective-permute-start(bf16[256,256]{0,1:T(8,128)(2,1)S(1)} %multiply_convert_fusion.5), channel_id=1, source_target_pairs={{0,8},{4,12},{8,0},{12,4},{1,9},{5,13},{9,1},{13,5},{2,10},{6,14},... | collective-permute-start | bytes 393224 | tf_op jit(solution)/shard_map/ppermute | solution.py:19
  78.4 2.4 %collective-permute-done.36 = bf16[256,256]{0,1:T(8,128)(2,1)S(1)} collective-permute-done((bf16[256,256]{0,1:T(8,128)(2,1)S(1)}, bf16[256,256]{0,1:T(8,128)(2,1)S(1)}, u32[]{:S(2)}, u32[]{:S(2)}) %collective-permute-start.36) | collective-permute-done | bytes 131104 | tf_op jit(solution)/shard_map/ppermute | solution.py:19
  85.3 2.0 %collective-permute-done.38 = bf16[256,256]{0,1:T(8,128)(2,1)S(1)} collective-permute-done((bf16[256,256]{0,1:T(8,128)(2,1)S(1)}, bf16[256,256]{0,1:T(8,128)(2,1)S(1)}, u32[]{:S(2)}, u32[]{:S(2)}) %collective-permute-start.38) | collective-permute-done | bytes 131104 | tf_op jit(solution)/shard_map/ppermute | solution.py:19
  88.5 1.7 %collective-permute-start.41 = (bf16[512,256]{0,1:T(8,128)(2,1)S(1)}, bf16[512,256]{0,1:T(8,128)(2,1)S(1)}, u32[]{:S(2)}, u32[]{:S(2)}) collective-permute-start(bf16[512,256]{0,1:T(8,128)(2,1)S(1)} %pad_maximum_fusion.1), channel_id=1, source_target_pairs={{0,1},{1,0},{2,3},{3,2},{4,5},{5,4},{6,7},{7,6},{8,9},{9,8},{10,11... | collective-permute-start | bytes 786440 | tf_op jit(solution)/shard_map/ppermute | solution.py:19
  91.0 1.4 collective-permute-start.43
  93.4 1.5 collective-permute-done.41
  96.1 1.3 collective-permute-done.42
  99.6 2.0 %collective-permute-start.46 = (f32[256]{0:T(256)S(1)}, f32[256]{0:T(256)S(1)}, u32[]{:S(2)}, u32[]{:S(2)}) collective-permute-start(f32[256]{0:T(256)S(1)} %get-tuple-element.108), channel_id=1, source_target_pairs={{0,4},{4,0},{8,12},{12,8},{1,5},{5,1},{9,13},{13,9},{2,6},{6,2},{1... | collective-permute-start | bytes 3080 | tf_op jit(solution)/shard_map/ppermute | solution.py:19
  103.2 3.5 %collective-permute-start.47 = (f32[256]{0:T(256)S(1)}, f32[256]{0:T(256)S(1)}, u32[]{:S(2)}, u32[]{:S(2)}) collective-permute-start(f32[256]{0:T(256)S(1)} %add.172), channel_id=1, source_target_pairs={{0,3},{1,2},{2,1},{3,0},{4,7},{5,6},{6,5},{7,4},{8,11},{9,10},{10,... | collective-permute-start | bytes 3080 | tf_op jit(solution)/shard_map/ppermute | solution.py:19
  108.6 2.5 %collective-permute-done.48 = f32[256]{0:T(256)S(1)} collective-permute-done((f32[256]{0:T(256)S(1)}, f32[256]{0:T(256)S(1)}, u32[]{:S(2)}, u32[]{:S(2)}) %collective-permute-start.48) | collective-permute-done | bytes 1056 | tf_op jit(solution)/shard_map/ppermute | solution.py:19
  112.1 1.9 %copy.6 = bf16[1,768,256]{2,1,0:T(8,128)(2,1)} copy(bf16[1,768,256]{1,2,0:T(8,128)(2,1)} %fusion.20) | data formatting | bytes 786432
  114.0 2.2 %fusion.5 = bf16[1024,256]{0,1:T(8,128)(2,1)S(1)} fusion(bf16[768,1024]{1,0:T(8,128)(2,1)} %copy-done.2, bf16[768,256]{0,1:T(8,128)(2,1)S(1)} %get-tuple-element.90, bf16[768,256]{0,1:T(8,128)(2,1)} %collective-permute-done.50, f32[256]{0:T(256)S(1)} %collective-permute-done.51, f32[256]{0:T(256)S(1)} %get-tuple-element.91), kind=kOutput, calls=%fused_computation.17 | convolution fusion | flops 404881408 | bytes 2885632 | tf_op jit(solution)/shard_map/dot_general | solution.py:191
  116.3 2.0 %fusion.54 = (bf16[1536,256]{0,1:T(8,128)(2,1)S(1)}, f32[1536,256]{0,1:T(8,128)S(1)}) fusion(bf16[768,1536]{1,0:T(8,128)(2,1)S(1)} %get-tuple-element.61, bf16[768,256]{0,1:T(8,128)(2,1)S(1)} %get-tuple-element.90, bf16[768,256]{0,1:T(8,128)(2,1)} %collective-permute-done.50, f32[256]{0:T(256)S(1)} %collective-permute-done.51, f32[256]{0:T(256)S(1)} %get-tuple-element.91), kind=kOutput, calls=%fused_computation.126 | convolution fusion | flops 606339072 | bytes 5507072 | tf_op jit(solution)/shard_map/dot_general | solution.py:191
  118.6 1.4 collective-permute-start.56
  122.6 1.9 %fusion.55 = (bf16[1536,256]{0,1:T(8,128)(2,1)S(1)}, f32[1536,256]{0,1:T(8,128)S(1)}) fusion(bf16[768,1536]{1,0:T(8,128)(2,1)S(1)} %copy-done.1, bf16[768,256]{0,1:T(8,128)(2,1)S(1)} %get-tuple-element.90, bf16[768,256]{0,1:T(8,128)(2,1)} %collective-permute-done.50, f32[256]{0:T(256)S(1)} %collective-permute-done.51, f32[256]{0:T(256)S(1)} %get-tuple-element.91), kind=kOutput, calls=%fused_computation.127 | convolution fusion | flops 606339072 | bytes 5507072 | tf_op jit(solution)/shard_map/dot_general | solution.py:191
  124.5 3.7 %collective-permute-done.54 = bf16[512,256]{0,1:T(8,128)(2,1)S(1)} collective-permute-done((bf16[512,256]{0,1:T(8,128)(2,1)S(1)}, bf16[512,256]{0,1:T(8,128)(2,1)S(1)}, u32[]{:S(2)}, u32[]{:S(2)}) %collective-permute-start.54) | collective-permute-done | bytes 262176 | tf_op jit(solution)/shard_map/ppermute | solution.py:19
  128.2 2.0 %collective-permute-start.60 = (bf16[256,256]{0,1:T(8,128)(2,1)S(1)}, bf16[256,256]{0,1:T(8,128)(2,1)S(1)}, u32[]{:S(2)}, u32[]{:S(2)}) collective-permute-start(bf16[256,256]{0,1:T(8,128)(2,1)S(1)} %get-tuple-element.97), channel_id=1, source_target_pairs={{0,12},{4,8},{8,4},{12,0},{1,13},{5,9},{9,5},{13,1},{2,14},{6,10},... | collective-permute-start | bytes 393224 | tf_op jit(solution)/shard_map/ppermute | solution.py:19
  130.7 1.7 %collective-permute-start.52 = (bf16[256,256]{0,1:T(8,128)(2,1)S(1)}, bf16[256,256]{0,1:T(8,128)(2,1)S(1)}, u32[]{:S(2)}, u32[]{:S(2)}) collective-permute-start(bf16[256,256]{0,1:T(8,128)(2,1)S(1)} %get-tuple-element.106), channel_id=1, source_target_pairs={{0,4},{4,0},{8,12},{12,8},{1,5},{5,1},{9,13},{13,9},{2,6},{6,2},{1... | collective-permute-start | bytes 393224 | tf_op jit(solution)/shard_map/ppermute | solution.py:19
  133.1 2.1 %collective-permute-done.61 = bf16[256,256]{0,1:T(8,128)(2,1)S(1)} collective-permute-done((bf16[256,256]{0,1:T(8,128)(2,1)S(1)}, bf16[256,256]{0,1:T(8,128)(2,1)S(1)}, u32[]{:S(2)}, u32[]{:S(2)}) %collective-permute-start.61) | collective-permute-done | bytes 131104 | tf_op jit(solution)/shard_map/ppermute | solution.py:19
  135.4 2.1 %collective-permute-start.62 = (bf16[256,256]{0,1:T(8,128)(2,1)S(1)}, bf16[256,256]{0,1:T(8,128)(2,1)S(1)}, u32[]{:S(2)}, u32[]{:S(2)}) collective-permute-start(bf16[256,256]{0,1:T(8,128)(2,1)S(1)} %get-tuple-element.95), channel_id=1, source_target_pairs={{0,2},{1,3},{2,0},{3,1},{4,6},{5,7},{6,4},{7,5},{8,10},{9,11},{10,... | collective-permute-start | bytes 393224 | tf_op jit(solution)/shard_map/ppermute | solution.py:19
  137.5 1.8 %collective-permute-start.57 = (bf16[256,256]{0,1:T(8,128)(2,1)S(1)}, bf16[256,256]{0,1:T(8,128)(2,1)S(1)}, u32[]{:S(2)}, u32[]{:S(2)}) collective-permute-start(bf16[256,256]{0,1:T(8,128)(2,1)S(1)} %add_convert_fusion.1), channel_id=1, source_target_pairs={{0,12},{4,8},{8,4},{12,0},{1,13},{5,9},{9,5},{13,1},{2,14},{6,10},... | collective-permute-start | bytes 393224 | tf_op jit(solution)/shard_map/ppermute | solution.py:19
  140.1 3.3 %collective-permute-done.57 = bf16[256,256]{0,1:T(8,128)(2,1)S(1)} collective-permute-done((bf16[256,256]{0,1:T(8,128)(2,1)S(1)}, bf16[256,256]{0,1:T(8,128)(2,1)S(1)}, u32[]{:S(2)}, u32[]{:S(2)}) %collective-permute-start.57) | collective-permute-done | bytes 131104 | tf_op jit(solution)/shard_map/ppermute | solution.py:19
  (178 shorter events, 44.3 us)
Async XLA Ops:
  1.7 12.2 %collective-permute-start.4 = (bf16[256,256]{0,1:T(8,128)(2,1)S(1)}, bf16[256,256]{0,1:T(8,128)(2,1)S(1)}, u32[]{:S(2)}, u32[]{:S(2)}) collective-permute-start(bf16[256,256]{0,1:T(8,128)(2,1)S(1)} %bitcast_convert_fusion), channel_id=1, source_target_pairs={{0,2},{1,3},{2,0},{3,1},{4,6},{5,7},{6,4},{7,5},{8,10},{9,11},{10,... | collective-permute-start | bytes 393224 | tf_op jit(solution)/shard_map/ppermute | solution.py:19
  5.8 8.1 %collective-permute-start.3 = (bf16[256,256]{0,1:T(8,128)(2,1)S(1)}, bf16[256,256]{0,1:T(8,128)(2,1)S(1)}, u32[]{:S(2)}, u32[]{:S(2)}) collective-permute-start(bf16[256,256]{0,1:T(8,128)(2,1)S(1)} %bitcast_convert_fusion), channel_id=1, source_target_pairs={{0,1},{1,0},{2,3},{3,2},{4,5},{5,4},{6,7},{7,6},{8,9},{9,8},{10,11... | collective-permute-start | bytes 393224 | tf_op jit(solution)/shard_map/ppermute | solution.py:19
  7.4 9.5 %collective-permute-start.2 = (bf16[256,256]{0,1:T(8,128)(2,1)S(1)}, bf16[256,256]{0,1:T(8,128)(2,1)S(1)}, u32[]{:S(2)}, u32[]{:S(2)}) collective-permute-start(bf16[256,256]{0,1:T(8,128)(2,1)S(1)} %bitcast_convert_fusion), channel_id=1, source_target_pairs={{0,12},{4,8},{8,4},{12,0},{1,13},{5,9},{9,5},{13,1},{2,14},{6,10},... | collective-permute-start | bytes 393224 | tf_op jit(solution)/shard_map/ppermute | solution.py:19
  9.9 7.7 %collective-permute-start.1 = (bf16[256,256]{0,1:T(8,128)(2,1)S(1)}, bf16[256,256]{0,1:T(8,128)(2,1)S(1)}, u32[]{:S(2)}, u32[]{:S(2)}) collective-permute-start(bf16[256,256]{0,1:T(8,128)(2,1)S(1)} %bitcast_convert_fusion), channel_id=1, source_target_pairs={{0,8},{4,12},{8,0},{12,4},{1,9},{5,13},{9,1},{13,5},{2,10},{6,14},... | collective-permute-start | bytes 393224 | tf_op jit(solution)/shard_map/ppermute | solution.py:19
  10.4 7.7 %collective-permute-start = (bf16[256,256]{0,1:T(8,128)(2,1)S(1)}, bf16[256,256]{0,1:T(8,128)(2,1)S(1)}, u32[]{:S(2)}, u32[]{:S(2)}) collective-permute-start(bf16[256,256]{0,1:T(8,128)(2,1)S(1)} %bitcast_convert_fusion), channel_id=1, source_target_pairs={{0,4},{4,0},{8,12},{12,8},{1,5},{5,1},{9,13},{13,9},{2,6},{6,2},{1... | collective-permute-start | bytes 393224 | tf_op jit(solution)/shard_map/ppermute | solution.py:19
  14.0 5.0 %collective-permute-start.6 = (bf16[256,256]{0,1:T(8,128)(2,1)S(1)}, bf16[256,256]{0,1:T(8,128)(2,1)S(1)}, u32[]{:S(2)}, u32[]{:S(2)}) collective-permute-start(bf16[256,256]{0,1:T(8,128)(2,1)S(1)} %collective-permute-done.4), channel_id=1, source_target_pairs={{0,1},{1,0},{2,3},{3,2},{4,5},{5,4},{6,7},{7,6},{8,9},{9,8},{10,11... | collective-permute-start | bytes 393224 | tf_op jit(solution)/shard_map/ppermute | solution.py:19
  14.5 7.3 %collective-permute-start.5 = (bf16[256,256]{0,1:T(8,128)(2,1)S(1)}, bf16[256,256]{0,1:T(8,128)(2,1)S(1)}, u32[]{:S(2)}, u32[]{:S(2)}) collective-permute-start(bf16[256,256]{0,1:T(8,128)(2,1)S(1)} %collective-permute-done.4), channel_id=1, source_target_pairs={{0,12},{4,8},{8,4},{12,0},{1,13},{5,9},{9,5},{13,1},{2,14},{6,10},... | collective-permute-start | bytes 393224 | tf_op jit(solution)/shard_map/ppermute | solution.py:19
  17.0 10.6 %collective-permute-start.8 = (bf16[512,256]{0,1:T(8,128)(2,1)S(1)}, bf16[512,256]{0,1:T(8,128)(2,1)S(1)}, u32[]{:S(2)}, u32[]{:S(2)}) collective-permute-start(bf16[512,256]{0,1:T(8,128)(2,1)S(1)} %constant_dynamic-update-slice_fusion.6), channel_id=1, source_target_pairs={{0,8},{4,12},{8,0},{12,4},{1,9},{5,13},{9,1},{13,5},{2,10},{6,14},... | collective-permute-start | bytes 786440 | tf_op jit(solution)/shard_map/ppermute | solution.py:19
  17.5 10.0 %collective-permute-start.7 = (bf16[512,256]{0,1:T(8,128)(2,1)S(1)}, bf16[512,256]{0,1:T(8,128)(2,1)S(1)}, u32[]{:S(2)}, u32[]{:S(2)}) collective-permute-start(bf16[512,256]{0,1:T(8,128)(2,1)S(1)} %constant_dynamic-update-slice_fusion.6), channel_id=1, source_target_pairs={{0,4},{4,0},{8,12},{12,8},{1,5},{5,1},{9,13},{13,9},{2,6},{6,2},{1... | collective-permute-start | bytes 786440 | tf_op jit(solution)/shard_map/ppermute | solution.py:19
  21.8 6.8 %collective-permute-start.9 = (bf16[512,256]{0,1:T(8,128)(2,1)S(1)}, bf16[512,256]{0,1:T(8,128)(2,1)S(1)}, u32[]{:S(2)}, u32[]{:S(2)}) collective-permute-start(bf16[512,256]{0,1:T(8,128)(2,1)S(1)} %pad_maximum_fusion), channel_id=1, source_target_pairs={{0,1},{1,0},{2,3},{3,2},{4,5},{5,4},{6,7},{7,6},{8,9},{9,8},{10,11... | collective-permute-start | bytes 786440 | tf_op jit(solution)/shard_map/ppermute | solution.py:19
  24.3 5.0 %collective-permute-start.11 = (bf16[256,256]{0,1:T(8,128)(2,1)S(1)}, bf16[256,256]{0,1:T(8,128)(2,1)S(1)}, u32[]{:S(2)}, u32[]{:S(2)}) collective-permute-start(bf16[256,256]{0,1:T(8,128)(2,1)S(1)} %collective-permute-done.6), channel_id=1, source_target_pairs={{0,8},{4,12},{8,0},{12,4},{1,9},{5,13},{9,1},{13,5},{2,10},{6,14},... | collective-permute-start | bytes 393224 | tf_op jit(solution)/shard_map/ppermute | solution.py:19
  31.6 14.0 %collective-permute-start.18 = (bf16[768,256]{0,1:T(8,128)(2,1)S(1)}, bf16[768,256]{0,1:T(8,128)(2,1)S(1)}, u32[]{:S(2)}, u32[]{:S(2)}) collective-permute-start(bf16[768,256]{0,1:T(8,128)(2,1)S(1)} %get-tuple-element.115), channel_id=1, source_target_pairs={{0,16},{16,0},{1,17},{17,1},{2,18},{18,2},{3,19},{19,3},{4,20},{20... | collective-permute-start | bytes 1179656 | tf_op jit(solution)/shard_map/ppermute | solution.py:19
  38.4 5.4 %collective-permute-start.15 = (f32[256]{0:T(256)S(1)}, f32[256]{0:T(256)S(1)}, u32[]{:S(2)}, u32[]{:S(2)}) collective-permute-start(f32[256]{0:T(256)S(1)} %add.148), channel_id=1, source_target_pairs={{0,3},{1,2},{2,1},{3,0},{4,7},{5,6},{6,5},{7,4},{8,11},{9,10},{10,... | collective-permute-start | bytes 3080 | tf_op jit(solution)/shard_map/ppermute | solution.py:19
  46.3 11.7 %collective-permute-start.23 = (bf16[256,256]{0,1:T(8,128)(2,1)S(1)}, bf16[256,256]{0,1:T(8,128)(2,1)S(1)}, u32[]{:S(2)}, u32[]{:S(2)}) collective-permute-start(bf16[256,256]{0,1:T(8,128)(2,1)S(1)} %get-tuple-element.118), channel_id=1, source_target_pairs={{0,4},{4,0},{8,12},{12,8},{1,5},{5,1},{9,13},{13,9},{2,6},{6,2},{1... | collective-permute-start | bytes 393224 | tf_op jit(solution)/shard_map/ppermute | solution.py:19
  46.9 11.1 %collective-permute-start.24 = (bf16[256,256]{0,1:T(8,128)(2,1)S(1)}, bf16[256,256]{0,1:T(8,128)(2,1)S(1)}, u32[]{:S(2)}, u32[]{:S(2)}) collective-permute-start(bf16[256,256]{0,1:T(8,128)(2,1)S(1)} %get-tuple-element.119), channel_id=1, source_target_pairs={{0,8},{4,12},{8,0},{12,4},{1,9},{5,13},{9,1},{13,5},{2,10},{6,14},... | collective-permute-start | bytes 393224 | tf_op jit(solution)/shard_map/ppermute | solution.py:19
  47.2 8.1 %collective-permute-start.22 = (bf16[512,256]{0,1:T(8,128)(2,1)S(1)}, bf16[512,256]{0,1:T(8,128)(2,1)S(1)}, u32[]{:S(2)}, u32[]{:S(2)}) collective-permute-start(bf16[512,256]{0,1:T(8,128)(2,1)S(1)} %slice.262), channel_id=1, source_target_pairs={{0,1},{1,0},{2,3},{3,2},{4,5},{5,4},{6,7},{7,6},{8,9},{9,8},{10,11... | collective-permute-start | bytes 786440 | tf_op jit(solution)/shard_map/ppermute | solution.py:19
  50.1 10.2 %collective-permute-start.26 = (bf16[512,256]{0,1:T(8,128)(2,1)S(1)}, bf16[512,256]{0,1:T(8,128)(2,1)S(1)}, u32[]{:S(2)}, u32[]{:S(2)}) collective-permute-start(bf16[512,256]{0,1:T(8,128)(2,1)S(1)} %get-tuple-element.110), channel_id=1, source_target_pairs={{0,4},{4,0},{8,12},{12,8},{1,5},{5,1},{9,13},{13,9},{2,6},{6,2},{1... | collective-permute-start | bytes 786440 | tf_op jit(solution)/shard_map/ppermute | solution.py:19
  51.7 9.7 %collective-permute-start.27 = (bf16[512,256]{0,1:T(8,128)(2,1)S(1)}, bf16[512,256]{0,1:T(8,128)(2,1)S(1)}, u32[]{:S(2)}, u32[]{:S(2)}) collective-permute-start(bf16[512,256]{0,1:T(8,128)(2,1)S(1)} %get-tuple-element.111), channel_id=1, source_target_pairs={{0,8},{4,12},{8,0},{12,4},{1,9},{5,13},{9,1},{13,5},{2,10},{6,14},... | collective-permute-start | bytes 786440 | tf_op jit(solution)/shard_map/ppermute | solution.py:19
  55.3 7.8 %collective-permute-start.28 = (bf16[256,256]{0,1:T(8,128)(2,1)S(1)}, bf16[256,256]{0,1:T(8,128)(2,1)S(1)}, u32[]{:S(2)}, u32[]{:S(2)}) collective-permute-start(bf16[256,256]{0,1:T(8,128)(2,1)S(1)} %get-tuple-element.102), channel_id=1, source_target_pairs={{0,12},{4,8},{8,4},{12,0},{1,13},{5,9},{9,5},{13,1},{2,14},{6,10},... | collective-permute-start | bytes 393224 | tf_op jit(solution)/shard_map/ppermute | solution.py:19
  58.0 5.0 %collective-permute-start.29 = (bf16[256,256]{0,1:T(8,128)(2,1)S(1)}, bf16[256,256]{0,1:T(8,128)(2,1)S(1)}, u32[]{:S(2)}, u32[]{:S(2)}) collective-permute-start(bf16[256,256]{0,1:T(8,128)(2,1)S(1)} %add_convert_fusion.5), channel_id=1, source_target_pairs={{0,1},{1,0},{2,3},{3,2},{4,5},{5,4},{6,7},{7,6},{8,9},{9,8},{10,11... | collective-permute-start | bytes 393224 | tf_op jit(solution)/shard_map/ppermute | solution.py:19
  59.9 7.7 %collective-permute-start.20 = (bf16[256,256]{0,1:T(8,128)(2,1)S(1)}, bf16[256,256]{0,1:T(8,128)(2,1)S(1)}, u32[]{:S(2)}, u32[]{:S(2)}) collective-permute-start(bf16[256,256]{0,1:T(8,128)(2,1)S(1)} %get-tuple-element.112), channel_id=1, source_target_pairs={{0,4},{4,0},{8,12},{12,8},{1,5},{5,1},{9,13},{13,9},{2,6},{6,2},{1... | collective-permute-start | bytes 393224 | tf_op jit(solution)/shard_map/ppermute | solution.py:19
  60.4 7.2 %collective-permute-start.21 = (bf16[256,256]{0,1:T(8,128)(2,1)S(1)}, bf16[256,256]{0,1:T(8,128)(2,1)S(1)}, u32[]{:S(2)}, u32[]{:S(2)}) collective-permute-start(bf16[256,256]{0,1:T(8,128)(2,1)S(1)} %get-tuple-element.113), channel_id=1, source_target_pairs={{0,8},{4,12},{8,0},{12,4},{1,9},{5,13},{9,1},{13,5},{2,10},{6,14},... | collective-permute-start | bytes 393224 | tf_op jit(solution)/shard_map/ppermute | solution.py:19
  63.2 7.9 %collective-permute-start.30 = (bf16[256,256]{0,1:T(8,128)(2,1)S(1)}, bf16[256,256]{0,1:T(8,128)(2,1)S(1)}, u32[]{:S(2)}, u32[]{:S(2)}) collective-permute-start(bf16[256,256]{0,1:T(8,128)(2,1)S(1)} %get-tuple-element.100), channel_id=1, source_target_pairs={{0,2},{1,3},{2,0},{3,1},{4,6},{5,7},{6,4},{7,5},{8,10},{9,11},{10,... | collective-permute-start | bytes 393224 | tf_op jit(solution)/shard_map/ppermute | solution.py:19
  65.1 5.9 %collective-permute-start.25 = (bf16[256,256]{0,1:T(8,128)(2,1)S(1)}, bf16[256,256]{0,1:T(8,128)(2,1)S(1)}, u32[]{:S(2)}, u32[]{:S(2)}) collective-permute-start(bf16[256,256]{0,1:T(8,128)(2,1)S(1)} %add_convert_fusion.4), channel_id=1, source_target_pairs={{0,12},{4,8},{8,4},{12,0},{1,13},{5,9},{9,5},{13,1},{2,14},{6,10},... | collective-permute-start | bytes 393224 | tf_op jit(solution)/shard_map/ppermute | solution.py:19
  66.6 7.1 %collective-permute-start.31 = (bf16[256,256]{0,1:T(8,128)(2,1)S(1)}, bf16[256,256]{0,1:T(8,128)(2,1)S(1)}, u32[]{:S(2)}, u32[]{:S(2)}) collective-permute-start(bf16[256,256]{0,1:T(8,128)(2,1)S(1)} %add_convert_fusion.3), channel_id=1, source_target_pairs={{0,1},{1,0},{2,3},{3,2},{4,5},{5,4},{6,7},{7,6},{8,9},{9,8},{10,11... | collective-permute-start | bytes 393224 | tf_op jit(solution)/shard_map/ppermute | solution.py:19
  73.8 7.1 %collective-permute-start.36 = (bf16[256,256]{0,1:T(8,128)(2,1)S(1)}, bf16[256,256]{0,1:T(8,128)(2,1)S(1)}, u32[]{:S(2)}, u32[]{:S(2)}) collective-permute-start(bf16[256,256]{0,1:T(8,128)(2,1)S(1)} %multiply_convert_fusion.5), channel_id=1, source_target_pairs={{0,2},{1,3},{2,0},{3,1},{4,6},{5,7},{6,4},{7,5},{8,10},{9,11},{10,... | collective-permute-start | bytes 393224 | tf_op jit(solution)/shard_map/ppermute | solution.py:19
  74.0 7.2 %collective-permute-start.35 = (bf16[256,256]{0,1:T(8,128)(2,1)S(1)}, bf16[256,256]{0,1:T(8,128)(2,1)S(1)}, u32[]{:S(2)}, u32[]{:S(2)}) collective-permute-start(bf16[256,256]{0,1:T(8,128)(2,1)S(1)} %multiply_convert_fusion.5), channel_id=1, source_target_pairs={{0,1},{1,0},{2,3},{3,2},{4,5},{5,4},{6,7},{7,6},{8,9},{9,8},{10,11... | collective-permute-start | bytes 393224 | tf_op jit(solution)/shard_map/ppermute | solution.py:19
  75.0 7.6 %collective-permute-start.34 = (bf16[256,256]{0,1:T(8,128)(2,1)S(1)}, bf16[256,256]{0,1:T(8,128)(2,1)S(1)}, u32[]{:S(2)}, u32[]{:S(2)}) collective-permute-start(bf16[256,256]{0,1:T(8,128)(2,1)S(1)} %multiply_convert_fusion.5), channel_id=1, source_target_pairs={{0,12},{4,8},{8,4},{12,0},{1,13},{5,9},{9,5},{13,1},{2,14},{6,10},... | collective-permute-start | bytes 393224 | tf_op jit(solution)/shard_map/ppermute | solution.py:19
  76.5 7.7 %collective-permute-start.33 = (bf16[256,256]{0,1:T(8,128)(2,1)S(1)}, bf16[256,256]{0,1:T(8,128)(2,1)S(1)}, u32[]{:S(2)}, u32[]{:S(2)}) collective-permute-start(bf16[256,256]{0,1:T(8,128)(2,1)S(1)} %multiply_convert_fusion.5), channel_id=1, source_target_pairs={{0,8},{4,12},{8,0},{12,4},{1,9},{5,13},{9,1},{13,5},{2,10},{6,14},... | collective-permute-start | bytes 393224 | tf_op jit(solution)/shard_map/ppermute | solution.py:19
  78.1 7.3 %collective-permute-start.32 = (bf16[256,256]{0,1:T(8,128)(2,1)S(1)}, bf16[256,256]{0,1:T(8,128)(2,1)S(1)}, u32[]{:S(2)}, u32[]{:S(2)}) collective-permute-start(bf16[256,256]{0,1:T(8,128)(2,1)S(1)} %multiply_convert_fusion.5), channel_id=1, source_target_pairs={{0,4},{4,0},{8,12},{12,8},{1,5},{5,1},{9,13},{13,9},{2,6},{6,2},{1... | collective-permute-start | bytes 393224 | tf_op jit(solution)/shard_map/ppermute | solution.py:19
  81.2 6.1 %collective-permute-start.38 = (bf16[256,256]{0,1:T(8,128)(2,1)S(1)}, bf16[256,256]{0,1:T(8,128)(2,1)S(1)}, u32[]{:S(2)}, u32[]{:S(2)}) collective-permute-start(bf16[256,256]{0,1:T(8,128)(2,1)S(1)} %collective-permute-done.36), channel_id=1, source_target_pairs={{0,1},{1,0},{2,3},{3,2},{4,5},{5,4},{6,7},{7,6},{8,9},{9,8},{10,11... | collective-permute-start | bytes 393224 | tf_op jit(solution)/shard_map/ppermute | solution.py:19
  81.7 6.7 %collective-permute-start.37 = (bf16[256,256]{0,1:T(8,128)(2,1)S(1)}, bf16[256,256]{0,1:T(8,128)(2,1)S(1)}, u32[]{:S(2)}, u32[]{:S(2)}) collective-permute-start(bf16[256,256]{0,1:T(8,128)(2,1)S(1)} %collective-permute-done.36), channel_id=1, source_target_pairs={{0,12},{4,8},{8,4},{12,0},{1,13},{5,9},{9,5},{13,1},{2,14},{6,10},... | collective-permute-start | bytes 393224 | tf_op jit(solution)/shard_map/ppermute | solution.py:19
  82.6 9.9 %collective-permute-start.40 = (bf16[512,256]{0,1:T(8,128)(2,1)S(1)}, bf16[512,256]{0,1:T(8,128)(2,1)S(1)}, u32[]{:S(2)}, u32[]{:S(2)}) collective-permute-start(bf16[512,256]{0,1:T(8,128)(2,1)S(1)} %constant_dynamic-update-slice_fusion.20), channel_id=1, source_target_pairs={{0,8},{4,12},{8,0},{12,4},{1,9},{5,13},{9,1},{13,5},{2,10},{6,14},... | collective-permute-start | bytes 786440 | tf_op jit(solution)/shard_map/ppermute | solution.py:19
  84.1 8.3 %collective-permute-start.39 = (bf16[512,256]{0,1:T(8,128)(2,1)S(1)}, bf16[512,256]{0,1:T(8,128)(2,1)S(1)}, u32[]{:S(2)}, u32[]{:S(2)}) collective-permute-start(bf16[512,256]{0,1:T(8,128)(2,1)S(1)} %constant_dynamic-update-slice_fusion.20), channel_id=1, source_target_pairs={{0,4},{4,0},{8,12},{12,8},{1,5},{5,1},{9,13},{13,9},{2,6},{6,2},{1... | collective-permute-start | bytes 786440 | tf_op jit(solution)/shard_map/ppermute | solution.py:19
  88.5 6.4 %collective-permute-start.41 = (bf16[512,256]{0,1:T(8,128)(2,1)S(1)}, bf16[512,256]{0,1:T(8,128)(2,1)S(1)}, u32[]{:S(2)}, u32[]{:S(2)}) collective-permute-start(bf16[512,256]{0,1:T(8,128)(2,1)S(1)} %pad_maximum_fusion.1), channel_id=1, source_target_pairs={{0,1},{1,0},{2,3},{3,2},{4,5},{5,4},{6,7},{7,6},{8,9},{9,8},{10,11... | collective-permute-start | bytes 786440 | tf_op jit(solution)/shard_map/ppermute | solution.py:19
  91.0 5.0 %collective-permute-start.43 = (bf16[256,256]{0,1:T(8,128)(2,1)S(1)}, bf16[256,256]{0,1:T(8,128)(2,1)S(1)}, u32[]{:S(2)}, u32[]{:S(2)}) collective-permute-start(bf16[256,256]{0,1:T(8,128)(2,1)S(1)} %collective-permute-done.38), channel_id=1, source_target_pairs={{0,8},{4,12},{8,0},{12,4},{1,9},{5,13},{9,1},{13,5},{2,10},{6,14},... | collective-permute-start | bytes 393224 | tf_op jit(solution)/shard_map/ppermute | solution.py:19
  103.2 5.4 %collective-permute-start.47 = (f32[256]{0:T(256)S(1)}, f32[256]{0:T(256)S(1)}, u32[]{:S(2)}, u32[]{:S(2)}) collective-permute-start(f32[256]{0:T(256)S(1)} %add.172), channel_id=1, source_target_pairs={{0,3},{1,2},{2,1},{3,0},{4,7},{5,6},{6,5},{7,4},{8,11},{9,10},{10,... | collective-permute-start | bytes 3080 | tf_op jit(solution)/shard_map/ppermute | solution.py:19
  107.6 6.4 %collective-permute-start.50 = (bf16[768,256]{0,1:T(8,128)(2,1)S(1)}, bf16[768,256]{0,1:T(8,128)(2,1)}, u32[]{:S(2)}, u32[]{:S(2)}) collective-permute-start(bf16[768,256]{0,1:T(8,128)(2,1)S(1)} %get-tuple-element.90), channel_id=1, source_target_pairs={{0,16},{16,0},{1,17},{17,1},{2,18},{18,2},{3,19},{19,3},{4,20},{20... | collective-permute-start | bytes 1179656 | tf_op jit(solution)/shard_map/ppermute | solution.py:19
  118.4 11.8 %collective-permute-start.55 = (bf16[256,256]{0,1:T(8,128)(2,1)S(1)}, bf16[256,256]{0,1:T(8,128)(2,1)S(1)}, u32[]{:S(2)}, u32[]{:S(2)}) collective-permute-start(bf16[256,256]{0,1:T(8,128)(2,1)S(1)} %get-tuple-element.116), channel_id=1, source_target_pairs={{0,4},{4,0},{8,12},{12,8},{1,5},{5,1},{9,13},{13,9},{2,6},{6,2},{1... | collective-permute-start | bytes 393224 | tf_op jit(solution)/shard_map/ppermute | solution.py:19
  118.6 11.5 %collective-permute-start.56 = (bf16[256,256]{0,1:T(8,128)(2,1)S(1)}, bf16[256,256]{0,1:T(8,128)(2,1)S(1)}, u32[]{:S(2)}, u32[]{:S(2)}) collective-permute-start(bf16[256,256]{0,1:T(8,128)(2,1)S(1)} %get-tuple-element.117), channel_id=1, source_target_pairs={{0,8},{4,12},{8,0},{12,4},{1,9},{5,13},{9,1},{13,5},{2,10},{6,14},... | collective-permute-start | bytes 393224 | tf_op jit(solution)/shard_map/ppermute | solution.py:19
  120.0 8.1 %collective-permute-start.54 = (bf16[512,256]{0,1:T(8,128)(2,1)S(1)}, bf16[512,256]{0,1:T(8,128)(2,1)S(1)}, u32[]{:S(2)}, u32[]{:S(2)}) collective-permute-start(bf16[512,256]{0,1:T(8,128)(2,1)S(1)} %slice.287), channel_id=1, source_target_pairs={{0,1},{1,0},{2,3},{3,2},{4,5},{5,4},{6,7},{7,6},{8,9},{9,8},{10,11... | collective-permute-start | bytes 786440 | tf_op jit(solution)/shard_map/ppermute | solution.py:19
  121.1 11.3 %collective-permute-start.58 = (bf16[512,256]{0,1:T(8,128)(2,1)S(1)}, bf16[512,256]{0,1:T(8,128)(2,1)S(1)}, u32[]{:S(2)}, u32[]{:S(2)}) collective-permute-start(bf16[512,256]{0,1:T(8,128)(2,1)S(1)} %get-tuple-element.104), channel_id=1, source_target_pairs={{0,4},{4,0},{8,12},{12,8},{1,5},{5,1},{9,13},{13,9},{2,6},{6,2},{1... | collective-permute-start | bytes 786440 | tf_op jit(solution)/shard_map/ppermute | solution.py:19
  121.8 11.3 %collective-permute-start.59 = (bf16[512,256]{0,1:T(8,128)(2,1)S(1)}, bf16[512,256]{0,1:T(8,128)(2,1)S(1)}, u32[]{:S(2)}, u32[]{:S(2)}) collective-permute-start(bf16[512,256]{0,1:T(8,128)(2,1)S(1)} %get-tuple-element.105), channel_id=1, source_target_pairs={{0,8},{4,12},{8,0},{12,4},{1,9},{5,13},{9,1},{13,5},{2,10},{6,14},... | collective-permute-start | bytes 786440 | tf_op jit(solution)/shard_map/ppermute | solution.py:19
  128.2 7.1 %collective-permute-start.60 = (bf16[256,256]{0,1:T(8,128)(2,1)S(1)}, bf16[256,256]{0,1:T(8,128)(2,1)S(1)}, u32[]{:S(2)}, u32[]{:S(2)}) collective-permute-start(bf16[256,256]{0,1:T(8,128)(2,1)S(1)} %get-tuple-element.97), channel_id=1, source_target_pairs={{0,12},{4,8},{8,4},{12,0},{1,13},{5,9},{9,5},{13,1},{2,14},{6,10},... | collective-permute-start | bytes 393224 | tf_op jit(solution)/shard_map/ppermute | solution.py:19
  130.7 9.4 %collective-permute-start.52 = (bf16[256,256]{0,1:T(8,128)(2,1)S(1)}, bf16[256,256]{0,1:T(8,128)(2,1)S(1)}, u32[]{:S(2)}, u32[]{:S(2)}) collective-permute-start(bf16[256,256]{0,1:T(8,128)(2,1)S(1)} %get-tuple-element.106), channel_id=1, source_target_pairs={{0,4},{4,0},{8,12},{12,8},{1,5},{5,1},{9,13},{13,9},{2,6},{6,2},{1... | collective-permute-start | bytes 393224 | tf_op jit(solution)/shard_map/ppermute | solution.py:19
  132.4 7.7 %collective-permute-start.53 = (bf16[256,256]{0,1:T(8,128)(2,1)S(1)}, bf16[256,256]{0,1:T(8,128)(2,1)S(1)}, u32[]{:S(2)}, u32[]{:S(2)}) collective-permute-start(bf16[256,256]{0,1:T(8,128)(2,1)S(1)} %get-tuple-element.107), channel_id=1, source_target_pairs={{0,8},{4,12},{8,0},{12,4},{1,9},{5,13},{9,1},{13,5},{2,10},{6,14},... | collective-permute-start | bytes 393224 | tf_op jit(solution)/shard_map/ppermute | solution.py:19
  135.4 8.1 %collective-permute-start.62 = (bf16[256,256]{0,1:T(8,128)(2,1)S(1)}, bf16[256,256]{0,1:T(8,128)(2,1)S(1)}, u32[]{:S(2)}, u32[]{:S(2)}) collective-permute-start(bf16[256,256]{0,1:T(8,128)(2,1)S(1)} %get-tuple-element.95), channel_id=1, source_target_pairs={{0,2},{1,3},{2,0},{3,1},{4,6},{5,7},{6,4},{7,5},{8,10},{9,11},{10,... | collective-permute-start | bytes 393224 | tf_op jit(solution)/shard_map/ppermute | solution.py:19
  137.5 5.9 %collective-permute-start.57 = (bf16[256,256]{0,1:T(8,128)(2,1)S(1)}, bf16[256,256]{0,1:T(8,128)(2,1)S(1)}, u32[]{:S(2)}, u32[]{:S(2)}) collective-permute-start(bf16[256,256]{0,1:T(8,128)(2,1)S(1)} %add_convert_fusion.1), channel_id=1, source_target_pairs={{0,12},{4,8},{8,4},{12,0},{1,13},{5,9},{9,5},{13,1},{2,14},{6,10},... | collective-permute-start | bytes 393224 | tf_op jit(solution)/shard_map/ppermute | solution.py:19
  (19 other events, 231.4 us)

commit v5 on v3

--- a/solution.py
+++ b/solution.py
@@ -73,7 +73,7 @@
     def summed(first, *others):
         return lax.optimization_barrier(sum(others, first).astype(jnp.bfloat16))
 
-    near_across, far_across = send("feat", 1, b[3, 1], b[3, 3])
+    (far_across,), (near_across,) = send("feat", 1, b[3, 3]), send("feat", 1, b[3, 1])
     (left,), (right,) = send("row", 1, b[1, 3]), send("row", 2, b[2, 3])
     ones, twos = zip(*[send("row", r, b[r, 1], b[r, 2]) for r in (1, 2)])
     far_across = summed(b[3, 2], far_across)
@@ -146,7 +146,7 @@
         in_specs=[pl.BlockSpec(memory_space=pl.ANY)],
         out_specs=[pl.BlockSpec(memory_space=pl.ANY) for places in ARRIVALS],
         scratch_shapes=[pltpu.SemaphoreType.DMA((count,))],
-        compiler_params=pltpu.CompilerParams(vmem_limit_bytes=44 << 20),
+        compiler_params=pltpu.CompilerParams(vmem_limit_bytes=1 << 20),
         cost_estimate=pl.CostEstimate(
             flops=0, bytes_accessed=2 * samples.size * 2, transcendentals=0
         ),
@@ -170,7 +170,7 @@
         summed_proj = 0.0
         for g, places in enumerate(ARRIVALS):
             blocks = [dirs[p] for p in places]
-            blocks = lax.optimization_barrier(blocks + [dirs[3, 2]])[: len(places)]
+            blocks = lax.optimization_barrier(blocks + [dirs[0, 3]])[: len(places)]
             part = jnp.dot(
                 groups[g], join(*blocks), preferred_element_type=jnp.float32
             )

time: 140 us -> 145 us (1.036)
  waiting for transfers between devices: 43.5 us -> 50.9 us
  starting transfers between devices: 76.1 us -> 72.6 us
  local copies, waits for them, and re-layouts: 3.45 us -> 6.23 us
  Pallas kernels: 3 us -> 1.06 us
    ppermute x64 -> x66, waiting for transfers between devices: 43.5 us -> 50.9 us  [xor_move(): return lax.ppermute(block, axis, [(i, i ^ mask) for i in range(count)])]
    ppermute x64 -> x66, starting transfers between devices: 76.1 us -> 72.6 us  [xor_move(): return lax.ppermute(block, axis, [(i, i ^ mask) for i in range(count)])]
    unnamed x33 -> x35, local copies, waits for them, and re-layouts: 3.09 us -> 5.87 us
    pallas_call x1, Pallas kernels: 3 us -> 1.06 us  [regroup(): pl.pallas_call(kernel, out_shape=[jax.ShapeDtypeStruct((rows_here, len(pl...]
  transfers between devices with their start and end apart: 64 -> 66, of which waited for: 35 -> 38; matrix products, arithmetic and copies ran while one was open for 6% -> 6% of each run, Pallas kernels for 2% -> 1%
where the time goes in v5:
time: 145 us
  starting transfers between devices  72.6 us (50%)
  waiting for transfers between devices  50.9 us (35%)
  matrix products  10.8 us (7%)
  local copies, waits for them, and re-layouts  6.23 us (4%)
  other arithmetic  1.89 us (1%)
    ppermute x66, starting transfers between devices, xor_move(): return lax.ppermute(block, axis, [(i, i ^ mask) for i in range(count)])  72.6 us
    ppermute x66, waiting for transfers between devices, xor_move(): return lax.ppermute(block, axis, [(i, i ^ mask) for i in range(count)])  50.9 us
    dot_general x6, matrix products, on_device(): lax.dot_general(groups[g], residue, (((0,), (0,)), ((), ())), preferred_e...  6.19 us
    unnamed x35, local copies, waits for them, and re-layouts  5.87 us
    dot_general x6, matrix products, on_device(): part = jnp.dot(groups[g], join(*blocks), preferred_element_type=jnp.float32)  4.59 us
  transfers between devices with their start and end apart: 66, of which 38 were waited for; matrix products, arithmetic and copies ran while one was open for 6% of the time, Pallas kernels for 1%

profile of v5, /device:TPU:0, one launch (start us, length us, event | category | flops | bytes accessed | tf_op | source)
XLA Modules:
  0.0 144.8 jit_solution(4591016445736335786)
XLA Ops:
  1.7 4.1 %collective-permute-start.4 = (bf16[256,256]{0,1:T(8,128)(2,1)S(1)}, bf16[256,256]{0,1:T(8,128)(2,1)S(1)}, u32[]{:S(2)}, u32[]{:S(2)}) collective-permute-start(bf16[256,256]{0,1:T(8,128)(2,1)S(1)} %bitcast_convert_fusion), channel_id=1, source_target_pairs={{0,2},{1,3},{2,0},{3,1},{4,6},{5,7},{6,4},{7,5},{8,10},{9,11},{10,... | collective-permute-start | bytes 393224 | tf_op jit(solution)/shard_map/ppermute | solution.py:19
  5.8 1.6 %collective-permute-start.3 = (bf16[256,256]{0,1:T(8,128)(2,1)S(1)}, bf16[256,256]{0,1:T(8,128)(2,1)S(1)}, u32[]{:S(2)}, u32[]{:S(2)}) collective-permute-start(bf16[256,256]{0,1:T(8,128)(2,1)S(1)} %bitcast_convert_fusion), channel_id=1, source_target_pairs={{0,1},{1,0},{2,3},{3,2},{4,5},{5,4},{6,7},{7,6},{8,9},{9,8},{10,11... | collective-permute-start | bytes 393224 | tf_op jit(solution)/shard_map/ppermute | solution.py:19
  7.4 2.4 %collective-permute-start.2 = (bf16[256,256]{0,1:T(8,128)(2,1)S(1)}, bf16[256,256]{0,1:T(8,128)(2,1)S(1)}, u32[]{:S(2)}, u32[]{:S(2)}) collective-permute-start(bf16[256,256]{0,1:T(8,128)(2,1)S(1)} %bitcast_convert_fusion), channel_id=1, source_target_pairs={{0,12},{4,8},{8,4},{12,0},{1,13},{5,9},{9,5},{13,1},{2,14},{6,10},... | collective-permute-start | bytes 393224 | tf_op jit(solution)/shard_map/ppermute | solution.py:19
  10.9 2.8 %copy-done.2 = bf16[1,768,4096]{2,1,0:T(8,128)(2,1)S(1)} copy-done((bf16[1,768,4096]{2,1,0:T(8,128)(2,1)S(1)}, bf16[1,768,4096]{2,1,0:T(8,128)(2,1)}, u32[]{:S(2)}) %copy-start.2) | copy-done | bytes 6291480
  14.8 2.5 %collective-permute-start.6 = (bf16[256,256]{0,1:T(8,128)(2,1)S(1)}, bf16[256,256]{0,1:T(8,128)(2,1)S(1)}, u32[]{:S(2)}, u32[]{:S(2)}) collective-permute-start(bf16[256,256]{0,1:T(8,128)(2,1)S(1)} %collective-permute-done.4), channel_id=1, source_target_pairs={{0,12},{4,8},{8,4},{12,0},{1,13},{5,9},{9,5},{13,1},{2,14},{6,10},... | collective-permute-start | bytes 393224 | tf_op jit(solution)/shard_map/ppermute | solution.py:19
  19.0 3.3 %collective-permute-done.5 = bf16[256,256]{0,1:T(8,128)(2,1)S(1)} collective-permute-done((bf16[256,256]{0,1:T(8,128)(2,1)S(1)}, bf16[256,256]{0,1:T(8,128)(2,1)S(1)}, u32[]{:S(2)}, u32[]{:S(2)}) %collective-permute-start.5) | collective-permute-done | bytes 131104 | tf_op jit(solution)/shard_map/ppermute | solution.py:19
  24.9 1.7 %collective-permute-start.10 = (bf16[256,256]{0,1:T(8,128)(2,1)S(1)}, bf16[256,256]{0,1:T(8,128)(2,1)S(1)}, u32[]{:S(2)}, u32[]{:S(2)}) collective-permute-start(bf16[256,256]{0,1:T(8,128)(2,1)S(1)} %collective-permute-done.5), channel_id=1, source_target_pairs={{0,4},{4,0},{8,12},{12,8},{1,5},{5,1},{9,13},{13,9},{2,6},{6,2},{1... | collective-permute-start | bytes 393224 | tf_op jit(solution)/shard_map/ppermute | solution.py:19
  30.7 1.4 collective-permute-start.12
  32.1 1.8 %collective-permute-start.13 = (f32[256]{0:T(256)S(1)}, f32[256]{0:T(256)S(1)}, u32[]{:S(2)}, u32[]{:S(2)}) collective-permute-start(f32[256]{0:T(256)S(1)} %get-tuple-element.116), channel_id=1, source_target_pairs={{0,8},{4,12},{8,0},{12,4},{1,9},{5,13},{9,1},{13,5},{2,10},{6,14},... | collective-permute-start | bytes 3080 | tf_op jit(solution)/shard_map/ppermute | solution.py:19
  35.7 1.8 %collective-permute-done.14 = f32[256]{0:T(256)S(1)} collective-permute-done((f32[256]{0:T(256)S(1)}, f32[256]{0:T(256)S(1)}, u32[]{:S(2)}, u32[]{:S(2)}) %collective-permute-start.14) | collective-permute-done | bytes 1056 | tf_op jit(solution)/shard_map/ppermute | solution.py:19
  38.5 2.1 %collective-permute-start.16 = (f32[256]{0:T(256)S(1)}, f32[256]{0:T(256)S(1)}, u32[]{:S(2)}, u32[]{:S(2)}) collective-permute-start(f32[256]{0:T(256)S(1)} %add.148), channel_id=1, source_target_pairs={{0,2},{1,3},{2,0},{3,1},{4,6},{5,7},{6,4},{7,5},{8,10},{9,11},{10,... | collective-permute-start | bytes 3080 | tf_op jit(solution)/shard_map/ppermute | solution.py:19
  40.6 1.3 collective-permute-start.17
  46.1 1.3 collective-permute-start.30
  50.2 1.4 collective-permute-start.22
  52.5 2.1 %collective-permute-done.24 = bf16[256,256]{0,1:T(8,128)(2,1)S(1)} collective-permute-done((bf16[256,256]{0,1:T(8,128)(2,1)S(1)}, bf16[256,256]{0,1:T(8,128)(2,1)S(1)}, u32[]{:S(2)}, u32[]{:S(2)}) %collective-permute-start.24) | collective-permute-done | bytes 131104 | tf_op jit(solution)/shard_map/ppermute | solution.py:19
  55.0 1.6 %collective-permute-start.25 = (bf16[256,256]{0,1:T(8,128)(2,1)S(1)}, bf16[256,256]{0,1:T(8,128)(2,1)S(1)}, u32[]{:S(2)}, u32[]{:S(2)}) collective-permute-start(bf16[256,256]{0,1:T(8,128)(2,1)S(1)} %get-tuple-element.104), channel_id=1, source_target_pairs={{0,12},{4,8},{8,4},{12,0},{1,13},{5,9},{9,5},{13,1},{2,14},{6,10},... | collective-permute-start | bytes 393224 | tf_op jit(solution)/shard_map/ppermute | solution.py:19
  56.6 1.2 collective-permute-start.28
  57.9 3.8 %collective-permute-done.28 = bf16[256,256]{0,1:T(8,128)(2,1)S(1)} collective-permute-done((bf16[256,256]{0,1:T(8,128)(2,1)S(1)}, bf16[256,256]{0,1:T(8,128)(2,1)S(1)}, u32[]{:S(2)}, u32[]{:S(2)}) %collective-permute-start.28) | collective-permute-done | bytes 131104 | tf_op jit(solution)/shard_map/ppermute | solution.py:19
  61.7 1.6 %collective-permute-start.20 = (bf16[256,256]{0,1:T(8,128)(2,1)S(1)}, bf16[256,256]{0,1:T(8,128)(2,1)S(1)}, u32[]{:S(2)}, u32[]{:S(2)}) collective-permute-start(bf16[256,256]{0,1:T(8,128)(2,1)S(1)} %get-tuple-element.112), channel_id=1, source_target_pairs={{0,4},{4,0},{8,12},{12,8},{1,5},{5,1},{9,13},{13,9},{2,6},{6,2},{1... | collective-permute-start | bytes 393224 | tf_op jit(solution)/shard_map/ppermute | solution.py:19
  63.7 2.3 %collective-permute-done.23 = bf16[512,256]{0,1:T(8,128)(2,1)S(1)} collective-permute-done((bf16[512,256]{0,1:T(8,128)(2,1)S(1)}, bf16[512,256]{0,1:T(8,128)(2,1)S(1)}, u32[]{:S(2)}, u32[]{:S(2)}) %collective-permute-start.23) | collective-permute-done | bytes 262176 | tf_op jit(solution)/shard_map/ppermute | solution.py:19
  67.1 1.7 %collective-permute-start.32 = (bf16[256,256]{0,1:T(8,128)(2,1)S(1)}, bf16[256,256]{0,1:T(8,128)(2,1)S(1)}, u32[]{:S(2)}, u32[]{:S(2)}) collective-permute-start(bf16[256,256]{0,1:T(8,128)(2,1)S(1)} %add_convert_fusion.3), channel_id=1, source_target_pairs={{0,1},{1,0},{2,3},{3,2},{4,5},{5,4},{6,7},{7,6},{8,9},{9,8},{10,11... | collective-permute-start | bytes 393224 | tf_op jit(solution)/shard_map/ppermute | solution.py:19
  68.8 4.6 %collective-permute-done.29 = bf16[256,256]{0,1:T(8,128)(2,1)S(1)} collective-permute-done((bf16[256,256]{0,1:T(8,128)(2,1)S(1)}, bf16[256,256]{0,1:T(8,128)(2,1)S(1)}, u32[]{:S(2)}, u32[]{:S(2)}) %collective-permute-start.29) | collective-permute-done | bytes 131104 | tf_op jit(solution)/shard_map/ppermute | solution.py:19
  75.5 2.0 %collective-permute-start.37 = (bf16[256,256]{0,1:T(8,128)(2,1)S(1)}, bf16[256,256]{0,1:T(8,128)(2,1)S(1)}, u32[]{:S(2)}, u32[]{:S(2)}) collective-permute-start(bf16[256,256]{0,1:T(8,128)(2,1)S(1)} %get-tuple-element.70), channel_id=1, source_target_pairs={{0,2},{1,3},{2,0},{3,1},{4,6},{5,7},{6,4},{7,5},{8,10},{9,11},{10,... | collective-permute-start | bytes 393224 | tf_op jit(solution)/shard_map/ppermute | solution.py:19
  78.3 2.5 %collective-permute-start.34 = (bf16[256,256]{0,1:T(8,128)(2,1)S(1)}, bf16[256,256]{0,1:T(8,128)(2,1)S(1)}, u32[]{:S(2)}, u32[]{:S(2)}) collective-permute-start(bf16[256,256]{0,1:T(8,128)(2,1)S(1)} %get-tuple-element.70), channel_id=1, source_target_pairs={{0,8},{4,12},{8,0},{12,4},{1,9},{5,13},{9,1},{13,5},{2,10},{6,14},... | collective-permute-start | bytes 393224 | tf_op jit(solution)/shard_map/ppermute | solution.py:19
  82.7 2.0 %collective-permute-done.36 = bf16[256,256]{0,1:T(8,128)(2,1)S(1)} collective-permute-done((bf16[256,256]{0,1:T(8,128)(2,1)S(1)}, bf16[256,256]{0,1:T(8,128)(2,1)S(1)}, u32[]{:S(2)}, u32[]{:S(2)}) %collective-permute-start.36) | collective-permute-done | bytes 131104 | tf_op jit(solution)/shard_map/ppermute | solution.py:19
  85.4 1.6 %collective-permute-start.41 = (bf16[512,256]{0,1:T(8,128)(2,1)S(1)}, bf16[512,256]{0,1:T(8,128)(2,1)S(1)}, u32[]{:S(2)}, u32[]{:S(2)}) collective-permute-start(bf16[512,256]{0,1:T(8,128)(2,1)S(1)} %constant_dynamic-update-slice_fusion.20), channel_id=1, source_target_pairs={{0,8},{4,12},{8,0},{12,4},{1,9},{5,13},{9,1},{13,5},{2,10},{6,14},... | collective-permute-start | bytes 786440 | tf_op jit(solution)/shard_map/ppermute | solution.py:19
  87.4 1.5 %collective-permute-start.40 = (bf16[512,256]{0,1:T(8,128)(2,1)S(1)}, bf16[512,256]{0,1:T(8,128)(2,1)S(1)}, u32[]{:S(2)}, u32[]{:S(2)}) collective-permute-start(bf16[512,256]{0,1:T(8,128)(2,1)S(1)} %constant_dynamic-update-slice_fusion.20), channel_id=1, source_target_pairs={{0,4},{4,0},{8,12},{12,8},{1,5},{5,1},{9,13},{13,9},{2,6},{6,2},{1... | collective-permute-start | bytes 786440 | tf_op jit(solution)/shard_map/ppermute | solution.py:19
  88.9 2.2 %collective-permute-done.38 = bf16[256,256]{0,1:T(8,128)(2,1)S(1)} collective-permute-done((bf16[256,256]{0,1:T(8,128)(2,1)S(1)}, bf16[256,256]{0,1:T(8,128)(2,1)S(1)}, u32[]{:S(2)}, u32[]{:S(2)}) %collective-permute-start.38) | collective-permute-done | bytes 131104 | tf_op jit(solution)/shard_map/ppermute | solution.py:19
  93.5 1.3 collective-permute-start.43
  95.8 2.4 %collective-permute-done.42 = bf16[512,256]{0,1:T(8,128)(2,1)S(1)} collective-permute-done((bf16[512,256]{0,1:T(8,128)(2,1)S(1)}, bf16[512,256]{0,1:T(8,128)(2,1)S(1)}, u32[]{:S(2)}, u32[]{:S(2)}) %collective-permute-start.42) | collective-permute-done | bytes 262176 | tf_op jit(solution)/shard_map/ppermute | solution.py:19
  99.2 1.4 collective-permute-start.45
  100.6 1.5 %collective-permute-start.46 = (f32[256]{0:T(256)S(1)}, f32[256]{0:T(256)S(1)}, u32[]{:S(2)}, u32[]{:S(2)}) collective-permute-start(f32[256]{0:T(256)S(1)} %get-tuple-element.110), channel_id=1, source_target_pairs={{0,8},{4,12},{8,0},{12,4},{1,9},{5,13},{9,1},{13,5},{2,10},{6,14},... | collective-permute-start | bytes 3080 | tf_op jit(solution)/shard_map/ppermute | solution.py:19
  104.1 1.5 %collective-permute-done.47 = f32[256]{0:T(256)S(1)} collective-permute-done((f32[256]{0:T(256)S(1)}, f32[256]{0:T(256)S(1)}, u32[]{:S(2)}, u32[]{:S(2)}) %collective-permute-start.47) | collective-permute-done | bytes 1056 | tf_op jit(solution)/shard_map/ppermute | solution.py:19
  106.4 2.1 %collective-permute-start.49 = (f32[256]{0:T(256)S(1)}, f32[256]{0:T(256)S(1)}, u32[]{:S(2)}, u32[]{:S(2)}) collective-permute-start(f32[256]{0:T(256)S(1)} %add.172), channel_id=1, source_target_pairs={{0,2},{1,3},{2,0},{3,1},{4,6},{5,7},{6,4},{7,5},{8,10},{9,11},{10,... | collective-permute-start | bytes 3080 | tf_op jit(solution)/shard_map/ppermute | solution.py:19
  108.5 1.5 %collective-permute-start.50 = (f32[256]{0:T(256)S(1)}, f32[256]{0:T(256)S(1)}, u32[]{:S(2)}, u32[]{:S(2)}) collective-permute-start(f32[256]{0:T(256)S(1)} %add.172), channel_id=1, source_target_pairs={{0,1},{1,0},{2,3},{3,2},{4,5},{5,4},{6,7},{7,6},{8,9},{9,8},{10,11... | collective-permute-start | bytes 3080 | tf_op jit(solution)/shard_map/ppermute | solution.py:19
  113.3 2.0 %fusion.5 = bf16[1024,256]{0,1:T(8,128)(2,1)S(1)} fusion(bf16[768,1024]{1,0:T(8,128)(2,1)} %copy-done.3, bf16[768,256]{0,1:T(8,128)(2,1)S(1)} %get-tuple-element.90, bf16[768,256]{0,1:T(8,128)(2,1)S(1)} %collective-permute-done.51, f32[256]{0:T(256)S(1)} %collective-permute-done.52, f32[256]{0:T(256)S(1)} %get-tuple-element.91), kind=kOutput, calls=%fused_computation.17 | convolution fusion | flops 404881408 | bytes 2885632 | tf_op jit(solution)/shard_map/dot_general | solution.py:190
  117.2 1.8 %collective-permute-start.59 = (bf16[256,256]{0,1:T(8,128)(2,1)S(1)}, bf16[256,256]{0,1:T(8,128)(2,1)S(1)}, u32[]{:S(2)}, u32[]{:S(2)}) collective-permute-start(bf16[256,256]{0,1:T(8,128)(2,1)S(1)} %get-tuple-element.120), channel_id=1, source_target_pairs={{0,4},{4,0},{8,12},{12,8},{1,5},{5,1},{9,13},{13,9},{2,6},{6,2},{1... | collective-permute-start | bytes 393224 | tf_op jit(solution)/shard_map/ppermute | solution.py:19
  120.5 1.5 %collective-permute-start.56 = (bf16[512,256]{0,1:T(8,128)(2,1)S(1)}, bf16[512,256]{0,1:T(8,128)(2,1)S(1)}, u32[]{:S(2)}, u32[]{:S(2)}) collective-permute-start(bf16[512,256]{0,1:T(8,128)(2,1)S(1)} %get-tuple-element.109), channel_id=1, source_target_pairs={{0,8},{4,12},{8,0},{12,4},{1,9},{5,13},{9,1},{13,5},{2,10},{6,14},... | collective-permute-start | bytes 786440 | tf_op jit(solution)/shard_map/ppermute | solution.py:19
  122.9 1.4 collective-permute-done.57
  125.4 1.5 %collective-permute-start.61 = (bf16[256,256]{0,1:T(8,128)(2,1)S(1)}, bf16[256,256]{0,1:T(8,128)(2,1)S(1)}, u32[]{:S(2)}, u32[]{:S(2)}) collective-permute-start(bf16[256,256]{0,1:T(8,128)(2,1)S(1)} %add_convert_fusion.2), channel_id=1, source_target_pairs={{0,1},{1,0},{2,3},{3,2},{4,5},{5,4},{6,7},{7,6},{8,9},{9,8},{10,11... | collective-permute-start | bytes 393224 | tf_op jit(solution)/shard_map/ppermute | solution.py:19
  127.7 1.4 collective-permute-done.55
  129.1 1.3 collective-permute-start.54
  130.4 1.5 %collective-permute-start.63 = (bf16[256,256]{0,1:T(8,128)(2,1)S(1)}, bf16[256,256]{0,1:T(8,128)(2,1)S(1)}, u32[]{:S(2)}, u32[]{:S(2)}) collective-permute-start(bf16[256,256]{0,1:T(8,128)(2,1)S(1)} %get-tuple-element.118), channel_id=1, source_target_pairs={{0,1},{1,0},{2,3},{3,2},{4,5},{5,4},{6,7},{7,6},{8,9},{9,8},{10,11... | collective-permute-start | bytes 393224 | tf_op jit(solution)/shard_map/ppermute | solution.py:19
  132.7 2.6 %collective-permute-done.63 = bf16[256,256]{0,1:T(8,128)(2,1)S(1)} collective-permute-done((bf16[256,256]{0,1:T(8,128)(2,1)S(1)}, bf16[256,256]{0,1:T(8,128)(2,1)S(1)}, u32[]{:S(2)}, u32[]{:S(2)}) %collective-permute-start.63) | collective-permute-done | bytes 131104 | tf_op jit(solution)/shard_map/ppermute | solution.py:19
  136.4 1.5 %collective-permute-start.65 = (bf16[256,256]{0,1:T(8,128)(2,1)S(1)}, bf16[256,256]{0,1:T(8,128)(2,1)S(1)}, u32[]{:S(2)}, u32[]{:S(2)}) collective-permute-start(bf16[256,256]{0,1:T(8,128)(2,1)S(1)} %add_convert_fusion), channel_id=1, source_target_pairs={{0,1},{1,0},{2,3},{3,2},{4,5},{5,4},{6,7},{7,6},{8,9},{9,8},{10,11... | collective-permute-start | bytes 393224 | tf_op jit(solution)/shard_map/ppermute | solution.py:19
  138.0 1.5 %collective-permute-start.64 = (bf16[256,256]{0,1:T(8,128)(2,1)S(1)}, bf16[256,256]{0,1:T(8,128)(2,1)S(1)}, u32[]{:S(2)}, u32[]{:S(2)}) collective-permute-start(bf16[256,256]{0,1:T(8,128)(2,1)S(1)} %add_convert_fusion.1), channel_id=1, source_target_pairs={{0,12},{4,8},{8,4},{12,0},{1,13},{5,9},{9,5},{13,1},{2,14},{6,10},... | collective-permute-start | bytes 393224 | tf_op jit(solution)/shard_map/ppermute | solution.py:19
  139.5 2.0 %collective-permute-done.62 = bf16[256,256]{0,1:T(8,128)(2,1)S(1)} collective-permute-done((bf16[256,256]{0,1:T(8,128)(2,1)S(1)}, bf16[256,256]{0,1:T(8,128)(2,1)S(1)}, u32[]{:S(2)}, u32[]{:S(2)}) %collective-permute-start.62) | collective-permute-done | bytes 131104 | tf_op jit(solution)/shard_map/ppermute | solution.py:19
  141.5 1.2 collective-permute-done.65
  (182 shorter events, 50.5 us)
Async XLA Ops:
  1.7 13.0 %collective-permute-start.4 = (bf16[256,256]{0,1:T(8,128)(2,1)S(1)}, bf16[256,256]{0,1:T(8,128)(2,1)S(1)}, u32[]{:S(2)}, u32[]{:S(2)}) collective-permute-start(bf16[256,256]{0,1:T(8,128)(2,1)S(1)} %bitcast_convert_fusion), channel_id=1, source_target_pairs={{0,2},{1,3},{2,0},{3,1},{4,6},{5,7},{6,4},{7,5},{8,10},{9,11},{10,... | collective-permute-start | bytes 393224 | tf_op jit(solution)/shard_map/ppermute | solution.py:19
  5.8 9.0 %collective-permute-start.3 = (bf16[256,256]{0,1:T(8,128)(2,1)S(1)}, bf16[256,256]{0,1:T(8,128)(2,1)S(1)}, u32[]{:S(2)}, u32[]{:S(2)}) collective-permute-start(bf16[256,256]{0,1:T(8,128)(2,1)S(1)} %bitcast_convert_fusion), channel_id=1, source_target_pairs={{0,1},{1,0},{2,3},{3,2},{4,5},{5,4},{6,7},{7,6},{8,9},{9,8},{10,11... | collective-permute-start | bytes 393224 | tf_op jit(solution)/shard_map/ppermute | solution.py:19
  7.4 10.4 %collective-permute-start.2 = (bf16[256,256]{0,1:T(8,128)(2,1)S(1)}, bf16[256,256]{0,1:T(8,128)(2,1)S(1)}, u32[]{:S(2)}, u32[]{:S(2)}) collective-permute-start(bf16[256,256]{0,1:T(8,128)(2,1)S(1)} %bitcast_convert_fusion), channel_id=1, source_target_pairs={{0,12},{4,8},{8,4},{12,0},{1,13},{5,9},{9,5},{13,1},{2,14},{6,10},... | collective-permute-start | bytes 393224 | tf_op jit(solution)/shard_map/ppermute | solution.py:19
  9.9 8.6 %collective-permute-start.1 = (bf16[256,256]{0,1:T(8,128)(2,1)S(1)}, bf16[256,256]{0,1:T(8,128)(2,1)S(1)}, u32[]{:S(2)}, u32[]{:S(2)}) collective-permute-start(bf16[256,256]{0,1:T(8,128)(2,1)S(1)} %bitcast_convert_fusion), channel_id=1, source_target_pairs={{0,8},{4,12},{8,0},{12,4},{1,9},{5,13},{9,1},{13,5},{2,10},{6,14},... | collective-permute-start | bytes 393224 | tf_op jit(solution)/shard_map/ppermute | solution.py:19
  10.4 8.6 %collective-permute-start = (bf16[256,256]{0,1:T(8,128)(2,1)S(1)}, bf16[256,256]{0,1:T(8,128)(2,1)S(1)}, u32[]{:S(2)}, u32[]{:S(2)}) collective-permute-start(bf16[256,256]{0,1:T(8,128)(2,1)S(1)} %bitcast_convert_fusion), channel_id=1, source_target_pairs={{0,4},{4,0},{8,12},{12,8},{1,5},{5,1},{9,13},{13,9},{2,6},{6,2},{1... | collective-permute-start | bytes 393224 | tf_op jit(solution)/shard_map/ppermute | solution.py:19
  14.8 7.5 %collective-permute-start.6 = (bf16[256,256]{0,1:T(8,128)(2,1)S(1)}, bf16[256,256]{0,1:T(8,128)(2,1)S(1)}, u32[]{:S(2)}, u32[]{:S(2)}) collective-permute-start(bf16[256,256]{0,1:T(8,128)(2,1)S(1)} %collective-permute-done.4), channel_id=1, source_target_pairs={{0,12},{4,8},{8,4},{12,0},{1,13},{5,9},{9,5},{13,1},{2,14},{6,10},... | collective-permute-start | bytes 393224 | tf_op jit(solution)/shard_map/ppermute | solution.py:19
  17.8 9.0 %collective-permute-start.8 = (bf16[512,256]{0,1:T(8,128)(2,1)S(1)}, bf16[512,256]{0,1:T(8,128)(2,1)S(1)}, u32[]{:S(2)}, u32[]{:S(2)}) collective-permute-start(bf16[512,256]{0,1:T(8,128)(2,1)S(1)} %constant_dynamic-update-slice_fusion.6), channel_id=1, source_target_pairs={{0,8},{4,12},{8,0},{12,4},{1,9},{5,13},{9,1},{13,5},{2,10},{6,14},... | collective-permute-start | bytes 786440 | tf_op jit(solution)/shard_map/ppermute | solution.py:19
  18.4 8.6 %collective-permute-start.7 = (bf16[512,256]{0,1:T(8,128)(2,1)S(1)}, bf16[512,256]{0,1:T(8,128)(2,1)S(1)}, u32[]{:S(2)}, u32[]{:S(2)}) collective-permute-start(bf16[512,256]{0,1:T(8,128)(2,1)S(1)} %constant_dynamic-update-slice_fusion.6), channel_id=1, source_target_pairs={{0,4},{4,0},{8,12},{12,8},{1,5},{5,1},{9,13},{13,9},{2,6},{6,2},{1... | collective-permute-start | bytes 786440 | tf_op jit(solution)/shard_map/ppermute | solution.py:19
  22.3 6.4 %collective-permute-start.9 = (bf16[512,256]{0,1:T(8,128)(2,1)S(1)}, bf16[512,256]{0,1:T(8,128)(2,1)S(1)}, u32[]{:S(2)}, u32[]{:S(2)}) collective-permute-start(bf16[512,256]{0,1:T(8,128)(2,1)S(1)} %pad_maximum_fusion), channel_id=1, source_target_pairs={{0,1},{1,0},{2,3},{3,2},{4,5},{5,4},{6,7},{7,6},{8,9},{9,8},{10,11... | collective-permute-start | bytes 786440 | tf_op jit(solution)/shard_map/ppermute | solution.py:19
  23.8 5.0 %collective-permute-start.11 = (bf16[256,256]{0,1:T(8,128)(2,1)S(1)}, bf16[256,256]{0,1:T(8,128)(2,1)S(1)}, u32[]{:S(2)}, u32[]{:S(2)}) collective-permute-start(bf16[256,256]{0,1:T(8,128)(2,1)S(1)} %collective-permute-done.5), channel_id=1, source_target_pairs={{0,8},{4,12},{8,0},{12,4},{1,9},{5,13},{9,1},{13,5},{2,10},{6,14},... | collective-permute-start | bytes 393224 | tf_op jit(solution)/shard_map/ppermute | solution.py:19
  30.6 14.8 %collective-permute-start.18 = (bf16[768,256]{0,1:T(8,128)(2,1)S(1)}, bf16[768,256]{0,1:T(8,128)(2,1)S(1)}, u32[]{:S(2)}, u32[]{:S(2)}) collective-permute-start(bf16[768,256]{0,1:T(8,128)(2,1)S(1)} %get-tuple-element.117), channel_id=1, source_target_pairs={{0,16},{16,0},{1,17},{17,1},{2,18},{18,2},{3,19},{19,3},{4,20},{20... | collective-permute-start | bytes 1179656 | tf_op jit(solution)/shard_map/ppermute | solution.py:19
  37.5 5.4 %collective-permute-start.15 = (f32[256]{0:T(256)S(1)}, f32[256]{0:T(256)S(1)}, u32[]{:S(2)}, u32[]{:S(2)}) collective-permute-start(f32[256]{0:T(256)S(1)} %add.148), channel_id=1, source_target_pairs={{0,3},{1,2},{2,1},{3,0},{4,7},{5,6},{6,5},{7,4},{8,11},{9,10},{10,... | collective-permute-start | bytes 3080 | tf_op jit(solution)/shard_map/ppermute | solution.py:19
  46.1 20.0 %collective-permute-start.30 = (bf16[256,256]{0,1:T(8,128)(2,1)S(1)}, bf16[256,256]{0,1:T(8,128)(2,1)S(1)}, u32[]{:S(2)}, u32[]{:S(2)}) collective-permute-start(bf16[256,256]{0,1:T(8,128)(2,1)S(1)} %get-tuple-element.122), channel_id=1, source_target_pairs={{0,1},{1,0},{2,3},{3,2},{4,5},{5,4},{6,7},{7,6},{8,9},{9,8},{10,11... | collective-permute-start | bytes 393224 | tf_op jit(solution)/shard_map/ppermute | solution.py:19
  47.4 7.6 %collective-permute-start.27 = (bf16[256,256]{0,1:T(8,128)(2,1)S(1)}, bf16[256,256]{0,1:T(8,128)(2,1)S(1)}, u32[]{:S(2)}, u32[]{:S(2)}) collective-permute-start(bf16[256,256]{0,1:T(8,128)(2,1)S(1)} %get-tuple-element.123), channel_id=1, source_target_pairs={{0,8},{4,12},{8,0},{12,4},{1,9},{5,13},{9,1},{13,5},{2,10},{6,14},... | collective-permute-start | bytes 393224 | tf_op jit(solution)/shard_map/ppermute | solution.py:19
  47.7 8.9 %collective-permute-start.26 = (bf16[256,256]{0,1:T(8,128)(2,1)S(1)}, bf16[256,256]{0,1:T(8,128)(2,1)S(1)}, u32[]{:S(2)}, u32[]{:S(2)}) collective-permute-start(bf16[256,256]{0,1:T(8,128)(2,1)S(1)} %get-tuple-element.124), channel_id=1, source_target_pairs={{0,4},{4,0},{8,12},{12,8},{1,5},{5,1},{9,13},{13,9},{2,6},{6,2},{1... | collective-permute-start | bytes 393224 | tf_op jit(solution)/shard_map/ppermute | solution.py:19
  48.7 5.9 %collective-permute-start.24 = (bf16[256,256]{0,1:T(8,128)(2,1)S(1)}, bf16[256,256]{0,1:T(8,128)(2,1)S(1)}, u32[]{:S(2)}, u32[]{:S(2)}) collective-permute-start(bf16[256,256]{0,1:T(8,128)(2,1)S(1)} %get-tuple-element.125), channel_id=1, source_target_pairs={{0,1},{1,0},{2,3},{3,2},{4,5},{5,4},{6,7},{7,6},{8,9},{9,8},{10,11... | collective-permute-start | bytes 393224 | tf_op jit(solution)/shard_map/ppermute | solution.py:19
  50.2 13.4 %collective-permute-start.22 = (bf16[512,256]{0,1:T(8,128)(2,1)S(1)}, bf16[512,256]{0,1:T(8,128)(2,1)S(1)}, u32[]{:S(2)}, u32[]{:S(2)}) collective-permute-start(bf16[512,256]{0,1:T(8,128)(2,1)S(1)} %get-tuple-element.114), channel_id=1, source_target_pairs={{0,4},{4,0},{8,12},{12,8},{1,5},{5,1},{9,13},{13,9},{2,6},{6,2},{1... | collective-permute-start | bytes 786440 | tf_op jit(solution)/shard_map/ppermute | solution.py:19
  54.5 11.4 %collective-permute-start.23 = (bf16[512,256]{0,1:T(8,128)(2,1)S(1)}, bf16[512,256]{0,1:T(8,128)(2,1)S(1)}, u32[]{:S(2)}, u32[]{:S(2)}) collective-permute-start(bf16[512,256]{0,1:T(8,128)(2,1)S(1)} %get-tuple-element.115), channel_id=1, source_target_pairs={{0,8},{4,12},{8,0},{12,4},{1,9},{5,13},{9,1},{13,5},{2,10},{6,14},... | collective-permute-start | bytes 786440 | tf_op jit(solution)/shard_map/ppermute | solution.py:19
  55.0 8.2 %collective-permute-start.25 = (bf16[256,256]{0,1:T(8,128)(2,1)S(1)}, bf16[256,256]{0,1:T(8,128)(2,1)S(1)}, u32[]{:S(2)}, u32[]{:S(2)}) collective-permute-start(bf16[256,256]{0,1:T(8,128)(2,1)S(1)} %get-tuple-element.104), channel_id=1, source_target_pairs={{0,12},{4,8},{8,4},{12,0},{1,13},{5,9},{9,5},{13,1},{2,14},{6,10},... | collective-permute-start | bytes 393224 | tf_op jit(solution)/shard_map/ppermute | solution.py:19
  61.7 7.2 %collective-permute-start.20 = (bf16[256,256]{0,1:T(8,128)(2,1)S(1)}, bf16[256,256]{0,1:T(8,128)(2,1)S(1)}, u32[]{:S(2)}, u32[]{:S(2)}) collective-permute-start(bf16[256,256]{0,1:T(8,128)(2,1)S(1)} %get-tuple-element.112), channel_id=1, source_target_pairs={{0,4},{4,0},{8,12},{12,8},{1,5},{5,1},{9,13},{13,9},{2,6},{6,2},{1... | collective-permute-start | bytes 393224 | tf_op jit(solution)/shard_map/ppermute | solution.py:19
  63.3 5.6 %collective-permute-start.21 = (bf16[256,256]{0,1:T(8,128)(2,1)S(1)}, bf16[256,256]{0,1:T(8,128)(2,1)S(1)}, u32[]{:S(2)}, u32[]{:S(2)}) collective-permute-start(bf16[256,256]{0,1:T(8,128)(2,1)S(1)} %get-tuple-element.113), channel_id=1, source_target_pairs={{0,8},{4,12},{8,0},{12,4},{1,9},{5,13},{9,1},{13,5},{2,10},{6,14},... | collective-permute-start | bytes 393224 | tf_op jit(solution)/shard_map/ppermute | solution.py:19
  66.1 7.3 %collective-permute-start.29 = (bf16[256,256]{0,1:T(8,128)(2,1)S(1)}, bf16[256,256]{0,1:T(8,128)(2,1)S(1)}, u32[]{:S(2)}, u32[]{:S(2)}) collective-permute-start(bf16[256,256]{0,1:T(8,128)(2,1)S(1)} %get-tuple-element.103), channel_id=1, source_target_pairs={{0,2},{1,3},{2,0},{3,1},{4,6},{5,7},{6,4},{7,5},{8,10},{9,11},{10,... | collective-permute-start | bytes 393224 | tf_op jit(solution)/shard_map/ppermute | solution.py:19
  67.1 6.4 %collective-permute-start.32 = (bf16[256,256]{0,1:T(8,128)(2,1)S(1)}, bf16[256,256]{0,1:T(8,128)(2,1)S(1)}, u32[]{:S(2)}, u32[]{:S(2)}) collective-permute-start(bf16[256,256]{0,1:T(8,128)(2,1)S(1)} %add_convert_fusion.3), channel_id=1, source_target_pairs={{0,1},{1,0},{2,3},{3,2},{4,5},{5,4},{6,7},{7,6},{8,9},{9,8},{10,11... | collective-permute-start | bytes 393224 | tf_op jit(solution)/shard_map/ppermute | solution.py:19
  68.8 5.9 %collective-permute-start.31 = (bf16[256,256]{0,1:T(8,128)(2,1)S(1)}, bf16[256,256]{0,1:T(8,128)(2,1)S(1)}, u32[]{:S(2)}, u32[]{:S(2)}) collective-permute-start(bf16[256,256]{0,1:T(8,128)(2,1)S(1)} %add_convert_fusion.4), channel_id=1, source_target_pairs={{0,12},{4,8},{8,4},{12,0},{1,13},{5,9},{9,5},{13,1},{2,14},{6,10},... | collective-permute-start | bytes 393224 | tf_op jit(solution)/shard_map/ppermute | solution.py:19
  75.5 7.2 %collective-permute-start.37 = (bf16[256,256]{0,1:T(8,128)(2,1)S(1)}, bf16[256,256]{0,1:T(8,128)(2,1)S(1)}, u32[]{:S(2)}, u32[]{:S(2)}) collective-permute-start(bf16[256,256]{0,1:T(8,128)(2,1)S(1)} %get-tuple-element.70), channel_id=1, source_target_pairs={{0,2},{1,3},{2,0},{3,1},{4,6},{5,7},{6,4},{7,5},{8,10},{9,11},{10,... | collective-permute-start | bytes 393224 | tf_op jit(solution)/shard_map/ppermute | solution.py:19
  77.5 7.2 %collective-permute-start.36 = (bf16[256,256]{0,1:T(8,128)(2,1)S(1)}, bf16[256,256]{0,1:T(8,128)(2,1)S(1)}, u32[]{:S(2)}, u32[]{:S(2)}) collective-permute-start(bf16[256,256]{0,1:T(8,128)(2,1)S(1)} %get-tuple-element.70), channel_id=1, source_target_pairs={{0,1},{1,0},{2,3},{3,2},{4,5},{5,4},{6,7},{7,6},{8,9},{9,8},{10,11... | collective-permute-start | bytes 393224 | tf_op jit(solution)/shard_map/ppermute | solution.py:19
  78.1 7.3 %collective-permute-start.35 = (bf16[256,256]{0,1:T(8,128)(2,1)S(1)}, bf16[256,256]{0,1:T(8,128)(2,1)S(1)}, u32[]{:S(2)}, u32[]{:S(2)}) collective-permute-start(bf16[256,256]{0,1:T(8,128)(2,1)S(1)} %get-tuple-element.70), channel_id=1, source_target_pairs={{0,12},{4,8},{8,4},{12,0},{1,13},{5,9},{9,5},{13,1},{2,14},{6,10},... | collective-permute-start | bytes 393224 | tf_op jit(solution)/shard_map/ppermute | solution.py:19
  78.3 9.1 %collective-permute-start.34 = (bf16[256,256]{0,1:T(8,128)(2,1)S(1)}, bf16[256,256]{0,1:T(8,128)(2,1)S(1)}, u32[]{:S(2)}, u32[]{:S(2)}) collective-permute-start(bf16[256,256]{0,1:T(8,128)(2,1)S(1)} %get-tuple-element.70), channel_id=1, source_target_pairs={{0,8},{4,12},{8,0},{12,4},{1,9},{5,13},{9,1},{13,5},{2,10},{6,14},... | collective-permute-start | bytes 393224 | tf_op jit(solution)/shard_map/ppermute | solution.py:19
  80.8 8.1 %collective-permute-start.33 = (bf16[256,256]{0,1:T(8,128)(2,1)S(1)}, bf16[256,256]{0,1:T(8,128)(2,1)S(1)}, u32[]{:S(2)}, u32[]{:S(2)}) collective-permute-start(bf16[256,256]{0,1:T(8,128)(2,1)S(1)} %get-tuple-element.70), channel_id=1, source_target_pairs={{0,4},{4,0},{8,12},{12,8},{1,5},{5,1},{9,13},{13,9},{2,6},{6,2},{1... | collective-permute-start | bytes 393224 | tf_op jit(solution)/shard_map/ppermute | solution.py:19
  84.7 7.0 %collective-permute-start.39 = (bf16[256,256]{0,1:T(8,128)(2,1)S(1)}, bf16[256,256]{0,1:T(8,128)(2,1)S(1)}, u32[]{:S(2)}, u32[]{:S(2)}) collective-permute-start(bf16[256,256]{0,1:T(8,128)(2,1)S(1)} %collective-permute-done.37), channel_id=1, source_target_pairs={{0,12},{4,8},{8,4},{12,0},{1,13},{5,9},{9,5},{13,1},{2,14},{6,10},... | collective-permute-start | bytes 393224 | tf_op jit(solution)/shard_map/ppermute | solution.py:19
  84.7 6.4 %collective-permute-start.38 = (bf16[256,256]{0,1:T(8,128)(2,1)S(1)}, bf16[256,256]{0,1:T(8,128)(2,1)S(1)}, u32[]{:S(2)}, u32[]{:S(2)}) collective-permute-start(bf16[256,256]{0,1:T(8,128)(2,1)S(1)} %collective-permute-done.37), channel_id=1, source_target_pairs={{0,1},{1,0},{2,3},{3,2},{4,5},{5,4},{6,7},{7,6},{8,9},{9,8},{10,11... | collective-permute-start | bytes 393224 | tf_op jit(solution)/shard_map/ppermute | solution.py:19
  85.4 9.5 %collective-permute-start.41 = (bf16[512,256]{0,1:T(8,128)(2,1)S(1)}, bf16[512,256]{0,1:T(8,128)(2,1)S(1)}, u32[]{:S(2)}, u32[]{:S(2)}) collective-permute-start(bf16[512,256]{0,1:T(8,128)(2,1)S(1)} %constant_dynamic-update-slice_fusion.20), channel_id=1, source_target_pairs={{0,8},{4,12},{8,0},{12,4},{1,9},{5,13},{9,1},{13,5},{2,10},{6,14},... | collective-permute-start | bytes 786440 | tf_op jit(solution)/shard_map/ppermute | solution.py:19
  87.4 7.5 %collective-permute-start.40 = (bf16[512,256]{0,1:T(8,128)(2,1)S(1)}, bf16[512,256]{0,1:T(8,128)(2,1)S(1)}, u32[]{:S(2)}, u32[]{:S(2)}) collective-permute-start(bf16[512,256]{0,1:T(8,128)(2,1)S(1)} %constant_dynamic-update-slice_fusion.20), channel_id=1, source_target_pairs={{0,4},{4,0},{8,12},{12,8},{1,5},{5,1},{9,13},{13,9},{2,6},{6,2},{1... | collective-permute-start | bytes 786440 | tf_op jit(solution)/shard_map/ppermute | solution.py:19
  91.8 6.4 %collective-permute-start.42 = (bf16[512,256]{0,1:T(8,128)(2,1)S(1)}, bf16[512,256]{0,1:T(8,128)(2,1)S(1)}, u32[]{:S(2)}, u32[]{:S(2)}) collective-permute-start(bf16[512,256]{0,1:T(8,128)(2,1)S(1)} %pad_maximum_fusion.1), channel_id=1, source_target_pairs={{0,1},{1,0},{2,3},{3,2},{4,5},{5,4},{6,7},{7,6},{8,9},{9,8},{10,11... | collective-permute-start | bytes 786440 | tf_op jit(solution)/shard_map/ppermute | solution.py:19
  92.8 5.5 %collective-permute-start.44 = (bf16[256,256]{0,1:T(8,128)(2,1)S(1)}, bf16[256,256]{0,1:T(8,128)(2,1)S(1)}, u32[]{:S(2)}, u32[]{:S(2)}) collective-permute-start(bf16[256,256]{0,1:T(8,128)(2,1)S(1)} %collective-permute-done.38), channel_id=1, source_target_pairs={{0,8},{4,12},{8,0},{12,4},{1,9},{5,13},{9,1},{13,5},{2,10},{6,14},... | collective-permute-start | bytes 393224 | tf_op jit(solution)/shard_map/ppermute | solution.py:19
  105.6 5.4 %collective-permute-start.48 = (f32[256]{0:T(256)S(1)}, f32[256]{0:T(256)S(1)}, u32[]{:S(2)}, u32[]{:S(2)}) collective-permute-start(f32[256]{0:T(256)S(1)} %add.172), channel_id=1, source_target_pairs={{0,3},{1,2},{2,1},{3,0},{4,7},{5,6},{6,5},{7,4},{8,11},{9,10},{10,... | collective-permute-start | bytes 3080 | tf_op jit(solution)/shard_map/ppermute | solution.py:19
  116.3 9.0 %collective-permute-start.60 = (bf16[256,256]{0,1:T(8,128)(2,1)S(1)}, bf16[256,256]{0,1:T(8,128)(2,1)S(1)}, u32[]{:S(2)}, u32[]{:S(2)}) collective-permute-start(bf16[256,256]{0,1:T(8,128)(2,1)S(1)} %get-tuple-element.119), channel_id=1, source_target_pairs={{0,8},{4,12},{8,0},{12,4},{1,9},{5,13},{9,1},{13,5},{2,10},{6,14},... | collective-permute-start | bytes 393224 | tf_op jit(solution)/shard_map/ppermute | solution.py:19
  117.2 8.1 %collective-permute-start.59 = (bf16[256,256]{0,1:T(8,128)(2,1)S(1)}, bf16[256,256]{0,1:T(8,128)(2,1)S(1)}, u32[]{:S(2)}, u32[]{:S(2)}) collective-permute-start(bf16[256,256]{0,1:T(8,128)(2,1)S(1)} %get-tuple-element.120), channel_id=1, source_target_pairs={{0,4},{4,0},{8,12},{12,8},{1,5},{5,1},{9,13},{13,9},{2,6},{6,2},{1... | collective-permute-start | bytes 393224 | tf_op jit(solution)/shard_map/ppermute | solution.py:19
  119.0 5.3 %collective-permute-start.57 = (bf16[256,256]{0,1:T(8,128)(2,1)S(1)}, bf16[256,256]{0,1:T(8,128)(2,1)S(1)}, u32[]{:S(2)}, u32[]{:S(2)}) collective-permute-start(bf16[256,256]{0,1:T(8,128)(2,1)S(1)} %get-tuple-element.121), channel_id=1, source_target_pairs={{0,1},{1,0},{2,3},{3,2},{4,5},{5,4},{6,7},{7,6},{8,9},{9,8},{10,11... | collective-permute-start | bytes 393224 | tf_op jit(solution)/shard_map/ppermute | solution.py:19
  119.9 9.2 %collective-permute-start.55 = (bf16[512,256]{0,1:T(8,128)(2,1)S(1)}, bf16[512,256]{0,1:T(8,128)(2,1)S(1)}, u32[]{:S(2)}, u32[]{:S(2)}) collective-permute-start(bf16[512,256]{0,1:T(8,128)(2,1)S(1)} %get-tuple-element.108), channel_id=1, source_target_pairs={{0,4},{4,0},{8,12},{12,8},{1,5},{5,1},{9,13},{13,9},{2,6},{6,2},{1... | collective-permute-start | bytes 786440 | tf_op jit(solution)/shard_map/ppermute | solution.py:19
  120.5 9.9 %collective-permute-start.56 = (bf16[512,256]{0,1:T(8,128)(2,1)S(1)}, bf16[512,256]{0,1:T(8,128)(2,1)S(1)}, u32[]{:S(2)}, u32[]{:S(2)}) collective-permute-start(bf16[512,256]{0,1:T(8,128)(2,1)S(1)} %get-tuple-element.109), channel_id=1, source_target_pairs={{0,8},{4,12},{8,0},{12,4},{1,9},{5,13},{9,1},{13,5},{2,10},{6,14},... | collective-permute-start | bytes 786440 | tf_op jit(solution)/shard_map/ppermute | solution.py:19
  124.3 8.3 %collective-permute-start.58 = (bf16[256,256]{0,1:T(8,128)(2,1)S(1)}, bf16[256,256]{0,1:T(8,128)(2,1)S(1)}, u32[]{:S(2)}, u32[]{:S(2)}) collective-permute-start(bf16[256,256]{0,1:T(8,128)(2,1)S(1)} %get-tuple-element.99), channel_id=1, source_target_pairs={{0,12},{4,8},{8,4},{12,0},{1,13},{5,9},{9,5},{13,1},{2,14},{6,10},... | collective-permute-start | bytes 393224 | tf_op jit(solution)/shard_map/ppermute | solution.py:19
  125.4 6.5 %collective-permute-start.61 = (bf16[256,256]{0,1:T(8,128)(2,1)S(1)}, bf16[256,256]{0,1:T(8,128)(2,1)S(1)}, u32[]{:S(2)}, u32[]{:S(2)}) collective-permute-start(bf16[256,256]{0,1:T(8,128)(2,1)S(1)} %add_convert_fusion.2), channel_id=1, source_target_pairs={{0,1},{1,0},{2,3},{3,2},{4,5},{5,4},{6,7},{7,6},{8,9},{9,8},{10,11... | collective-permute-start | bytes 393224 | tf_op jit(solution)/shard_map/ppermute | solution.py:19
  126.9 12.5 %collective-permute-start.53 = (bf16[256,256]{0,1:T(8,128)(2,1)S(1)}, bf16[256,256]{0,1:T(8,128)(2,1)S(1)}, u32[]{:S(2)}, u32[]{:S(2)}) collective-permute-start(bf16[256,256]{0,1:T(8,128)(2,1)S(1)} %get-tuple-element.106), channel_id=1, source_target_pairs={{0,4},{4,0},{8,12},{12,8},{1,5},{5,1},{9,13},{13,9},{2,6},{6,2},{1... | collective-permute-start | bytes 393224 | tf_op jit(solution)/shard_map/ppermute | solution.py:19
  129.1 10.4 %collective-permute-start.54 = (bf16[256,256]{0,1:T(8,128)(2,1)S(1)}, bf16[256,256]{0,1:T(8,128)(2,1)S(1)}, u32[]{:S(2)}, u32[]{:S(2)}) collective-permute-start(bf16[256,256]{0,1:T(8,128)(2,1)S(1)} %get-tuple-element.107), channel_id=1, source_target_pairs={{0,8},{4,12},{8,0},{12,4},{1,9},{5,13},{9,1},{13,5},{2,10},{6,14},... | collective-permute-start | bytes 393224 | tf_op jit(solution)/shard_map/ppermute | solution.py:19
  135.4 6.0 %collective-permute-start.62 = (bf16[256,256]{0,1:T(8,128)(2,1)S(1)}, bf16[256,256]{0,1:T(8,128)(2,1)S(1)}, u32[]{:S(2)}, u32[]{:S(2)}) collective-permute-start(bf16[256,256]{0,1:T(8,128)(2,1)S(1)} %get-tuple-element.98), channel_id=1, source_target_pairs={{0,2},{1,3},{2,0},{3,1},{4,6},{5,7},{6,4},{7,5},{8,10},{9,11},{10,... | collective-permute-start | bytes 393224 | tf_op jit(solution)/shard_map/ppermute | solution.py:19
  136.4 6.3 %collective-permute-start.65 = (bf16[256,256]{0,1:T(8,128)(2,1)S(1)}, bf16[256,256]{0,1:T(8,128)(2,1)S(1)}, u32[]{:S(2)}, u32[]{:S(2)}) collective-permute-start(bf16[256,256]{0,1:T(8,128)(2,1)S(1)} %add_convert_fusion), channel_id=1, source_target_pairs={{0,1},{1,0},{2,3},{3,2},{4,5},{5,4},{6,7},{7,6},{8,9},{9,8},{10,11... | collective-permute-start | bytes 393224 | tf_op jit(solution)/shard_map/ppermute | solution.py:19
  138.0 5.9 %collective-permute-start.64 = (bf16[256,256]{0,1:T(8,128)(2,1)S(1)}, bf16[256,256]{0,1:T(8,128)(2,1)S(1)}, u32[]{:S(2)}, u32[]{:S(2)}) collective-permute-start(bf16[256,256]{0,1:T(8,128)(2,1)S(1)} %add_convert_fusion.1), channel_id=1, source_target_pairs={{0,12},{4,8},{8,4},{12,0},{1,13},{5,9},{9,5},{13,1},{2,14},{6,10},... | collective-permute-start | bytes 393224 | tf_op jit(solution)/shard_map/ppermute | solution.py:19
  (23 other events, 258.8 us)

commit v6 on v3

--- a/solution.py
+++ b/solution.py
@@ -154,6 +154,24 @@
     )(samples)
 
 
+def scaled(proj, scaling):
+    def kernel(proj_ref, scaling_ref, out_ref):
+        columns = proj_ref[...].astype(jnp.float32)
+        out_ref[...] = (columns.T * scaling_ref[...]).astype(out_ref.dtype)
+
+    return pl.pallas_call(
+        kernel,
+        out_shape=jax.ShapeDtypeStruct(proj.shape, proj.dtype),
+        in_specs=[pl.BlockSpec(memory_space=pltpu.VMEM)] * 2,
+        out_specs=pl.BlockSpec(memory_space=pltpu.VMEM),
+        compiler_params=pltpu.CompilerParams(vmem_limit_bytes=8 << 20),
+        cost_estimate=pl.CostEstimate(
+            flops=proj.size, bytes_accessed=4 * proj.size, transcendentals=0
+        ),
+        name="scaled",
+    )(proj.T, scaling[None])
+
+
 def on_device(views, weights):
     samples = views[0]
     own_rows = weights[0]
@@ -170,7 +188,7 @@
         summed_proj = 0.0
         for g, places in enumerate(ARRIVALS):
             blocks = [dirs[p] for p in places]
-            blocks = lax.optimization_barrier(blocks + [dirs[3, 2]])[: len(places)]
+            blocks = lax.optimization_barrier(blocks + [dirs[0, 3]])[: len(places)]
             part = jnp.dot(
                 groups[g], join(*blocks), preferred_element_type=jnp.float32
             )
@@ -193,11 +211,10 @@
             for i, place in enumerate(ARRIVALS[g]):
                 shares[place] = share[i * depth : (i + 1) * depth]
         if sweep == ITERS - 1:
-            kept_proj, shown_scaling = lax.optimization_barrier((kept_proj, scaling))
-            own_proj = (kept_proj.astype(jnp.float32) * shown_scaling).astype(jnp.bfloat16)
+            shown = scaled(kept_proj, scaling)
         grad = scatter(shares) / row_total
         own_rows = width_root * (own_rows * scaling - step_rate * grad)
-    return (own_rows[None], own_proj[None])
+    return (own_rows[None], shown[None])
 
 
 def solution(mesh):

time: 140 us -> 137 us (0.979)
  starting transfers between devices: 76.1 us -> 74.5 us
  matrix products: 10.8 us -> 9.38 us
    ppermute x64, starting transfers between devices: 76.1 us -> 74.5 us  [xor_move(): return lax.ppermute(block, axis, [(i, i ^ mask) for i in range(count)])]
    dot_general x6, matrix products: 6.16 us -> 4.76 us  [on_device(): lax.dot_general(groups[g], residue, (((0,), (0,)), ((), ())), preferred_e...]
    unnamed x33 -> x24, local copies, waits for them, and re-layouts: 3.09 us -> 2.15 us
  transfers between devices with their start and end apart: 64 -> 64, of which waited for: 35 -> 34; matrix products, arithmetic and copies ran while one was open for 6% -> 5% of each run, Pallas kernels for 2% -> 3%
where the time goes in v6:
time: 137 us
  starting transfers between devices  74.5 us (54%)
  waiting for transfers between devices  44.7 us (33%)
  matrix products  9.38 us (7%)
  Pallas kernels  3.92 us (3%)
  local copies, waits for them, and re-layouts  2.51 us (2%)
    ppermute x64, starting transfers between devices, xor_move(): return lax.ppermute(block, axis, [(i, i ^ mask) for i in range(count)])  74.5 us
    ppermute x64, waiting for transfers between devices, xor_move(): return lax.ppermute(block, axis, [(i, i ^ mask) for i in range(count)])  44.7 us
    dot_general x6, matrix products, on_device(): lax.dot_general(groups[g], residue, (((0,), (0,)), ((), ())), preferred_e...  4.76 us
    dot_general x6, matrix products, on_device(): part = jnp.dot(groups[g], join(*blocks), preferred_element_type=jnp.float32)  4.62 us
    pallas_call x1, Pallas kernels, regroup(): pl.pallas_call(kernel, out_shape=[jax.ShapeDtypeStruct((rows_here, len(pl...  3 us
  transfers between devices with their start and end apart: 64, of which 34 were waited for; matrix products, arithmetic and copies ran while one was open for 5% of the time, Pallas kernels for 3%

profile of v6, /device:TPU:0, one launch (start us, length us, event | category | flops | bytes accessed | tf_op | source)
XLA Modules:
  0.0 137.2 jit_solution(9962733147474460533)
XLA Ops:
  1.7 4.1 %collective-permute-start.4 = (bf16[256,256]{0,1:T(8,128)(2,1)S(1)}, bf16[256,256]{0,1:T(8,128)(2,1)S(1)}, u32[]{:S(2)}, u32[]{:S(2)}) collective-permute-start(bf16[256,256]{0,1:T(8,128)(2,1)S(1)} %bitcast_convert_fusion), channel_id=1, source_target_pairs={{0,2},{1,3},{2,0},{3,1},{4,6},{5,7},{6,4},{7,5},{8,10},{9,11},{10,... | collective-permute-start | bytes 393224 | tf_op jit(solution)/shard_map/ppermute | solution.py:19
  5.8 1.6 %collective-permute-start.3 = (bf16[256,256]{0,1:T(8,128)(2,1)S(1)}, bf16[256,256]{0,1:T(8,128)(2,1)S(1)}, u32[]{:S(2)}, u32[]{:S(2)}) collective-permute-start(bf16[256,256]{0,1:T(8,128)(2,1)S(1)} %bitcast_convert_fusion), channel_id=1, source_target_pairs={{0,1},{1,0},{2,3},{3,2},{4,5},{5,4},{6,7},{7,6},{8,9},{9,8},{10,11... | collective-permute-start | bytes 393224 | tf_op jit(solution)/shard_map/ppermute | solution.py:19
  7.4 2.4 %collective-permute-start.2 = (bf16[256,256]{0,1:T(8,128)(2,1)S(1)}, bf16[256,256]{0,1:T(8,128)(2,1)S(1)}, u32[]{:S(2)}, u32[]{:S(2)}) collective-permute-start(bf16[256,256]{0,1:T(8,128)(2,1)S(1)} %bitcast_convert_fusion), channel_id=1, source_target_pairs={{0,12},{4,8},{8,4},{12,0},{1,13},{5,9},{9,5},{13,1},{2,14},{6,10},... | collective-permute-start | bytes 393224 | tf_op jit(solution)/shard_map/ppermute | solution.py:19
  10.9 3.0 %regroup.1 = (bf16[768,1536]{1,0:T(8,128)(2,1)S(1)}, bf16[768,1536]{1,0:T(8,128)(2,1)S(1)}, bf16[768,1024]{1,0:T(8,128)(2,1)S(1)}) custom-call(bf16[768,4096]{1,0:T(8,128)(2,1)} %bitcast.62), custom_call_target="tpu_custom_call" | custom-call | bytes 12582912 | tf_op jit(solution)/shard_map/regroup/pallas_call | solution.py:140
  13.9 2.5 %collective-permute-start.6 = (bf16[256,256]{0,1:T(8,128)(2,1)S(1)}, bf16[256,256]{0,1:T(8,128)(2,1)S(1)}, u32[]{:S(2)}, u32[]{:S(2)}) collective-permute-start(bf16[256,256]{0,1:T(8,128)(2,1)S(1)} %collective-permute-done.4), channel_id=1, source_target_pairs={{0,12},{4,8},{8,4},{12,0},{1,13},{5,9},{9,5},{13,1},{2,14},{6,10},... | collective-permute-start | bytes 393224 | tf_op jit(solution)/shard_map/ppermute | solution.py:19
  18.1 3.4 %collective-permute-done.5 = bf16[256,256]{0,1:T(8,128)(2,1)S(1)} collective-permute-done((bf16[256,256]{0,1:T(8,128)(2,1)S(1)}, bf16[256,256]{0,1:T(8,128)(2,1)S(1)}, u32[]{:S(2)}, u32[]{:S(2)}) %collective-permute-start.5) | collective-permute-done | bytes 131104 | tf_op jit(solution)/shard_map/ppermute | solution.py:19
  24.0 1.8 %collective-permute-start.10 = (bf16[256,256]{0,1:T(8,128)(2,1)S(1)}, bf16[256,256]{0,1:T(8,128)(2,1)S(1)}, u32[]{:S(2)}, u32[]{:S(2)}) collective-permute-start(bf16[256,256]{0,1:T(8,128)(2,1)S(1)} %collective-permute-done.5), channel_id=1, source_target_pairs={{0,4},{4,0},{8,12},{12,8},{1,5},{5,1},{9,13},{13,9},{2,6},{6,2},{1... | collective-permute-start | bytes 393224 | tf_op jit(solution)/shard_map/ppermute | solution.py:19
  29.7 1.5 %collective-permute-start.12 = (f32[256]{0:T(256)S(1)}, f32[256]{0:T(256)S(1)}, u32[]{:S(2)}, u32[]{:S(2)}) collective-permute-start(f32[256]{0:T(256)S(1)} %get-tuple-element.112), channel_id=1, source_target_pairs={{0,12},{4,8},{8,4},{12,0},{1,13},{5,9},{9,5},{13,1},{2,14},{6,10},... | collective-permute-start | bytes 3080 | tf_op jit(solution)/shard_map/ppermute | solution.py:19
  31.3 1.8 %collective-permute-start.13 = (f32[256]{0:T(256)S(1)}, f32[256]{0:T(256)S(1)}, u32[]{:S(2)}, u32[]{:S(2)}) collective-permute-start(f32[256]{0:T(256)S(1)} %get-tuple-element.112), channel_id=1, source_target_pairs={{0,8},{4,12},{8,0},{12,4},{1,9},{5,13},{9,1},{13,5},{2,10},{6,14},... | collective-permute-start | bytes 3080 | tf_op jit(solution)/shard_map/ppermute | solution.py:19
  34.8 1.8 %collective-permute-done.14 = f32[256]{0:T(256)S(1)} collective-permute-done((f32[256]{0:T(256)S(1)}, f32[256]{0:T(256)S(1)}, u32[]{:S(2)}, u32[]{:S(2)}) %collective-permute-start.14) | collective-permute-done | bytes 1056 | tf_op jit(solution)/shard_map/ppermute | solution.py:19
  36.6 1.3 collective-permute-start.15
  37.9 1.7 %collective-permute-start.16 = (f32[256]{0:T(256)S(1)}, f32[256]{0:T(256)S(1)}, u32[]{:S(2)}, u32[]{:S(2)}) collective-permute-start(f32[256]{0:T(256)S(1)} %add.148), channel_id=1, source_target_pairs={{0,2},{1,3},{2,0},{3,1},{4,6},{5,7},{6,4},{7,5},{8,10},{9,11},{10,... | collective-permute-start | bytes 3080 | tf_op jit(solution)/shard_map/ppermute | solution.py:19
  39.6 1.3 collective-permute-start.17
  46.4 1.3 collective-permute-start.24
  49.8 1.8 %collective-permute-start.23 = (bf16[512,256]{0,1:T(8,128)(2,1)S(1)}, bf16[512,256]{0,1:T(8,128)(2,1)S(1)}, u32[]{:S(2)}, u32[]{:S(2)}) collective-permute-start(bf16[512,256]{0,1:T(8,128)(2,1)S(1)} %get-tuple-element.111), channel_id=1, source_target_pairs={{0,8},{4,12},{8,0},{12,4},{1,9},{5,13},{9,1},{13,5},{2,10},{6,14},... | collective-permute-start | bytes 786440 | tf_op jit(solution)/shard_map/ppermute | solution.py:19
  52.4 1.8 %collective-permute-done.24 = bf16[512,256]{0,1:T(8,128)(2,1)S(1)} collective-permute-done((bf16[512,256]{0,1:T(8,128)(2,1)S(1)}, bf16[512,256]{0,1:T(8,128)(2,1)S(1)}, u32[]{:S(2)}, u32[]{:S(2)}) %collective-permute-start.24) | collective-permute-done | bytes 262176 | tf_op jit(solution)/shard_map/ppermute | solution.py:19
  54.3 2.3 %collective-permute-start.25 = (bf16[256,256]{0,1:T(8,128)(2,1)S(1)}, bf16[256,256]{0,1:T(8,128)(2,1)S(1)}, u32[]{:S(2)}, u32[]{:S(2)}) collective-permute-start(bf16[256,256]{0,1:T(8,128)(2,1)S(1)} %get-tuple-element.100), channel_id=1, source_target_pairs={{0,12},{4,8},{8,4},{12,0},{1,13},{5,9},{9,5},{13,1},{2,14},{6,10},... | collective-permute-start | bytes 393224 | tf_op jit(solution)/shard_map/ppermute | solution.py:19
  56.7 1.4 %collective-permute-start.28 = (bf16[256,256]{0,1:T(8,128)(2,1)S(1)}, bf16[256,256]{0,1:T(8,128)(2,1)S(1)}, u32[]{:S(2)}, u32[]{:S(2)}) collective-permute-start(bf16[256,256]{0,1:T(8,128)(2,1)S(1)} %add_convert_fusion.5), channel_id=1, source_target_pairs={{0,1},{1,0},{2,3},{3,2},{4,5},{5,4},{6,7},{7,6},{8,9},{9,8},{10,11... | collective-permute-start | bytes 393224 | tf_op jit(solution)/shard_map/ppermute | solution.py:19
  59.4 2.3 %collective-permute-done.28 = bf16[256,256]{0,1:T(8,128)(2,1)S(1)} collective-permute-done((bf16[256,256]{0,1:T(8,128)(2,1)S(1)}, bf16[256,256]{0,1:T(8,128)(2,1)S(1)}, u32[]{:S(2)}, u32[]{:S(2)}) %collective-permute-start.28) | collective-permute-done | bytes 131104 | tf_op jit(solution)/shard_map/ppermute | solution.py:19
  61.9 1.3 collective-permute-start.29
  63.2 1.2 collective-permute-start.31
  64.4 1.4 %collective-permute-start.30 = (bf16[256,256]{0,1:T(8,128)(2,1)S(1)}, bf16[256,256]{0,1:T(8,128)(2,1)S(1)}, u32[]{:S(2)}, u32[]{:S(2)}) collective-permute-start(bf16[256,256]{0,1:T(8,128)(2,1)S(1)} %add_convert_fusion.4), channel_id=1, source_target_pairs={{0,12},{4,8},{8,4},{12,0},{1,13},{5,9},{9,5},{13,1},{2,14},{6,10},... | collective-permute-start | bytes 393224 | tf_op jit(solution)/shard_map/ppermute | solution.py:19
  65.8 3.4 %collective-permute-done.29 = bf16[256,256]{0,1:T(8,128)(2,1)S(1)} collective-permute-done((bf16[256,256]{0,1:T(8,128)(2,1)S(1)}, bf16[256,256]{0,1:T(8,128)(2,1)S(1)}, u32[]{:S(2)}, u32[]{:S(2)}) %collective-permute-start.29) | collective-permute-done | bytes 131104 | tf_op jit(solution)/shard_map/ppermute | solution.py:19
  70.4 2.0 %collective-permute-start.36 = (bf16[256,256]{0,1:T(8,128)(2,1)S(1)}, bf16[256,256]{0,1:T(8,128)(2,1)S(1)}, u32[]{:S(2)}, u32[]{:S(2)}) collective-permute-start(bf16[256,256]{0,1:T(8,128)(2,1)S(1)} %get-tuple-element.68), channel_id=1, source_target_pairs={{0,2},{1,3},{2,0},{3,1},{4,6},{5,7},{6,4},{7,5},{8,10},{9,11},{10,... | collective-permute-start | bytes 393224 | tf_op jit(solution)/shard_map/ppermute | solution.py:19
  73.0 2.0 %collective-permute-start.34 = (bf16[256,256]{0,1:T(8,128)(2,1)S(1)}, bf16[256,256]{0,1:T(8,128)(2,1)S(1)}, u32[]{:S(2)}, u32[]{:S(2)}) collective-permute-start(bf16[256,256]{0,1:T(8,128)(2,1)S(1)} %get-tuple-element.68), channel_id=1, source_target_pairs={{0,12},{4,8},{8,4},{12,0},{1,13},{5,9},{9,5},{13,1},{2,14},{6,10},... | collective-permute-start | bytes 393224 | tf_op jit(solution)/shard_map/ppermute | solution.py:19
  76.5 1.3 collective-permute-done.36
  77.8 1.7 %collective-permute-done.35 = bf16[256,256]{0,1:T(8,128)(2,1)S(1)} collective-permute-done((bf16[256,256]{0,1:T(8,128)(2,1)S(1)}, bf16[256,256]{0,1:T(8,128)(2,1)S(1)}, u32[]{:S(2)}, u32[]{:S(2)}) %collective-permute-start.35) | collective-permute-done | bytes 131104 | tf_op jit(solution)/shard_map/ppermute | solution.py:19
  82.4 1.4 %collective-permute-start.39 = (bf16[512,256]{0,1:T(8,128)(2,1)S(1)}, bf16[512,256]{0,1:T(8,128)(2,1)S(1)}, u32[]{:S(2)}, u32[]{:S(2)}) collective-permute-start(bf16[512,256]{0,1:T(8,128)(2,1)S(1)} %constant_dynamic-update-slice_fusion.20), channel_id=1, source_target_pairs={{0,4},{4,0},{8,12},{12,8},{1,5},{5,1},{9,13},{13,9},{2,6},{6,2},{1... | collective-permute-start | bytes 786440 | tf_op jit(solution)/shard_map/ppermute | solution.py:19
  83.8 2.6 %collective-permute-done.37 = bf16[256,256]{0,1:T(8,128)(2,1)S(1)} collective-permute-done((bf16[256,256]{0,1:T(8,128)(2,1)S(1)}, bf16[256,256]{0,1:T(8,128)(2,1)S(1)}, u32[]{:S(2)}, u32[]{:S(2)}) %collective-permute-start.37) | collective-permute-done | bytes 131104 | tf_op jit(solution)/shard_map/ppermute | solution.py:19
  87.7 1.3 collective-permute-start.43
  88.9 1.3 collective-permute-start.42
  91.2 1.8 %collective-permute-done.41 = bf16[512,256]{0,1:T(8,128)(2,1)S(1)} collective-permute-done((bf16[512,256]{0,1:T(8,128)(2,1)S(1)}, bf16[512,256]{0,1:T(8,128)(2,1)S(1)}, u32[]{:S(2)}, u32[]{:S(2)}) %collective-permute-start.41) | collective-permute-done | bytes 262176 | tf_op jit(solution)/shard_map/ppermute | solution.py:19
  94.7 1.3 collective-permute-start.44
  96.0 1.4 %collective-permute-start.45 = (f32[256]{0:T(256)S(1)}, f32[256]{0:T(256)S(1)}, u32[]{:S(2)}, u32[]{:S(2)}) collective-permute-start(f32[256]{0:T(256)S(1)} %get-tuple-element.106), channel_id=1, source_target_pairs={{0,8},{4,12},{8,0},{12,4},{1,9},{5,13},{9,1},{13,5},{2,10},{6,14},... | collective-permute-start | bytes 3080 | tf_op jit(solution)/shard_map/ppermute | solution.py:19
  99.6 1.4 %collective-permute-done.46 = f32[256]{0:T(256)S(1)} collective-permute-done((f32[256]{0:T(256)S(1)}, f32[256]{0:T(256)S(1)}, u32[]{:S(2)}, u32[]{:S(2)}) %collective-permute-start.46) | collective-permute-done | bytes 1056 | tf_op jit(solution)/shard_map/ppermute | solution.py:19
  101.1 1.7 %collective-permute-start.47 = (f32[256]{0:T(256)S(1)}, f32[256]{0:T(256)S(1)}, u32[]{:S(2)}, u32[]{:S(2)}) collective-permute-start(f32[256]{0:T(256)S(1)} %add.172), channel_id=1, source_target_pairs={{0,3},{1,2},{2,1},{3,0},{4,7},{5,6},{6,5},{7,4},{8,11},{9,10},{10,... | collective-permute-start | bytes 3080 | tf_op jit(solution)/shard_map/ppermute | solution.py:19
  102.8 1.3 collective-permute-start.48
  104.1 1.4 %collective-permute-start.49 = (f32[256]{0:T(256)S(1)}, f32[256]{0:T(256)S(1)}, u32[]{:S(2)}, u32[]{:S(2)}) collective-permute-start(f32[256]{0:T(256)S(1)} %add.172), channel_id=1, source_target_pairs={{0,1},{1,0},{2,3},{3,2},{4,5},{5,4},{6,7},{7,6},{8,9},{9,8},{10,11... | collective-permute-start | bytes 3080 | tf_op jit(solution)/shard_map/ppermute | solution.py:19
  114.5 1.4 %collective-permute-start.55 = (bf16[512,256]{0,1:T(8,128)(2,1)S(1)}, bf16[512,256]{0,1:T(8,128)(2,1)S(1)}, u32[]{:S(2)}, u32[]{:S(2)}) collective-permute-start(bf16[512,256]{0,1:T(8,128)(2,1)S(1)} %get-tuple-element.105), channel_id=1, source_target_pairs={{0,8},{4,12},{8,0},{12,4},{1,9},{5,13},{9,1},{13,5},{2,10},{6,14},... | collective-permute-start | bytes 786440 | tf_op jit(solution)/shard_map/ppermute | solution.py:19
  116.9 3.6 %collective-permute-done.56 = bf16[512,256]{0,1:T(8,128)(2,1)S(1)} collective-permute-done((bf16[512,256]{0,1:T(8,128)(2,1)S(1)}, bf16[512,256]{0,1:T(8,128)(2,1)S(1)}, u32[]{:S(2)}, u32[]{:S(2)}) %collective-permute-start.56) | collective-permute-done | bytes 262176 | tf_op jit(solution)/shard_map/ppermute | solution.py:19
  120.5 1.6 %collective-permute-start.57 = (bf16[256,256]{0,1:T(8,128)(2,1)S(1)}, bf16[256,256]{0,1:T(8,128)(2,1)S(1)}, u32[]{:S(2)}, u32[]{:S(2)}) collective-permute-start(bf16[256,256]{0,1:T(8,128)(2,1)S(1)} %get-tuple-element.95), channel_id=1, source_target_pairs={{0,12},{4,8},{8,4},{12,0},{1,13},{5,9},{9,5},{13,1},{2,14},{6,10},... | collective-permute-start | bytes 393224 | tf_op jit(solution)/shard_map/ppermute | solution.py:19
  122.2 1.5 %collective-permute-start.60 = (bf16[256,256]{0,1:T(8,128)(2,1)S(1)}, bf16[256,256]{0,1:T(8,128)(2,1)S(1)}, u32[]{:S(2)}, u32[]{:S(2)}) collective-permute-start(bf16[256,256]{0,1:T(8,128)(2,1)S(1)} %add_convert_fusion.2), channel_id=1, source_target_pairs={{0,1},{1,0},{2,3},{3,2},{4,5},{5,4},{6,7},{7,6},{8,9},{9,8},{10,11... | collective-permute-start | bytes 393224 | tf_op jit(solution)/shard_map/ppermute | solution.py:19
  125.3 1.9 %collective-permute-done.60 = bf16[256,256]{0,1:T(8,128)(2,1)S(1)} collective-permute-done((bf16[256,256]{0,1:T(8,128)(2,1)S(1)}, bf16[256,256]{0,1:T(8,128)(2,1)S(1)}, u32[]{:S(2)}, u32[]{:S(2)}) %collective-permute-start.60) | collective-permute-done | bytes 131104 | tf_op jit(solution)/shard_map/ppermute | solution.py:19
  127.6 1.5 %collective-permute-start.61 = (bf16[256,256]{0,1:T(8,128)(2,1)S(1)}, bf16[256,256]{0,1:T(8,128)(2,1)S(1)}, u32[]{:S(2)}, u32[]{:S(2)}) collective-permute-start(bf16[256,256]{0,1:T(8,128)(2,1)S(1)} %get-tuple-element.94), channel_id=1, source_target_pairs={{0,2},{1,3},{2,0},{3,1},{4,6},{5,7},{6,4},{7,5},{8,10},{9,11},{10,... | collective-permute-start | bytes 393224 | tf_op jit(solution)/shard_map/ppermute | solution.py:19
  129.1 1.3 collective-permute-start.63
  130.4 1.2 collective-permute-start.62
  131.7 3.3 %collective-permute-done.61 = bf16[256,256]{0,1:T(8,128)(2,1)S(1)} collective-permute-done((bf16[256,256]{0,1:T(8,128)(2,1)S(1)}, bf16[256,256]{0,1:T(8,128)(2,1)S(1)}, u32[]{:S(2)}, u32[]{:S(2)}) %collective-permute-start.61) | collective-permute-done | bytes 131104 | tf_op jit(solution)/shard_map/ppermute | solution.py:19
  135.0 1.3 collective-permute-done.62
  (169 shorter events, 47.2 us)
Async XLA Ops:
  1.7 12.2 %collective-permute-start.4 = (bf16[256,256]{0,1:T(8,128)(2,1)S(1)}, bf16[256,256]{0,1:T(8,128)(2,1)S(1)}, u32[]{:S(2)}, u32[]{:S(2)}) collective-permute-start(bf16[256,256]{0,1:T(8,128)(2,1)S(1)} %bitcast_convert_fusion), channel_id=1, source_target_pairs={{0,2},{1,3},{2,0},{3,1},{4,6},{5,7},{6,4},{7,5},{8,10},{9,11},{10,... | collective-permute-start | bytes 393224 | tf_op jit(solution)/shard_map/ppermute | solution.py:19
  5.8 8.1 %collective-permute-start.3 = (bf16[256,256]{0,1:T(8,128)(2,1)S(1)}, bf16[256,256]{0,1:T(8,128)(2,1)S(1)}, u32[]{:S(2)}, u32[]{:S(2)}) collective-permute-start(bf16[256,256]{0,1:T(8,128)(2,1)S(1)} %bitcast_convert_fusion), channel_id=1, source_target_pairs={{0,1},{1,0},{2,3},{3,2},{4,5},{5,4},{6,7},{7,6},{8,9},{9,8},{10,11... | collective-permute-start | bytes 393224 | tf_op jit(solution)/shard_map/ppermute | solution.py:19
  7.4 9.5 %collective-permute-start.2 = (bf16[256,256]{0,1:T(8,128)(2,1)S(1)}, bf16[256,256]{0,1:T(8,128)(2,1)S(1)}, u32[]{:S(2)}, u32[]{:S(2)}) collective-permute-start(bf16[256,256]{0,1:T(8,128)(2,1)S(1)} %bitcast_convert_fusion), channel_id=1, source_target_pairs={{0,12},{4,8},{8,4},{12,0},{1,13},{5,9},{9,5},{13,1},{2,14},{6,10},... | collective-permute-start | bytes 393224 | tf_op jit(solution)/shard_map/ppermute | solution.py:19
  9.9 7.6 %collective-permute-start.1 = (bf16[256,256]{0,1:T(8,128)(2,1)S(1)}, bf16[256,256]{0,1:T(8,128)(2,1)S(1)}, u32[]{:S(2)}, u32[]{:S(2)}) collective-permute-start(bf16[256,256]{0,1:T(8,128)(2,1)S(1)} %bitcast_convert_fusion), channel_id=1, source_target_pairs={{0,8},{4,12},{8,0},{12,4},{1,9},{5,13},{9,1},{13,5},{2,10},{6,14},... | collective-permute-start | bytes 393224 | tf_op jit(solution)/shard_map/ppermute | solution.py:19
  10.4 7.7 %collective-permute-start = (bf16[256,256]{0,1:T(8,128)(2,1)S(1)}, bf16[256,256]{0,1:T(8,128)(2,1)S(1)}, u32[]{:S(2)}, u32[]{:S(2)}) collective-permute-start(bf16[256,256]{0,1:T(8,128)(2,1)S(1)} %bitcast_convert_fusion), channel_id=1, source_target_pairs={{0,4},{4,0},{8,12},{12,8},{1,5},{5,1},{9,13},{13,9},{2,6},{6,2},{1... | collective-permute-start | bytes 393224 | tf_op jit(solution)/shard_map/ppermute | solution.py:19
  13.9 7.5 %collective-permute-start.6 = (bf16[256,256]{0,1:T(8,128)(2,1)S(1)}, bf16[256,256]{0,1:T(8,128)(2,1)S(1)}, u32[]{:S(2)}, u32[]{:S(2)}) collective-permute-start(bf16[256,256]{0,1:T(8,128)(2,1)S(1)} %collective-permute-done.4), channel_id=1, source_target_pairs={{0,12},{4,8},{8,4},{12,0},{1,13},{5,9},{9,5},{13,1},{2,14},{6,10},... | collective-permute-start | bytes 393224 | tf_op jit(solution)/shard_map/ppermute | solution.py:19
  16.9 9.2 %collective-permute-start.8 = (bf16[512,256]{0,1:T(8,128)(2,1)S(1)}, bf16[512,256]{0,1:T(8,128)(2,1)S(1)}, u32[]{:S(2)}, u32[]{:S(2)}) collective-permute-start(bf16[512,256]{0,1:T(8,128)(2,1)S(1)} %constant_dynamic-update-slice_fusion.6), channel_id=1, source_target_pairs={{0,8},{4,12},{8,0},{12,4},{1,9},{5,13},{9,1},{13,5},{2,10},{6,14},... | collective-permute-start | bytes 786440 | tf_op jit(solution)/shard_map/ppermute | solution.py:19
  17.5 8.6 %collective-permute-start.7 = (bf16[512,256]{0,1:T(8,128)(2,1)S(1)}, bf16[512,256]{0,1:T(8,128)(2,1)S(1)}, u32[]{:S(2)}, u32[]{:S(2)}) collective-permute-start(bf16[512,256]{0,1:T(8,128)(2,1)S(1)} %constant_dynamic-update-slice_fusion.6), channel_id=1, source_target_pairs={{0,4},{4,0},{8,12},{12,8},{1,5},{5,1},{9,13},{13,9},{2,6},{6,2},{1... | collective-permute-start | bytes 786440 | tf_op jit(solution)/shard_map/ppermute | solution.py:19
  21.4 6.4 %collective-permute-start.9 = (bf16[512,256]{0,1:T(8,128)(2,1)S(1)}, bf16[512,256]{0,1:T(8,128)(2,1)S(1)}, u32[]{:S(2)}, u32[]{:S(2)}) collective-permute-start(bf16[512,256]{0,1:T(8,128)(2,1)S(1)} %pad_maximum_fusion), channel_id=1, source_target_pairs={{0,1},{1,0},{2,3},{3,2},{4,5},{5,4},{6,7},{7,6},{8,9},{9,8},{10,11... | collective-permute-start | bytes 786440 | tf_op jit(solution)/shard_map/ppermute | solution.py:19
  22.9 5.0 %collective-permute-start.11 = (bf16[256,256]{0,1:T(8,128)(2,1)S(1)}, bf16[256,256]{0,1:T(8,128)(2,1)S(1)}, u32[]{:S(2)}, u32[]{:S(2)}) collective-permute-start(bf16[256,256]{0,1:T(8,128)(2,1)S(1)} %collective-permute-done.5), channel_id=1, source_target_pairs={{0,8},{4,12},{8,0},{12,4},{1,9},{5,13},{9,1},{13,5},{2,10},{6,14},... | collective-permute-start | bytes 393224 | tf_op jit(solution)/shard_map/ppermute | solution.py:19
  29.7 14.8 %collective-permute-start.18 = (bf16[768,256]{0,1:T(8,128)(2,1)S(1)}, bf16[768,256]{0,1:T(8,128)(2,1)S(1)}, u32[]{:S(2)}, u32[]{:S(2)}) collective-permute-start(bf16[768,256]{0,1:T(8,128)(2,1)S(1)} %get-tuple-element.113), channel_id=1, source_target_pairs={{0,16},{16,0},{1,17},{17,1},{2,18},{18,2},{3,19},{19,3},{4,20},{20... | collective-permute-start | bytes 1179656 | tf_op jit(solution)/shard_map/ppermute | solution.py:19
  36.6 5.4 %collective-permute-start.15 = (f32[256]{0:T(256)S(1)}, f32[256]{0:T(256)S(1)}, u32[]{:S(2)}, u32[]{:S(2)}) collective-permute-start(f32[256]{0:T(256)S(1)} %add.148), channel_id=1, source_target_pairs={{0,3},{1,2},{2,1},{3,0},{4,7},{5,6},{6,5},{7,4},{8,11},{9,10},{10,... | collective-permute-start | bytes 3080 | tf_op jit(solution)/shard_map/ppermute | solution.py:19
  45.1 11.5 %collective-permute-start.26 = (bf16[256,256]{0,1:T(8,128)(2,1)S(1)}, bf16[256,256]{0,1:T(8,128)(2,1)S(1)}, u32[]{:S(2)}, u32[]{:S(2)}) collective-permute-start(bf16[256,256]{0,1:T(8,128)(2,1)S(1)} %get-tuple-element.116), channel_id=1, source_target_pairs={{0,4},{4,0},{8,12},{12,8},{1,5},{5,1},{9,13},{13,9},{2,6},{6,2},{1... | collective-permute-start | bytes 393224 | tf_op jit(solution)/shard_map/ppermute | solution.py:19
  45.7 10.9 %collective-permute-start.27 = (bf16[256,256]{0,1:T(8,128)(2,1)S(1)}, bf16[256,256]{0,1:T(8,128)(2,1)S(1)}, u32[]{:S(2)}, u32[]{:S(2)}) collective-permute-start(bf16[256,256]{0,1:T(8,128)(2,1)S(1)} %get-tuple-element.117), channel_id=1, source_target_pairs={{0,8},{4,12},{8,0},{12,4},{1,9},{5,13},{9,1},{13,5},{2,10},{6,14},... | collective-permute-start | bytes 393224 | tf_op jit(solution)/shard_map/ppermute | solution.py:19
  46.4 7.8 %collective-permute-start.24 = (bf16[512,256]{0,1:T(8,128)(2,1)S(1)}, bf16[512,256]{0,1:T(8,128)(2,1)S(1)}, u32[]{:S(2)}, u32[]{:S(2)}) collective-permute-start(bf16[512,256]{0,1:T(8,128)(2,1)S(1)} %slice.265), channel_id=1, source_target_pairs={{0,1},{1,0},{2,3},{3,2},{4,5},{5,4},{6,7},{7,6},{8,9},{9,8},{10,11... | collective-permute-start | bytes 786440 | tf_op jit(solution)/shard_map/ppermute | solution.py:19
  48.7 9.9 %collective-permute-start.22 = (bf16[512,256]{0,1:T(8,128)(2,1)S(1)}, bf16[512,256]{0,1:T(8,128)(2,1)S(1)}, u32[]{:S(2)}, u32[]{:S(2)}) collective-permute-start(bf16[512,256]{0,1:T(8,128)(2,1)S(1)} %get-tuple-element.110), channel_id=1, source_target_pairs={{0,4},{4,0},{8,12},{12,8},{1,5},{5,1},{9,13},{13,9},{2,6},{6,2},{1... | collective-permute-start | bytes 786440 | tf_op jit(solution)/shard_map/ppermute | solution.py:19
  49.8 9.6 %collective-permute-start.23 = (bf16[512,256]{0,1:T(8,128)(2,1)S(1)}, bf16[512,256]{0,1:T(8,128)(2,1)S(1)}, u32[]{:S(2)}, u32[]{:S(2)}) collective-permute-start(bf16[512,256]{0,1:T(8,128)(2,1)S(1)} %get-tuple-element.111), channel_id=1, source_target_pairs={{0,8},{4,12},{8,0},{12,4},{1,9},{5,13},{9,1},{13,5},{2,10},{6,14},... | collective-permute-start | bytes 786440 | tf_op jit(solution)/shard_map/ppermute | solution.py:19
  54.3 7.4 %collective-permute-start.25 = (bf16[256,256]{0,1:T(8,128)(2,1)S(1)}, bf16[256,256]{0,1:T(8,128)(2,1)S(1)}, u32[]{:S(2)}, u32[]{:S(2)}) collective-permute-start(bf16[256,256]{0,1:T(8,128)(2,1)S(1)} %get-tuple-element.100), channel_id=1, source_target_pairs={{0,12},{4,8},{8,4},{12,0},{1,13},{5,9},{9,5},{13,1},{2,14},{6,10},... | collective-permute-start | bytes 393224 | tf_op jit(solution)/shard_map/ppermute | solution.py:19
  56.7 5.0 %collective-permute-start.28 = (bf16[256,256]{0,1:T(8,128)(2,1)S(1)}, bf16[256,256]{0,1:T(8,128)(2,1)S(1)}, u32[]{:S(2)}, u32[]{:S(2)}) collective-permute-start(bf16[256,256]{0,1:T(8,128)(2,1)S(1)} %add_convert_fusion.5), channel_id=1, source_target_pairs={{0,1},{1,0},{2,3},{3,2},{4,5},{5,4},{6,7},{7,6},{8,9},{9,8},{10,11... | collective-permute-start | bytes 393224 | tf_op jit(solution)/shard_map/ppermute | solution.py:19
  58.1 7.7 %collective-permute-start.20 = (bf16[256,256]{0,1:T(8,128)(2,1)S(1)}, bf16[256,256]{0,1:T(8,128)(2,1)S(1)}, u32[]{:S(2)}, u32[]{:S(2)}) collective-permute-start(bf16[256,256]{0,1:T(8,128)(2,1)S(1)} %get-tuple-element.108), channel_id=1, source_target_pairs={{0,4},{4,0},{8,12},{12,8},{1,5},{5,1},{9,13},{13,9},{2,6},{6,2},{1... | collective-permute-start | bytes 393224 | tf_op jit(solution)/shard_map/ppermute | solution.py:19
  58.5 7.3 %collective-permute-start.21 = (bf16[256,256]{0,1:T(8,128)(2,1)S(1)}, bf16[256,256]{0,1:T(8,128)(2,1)S(1)}, u32[]{:S(2)}, u32[]{:S(2)}) collective-permute-start(bf16[256,256]{0,1:T(8,128)(2,1)S(1)} %get-tuple-element.109), channel_id=1, source_target_pairs={{0,8},{4,12},{8,0},{12,4},{1,9},{5,13},{9,1},{13,5},{2,10},{6,14},... | collective-permute-start | bytes 393224 | tf_op jit(solution)/shard_map/ppermute | solution.py:19
  61.9 7.3 %collective-permute-start.29 = (bf16[256,256]{0,1:T(8,128)(2,1)S(1)}, bf16[256,256]{0,1:T(8,128)(2,1)S(1)}, u32[]{:S(2)}, u32[]{:S(2)}) collective-permute-start(bf16[256,256]{0,1:T(8,128)(2,1)S(1)} %get-tuple-element.99), channel_id=1, source_target_pairs={{0,2},{1,3},{2,0},{3,1},{4,6},{5,7},{6,4},{7,5},{8,10},{9,11},{10,... | collective-permute-start | bytes 393224 | tf_op jit(solution)/shard_map/ppermute | solution.py:19
  63.2 6.1 %collective-permute-start.31 = (bf16[256,256]{0,1:T(8,128)(2,1)S(1)}, bf16[256,256]{0,1:T(8,128)(2,1)S(1)}, u32[]{:S(2)}, u32[]{:S(2)}) collective-permute-start(bf16[256,256]{0,1:T(8,128)(2,1)S(1)} %add_convert_fusion.3), channel_id=1, source_target_pairs={{0,1},{1,0},{2,3},{3,2},{4,5},{5,4},{6,7},{7,6},{8,9},{9,8},{10,11... | collective-permute-start | bytes 393224 | tf_op jit(solution)/shard_map/ppermute | solution.py:19
  64.4 5.9 %collective-permute-start.30 = (bf16[256,256]{0,1:T(8,128)(2,1)S(1)}, bf16[256,256]{0,1:T(8,128)(2,1)S(1)}, u32[]{:S(2)}, u32[]{:S(2)}) collective-permute-start(bf16[256,256]{0,1:T(8,128)(2,1)S(1)} %add_convert_fusion.4), channel_id=1, source_target_pairs={{0,12},{4,8},{8,4},{12,0},{1,13},{5,9},{9,5},{13,1},{2,14},{6,10},... | collective-permute-start | bytes 393224 | tf_op jit(solution)/shard_map/ppermute | solution.py:19
  70.4 7.4 %collective-permute-start.36 = (bf16[256,256]{0,1:T(8,128)(2,1)S(1)}, bf16[256,256]{0,1:T(8,128)(2,1)S(1)}, u32[]{:S(2)}, u32[]{:S(2)}) collective-permute-start(bf16[256,256]{0,1:T(8,128)(2,1)S(1)} %get-tuple-element.68), channel_id=1, source_target_pairs={{0,2},{1,3},{2,0},{3,1},{4,6},{5,7},{6,4},{7,5},{8,10},{9,11},{10,... | collective-permute-start | bytes 393224 | tf_op jit(solution)/shard_map/ppermute | solution.py:19
  72.4 7.2 %collective-permute-start.35 = (bf16[256,256]{0,1:T(8,128)(2,1)S(1)}, bf16[256,256]{0,1:T(8,128)(2,1)S(1)}, u32[]{:S(2)}, u32[]{:S(2)}) collective-permute-start(bf16[256,256]{0,1:T(8,128)(2,1)S(1)} %get-tuple-element.68), channel_id=1, source_target_pairs={{0,1},{1,0},{2,3},{3,2},{4,5},{5,4},{6,7},{7,6},{8,9},{9,8},{10,11... | collective-permute-start | bytes 393224 | tf_op jit(solution)/shard_map/ppermute | solution.py:19
  73.0 8.1 %collective-permute-start.34 = (bf16[256,256]{0,1:T(8,128)(2,1)S(1)}, bf16[256,256]{0,1:T(8,128)(2,1)S(1)}, u32[]{:S(2)}, u32[]{:S(2)}) collective-permute-start(bf16[256,256]{0,1:T(8,128)(2,1)S(1)} %get-tuple-element.68), channel_id=1, source_target_pairs={{0,12},{4,8},{8,4},{12,0},{1,13},{5,9},{9,5},{13,1},{2,14},{6,10},... | collective-permute-start | bytes 393224 | tf_op jit(solution)/shard_map/ppermute | solution.py:19
  75.0 7.4 %collective-permute-start.33 = (bf16[256,256]{0,1:T(8,128)(2,1)S(1)}, bf16[256,256]{0,1:T(8,128)(2,1)S(1)}, u32[]{:S(2)}, u32[]{:S(2)}) collective-permute-start(bf16[256,256]{0,1:T(8,128)(2,1)S(1)} %get-tuple-element.68), channel_id=1, source_target_pairs={{0,8},{4,12},{8,0},{12,4},{1,9},{5,13},{9,1},{13,5},{2,10},{6,14},... | collective-permute-start | bytes 393224 | tf_op jit(solution)/shard_map/ppermute | solution.py:19
  75.8 8.0 %collective-permute-start.32 = (bf16[256,256]{0,1:T(8,128)(2,1)S(1)}, bf16[256,256]{0,1:T(8,128)(2,1)S(1)}, u32[]{:S(2)}, u32[]{:S(2)}) collective-permute-start(bf16[256,256]{0,1:T(8,128)(2,1)S(1)} %get-tuple-element.68), channel_id=1, source_target_pairs={{0,4},{4,0},{8,12},{12,8},{1,5},{5,1},{9,13},{13,9},{2,6},{6,2},{1... | collective-permute-start | bytes 393224 | tf_op jit(solution)/shard_map/ppermute | solution.py:19
  79.5 7.0 %collective-permute-start.38 = (bf16[256,256]{0,1:T(8,128)(2,1)S(1)}, bf16[256,256]{0,1:T(8,128)(2,1)S(1)}, u32[]{:S(2)}, u32[]{:S(2)}) collective-permute-start(bf16[256,256]{0,1:T(8,128)(2,1)S(1)} %collective-permute-done.36), channel_id=1, source_target_pairs={{0,12},{4,8},{8,4},{12,0},{1,13},{5,9},{9,5},{13,1},{2,14},{6,10},... | collective-permute-start | bytes 393224 | tf_op jit(solution)/shard_map/ppermute | solution.py:19
  80.0 6.3 %collective-permute-start.37 = (bf16[256,256]{0,1:T(8,128)(2,1)S(1)}, bf16[256,256]{0,1:T(8,128)(2,1)S(1)}, u32[]{:S(2)}, u32[]{:S(2)}) collective-permute-start(bf16[256,256]{0,1:T(8,128)(2,1)S(1)} %collective-permute-done.36), channel_id=1, source_target_pairs={{0,1},{1,0},{2,3},{3,2},{4,5},{5,4},{6,7},{7,6},{8,9},{9,8},{10,11... | collective-permute-start | bytes 393224 | tf_op jit(solution)/shard_map/ppermute | solution.py:19
  81.2 9.0 %collective-permute-start.40 = (bf16[512,256]{0,1:T(8,128)(2,1)S(1)}, bf16[512,256]{0,1:T(8,128)(2,1)S(1)}, u32[]{:S(2)}, u32[]{:S(2)}) collective-permute-start(bf16[512,256]{0,1:T(8,128)(2,1)S(1)} %constant_dynamic-update-slice_fusion.20), channel_id=1, source_target_pairs={{0,8},{4,12},{8,0},{12,4},{1,9},{5,13},{9,1},{13,5},{2,10},{6,14},... | collective-permute-start | bytes 786440 | tf_op jit(solution)/shard_map/ppermute | solution.py:19
  82.4 7.9 %collective-permute-start.39 = (bf16[512,256]{0,1:T(8,128)(2,1)S(1)}, bf16[512,256]{0,1:T(8,128)(2,1)S(1)}, u32[]{:S(2)}, u32[]{:S(2)}) collective-permute-start(bf16[512,256]{0,1:T(8,128)(2,1)S(1)} %constant_dynamic-update-slice_fusion.20), channel_id=1, source_target_pairs={{0,4},{4,0},{8,12},{12,8},{1,5},{5,1},{9,13},{13,9},{2,6},{6,2},{1... | collective-permute-start | bytes 786440 | tf_op jit(solution)/shard_map/ppermute | solution.py:19
  86.6 6.4 %collective-permute-start.41 = (bf16[512,256]{0,1:T(8,128)(2,1)S(1)}, bf16[512,256]{0,1:T(8,128)(2,1)S(1)}, u32[]{:S(2)}, u32[]{:S(2)}) collective-permute-start(bf16[512,256]{0,1:T(8,128)(2,1)S(1)} %pad_maximum_fusion.1), channel_id=1, source_target_pairs={{0,1},{1,0},{2,3},{3,2},{4,5},{5,4},{6,7},{7,6},{8,9},{9,8},{10,11... | collective-permute-start | bytes 786440 | tf_op jit(solution)/shard_map/ppermute | solution.py:19
  87.7 5.4 %collective-permute-start.43 = (bf16[256,256]{0,1:T(8,128)(2,1)S(1)}, bf16[256,256]{0,1:T(8,128)(2,1)S(1)}, u32[]{:S(2)}, u32[]{:S(2)}) collective-permute-start(bf16[256,256]{0,1:T(8,128)(2,1)S(1)} %collective-permute-done.37), channel_id=1, source_target_pairs={{0,8},{4,12},{8,0},{12,4},{1,9},{5,13},{9,1},{13,5},{2,10},{6,14},... | collective-permute-start | bytes 393224 | tf_op jit(solution)/shard_map/ppermute | solution.py:19
  94.6 14.2 %collective-permute-start.50 = (bf16[768,256]{0,1:T(8,128)(2,1)S(1)}, bf16[768,256]{0,1:T(8,128)(2,1)S(1)}, u32[]{:S(2)}, u32[]{:S(2)}) collective-permute-start(bf16[768,256]{0,1:T(8,128)(2,1)S(1)} %get-tuple-element.107), channel_id=1, source_target_pairs={{0,16},{16,0},{1,17},{17,1},{2,18},{18,2},{3,19},{19,3},{4,20},{20... | collective-permute-start | bytes 1179656 | tf_op jit(solution)/shard_map/ppermute | solution.py:19
  101.1 5.4 %collective-permute-start.47 = (f32[256]{0:T(256)S(1)}, f32[256]{0:T(256)S(1)}, u32[]{:S(2)}, u32[]{:S(2)}) collective-permute-start(f32[256]{0:T(256)S(1)} %add.172), channel_id=1, source_target_pairs={{0,3},{1,2},{2,1},{3,0},{4,7},{5,6},{6,5},{7,4},{8,11},{9,10},{10,... | collective-permute-start | bytes 3080 | tf_op jit(solution)/shard_map/ppermute | solution.py:19
  110.5 11.6 %collective-permute-start.58 = (bf16[256,256]{0,1:T(8,128)(2,1)S(1)}, bf16[256,256]{0,1:T(8,128)(2,1)S(1)}, u32[]{:S(2)}, u32[]{:S(2)}) collective-permute-start(bf16[256,256]{0,1:T(8,128)(2,1)S(1)} %get-tuple-element.114), channel_id=1, source_target_pairs={{0,4},{4,0},{8,12},{12,8},{1,5},{5,1},{9,13},{13,9},{2,6},{6,2},{1... | collective-permute-start | bytes 393224 | tf_op jit(solution)/shard_map/ppermute | solution.py:19
  111.5 10.6 %collective-permute-start.59 = (bf16[256,256]{0,1:T(8,128)(2,1)S(1)}, bf16[256,256]{0,1:T(8,128)(2,1)S(1)}, u32[]{:S(2)}, u32[]{:S(2)}) collective-permute-start(bf16[256,256]{0,1:T(8,128)(2,1)S(1)} %get-tuple-element.115), channel_id=1, source_target_pairs={{0,8},{4,12},{8,0},{12,4},{1,9},{5,13},{9,1},{13,5},{2,10},{6,14},... | collective-permute-start | bytes 393224 | tf_op jit(solution)/shard_map/ppermute | solution.py:19
  112.5 7.9 %collective-permute-start.56 = (bf16[512,256]{0,1:T(8,128)(2,1)S(1)}, bf16[512,256]{0,1:T(8,128)(2,1)S(1)}, u32[]{:S(2)}, u32[]{:S(2)}) collective-permute-start(bf16[512,256]{0,1:T(8,128)(2,1)S(1)} %slice.290), channel_id=1, source_target_pairs={{0,1},{1,0},{2,3},{3,2},{4,5},{5,4},{6,7},{7,6},{8,9},{9,8},{10,11... | collective-permute-start | bytes 786440 | tf_op jit(solution)/shard_map/ppermute | solution.py:19
  113.5 11.0 %collective-permute-start.54 = (bf16[512,256]{0,1:T(8,128)(2,1)S(1)}, bf16[512,256]{0,1:T(8,128)(2,1)S(1)}, u32[]{:S(2)}, u32[]{:S(2)}) collective-permute-start(bf16[512,256]{0,1:T(8,128)(2,1)S(1)} %get-tuple-element.104), channel_id=1, source_target_pairs={{0,4},{4,0},{8,12},{12,8},{1,5},{5,1},{9,13},{13,9},{2,6},{6,2},{1... | collective-permute-start | bytes 786440 | tf_op jit(solution)/shard_map/ppermute | solution.py:19
  114.5 10.8 %collective-permute-start.55 = (bf16[512,256]{0,1:T(8,128)(2,1)S(1)}, bf16[512,256]{0,1:T(8,128)(2,1)S(1)}, u32[]{:S(2)}, u32[]{:S(2)}) collective-permute-start(bf16[512,256]{0,1:T(8,128)(2,1)S(1)} %get-tuple-element.105), channel_id=1, source_target_pairs={{0,8},{4,12},{8,0},{12,4},{1,9},{5,13},{9,1},{13,5},{2,10},{6,14},... | collective-permute-start | bytes 786440 | tf_op jit(solution)/shard_map/ppermute | solution.py:19
  120.5 6.9 %collective-permute-start.57 = (bf16[256,256]{0,1:T(8,128)(2,1)S(1)}, bf16[256,256]{0,1:T(8,128)(2,1)S(1)}, u32[]{:S(2)}, u32[]{:S(2)}) collective-permute-start(bf16[256,256]{0,1:T(8,128)(2,1)S(1)} %get-tuple-element.95), channel_id=1, source_target_pairs={{0,12},{4,8},{8,4},{12,0},{1,13},{5,9},{9,5},{13,1},{2,14},{6,10},... | collective-permute-start | bytes 393224 | tf_op jit(solution)/shard_map/ppermute | solution.py:19
  123.6 8.0 %collective-permute-start.52 = (bf16[256,256]{0,1:T(8,128)(2,1)S(1)}, bf16[256,256]{0,1:T(8,128)(2,1)S(1)}, u32[]{:S(2)}, u32[]{:S(2)}) collective-permute-start(bf16[256,256]{0,1:T(8,128)(2,1)S(1)} %get-tuple-element.102), channel_id=1, source_target_pairs={{0,4},{4,0},{8,12},{12,8},{1,5},{5,1},{9,13},{13,9},{2,6},{6,2},{1... | collective-permute-start | bytes 393224 | tf_op jit(solution)/shard_map/ppermute | solution.py:19
  124.5 7.2 %collective-permute-start.53 = (bf16[256,256]{0,1:T(8,128)(2,1)S(1)}, bf16[256,256]{0,1:T(8,128)(2,1)S(1)}, u32[]{:S(2)}, u32[]{:S(2)}) collective-permute-start(bf16[256,256]{0,1:T(8,128)(2,1)S(1)} %get-tuple-element.103), channel_id=1, source_target_pairs={{0,8},{4,12},{8,0},{12,4},{1,9},{5,13},{9,1},{13,5},{2,10},{6,14},... | collective-permute-start | bytes 393224 | tf_op jit(solution)/shard_map/ppermute | solution.py:19
  127.6 7.3 %collective-permute-start.61 = (bf16[256,256]{0,1:T(8,128)(2,1)S(1)}, bf16[256,256]{0,1:T(8,128)(2,1)S(1)}, u32[]{:S(2)}, u32[]{:S(2)}) collective-permute-start(bf16[256,256]{0,1:T(8,128)(2,1)S(1)} %get-tuple-element.94), channel_id=1, source_target_pairs={{0,2},{1,3},{2,0},{3,1},{4,6},{5,7},{6,4},{7,5},{8,10},{9,11},{10,... | collective-permute-start | bytes 393224 | tf_op jit(solution)/shard_map/ppermute | solution.py:19
  129.1 5.9 %collective-permute-start.63 = (bf16[256,256]{0,1:T(8,128)(2,1)S(1)}, bf16[256,256]{0,1:T(8,128)(2,1)S(1)}, u32[]{:S(2)}, u32[]{:S(2)}) collective-permute-start(bf16[256,256]{0,1:T(8,128)(2,1)S(1)} %add_convert_fusion), channel_id=1, source_target_pairs={{0,1},{1,0},{2,3},{3,2},{4,5},{5,4},{6,7},{7,6},{8,9},{9,8},{10,11... | collective-permute-start | bytes 393224 | tf_op jit(solution)/shard_map/ppermute | solution.py:19
  130.4 5.9 %collective-permute-start.62 = (bf16[256,256]{0,1:T(8,128)(2,1)S(1)}, bf16[256,256]{0,1:T(8,128)(2,1)S(1)}, u32[]{:S(2)}, u32[]{:S(2)}) collective-permute-start(bf16[256,256]{0,1:T(8,128)(2,1)S(1)} %add_convert_fusion.1), channel_id=1, source_target_pairs={{0,12},{4,8},{8,4},{12,0},{1,13},{5,9},{9,5},{13,1},{2,14},{6,10},... | collective-permute-start | bytes 393224 | tf_op jit(solution)/shard_map/ppermute | solution.py:19
  (16 other events, 61.7 us)

commit v7 on v6

--- a/solution.py
+++ b/solution.py
@@ -66,12 +66,12 @@
 
 def scatter(b):
     def send(axis, mask, *blocks):
-        half = [block.astype(jnp.bfloat16) for block in blocks]
-        got = xor_move(half[0] if len(half) == 1 else join(*half), axis, mask)
-        return [part.astype(jnp.float32) for part in (split(got) if len(half) > 1 else [got])]
+        got = xor_move(blocks[0] if len(blocks) == 1 else join(*blocks), axis, mask)
+        return [part.astype(jnp.float32) for part in (split(got) if len(blocks) > 1 else [got])]
 
     def summed(first, *others):
-        return lax.optimization_barrier(sum(others, first).astype(jnp.bfloat16))
+        sums = sum(others, first.astype(jnp.float32))
+        return lax.optimization_barrier(sums.astype(jnp.bfloat16))
 
     near_across, far_across = send("feat", 1, b[3, 1], b[3, 3])
     (left,), (right,) = send("row", 1, b[1, 3]), send("row", 2, b[2, 3])
@@ -87,7 +87,7 @@
         send("row", 3, near_across),
         send("feat", 1, one),
     )
-    near = b[0, 0] + send("row", 1, b[1, 0])[0] + send("row", 2, b[2, 0])[0]
+    near = b[0, 0].astype(jnp.float32) + send("row", 1, b[1, 0])[0] + send("row", 2, b[2, 0])[0]
     return lax.optimization_barrier(near + two) + near_across + one
 
 
@@ -182,9 +182,10 @@
         return any_mesh(samples, own_rows)
     row_total = rows_here * rows * feats
     width_root = math.sqrt(width)
-    groups = regroup(samples, depth)
     for sweep in range(ITERS):
         dirs = gather(own_rows.astype(jnp.bfloat16))
+        if sweep == 0:
+            groups = regroup(after(samples, dirs[1, 0]), depth)
         summed_proj = 0.0
         for g, places in enumerate(ARRIVALS):
             blocks = [dirs[p] for p in places]
@@ -207,7 +208,7 @@
         for g in (2, 1, 0):
             share = lax.dot_general(
                 groups[g], residue, (((0,), (0,)), ((), ())), preferred_element_type=jnp.float32
-            )
+            ).astype(jnp.bfloat16)
             for i, place in enumerate(ARRIVALS[g]):
                 shares[place] = share[i * depth : (i + 1) * depth]
         if sweep == ITERS - 1:

time: 137 us -> 151 us (1.10)
  waiting for transfers between devices: 44.7 us -> 51.6 us
  local copies, waits for them, and re-layouts: 2.51 us -> 6.22 us
  other arithmetic: 1.04 us -> 3.44 us
    ppermute x64, waiting for transfers between devices: 44.7 us -> 51.6 us  [xor_move(): return lax.ppermute(block, axis, [(i, i ^ mask) for i in range(count)])]
    slice x6, local copies, waits for them, and re-layouts: 0.11 us -> 2.05 us  [split(): return (pair[:deep], pair[deep:])]
  transfers between devices with their start and end apart: 64 -> 64, of which waited for: 34 -> 28; matrix products, arithmetic and copies ran while one was open for 5% -> 8% of each run, Pallas kernels for 3% -> 3%
where the time goes in v7:
time: 151 us
  starting transfers between devices  73.5 us (49%)
  waiting for transfers between devices  51.6 us (34%)
  matrix products  10.5 us (7%)
  local copies, waits for them, and re-layouts  6.22 us (4%)
  Pallas kernels  3.92 us (3%)
  other arithmetic  3.44 us (2%)
    ppermute x64, starting transfers between devices, xor_move(): return lax.ppermute(block, axis, [(i, i ^ mask) for i in range(count)])  73.5 us
    ppermute x64, waiting for transfers between devices, xor_move(): return lax.ppermute(block, axis, [(i, i ^ mask) for i in range(count)])  51.6 us
    dot_general x6, matrix products, on_device(): part = jnp.dot(groups[g], join(*blocks), preferred_element_type=jnp.float32)  5.39 us
    dot_general x6, matrix products, on_device(): lax.dot_general(groups[g], residue, (((0,), (0,)), ((), ())), preferred_e...  5.13 us
  transfers between devices with their start and end apart: 64, of which 28 were waited for; matrix products, arithmetic and copies ran while one was open for 8% of the time, Pallas kernels for 3%

profile of v7, /device:TPU:0, one launch (start us, length us, event | category | flops | bytes accessed | tf_op | source)
XLA Modules:
  0.0 150.6 jit_solution(5760566690670983242)
XLA Ops:
  1.6 3.1 %collective-permute-start.3 = (bf16[256,256]{1,0:T(8,128)(2,1)S(1)}, bf16[256,256]{1,0:T(8,128)(2,1)S(1)}, u32[]{:S(2)}, u32[]{:S(2)}) collective-permute-start(bf16[256,256]{1,0:T(8,128)(2,1)S(1)} %bitcast_convert_fusion), channel_id=1, source_target_pairs={{0,1},{1,0},{2,3},{3,2},{4,5},{5,4},{6,7},{7,6},{8,9},{9,8},{10,11... | collective-permute-start | bytes 393224 | tf_op jit(solution)/shard_map/ppermute | solution.py:19
  4.7 2.6 %collective-permute-start.4 = (bf16[256,256]{1,0:T(8,128)(2,1)S(1)}, bf16[256,256]{1,0:T(8,128)(2,1)S(1)}, u32[]{:S(2)}, u32[]{:S(2)}) collective-permute-start(bf16[256,256]{1,0:T(8,128)(2,1)S(1)} %bitcast_convert_fusion), channel_id=1, source_target_pairs={{0,2},{1,3},{2,0},{3,1},{4,6},{5,7},{6,4},{7,5},{8,10},{9,11},{10,... | collective-permute-start | bytes 393224 | tf_op jit(solution)/shard_map/ppermute | solution.py:19
  7.3 1.5 collective-permute-start
  8.8 1.5 %collective-permute-start.1 = (bf16[256,256]{1,0:T(8,128)(2,1)S(1)}, bf16[256,256]{1,0:T(8,128)(2,1)S(1)}, u32[]{:S(2)}, u32[]{:S(2)}) collective-permute-start(bf16[256,256]{1,0:T(8,128)(2,1)S(1)} %bitcast_convert_fusion), channel_id=1, source_target_pairs={{0,8},{4,12},{8,0},{12,4},{1,9},{5,13},{9,1},{13,5},{2,10},{6,14},... | collective-permute-start | bytes 393224 | tf_op jit(solution)/shard_map/ppermute | solution.py:19
  10.8 2.6 %collective-permute-done.4 = bf16[256,256]{1,0:T(8,128)(2,1)S(1)} collective-permute-done((bf16[256,256]{1,0:T(8,128)(2,1)S(1)}, bf16[256,256]{1,0:T(8,128)(2,1)S(1)}, u32[]{:S(2)}, u32[]{:S(2)}) %collective-permute-start.4) | collective-permute-done | bytes 131104 | tf_op jit(solution)/shard_map/ppermute | solution.py:19
  13.9 1.6 %collective-permute-start.7 = (bf16[512,256]{1,0:T(8,128)(2,1)S(1)}, bf16[512,256]{1,0:T(8,128)(2,1)S(1)}, u32[]{:S(2)}, u32[]{:S(2)}) collective-permute-start(bf16[512,256]{1,0:T(8,128)(2,1)S(1)} %constant_dynamic-update-slice_fusion.6), channel_id=1, source_target_pairs={{0,4},{4,0},{8,12},{12,8},{1,5},{5,1},{9,13},{13,9},{2,6},{6,2},{1... | collective-permute-start | bytes 786440 | tf_op jit(solution)/shard_map/ppermute | solution.py:19
  15.4 1.5 %collective-permute-start.8 = (bf16[512,256]{1,0:T(8,128)(2,1)S(1)}, bf16[512,256]{1,0:T(8,128)(2,1)S(1)}, u32[]{:S(2)}, u32[]{:S(2)}) collective-permute-start(bf16[512,256]{1,0:T(8,128)(2,1)S(1)} %constant_dynamic-update-slice_fusion.6), channel_id=1, source_target_pairs={{0,8},{4,12},{8,0},{12,4},{1,9},{5,13},{9,1},{13,5},{2,10},{6,14},... | collective-permute-start | bytes 786440 | tf_op jit(solution)/shard_map/ppermute | solution.py:19
  17.0 3.0 %regroup.1 = (bf16[768,1536]{1,0:T(8,128)(2,1)S(1)}, bf16[768,1536]{1,0:T(8,128)(2,1)S(1)}, bf16[768,1024]{1,0:T(8,128)(2,1)S(1)}) custom-call(bf16[768,4096]{1,0:T(8,128)(2,1)} %bitcast.33), custom_call_target="tpu_custom_call" | custom-call | bytes 12582912 | tf_op jit(solution)/shard_map/regroup/pallas_call | solution.py:140
  21.4 4.5 %collective-permute-done.6 = bf16[256,256]{1,0:T(8,128)(2,1)S(1)} collective-permute-done((bf16[256,256]{1,0:T(8,128)(2,1)S(1)}, bf16[256,256]{1,0:T(8,128)(2,1)S(1)}, u32[]{:S(2)}, u32[]{:S(2)}) %collective-permute-start.6) | collective-permute-done | bytes 131104 | tf_op jit(solution)/shard_map/ppermute | solution.py:19
  25.9 1.6 %collective-permute-start.9 = (bf16[512,256]{1,0:T(8,128)(2,1)S(1)}, bf16[512,256]{1,0:T(8,128)(2,1)S(1)}, u32[]{:S(2)}, u32[]{:S(2)}) collective-permute-start(bf16[512,256]{1,0:T(8,128)(2,1)S(1)} %pad_maximum_fusion), channel_id=1, source_target_pairs={{0,1},{1,0},{2,3},{3,2},{4,5},{5,4},{6,7},{7,6},{8,9},{9,8},{10,11... | collective-permute-start | bytes 786440 | tf_op jit(solution)/shard_map/ppermute | solution.py:19
  29.6 2.8 %collective-permute-done.9 = bf16[512,256]{1,0:T(8,128)(2,1)S(1)} collective-permute-done((bf16[512,256]{1,0:T(8,128)(2,1)S(1)}, bf16[512,256]{1,0:T(8,128)(2,1)S(1)}, u32[]{:S(2)}, u32[]{:S(2)}) %collective-permute-start.9) | collective-permute-done | bytes 262176 | tf_op jit(solution)/shard_map/ppermute | solution.py:19
  33.8 1.5 collective-permute-start.12
  35.3 1.5 %collective-permute-start.13 = (f32[256]{0:T(256)S(1)}, f32[256]{0:T(256)S(1)}, u32[]{:S(2)}, u32[]{:S(2)}) collective-permute-start(f32[256]{0:T(256)S(1)} %get-tuple-element.106), channel_id=1, source_target_pairs={{0,8},{4,12},{8,0},{12,4},{1,9},{5,13},{9,1},{13,5},{2,10},{6,14},... | collective-permute-start | bytes 3080 | tf_op jit(solution)/shard_map/ppermute | solution.py:19
  38.8 1.5 %collective-permute-done.14 = f32[256]{0:T(256)S(1)} collective-permute-done((f32[256]{0:T(256)S(1)}, f32[256]{0:T(256)S(1)}, u32[]{:S(2)}, u32[]{:S(2)}) %collective-permute-start.14) | collective-permute-done | bytes 1056 | tf_op jit(solution)/shard_map/ppermute | solution.py:19
  40.4 2.6 %collective-permute-start.15 = (f32[256]{0:T(256)S(1)}, f32[256]{0:T(256)S(1)}, u32[]{:S(2)}, u32[]{:S(2)}) collective-permute-start(f32[256]{0:T(256)S(1)} %add.148), channel_id=1, source_target_pairs={{0,3},{1,2},{2,1},{3,0},{4,7},{5,6},{6,5},{7,4},{8,11},{9,10},{10,... | collective-permute-start | bytes 3080 | tf_op jit(solution)/shard_map/ppermute | solution.py:19
  43.0 1.8 %collective-permute-start.17 = (f32[256]{0:T(256)S(1)}, f32[256]{0:T(256)S(1)}, u32[]{:S(2)}, u32[]{:S(2)}) collective-permute-start(f32[256]{0:T(256)S(1)} %add.148), channel_id=1, source_target_pairs={{0,1},{1,0},{2,3},{3,2},{4,5},{5,4},{6,7},{7,6},{8,9},{9,8},{10,11... | collective-permute-start | bytes 3080 | tf_op jit(solution)/shard_map/ppermute | solution.py:19
  45.7 1.7 %collective-permute-done.16 = f32[256]{0:T(256)S(1)} collective-permute-done((f32[256]{0:T(256)S(1)}, f32[256]{0:T(256)S(1)}, u32[]{:S(2)}, u32[]{:S(2)}) %collective-permute-start.16) | collective-permute-done | bytes 1056 | tf_op jit(solution)/shard_map/ppermute | solution.py:19
  53.3 1.5 %collective-permute-start.23 = (bf16[512,256]{1,0:T(8,128)(2,1)S(1)}, bf16[512,256]{1,0:T(8,128)(2,1)S(1)}, u32[]{:S(2)}, u32[]{:S(2)}) collective-permute-start(bf16[512,256]{1,0:T(8,128)(2,1)S(1)} %get-tuple-element.105), channel_id=1, source_target_pairs={{0,8},{4,12},{8,0},{12,4},{1,9},{5,13},{9,1},{13,5},{2,10},{6,14},... | collective-permute-start | bytes 786440 | tf_op jit(solution)/shard_map/ppermute | solution.py:19
  54.8 1.5 collective-permute-start.22
  56.3 3.3 %collective-permute-done.24 = bf16[512,256]{1,0:T(8,128)(2,1)S(1)} collective-permute-done((bf16[512,256]{1,0:T(8,128)(2,1)S(1)}, bf16[512,256]{1,0:T(8,128)(2,1)S(1)}, u32[]{:S(2)}, u32[]{:S(2)}) %collective-permute-start.24) | collective-permute-done | bytes 262176 | tf_op jit(solution)/shard_map/ppermute | solution.py:19
  60.1 1.6 %collective-permute-start.25 = (bf16[256,256]{1,0:T(8,128)(2,1)S(1)}, bf16[256,256]{1,0:T(8,128)(2,1)S(1)}, u32[]{:S(2)}, u32[]{:S(2)}) collective-permute-start(bf16[256,256]{1,0:T(8,128)(2,1)S(1)} %add_convert_fusion.9), channel_id=1, source_target_pairs={{0,12},{4,8},{8,4},{12,0},{1,13},{5,9},{9,5},{13,1},{2,14},{6,10},... | collective-permute-start | bytes 393224 | tf_op jit(solution)/shard_map/ppermute | solution.py:19
  62.8 2.7 %collective-permute-done.23 = bf16[512,256]{1,0:T(8,128)(2,1)S(1)} collective-permute-done((bf16[512,256]{1,0:T(8,128)(2,1)S(1)}, bf16[512,256]{1,0:T(8,128)(2,1)S(1)}, u32[]{:S(2)}, u32[]{:S(2)}) %collective-permute-start.23) | collective-permute-done | bytes 262176 | tf_op jit(solution)/shard_map/ppermute | solution.py:19
  66.7 1.9 %collective-permute-done.25 = bf16[256,256]{1,0:T(8,128)(2,1)S(1)} collective-permute-done((bf16[256,256]{1,0:T(8,128)(2,1)S(1)}, bf16[256,256]{1,0:T(8,128)(2,1)S(1)}, u32[]{:S(2)}, u32[]{:S(2)}) %collective-permute-start.25) | collective-permute-done | bytes 131104 | tf_op jit(solution)/shard_map/ppermute | solution.py:19
  68.7 1.2 collective-permute-start.29
  69.9 2.1 %collective-permute-start.31 = (bf16[256,256]{1,0:T(8,128)(2,1)S(1)}, bf16[256,256]{1,0:T(8,128)(2,1)S(1)}, u32[]{:S(2)}, u32[]{:S(2)}) collective-permute-start(bf16[256,256]{1,0:T(8,128)(2,1)S(1)} %add_convert_fusion.5), channel_id=1, source_target_pairs={{0,1},{1,0},{2,3},{3,2},{4,5},{5,4},{6,7},{7,6},{8,9},{9,8},{10,11... | collective-permute-start | bytes 393224 | tf_op jit(solution)/shard_map/ppermute | solution.py:19
  72.0 4.0 %collective-permute-done.29 = bf16[256,256]{1,0:T(8,128)(2,1)S(1)} collective-permute-done((bf16[256,256]{1,0:T(8,128)(2,1)S(1)}, bf16[256,256]{1,0:T(8,128)(2,1)S(1)}, u32[]{:S(2)}, u32[]{:S(2)}) %collective-permute-start.29) | collective-permute-done | bytes 131104 | tf_op jit(solution)/shard_map/ppermute | solution.py:19
  76.3 1.8 %collective-permute-start.35 = (bf16[256,256]{1,0:T(8,128)(2,1)S(1)}, bf16[256,256]{1,0:T(8,128)(2,1)S(1)}, u32[]{:S(2)}, u32[]{:S(2)}) collective-permute-start(bf16[256,256]{1,0:T(8,128)(2,1)S(1)} %get-tuple-element.70), channel_id=1, source_target_pairs={{0,1},{1,0},{2,3},{3,2},{4,5},{5,4},{6,7},{7,6},{8,9},{9,8},{10,11... | collective-permute-start | bytes 393224 | tf_op jit(solution)/shard_map/ppermute | solution.py:19
  78.0 3.3 %collective-permute-start.36 = (bf16[256,256]{1,0:T(8,128)(2,1)S(1)}, bf16[256,256]{1,0:T(8,128)(2,1)S(1)}, u32[]{:S(2)}, u32[]{:S(2)}) collective-permute-start(bf16[256,256]{1,0:T(8,128)(2,1)S(1)} %get-tuple-element.70), channel_id=1, source_target_pairs={{0,2},{1,3},{2,0},{3,1},{4,6},{5,7},{6,4},{7,5},{8,10},{9,11},{10,... | collective-permute-start | bytes 393224 | tf_op jit(solution)/shard_map/ppermute | solution.py:19
  81.3 3.5 %collective-permute-start.34 = (bf16[256,256]{1,0:T(8,128)(2,1)S(1)}, bf16[256,256]{1,0:T(8,128)(2,1)S(1)}, u32[]{:S(2)}, u32[]{:S(2)}) collective-permute-start(bf16[256,256]{1,0:T(8,128)(2,1)S(1)} %get-tuple-element.70), channel_id=1, source_target_pairs={{0,12},{4,8},{8,4},{12,0},{1,13},{5,9},{9,5},{13,1},{2,14},{6,10},... | collective-permute-start | bytes 393224 | tf_op jit(solution)/shard_map/ppermute | solution.py:19
  84.8 2.3 %collective-permute-start.37 = (bf16[256,256]{1,0:T(8,128)(2,1)S(1)}, bf16[256,256]{1,0:T(8,128)(2,1)S(1)}, u32[]{:S(2)}, u32[]{:S(2)}) collective-permute-start(bf16[256,256]{1,0:T(8,128)(2,1)S(1)} %collective-permute-done.36), channel_id=1, source_target_pairs={{0,1},{1,0},{2,3},{3,2},{4,5},{5,4},{6,7},{7,6},{8,9},{9,8},{10,11... | collective-permute-start | bytes 393224 | tf_op jit(solution)/shard_map/ppermute | solution.py:19
  88.6 1.9 %collective-permute-done.33 = bf16[256,256]{1,0:T(8,128)(2,1)S(1)} collective-permute-done((bf16[256,256]{1,0:T(8,128)(2,1)S(1)}, bf16[256,256]{1,0:T(8,128)(2,1)S(1)}, u32[]{:S(2)}, u32[]{:S(2)}) %collective-permute-start.33) | collective-permute-done | bytes 131104 | tf_op jit(solution)/shard_map/ppermute | solution.py:19
  90.5 1.4 collective-permute-start.38
  92.0 1.7 %fusion.31 = f32[768,256]{1,0:T(8,128)} fusion(bf16[768,1536]{1,0:T(8,128)(2,1)S(1)} %get-tuple-element.47, bf16[1536,256]{1,0:T(8,128)(2,1)S(1)} %constant_dynamic-update-slice_fusion.14), kind=kOutput, calls=%fused_computation.97 | convolution fusion | flops 603979776 | bytes 3932160 | tf_op jit(solution)/shard_map/dot_general | solution.py:193
  93.7 2.7 %collective-permute-done.38 = bf16[256,256]{1,0:T(8,128)(2,1)S(1)} collective-permute-done((bf16[256,256]{1,0:T(8,128)(2,1)S(1)}, bf16[256,256]{1,0:T(8,128)(2,1)S(1)}, u32[]{:S(2)}, u32[]{:S(2)}) %collective-permute-start.38) | collective-permute-done | bytes 131104 | tf_op jit(solution)/shard_map/ppermute | solution.py:19
  97.1 1.4 copy.4
  99.6 1.8 %collective-permute-start.42 = (bf16[256,256]{1,0:T(8,128)(2,1)}, bf16[256,256]{1,0:T(8,128)(2,1)S(1)}, u32[]{:S(2)}, u32[]{:S(2)}) collective-permute-start(bf16[256,256]{1,0:T(8,128)(2,1)} %copy-done.5), channel_id=1, source_target_pairs={{0,4},{4,0},{8,12},{12,8},{1,5},{5,1},{9,13},{13,9},{2,6},{6,2},{1... | collective-permute-start | bytes 393224 | tf_op jit(solution)/shard_map/ppermute | solution.py:19
  105.4 1.3 collective-permute-done.43
  108.4 2.0 %collective-permute-start.45 = (f32[256]{0:T(256)S(1)}, f32[256]{0:T(256)S(1)}, u32[]{:S(2)}, u32[]{:S(2)}) collective-permute-start(f32[256]{0:T(256)S(1)} %get-tuple-element.98), channel_id=1, source_target_pairs={{0,8},{4,12},{8,0},{12,4},{1,9},{5,13},{9,1},{13,5},{2,10},{6,14},... | collective-permute-start | bytes 3080 | tf_op jit(solution)/shard_map/ppermute | solution.py:19
  112.0 1.9 %collective-permute-done.46 = f32[256]{0:T(256)S(1)} collective-permute-done((f32[256]{0:T(256)S(1)}, f32[256]{0:T(256)S(1)}, u32[]{:S(2)}, u32[]{:S(2)}) %collective-permute-start.46) | collective-permute-done | bytes 1056 | tf_op jit(solution)/shard_map/ppermute | solution.py:19
  114.0 2.0 %collective-permute-start.47 = (f32[256]{0:T(256)S(1)}, f32[256]{0:T(256)S(1)}, u32[]{:S(2)}, u32[]{:S(2)}) collective-permute-start(f32[256]{0:T(256)S(1)} %add.172), channel_id=1, source_target_pairs={{0,3},{1,2},{2,1},{3,0},{4,7},{5,6},{6,5},{7,4},{8,11},{9,10},{10,... | collective-permute-start | bytes 3080 | tf_op jit(solution)/shard_map/ppermute | solution.py:19
  116.5 1.8 %collective-permute-start.49 = (f32[256]{0:T(256)S(1)}, f32[256]{0:T(256)S(1)}, u32[]{:S(2)}, u32[]{:S(2)}) collective-permute-start(f32[256]{0:T(256)S(1)} %add.172), channel_id=1, source_target_pairs={{0,1},{1,0},{2,3},{3,2},{4,5},{5,4},{6,7},{7,6},{8,9},{9,8},{10,11... | collective-permute-start | bytes 3080 | tf_op jit(solution)/shard_map/ppermute | solution.py:19
  124.5 1.6 %collective-permute-start.58 = (bf16[256,256]{1,0:T(8,128)(2,1)S(1)}, bf16[256,256]{1,0:T(8,128)(2,1)S(1)}, u32[]{:S(2)}, u32[]{:S(2)}) collective-permute-start(bf16[256,256]{1,0:T(8,128)(2,1)S(1)} %get-tuple-element.108), channel_id=1, source_target_pairs={{0,4},{4,0},{8,12},{12,8},{1,5},{5,1},{9,13},{13,9},{2,6},{6,2},{1... | collective-permute-start | bytes 393224 | tf_op jit(solution)/shard_map/ppermute | solution.py:19
  127.9 1.4 collective-permute-start.54
  130.3 3.8 %collective-permute-done.56 = bf16[512,256]{1,0:T(8,128)(2,1)S(1)} collective-permute-done((bf16[512,256]{1,0:T(8,128)(2,1)S(1)}, bf16[512,256]{1,0:T(8,128)(2,1)S(1)}, u32[]{:S(2)}, u32[]{:S(2)}) %collective-permute-start.56) | collective-permute-done | bytes 262176 | tf_op jit(solution)/shard_map/ppermute | solution.py:19
  137.3 1.6 %collective-permute-start.52 = (bf16[256,256]{1,0:T(8,128)(2,1)S(1)}, bf16[256,256]{1,0:T(8,128)(2,1)S(1)}, u32[]{:S(2)}, u32[]{:S(2)}) collective-permute-start(bf16[256,256]{1,0:T(8,128)(2,1)S(1)} %get-tuple-element.95), channel_id=1, source_target_pairs={{0,4},{4,0},{8,12},{12,8},{1,5},{5,1},{9,13},{13,9},{2,6},{6,2},{1... | collective-permute-start | bytes 393224 | tf_op jit(solution)/shard_map/ppermute | solution.py:19
  138.9 1.6 %collective-permute-start.62 = (bf16[256,256]{1,0:T(8,128)(2,1)S(1)}, bf16[256,256]{1,0:T(8,128)(2,1)S(1)}, u32[]{:S(2)}, u32[]{:S(2)}) collective-permute-start(bf16[256,256]{1,0:T(8,128)(2,1)S(1)} %add_convert_fusion.1), channel_id=1, source_target_pairs={{0,12},{4,8},{8,4},{12,0},{1,13},{5,9},{9,5},{13,1},{2,14},{6,10},... | collective-permute-start | bytes 393224 | tf_op jit(solution)/shard_map/ppermute | solution.py:19
  142.2 1.5 %collective-permute-start.61 = (bf16[256,256]{1,0:T(8,128)(2,1)S(1)}, bf16[256,256]{1,0:T(8,128)(2,1)S(1)}, u32[]{:S(2)}, u32[]{:S(2)}) collective-permute-start(bf16[256,256]{1,0:T(8,128)(2,1)S(1)} %add_convert_fusion.2), channel_id=1, source_target_pairs={{0,2},{1,3},{2,0},{3,1},{4,6},{5,7},{6,4},{7,5},{8,10},{9,11},{10,... | collective-permute-start | bytes 393224 | tf_op jit(solution)/shard_map/ppermute | solution.py:19
  144.1 5.5 %collective-permute-done.61 = bf16[256,256]{1,0:T(8,128)(2,1)S(1)} collective-permute-done((bf16[256,256]{1,0:T(8,128)(2,1)S(1)}, bf16[256,256]{1,0:T(8,128)(2,1)S(1)}, u32[]{:S(2)}, u32[]{:S(2)}) %collective-permute-start.61) | collective-permute-done | bytes 131104 | tf_op jit(solution)/shard_map/ppermute | solution.py:19
  (183 shorter events, 44.6 us)
Async XLA Ops:
  1.6 9.2 %collective-permute-start.3 = (bf16[256,256]{1,0:T(8,128)(2,1)S(1)}, bf16[256,256]{1,0:T(8,128)(2,1)S(1)}, u32[]{:S(2)}, u32[]{:S(2)}) collective-permute-start(bf16[256,256]{1,0:T(8,128)(2,1)S(1)} %bitcast_convert_fusion), channel_id=1, source_target_pairs={{0,1},{1,0},{2,3},{3,2},{4,5},{5,4},{6,7},{7,6},{8,9},{9,8},{10,11... | collective-permute-start | bytes 393224 | tf_op jit(solution)/shard_map/ppermute | solution.py:19
  4.7 8.7 %collective-permute-start.4 = (bf16[256,256]{1,0:T(8,128)(2,1)S(1)}, bf16[256,256]{1,0:T(8,128)(2,1)S(1)}, u32[]{:S(2)}, u32[]{:S(2)}) collective-permute-start(bf16[256,256]{1,0:T(8,128)(2,1)S(1)} %bitcast_convert_fusion), channel_id=1, source_target_pairs={{0,2},{1,3},{2,0},{3,1},{4,6},{5,7},{6,4},{7,5},{8,10},{9,11},{10,... | collective-permute-start | bytes 393224 | tf_op jit(solution)/shard_map/ppermute | solution.py:19
  7.3 8.2 %collective-permute-start = (bf16[256,256]{1,0:T(8,128)(2,1)S(1)}, bf16[256,256]{1,0:T(8,128)(2,1)S(1)}, u32[]{:S(2)}, u32[]{:S(2)}) collective-permute-start(bf16[256,256]{1,0:T(8,128)(2,1)S(1)} %bitcast_convert_fusion), channel_id=1, source_target_pairs={{0,4},{4,0},{8,12},{12,8},{1,5},{5,1},{9,13},{13,9},{2,6},{6,2},{1... | collective-permute-start | bytes 393224 | tf_op jit(solution)/shard_map/ppermute | solution.py:19
  8.8 11.2 %collective-permute-start.1 = (bf16[256,256]{1,0:T(8,128)(2,1)S(1)}, bf16[256,256]{1,0:T(8,128)(2,1)S(1)}, u32[]{:S(2)}, u32[]{:S(2)}) collective-permute-start(bf16[256,256]{1,0:T(8,128)(2,1)S(1)} %bitcast_convert_fusion), channel_id=1, source_target_pairs={{0,8},{4,12},{8,0},{12,4},{1,9},{5,13},{9,1},{13,5},{2,10},{6,14},... | collective-permute-start | bytes 393224 | tf_op jit(solution)/shard_map/ppermute | solution.py:19
  10.3 10.3 %collective-permute-start.2 = (bf16[256,256]{1,0:T(8,128)(2,1)S(1)}, bf16[256,256]{1,0:T(8,128)(2,1)S(1)}, u32[]{:S(2)}, u32[]{:S(2)}) collective-permute-start(bf16[256,256]{1,0:T(8,128)(2,1)S(1)} %bitcast_convert_fusion), channel_id=1, source_target_pairs={{0,12},{4,8},{8,4},{12,0},{1,13},{5,9},{9,5},{13,1},{2,14},{6,10},... | collective-permute-start | bytes 393224 | tf_op jit(solution)/shard_map/ppermute | solution.py:19
  13.4 7.1 %collective-permute-start.5 = (bf16[256,256]{1,0:T(8,128)(2,1)S(1)}, bf16[256,256]{1,0:T(8,128)(2,1)S(1)}, u32[]{:S(2)}, u32[]{:S(2)}) collective-permute-start(bf16[256,256]{1,0:T(8,128)(2,1)S(1)} %collective-permute-done.4), channel_id=1, source_target_pairs={{0,1},{1,0},{2,3},{3,2},{4,5},{5,4},{6,7},{7,6},{8,9},{9,8},{10,11... | collective-permute-start | bytes 393224 | tf_op jit(solution)/shard_map/ppermute | solution.py:19
  13.9 14.8 %collective-permute-start.7 = (bf16[512,256]{1,0:T(8,128)(2,1)S(1)}, bf16[512,256]{1,0:T(8,128)(2,1)S(1)}, u32[]{:S(2)}, u32[]{:S(2)}) collective-permute-start(bf16[512,256]{1,0:T(8,128)(2,1)S(1)} %constant_dynamic-update-slice_fusion.6), channel_id=1, source_target_pairs={{0,4},{4,0},{8,12},{12,8},{1,5},{5,1},{9,13},{13,9},{2,6},{6,2},{1... | collective-permute-start | bytes 786440 | tf_op jit(solution)/shard_map/ppermute | solution.py:19
  15.4 13.2 %collective-permute-start.8 = (bf16[512,256]{1,0:T(8,128)(2,1)S(1)}, bf16[512,256]{1,0:T(8,128)(2,1)S(1)}, u32[]{:S(2)}, u32[]{:S(2)}) collective-permute-start(bf16[512,256]{1,0:T(8,128)(2,1)S(1)} %constant_dynamic-update-slice_fusion.6), channel_id=1, source_target_pairs={{0,8},{4,12},{8,0},{12,4},{1,9},{5,13},{9,1},{13,5},{2,10},{6,14},... | collective-permute-start | bytes 786440 | tf_op jit(solution)/shard_map/ppermute | solution.py:19
  20.0 5.9 %collective-permute-start.6 = (bf16[256,256]{1,0:T(8,128)(2,1)S(1)}, bf16[256,256]{1,0:T(8,128)(2,1)S(1)}, u32[]{:S(2)}, u32[]{:S(2)}) collective-permute-start(bf16[256,256]{1,0:T(8,128)(2,1)S(1)} %collective-permute-done.4), channel_id=1, source_target_pairs={{0,12},{4,8},{8,4},{12,0},{1,13},{5,9},{9,5},{13,1},{2,14},{6,10},... | collective-permute-start | bytes 393224 | tf_op jit(solution)/shard_map/ppermute | solution.py:19
  25.9 6.4 %collective-permute-start.9 = (bf16[512,256]{1,0:T(8,128)(2,1)S(1)}, bf16[512,256]{1,0:T(8,128)(2,1)S(1)}, u32[]{:S(2)}, u32[]{:S(2)}) collective-permute-start(bf16[512,256]{1,0:T(8,128)(2,1)S(1)} %pad_maximum_fusion), channel_id=1, source_target_pairs={{0,1},{1,0},{2,3},{3,2},{4,5},{5,4},{6,7},{7,6},{8,9},{9,8},{10,11... | collective-permute-start | bytes 786440 | tf_op jit(solution)/shard_map/ppermute | solution.py:19
  33.7 15.0 %collective-permute-start.18 = (bf16[768,256]{1,0:T(8,128)(2,1)S(1)}, bf16[768,256]{1,0:T(8,128)(2,1)S(1)}, u32[]{:S(2)}, u32[]{:S(2)}) collective-permute-start(bf16[768,256]{1,0:T(8,128)(2,1)S(1)} %get-tuple-element.107), channel_id=1, source_target_pairs={{0,16},{16,0},{1,17},{17,1},{2,18},{18,2},{3,19},{19,3},{4,20},{20... | collective-permute-start | bytes 1179656 | tf_op jit(solution)/shard_map/ppermute | solution.py:19
  40.4 5.4 %collective-permute-start.15 = (f32[256]{0:T(256)S(1)}, f32[256]{0:T(256)S(1)}, u32[]{:S(2)}, u32[]{:S(2)}) collective-permute-start(f32[256]{0:T(256)S(1)} %add.148), channel_id=1, source_target_pairs={{0,3},{1,2},{2,1},{3,0},{4,7},{5,6},{6,5},{7,4},{8,11},{9,10},{10,... | collective-permute-start | bytes 3080 | tf_op jit(solution)/shard_map/ppermute | solution.py:19
  51.2 8.5 %collective-permute-start.24 = (bf16[512,256]{1,0:T(8,128)(2,1)S(1)}, bf16[512,256]{1,0:T(8,128)(2,1)S(1)}, u32[]{:S(2)}, u32[]{:S(2)}) collective-permute-start(bf16[512,256]{1,0:T(8,128)(2,1)S(1)} %concatenate.68), channel_id=1, source_target_pairs={{0,1},{1,0},{2,3},{3,2},{4,5},{5,4},{6,7},{7,6},{8,9},{9,8},{10,11... | collective-permute-start | bytes 786440 | tf_op jit(solution)/shard_map/ppermute | solution.py:19
  52.2 7.9 %collective-permute-start.27 = (bf16[256,256]{1,0:T(8,128)(2,1)S(1)}, bf16[256,256]{1,0:T(8,128)(2,1)S(1)}, u32[]{:S(2)}, u32[]{:S(2)}) collective-permute-start(bf16[256,256]{1,0:T(8,128)(2,1)S(1)} %get-tuple-element.111), channel_id=1, source_target_pairs={{0,8},{4,12},{8,0},{12,4},{1,9},{5,13},{9,1},{13,5},{2,10},{6,14},... | collective-permute-start | bytes 393224 | tf_op jit(solution)/shard_map/ppermute | solution.py:19
  52.8 8.9 %collective-permute-start.26 = (bf16[256,256]{1,0:T(8,128)(2,1)S(1)}, bf16[256,256]{1,0:T(8,128)(2,1)S(1)}, u32[]{:S(2)}, u32[]{:S(2)}) collective-permute-start(bf16[256,256]{1,0:T(8,128)(2,1)S(1)} %get-tuple-element.110), channel_id=1, source_target_pairs={{0,4},{4,0},{8,12},{12,8},{1,5},{5,1},{9,13},{13,9},{2,6},{6,2},{1... | collective-permute-start | bytes 393224 | tf_op jit(solution)/shard_map/ppermute | solution.py:19
  53.3 12.2 %collective-permute-start.23 = (bf16[512,256]{1,0:T(8,128)(2,1)S(1)}, bf16[512,256]{1,0:T(8,128)(2,1)S(1)}, u32[]{:S(2)}, u32[]{:S(2)}) collective-permute-start(bf16[512,256]{1,0:T(8,128)(2,1)S(1)} %get-tuple-element.105), channel_id=1, source_target_pairs={{0,8},{4,12},{8,0},{12,4},{1,9},{5,13},{9,1},{13,5},{2,10},{6,14},... | collective-permute-start | bytes 786440 | tf_op jit(solution)/shard_map/ppermute | solution.py:19
  54.8 11.2 %collective-permute-start.22 = (bf16[512,256]{1,0:T(8,128)(2,1)S(1)}, bf16[512,256]{1,0:T(8,128)(2,1)S(1)}, u32[]{:S(2)}, u32[]{:S(2)}) collective-permute-start(bf16[512,256]{1,0:T(8,128)(2,1)S(1)} %get-tuple-element.104), channel_id=1, source_target_pairs={{0,4},{4,0},{8,12},{12,8},{1,5},{5,1},{9,13},{13,9},{2,6},{6,2},{1... | collective-permute-start | bytes 786440 | tf_op jit(solution)/shard_map/ppermute | solution.py:19
  59.6 12.4 %collective-permute-start.21 = (bf16[256,256]{1,0:T(8,128)(2,1)S(1)}, bf16[256,256]{1,0:T(8,128)(2,1)S(1)}, u32[]{:S(2)}, u32[]{:S(2)}) collective-permute-start(bf16[256,256]{1,0:T(8,128)(2,1)S(1)} %get-tuple-element.102), channel_id=1, source_target_pairs={{0,8},{4,12},{8,0},{12,4},{1,9},{5,13},{9,1},{13,5},{2,10},{6,14},... | collective-permute-start | bytes 393224 | tf_op jit(solution)/shard_map/ppermute | solution.py:19
  60.1 8.5 %collective-permute-start.25 = (bf16[256,256]{1,0:T(8,128)(2,1)S(1)}, bf16[256,256]{1,0:T(8,128)(2,1)S(1)}, u32[]{:S(2)}, u32[]{:S(2)}) collective-permute-start(bf16[256,256]{1,0:T(8,128)(2,1)S(1)} %add_convert_fusion.9), channel_id=1, source_target_pairs={{0,12},{4,8},{8,4},{12,0},{1,13},{5,9},{9,5},{13,1},{2,14},{6,10},... | collective-permute-start | bytes 393224 | tf_op jit(solution)/shard_map/ppermute | solution.py:19
  65.5 6.5 %collective-permute-start.20 = (bf16[256,256]{1,0:T(8,128)(2,1)S(1)}, bf16[256,256]{1,0:T(8,128)(2,1)S(1)}, u32[]{:S(2)}, u32[]{:S(2)}) collective-permute-start(bf16[256,256]{1,0:T(8,128)(2,1)S(1)} %get-tuple-element.103), channel_id=1, source_target_pairs={{0,4},{4,0},{8,12},{12,8},{1,5},{5,1},{9,13},{13,9},{2,6},{6,2},{1... | collective-permute-start | bytes 393224 | tf_op jit(solution)/shard_map/ppermute | solution.py:19
  66.0 10.1 %collective-permute-start.30 = (bf16[256,256]{1,0:T(8,128)(2,1)S(1)}, bf16[256,256]{1,0:T(8,128)(2,1)S(1)}, u32[]{:S(2)}, u32[]{:S(2)}) collective-permute-start(bf16[256,256]{1,0:T(8,128)(2,1)S(1)} %add_convert_fusion.6), channel_id=1, source_target_pairs={{0,12},{4,8},{8,4},{12,0},{1,13},{5,9},{9,5},{13,1},{2,14},{6,10},... | collective-permute-start | bytes 393224 | tf_op jit(solution)/shard_map/ppermute | solution.py:19
  68.7 7.4 %collective-permute-start.29 = (bf16[256,256]{1,0:T(8,128)(2,1)S(1)}, bf16[256,256]{1,0:T(8,128)(2,1)S(1)}, u32[]{:S(2)}, u32[]{:S(2)}) collective-permute-start(bf16[256,256]{1,0:T(8,128)(2,1)S(1)} %add_convert_fusion.7), channel_id=1, source_target_pairs={{0,2},{1,3},{2,0},{3,1},{4,6},{5,7},{6,4},{7,5},{8,10},{9,11},{10,... | collective-permute-start | bytes 393224 | tf_op jit(solution)/shard_map/ppermute | solution.py:19
  69.9 6.2 %collective-permute-start.31 = (bf16[256,256]{1,0:T(8,128)(2,1)S(1)}, bf16[256,256]{1,0:T(8,128)(2,1)S(1)}, u32[]{:S(2)}, u32[]{:S(2)}) collective-permute-start(bf16[256,256]{1,0:T(8,128)(2,1)S(1)} %add_convert_fusion.5), channel_id=1, source_target_pairs={{0,1},{1,0},{2,3},{3,2},{4,5},{5,4},{6,7},{7,6},{8,9},{9,8},{10,11... | collective-permute-start | bytes 393224 | tf_op jit(solution)/shard_map/ppermute | solution.py:19
  76.3 8.6 %collective-permute-start.35 = (bf16[256,256]{1,0:T(8,128)(2,1)S(1)}, bf16[256,256]{1,0:T(8,128)(2,1)S(1)}, u32[]{:S(2)}, u32[]{:S(2)}) collective-permute-start(bf16[256,256]{1,0:T(8,128)(2,1)S(1)} %get-tuple-element.70), channel_id=1, source_target_pairs={{0,1},{1,0},{2,3},{3,2},{4,5},{5,4},{6,7},{7,6},{8,9},{9,8},{10,11... | collective-permute-start | bytes 393224 | tf_op jit(solution)/shard_map/ppermute | solution.py:19
  78.0 6.8 %collective-permute-start.36 = (bf16[256,256]{1,0:T(8,128)(2,1)S(1)}, bf16[256,256]{1,0:T(8,128)(2,1)S(1)}, u32[]{:S(2)}, u32[]{:S(2)}) collective-permute-start(bf16[256,256]{1,0:T(8,128)(2,1)S(1)} %get-tuple-element.70), channel_id=1, source_target_pairs={{0,2},{1,3},{2,0},{3,1},{4,6},{5,7},{6,4},{7,5},{8,10},{9,11},{10,... | collective-permute-start | bytes 393224 | tf_op jit(solution)/shard_map/ppermute | solution.py:19
  81.3 7.1 %collective-permute-start.32 = (bf16[256,256]{1,0:T(8,128)(2,1)S(1)}, bf16[256,256]{1,0:T(8,128)(2,1)S(1)}, u32[]{:S(2)}, u32[]{:S(2)}) collective-permute-start(bf16[256,256]{1,0:T(8,128)(2,1)S(1)} %get-tuple-element.70), channel_id=1, source_target_pairs={{0,4},{4,0},{8,12},{12,8},{1,5},{5,1},{9,13},{13,9},{2,6},{6,2},{1... | collective-permute-start | bytes 393224 | tf_op jit(solution)/shard_map/ppermute | solution.py:19
  81.3 9.2 %collective-permute-start.33 = (bf16[256,256]{1,0:T(8,128)(2,1)S(1)}, bf16[256,256]{1,0:T(8,128)(2,1)S(1)}, u32[]{:S(2)}, u32[]{:S(2)}) collective-permute-start(bf16[256,256]{1,0:T(8,128)(2,1)S(1)} %get-tuple-element.70), channel_id=1, source_target_pairs={{0,8},{4,12},{8,0},{12,4},{1,9},{5,13},{9,1},{13,5},{2,10},{6,14},... | collective-permute-start | bytes 393224 | tf_op jit(solution)/shard_map/ppermute | solution.py:19
  81.3 10.6 %collective-permute-start.34 = (bf16[256,256]{1,0:T(8,128)(2,1)S(1)}, bf16[256,256]{1,0:T(8,128)(2,1)S(1)}, u32[]{:S(2)}, u32[]{:S(2)}) collective-permute-start(bf16[256,256]{1,0:T(8,128)(2,1)S(1)} %get-tuple-element.70), channel_id=1, source_target_pairs={{0,12},{4,8},{8,4},{12,0},{1,13},{5,9},{9,5},{13,1},{2,14},{6,10},... | collective-permute-start | bytes 393224 | tf_op jit(solution)/shard_map/ppermute | solution.py:19
  84.8 7.1 %collective-permute-start.37 = (bf16[256,256]{1,0:T(8,128)(2,1)S(1)}, bf16[256,256]{1,0:T(8,128)(2,1)S(1)}, u32[]{:S(2)}, u32[]{:S(2)}) collective-permute-start(bf16[256,256]{1,0:T(8,128)(2,1)S(1)} %collective-permute-done.36), channel_id=1, source_target_pairs={{0,1},{1,0},{2,3},{3,2},{4,5},{5,4},{6,7},{7,6},{8,9},{9,8},{10,11... | collective-permute-start | bytes 393224 | tf_op jit(solution)/shard_map/ppermute | solution.py:19
  88.4 13.1 %collective-permute-start.39 = (bf16[512,256]{1,0:T(8,128)(2,1)}, bf16[512,256]{1,0:T(8,128)(2,1)}, u32[]{:S(2)}, u32[]{:S(2)}) collective-permute-start(bf16[512,256]{1,0:T(8,128)(2,1)} %constant_dynamic-update-slice_fusion.20), channel_id=1, source_target_pairs={{0,4},{4,0},{8,12},{12,8},{1,5},{5,1},{9,13},{13,9},{2,6},{6,2},{1... | collective-permute-start | bytes 786440 | tf_op jit(solution)/shard_map/ppermute | solution.py:19
  88.4 14.1 %collective-permute-start.40 = (bf16[512,256]{1,0:T(8,128)(2,1)}, bf16[512,256]{1,0:T(8,128)(2,1)}, u32[]{:S(2)}, u32[]{:S(2)}) collective-permute-start(bf16[512,256]{1,0:T(8,128)(2,1)} %constant_dynamic-update-slice_fusion.20), channel_id=1, source_target_pairs={{0,8},{4,12},{8,0},{12,4},{1,9},{5,13},{9,1},{13,5},{2,10},{6,14},... | collective-permute-start | bytes 786440 | tf_op jit(solution)/shard_map/ppermute | solution.py:19
  90.5 5.9 %collective-permute-start.38 = (bf16[256,256]{1,0:T(8,128)(2,1)S(1)}, bf16[256,256]{1,0:T(8,128)(2,1)S(1)}, u32[]{:S(2)}, u32[]{:S(2)}) collective-permute-start(bf16[256,256]{1,0:T(8,128)(2,1)S(1)} %collective-permute-done.36), channel_id=1, source_target_pairs={{0,12},{4,8},{8,4},{12,0},{1,13},{5,9},{9,5},{13,1},{2,14},{6,10},... | collective-permute-start | bytes 393224 | tf_op jit(solution)/shard_map/ppermute | solution.py:19
  98.5 6.8 %collective-permute-start.41 = (bf16[512,256]{1,0:T(8,128)(2,1)}, bf16[512,256]{1,0:T(8,128)(2,1)S(1)}, u32[]{:S(2)}, u32[]{:S(2)}) collective-permute-start(bf16[512,256]{1,0:T(8,128)(2,1)} %pad_maximum_fusion.1), channel_id=1, source_target_pairs={{0,1},{1,0},{2,3},{3,2},{4,5},{5,4},{6,7},{7,6},{8,9},{9,8},{10,11... | collective-permute-start | bytes 786440 | tf_op jit(solution)/shard_map/ppermute | solution.py:19
  99.6 5.7 %collective-permute-start.42 = (bf16[256,256]{1,0:T(8,128)(2,1)}, bf16[256,256]{1,0:T(8,128)(2,1)S(1)}, u32[]{:S(2)}, u32[]{:S(2)}) collective-permute-start(bf16[256,256]{1,0:T(8,128)(2,1)} %copy-done.5), channel_id=1, source_target_pairs={{0,4},{4,0},{8,12},{12,8},{1,5},{5,1},{9,13},{13,9},{2,6},{6,2},{1... | collective-permute-start | bytes 393224 | tf_op jit(solution)/shard_map/ppermute | solution.py:19
  101.5 5.2 %collective-permute-start.43 = (bf16[256,256]{1,0:T(8,128)(2,1)}, bf16[256,256]{1,0:T(8,128)(2,1)S(1)}, u32[]{:S(2)}, u32[]{:S(2)}) collective-permute-start(bf16[256,256]{1,0:T(8,128)(2,1)} %copy-done.5), channel_id=1, source_target_pairs={{0,8},{4,12},{8,0},{12,4},{1,9},{5,13},{9,1},{13,5},{2,10},{6,14},... | collective-permute-start | bytes 393224 | tf_op jit(solution)/shard_map/ppermute | solution.py:19
  107.4 14.2 %collective-permute-start.50 = (bf16[768,256]{0,1:T(8,128)(2,1)S(1)}, bf16[768,256]{0,1:T(8,128)(2,1)S(1)}, u32[]{:S(2)}, u32[]{:S(2)}) collective-permute-start(bf16[768,256]{0,1:T(8,128)(2,1)S(1)} %get-tuple-element.99), channel_id=1, source_target_pairs={{0,16},{16,0},{1,17},{17,1},{2,18},{18,2},{3,19},{19,3},{4,20},{20... | collective-permute-start | bytes 1179656 | tf_op jit(solution)/shard_map/ppermute | solution.py:19
  114.0 5.4 %collective-permute-start.47 = (f32[256]{0:T(256)S(1)}, f32[256]{0:T(256)S(1)}, u32[]{:S(2)}, u32[]{:S(2)}) collective-permute-start(f32[256]{0:T(256)S(1)} %add.172), channel_id=1, source_target_pairs={{0,3},{1,2},{2,1},{3,0},{4,7},{5,6},{6,5},{7,4},{8,11},{9,10},{10,... | collective-permute-start | bytes 3080 | tf_op jit(solution)/shard_map/ppermute | solution.py:19
  123.7 11.2 %collective-permute-start.59 = (bf16[256,256]{1,0:T(8,128)(2,1)S(1)}, bf16[256,256]{1,0:T(8,128)(2,1)S(1)}, u32[]{:S(2)}, u32[]{:S(2)}) collective-permute-start(bf16[256,256]{1,0:T(8,128)(2,1)S(1)} %get-tuple-element.109), channel_id=1, source_target_pairs={{0,8},{4,12},{8,0},{12,4},{1,9},{5,13},{9,1},{13,5},{2,10},{6,14},... | collective-permute-start | bytes 393224 | tf_op jit(solution)/shard_map/ppermute | solution.py:19
  124.5 11.5 %collective-permute-start.58 = (bf16[256,256]{1,0:T(8,128)(2,1)S(1)}, bf16[256,256]{1,0:T(8,128)(2,1)S(1)}, u32[]{:S(2)}, u32[]{:S(2)}) collective-permute-start(bf16[256,256]{1,0:T(8,128)(2,1)S(1)} %get-tuple-element.108), channel_id=1, source_target_pairs={{0,4},{4,0},{8,12},{12,8},{1,5},{5,1},{9,13},{13,9},{2,6},{6,2},{1... | collective-permute-start | bytes 393224 | tf_op jit(solution)/shard_map/ppermute | solution.py:19
  126.1 7.9 %collective-permute-start.56 = (bf16[512,256]{1,0:T(8,128)(2,1)S(1)}, bf16[512,256]{1,0:T(8,128)(2,1)S(1)}, u32[]{:S(2)}, u32[]{:S(2)}) collective-permute-start(bf16[512,256]{1,0:T(8,128)(2,1)S(1)} %concatenate.71), channel_id=1, source_target_pairs={{0,1},{1,0},{2,3},{3,2},{4,5},{5,4},{6,7},{7,6},{8,9},{9,8},{10,11... | collective-permute-start | bytes 786440 | tf_op jit(solution)/shard_map/ppermute | solution.py:19
  127.1 10.2 %collective-permute-start.55 = (bf16[512,256]{1,0:T(8,128)(2,1)S(1)}, bf16[512,256]{1,0:T(8,128)(2,1)S(1)}, u32[]{:S(2)}, u32[]{:S(2)}) collective-permute-start(bf16[512,256]{1,0:T(8,128)(2,1)S(1)} %get-tuple-element.97), channel_id=1, source_target_pairs={{0,8},{4,12},{8,0},{12,4},{1,9},{5,13},{9,1},{13,5},{2,10},{6,14},... | collective-permute-start | bytes 786440 | tf_op jit(solution)/shard_map/ppermute | solution.py:19
  127.9 11.0 %collective-permute-start.54 = (bf16[512,256]{1,0:T(8,128)(2,1)S(1)}, bf16[512,256]{1,0:T(8,128)(2,1)S(1)}, u32[]{:S(2)}, u32[]{:S(2)}) collective-permute-start(bf16[512,256]{1,0:T(8,128)(2,1)S(1)} %get-tuple-element.96), channel_id=1, source_target_pairs={{0,4},{4,0},{8,12},{12,8},{1,5},{5,1},{9,13},{13,9},{2,6},{6,2},{1... | collective-permute-start | bytes 786440 | tf_op jit(solution)/shard_map/ppermute | solution.py:19
  134.1 10.0 %collective-permute-start.53 = (bf16[256,256]{1,0:T(8,128)(2,1)S(1)}, bf16[256,256]{1,0:T(8,128)(2,1)S(1)}, u32[]{:S(2)}, u32[]{:S(2)}) collective-permute-start(bf16[256,256]{1,0:T(8,128)(2,1)S(1)} %get-tuple-element.94), channel_id=1, source_target_pairs={{0,8},{4,12},{8,0},{12,4},{1,9},{5,13},{9,1},{13,5},{2,10},{6,14},... | collective-permute-start | bytes 393224 | tf_op jit(solution)/shard_map/ppermute | solution.py:19
  134.9 7.2 %collective-permute-start.57 = (bf16[256,256]{1,0:T(8,128)(2,1)S(1)}, bf16[256,256]{1,0:T(8,128)(2,1)S(1)}, u32[]{:S(2)}, u32[]{:S(2)}) collective-permute-start(bf16[256,256]{1,0:T(8,128)(2,1)S(1)} %add_convert_fusion.4), channel_id=1, source_target_pairs={{0,12},{4,8},{8,4},{12,0},{1,13},{5,9},{9,5},{13,1},{2,14},{6,10},... | collective-permute-start | bytes 393224 | tf_op jit(solution)/shard_map/ppermute | solution.py:19
  137.3 6.8 %collective-permute-start.52 = (bf16[256,256]{1,0:T(8,128)(2,1)S(1)}, bf16[256,256]{1,0:T(8,128)(2,1)S(1)}, u32[]{:S(2)}, u32[]{:S(2)}) collective-permute-start(bf16[256,256]{1,0:T(8,128)(2,1)S(1)} %get-tuple-element.95), channel_id=1, source_target_pairs={{0,4},{4,0},{8,12},{12,8},{1,5},{5,1},{9,13},{13,9},{2,6},{6,2},{1... | collective-permute-start | bytes 393224 | tf_op jit(solution)/shard_map/ppermute | solution.py:19
  138.9 10.8 %collective-permute-start.62 = (bf16[256,256]{1,0:T(8,128)(2,1)S(1)}, bf16[256,256]{1,0:T(8,128)(2,1)S(1)}, u32[]{:S(2)}, u32[]{:S(2)}) collective-permute-start(bf16[256,256]{1,0:T(8,128)(2,1)S(1)} %add_convert_fusion.1), channel_id=1, source_target_pairs={{0,12},{4,8},{8,4},{12,0},{1,13},{5,9},{9,5},{13,1},{2,14},{6,10},... | collective-permute-start | bytes 393224 | tf_op jit(solution)/shard_map/ppermute | solution.py:19
  142.2 7.4 %collective-permute-start.61 = (bf16[256,256]{1,0:T(8,128)(2,1)S(1)}, bf16[256,256]{1,0:T(8,128)(2,1)S(1)}, u32[]{:S(2)}, u32[]{:S(2)}) collective-permute-start(bf16[256,256]{1,0:T(8,128)(2,1)S(1)} %add_convert_fusion.2), channel_id=1, source_target_pairs={{0,2},{1,3},{2,0},{3,1},{4,6},{5,7},{6,4},{7,5},{8,10},{9,11},{10,... | collective-permute-start | bytes 393224 | tf_op jit(solution)/shard_map/ppermute | solution.py:19
  143.8 5.9 %collective-permute-start.63 = (bf16[256,256]{1,0:T(8,128)(2,1)S(1)}, bf16[256,256]{1,0:T(8,128)(2,1)S(1)}, u32[]{:S(2)}, u32[]{:S(2)}) collective-permute-start(bf16[256,256]{1,0:T(8,128)(2,1)S(1)} %add_convert_fusion), channel_id=1, source_target_pairs={{0,1},{1,0},{2,3},{3,2},{4,5},{5,4},{6,7},{7,6},{8,9},{9,8},{10,11... | collective-permute-start | bytes 393224 | tf_op jit(solution)/shard_map/ppermute | solution.py:19
  (22 other events, 199.5 us)

commit v8 on v6

--- a/solution.py
+++ b/solution.py
@@ -32,12 +32,12 @@
 
 
 def join(*blocks):
-    return jnp.concatenate(blocks, axis=0)
+    return jnp.concatenate(blocks, axis=1)
 
 
 def split(pair):
-    deep = pair.shape[0] // 2
-    return pair[:deep], pair[deep:]
+    deep = pair.shape[1] // 2
+    return pair[:, :deep], pair[:, deep:]
 
 
 ARRIVALS = (
@@ -156,12 +156,12 @@
 
 def scaled(proj, scaling):
     def kernel(proj_ref, scaling_ref, out_ref):
-        columns = proj_ref[...].astype(jnp.float32)
-        out_ref[...] = (columns.T * scaling_ref[...]).astype(out_ref.dtype)
+        columns = proj_ref[...].astype(jnp.float32).T
+        out_ref[...] = (columns * scaling_ref[...]).astype(out_ref.dtype)
 
     return pl.pallas_call(
         kernel,
-        out_shape=jax.ShapeDtypeStruct(proj.shape, proj.dtype),
+        out_shape=jax.ShapeDtypeStruct(proj.shape[::-1], proj.dtype),
         in_specs=[pl.BlockSpec(memory_space=pltpu.VMEM)] * 2,
         out_specs=pl.BlockSpec(memory_space=pltpu.VMEM),
         compiler_params=pltpu.CompilerParams(vmem_limit_bytes=8 << 20),
@@ -169,7 +169,7 @@
             flops=proj.size, bytes_accessed=4 * proj.size, transcendentals=0
         ),
         name="scaled",
-    )(proj.T, scaling[None])
+    )(proj, scaling[None])
 
 
 def on_device(views, weights):
@@ -183,38 +183,44 @@
     row_total = rows_here * rows * feats
     width_root = math.sqrt(width)
     groups = regroup(samples, depth)
+    dirs_t = own_rows.T
     for sweep in range(ITERS):
-        dirs = gather(own_rows.astype(jnp.bfloat16))
+        dirs = gather(dirs_t.astype(jnp.bfloat16))
         summed_proj = 0.0
         for g, places in enumerate(ARRIVALS):
             blocks = [dirs[p] for p in places]
             blocks = lax.optimization_barrier(blocks + [dirs[0, 3]])[: len(places)]
-            part = jnp.dot(
-                groups[g], join(*blocks), preferred_element_type=jnp.float32
+            part = lax.dot_general(
+                join(*blocks),
+                groups[g],
+                (((1,), (1,)), ((), ())),
+                preferred_element_type=jnp.float32,
             )
-            summed_proj = lax.optimization_barrier(summed_proj + part) if g < 2 else summed_proj + part
+            summed_proj = summed_proj + part
+            if g < len(ARRIVALS) - 1:
+                summed_proj = lax.optimization_barrier(summed_proj)
         kept_proj = lax.optimization_barrier(summed_proj.astype(jnp.bfloat16))
         partner_proj = xor_move(kept_proj, "view", 1).astype(jnp.float32)
-        squares = jnp.sum(summed_proj * summed_proj, axis=0)
+        squares = jnp.sum(summed_proj * summed_proj, axis=1)
         scaling = lax.rsqrt(total(squares) / row_total + epsilon)
         partner_scaling = xor_move(scaling, "view", 1)
-        own_proj = (kept_proj.astype(jnp.float32) * scaling).astype(jnp.bfloat16)
-        partner_proj = (partner_proj * partner_scaling).astype(jnp.bfloat16)
+        own_proj = (kept_proj.astype(jnp.float32) * scaling[:, None]).astype(jnp.bfloat16)
+        partner_proj = (partner_proj * partner_scaling[:, None]).astype(jnp.bfloat16)
         residue = (own_proj.astype(jnp.float32) - partner_proj.astype(jnp.float32)).astype(
             jnp.bfloat16
         )
         shares = {}
         for g in (2, 1, 0):
             share = lax.dot_general(
-                groups[g], residue, (((0,), (0,)), ((), ())), preferred_element_type=jnp.float32
+                residue, groups[g], (((1,), (0,)), ((), ())), preferred_element_type=jnp.float32
             )
             for i, place in enumerate(ARRIVALS[g]):
-                shares[place] = share[i * depth : (i + 1) * depth]
+                shares[place] = share[:, i * depth : (i + 1) * depth]
         if sweep == ITERS - 1:
             shown = scaled(kept_proj, scaling)
         grad = scatter(shares) / row_total
-        own_rows = width_root * (own_rows * scaling - step_rate * grad)
-    return (own_rows[None], shown[None])
+        dirs_t = width_root * (dirs_t * scaling[:, None] - step_rate * grad)
+    return (dirs_t.T[None], shown[None])
 
 
 def solution(mesh):

time: 137 us -> 143 us (1.044)
  waiting for transfers between devices: 44.7 us -> 47.8 us
  starting transfers between devices: 74.5 us -> 76.7 us
    ppermute x64, waiting for transfers between devices: 44.7 us -> 47.8 us  [xor_move(): return lax.ppermute(block, axis, [(i, i ^ mask) for i in range(count)])]
    ppermute x64, starting transfers between devices: 74.5 us -> 76.7 us  [xor_move(): return lax.ppermute(block, axis, [(i, i ^ mask) for i in range(count)])]
  transfers between devices with their start and end apart: 64 -> 64, of which waited for: 34 -> 36; matrix products, arithmetic and copies ran while one was open for 5% -> 6% of each run, Pallas kernels for 3% -> 3%
where the time goes in v8:
time: 143 us
  starting transfers between devices  76.7 us (54%)
  waiting for transfers between devices  47.8 us (33%)
  matrix products  9.38 us (7%)
  Pallas kernels  3.92 us (3%)
  local copies, waits for them, and re-layouts  2.51 us (2%)
    ppermute x64, starting transfers between devices, xor_move(): return lax.ppermute(block, axis, [(i, i ^ mask) for i in range(count)])  76.7 us
    ppermute x64, waiting for transfers between devices, xor_move(): return lax.ppermute(block, axis, [(i, i ^ mask) for i in range(count)])  47.8 us
    dot_general x6, matrix products, on_device(): lax.dot_general(residue, groups[g], (((1,), (0,)), ((), ())), preferred_e...  4.76 us
    dot_general x6, matrix products, on_device(): lax.dot_general(join(*blocks), groups[g], (((1,), (1,)), ((), ())), prefe...  4.62 us
    pallas_call x1, Pallas kernels, regroup(): pl.pallas_call(kernel, out_shape=[jax.ShapeDtypeStruct((rows_here, len(pl...  3 us
  transfers between devices with their start and end apart: 64, of which 36 were waited for; matrix products, arithmetic and copies ran while one was open for 6% of the time, Pallas kernels for 3%

profile of v8, /device:TPU:0, one launch (start us, length us, event | category | flops | bytes accessed | tf_op | source)
XLA Modules:
  0.0 142.5 jit_solution(13627342364695346972)
XLA Ops:
  1.7 4.1 %collective-permute-start.4 = (bf16[256,256]{1,0:T(8,128)(2,1)S(1)}, bf16[256,256]{1,0:T(8,128)(2,1)S(1)}, u32[]{:S(2)}, u32[]{:S(2)}) collective-permute-start(bf16[256,256]{1,0:T(8,128)(2,1)S(1)} %fusion.28), channel_id=1, source_target_pairs={{0,2},{1,3},{2,0},{3,1},{4,6},{5,7},{6,4},{7,5},{8,10},{9,11},{10,... | collective-permute-start | bytes 393224 | tf_op jit(solution)/shard_map/ppermute | solution.py:19
  5.8 1.6 %collective-permute-start.3 = (bf16[256,256]{1,0:T(8,128)(2,1)S(1)}, bf16[256,256]{1,0:T(8,128)(2,1)S(1)}, u32[]{:S(2)}, u32[]{:S(2)}) collective-permute-start(bf16[256,256]{1,0:T(8,128)(2,1)S(1)} %fusion.28), channel_id=1, source_target_pairs={{0,1},{1,0},{2,3},{3,2},{4,5},{5,4},{6,7},{7,6},{8,9},{9,8},{10,11... | collective-permute-start | bytes 393224 | tf_op jit(solution)/shard_map/ppermute | solution.py:19
  7.4 2.4 %collective-permute-start.2 = (bf16[256,256]{1,0:T(8,128)(2,1)S(1)}, bf16[256,256]{1,0:T(8,128)(2,1)S(1)}, u32[]{:S(2)}, u32[]{:S(2)}) collective-permute-start(bf16[256,256]{1,0:T(8,128)(2,1)S(1)} %fusion.28), channel_id=1, source_target_pairs={{0,12},{4,8},{8,4},{12,0},{1,13},{5,9},{9,5},{13,1},{2,14},{6,10},... | collective-permute-start | bytes 393224 | tf_op jit(solution)/shard_map/ppermute | solution.py:19
  10.9 3.0 %regroup.1 = (bf16[768,1536]{1,0:T(8,128)(2,1)S(1)}, bf16[768,1536]{1,0:T(8,128)(2,1)S(1)}, bf16[768,1024]{1,0:T(8,128)(2,1)S(1)}) custom-call(bf16[768,4096]{1,0:T(8,128)(2,1)} %bitcast.37), custom_call_target="tpu_custom_call" | custom-call | bytes 12582912 | tf_op jit(solution)/shard_map/regroup/pallas_call | solution.py:140
  14.5 1.6 %collective-permute-start.8 = (bf16[256,512]{1,0:T(8,128)(2,1)S(1)}, bf16[256,512]{1,0:T(8,128)(2,1)S(1)}, u32[]{:S(2)}, u32[]{:S(2)}) collective-permute-start(bf16[256,512]{1,0:T(8,128)(2,1)S(1)} %constant_dynamic-update-slice_fusion.6), channel_id=1, source_target_pairs={{0,8},{4,12},{8,0},{12,4},{1,9},{5,13},{9,1},{13,5},{2,10},{6,14},... | collective-permute-start | bytes 786440 | tf_op jit(solution)/shard_map/ppermute | solution.py:19
  16.1 1.5 %collective-permute-start.7 = (bf16[256,512]{1,0:T(8,128)(2,1)S(1)}, bf16[256,512]{1,0:T(8,128)(2,1)S(1)}, u32[]{:S(2)}, u32[]{:S(2)}) collective-permute-start(bf16[256,512]{1,0:T(8,128)(2,1)S(1)} %constant_dynamic-update-slice_fusion.6), channel_id=1, source_target_pairs={{0,4},{4,0},{8,12},{12,8},{1,5},{5,1},{9,13},{13,9},{2,6},{6,2},{1... | collective-permute-start | bytes 786440 | tf_op jit(solution)/shard_map/ppermute | solution.py:19
  19.9 5.0 %collective-permute-done.6 = bf16[256,256]{1,0:T(8,128)(2,1)S(1)} collective-permute-done((bf16[256,256]{1,0:T(8,128)(2,1)S(1)}, bf16[256,256]{1,0:T(8,128)(2,1)S(1)}, u32[]{:S(2)}, u32[]{:S(2)}) %collective-permute-start.6) | collective-permute-done | bytes 131104 | tf_op jit(solution)/shard_map/ppermute | solution.py:19
  24.9 1.6 %collective-permute-start.9 = (bf16[256,512]{1,0:T(8,128)(2,1)S(1)}, bf16[256,512]{1,0:T(8,128)(2,1)S(1)}, u32[]{:S(2)}, u32[]{:S(2)}) collective-permute-start(bf16[256,512]{1,0:T(8,128)(2,1)S(1)} %pad_maximum_fusion), channel_id=1, source_target_pairs={{0,1},{1,0},{2,3},{3,2},{4,5},{5,4},{6,7},{7,6},{8,9},{9,8},{10,11... | collective-permute-start | bytes 786440 | tf_op jit(solution)/shard_map/ppermute | solution.py:19
  26.6 1.5 %collective-permute-start.10 = (bf16[256,256]{1,0:T(8,128)(2,1)S(1)}, bf16[256,256]{1,0:T(8,128)(2,1)S(1)}, u32[]{:S(2)}, u32[]{:S(2)}) collective-permute-start(bf16[256,256]{1,0:T(8,128)(2,1)S(1)} %collective-permute-done.5), channel_id=1, source_target_pairs={{0,4},{4,0},{8,12},{12,8},{1,5},{5,1},{9,13},{13,9},{2,6},{6,2},{1... | collective-permute-start | bytes 393224 | tf_op jit(solution)/shard_map/ppermute | solution.py:19
  28.1 2.0 %collective-permute-start.11 = (bf16[256,256]{1,0:T(8,128)(2,1)S(1)}, bf16[256,256]{1,0:T(8,128)(2,1)S(1)}, u32[]{:S(2)}, u32[]{:S(2)}) collective-permute-start(bf16[256,256]{1,0:T(8,128)(2,1)S(1)} %collective-permute-done.5), channel_id=1, source_target_pairs={{0,8},{4,12},{8,0},{12,4},{1,9},{5,13},{9,1},{13,5},{2,10},{6,14},... | collective-permute-start | bytes 393224 | tf_op jit(solution)/shard_map/ppermute | solution.py:19
  31.5 1.5 %collective-permute-done.11 = bf16[256,256]{1,0:T(8,128)(2,1)S(1)} collective-permute-done((bf16[256,256]{1,0:T(8,128)(2,1)S(1)}, bf16[256,256]{1,0:T(8,128)(2,1)S(1)}, u32[]{:S(2)}, u32[]{:S(2)}) %collective-permute-start.11) | collective-permute-done | bytes 131104 | tf_op jit(solution)/shard_map/ppermute | solution.py:19
  33.8 2.0 %collective-permute-start.12 = (f32[256]{0:T(256)S(1)}, f32[256]{0:T(256)S(1)}, u32[]{:S(2)}, u32[]{:S(2)}) collective-permute-start(f32[256]{0:T(256)S(1)} %get-tuple-element.112), channel_id=1, source_target_pairs={{0,12},{4,8},{8,4},{12,0},{1,13},{5,9},{9,5},{13,1},{2,14},{6,10},... | collective-permute-start | bytes 3080 | tf_op jit(solution)/shard_map/ppermute | solution.py:19
  35.9 1.5 %collective-permute-start.14 = (f32[256]{0:T(256)S(1)}, f32[256]{0:T(256)S(1)}, u32[]{:S(2)}, u32[]{:S(2)}) collective-permute-start(f32[256]{0:T(256)S(1)} %get-tuple-element.112), channel_id=1, source_target_pairs={{0,4},{4,0},{8,12},{12,8},{1,5},{5,1},{9,13},{13,9},{2,6},{6,2},{1... | collective-permute-start | bytes 3080 | tf_op jit(solution)/shard_map/ppermute | solution.py:19
  39.5 3.2 %collective-permute-start.15 = (f32[256]{0:T(256)S(1)}, f32[256]{0:T(256)S(1)}, u32[]{:S(2)}, u32[]{:S(2)}) collective-permute-start(f32[256]{0:T(256)S(1)} %add.148), channel_id=1, source_target_pairs={{0,3},{1,2},{2,1},{3,0},{4,7},{5,6},{6,5},{7,4},{8,11},{9,10},{10,... | collective-permute-start | bytes 3080 | tf_op jit(solution)/shard_map/ppermute | solution.py:19
  44.9 2.3 %collective-permute-done.16 = f32[256]{0:T(256)S(1)} collective-permute-done((f32[256]{0:T(256)S(1)}, f32[256]{0:T(256)S(1)}, u32[]{:S(2)}, u32[]{:S(2)}) %collective-permute-start.16) | collective-permute-done | bytes 1056 | tf_op jit(solution)/shard_map/ppermute | solution.py:19
  49.4 1.5 %collective-permute-start.26 = (bf16[256,256]{1,0:T(8,128)(2,1)S(1)}, bf16[256,256]{1,0:T(8,128)(2,1)S(1)}, u32[]{:S(2)}, u32[]{:S(2)}) collective-permute-start(bf16[256,256]{1,0:T(8,128)(2,1)S(1)} %get-tuple-element.116), channel_id=1, source_target_pairs={{0,4},{4,0},{8,12},{12,8},{1,5},{5,1},{9,13},{13,9},{2,6},{6,2},{1... | collective-permute-start | bytes 393224 | tf_op jit(solution)/shard_map/ppermute | solution.py:19
  50.9 1.9 %collective-permute-start.27 = (bf16[256,256]{1,0:T(8,128)(2,1)S(1)}, bf16[256,256]{1,0:T(8,128)(2,1)S(1)}, u32[]{:S(2)}, u32[]{:S(2)}) collective-permute-start(bf16[256,256]{1,0:T(8,128)(2,1)S(1)} %get-tuple-element.117), channel_id=1, source_target_pairs={{0,8},{4,12},{8,0},{12,4},{1,9},{5,13},{9,1},{13,5},{2,10},{6,14},... | collective-permute-start | bytes 393224 | tf_op jit(solution)/shard_map/ppermute | solution.py:19
  55.3 2.2 %collective-permute-done.24 = bf16[256,512]{1,0:T(8,128)(2,1)S(1)} collective-permute-done((bf16[256,512]{1,0:T(8,128)(2,1)S(1)}, bf16[256,512]{1,0:T(8,128)(2,1)S(1)}, u32[]{:S(2)}, u32[]{:S(2)}) %collective-permute-start.24) | collective-permute-done | bytes 262176 | tf_op jit(solution)/shard_map/ppermute | solution.py:19
  57.6 2.5 %collective-permute-start.25 = (bf16[256,256]{1,0:T(8,128)(2,1)S(1)}, bf16[256,256]{1,0:T(8,128)(2,1)S(1)}, u32[]{:S(2)}, u32[]{:S(2)}) collective-permute-start(bf16[256,256]{1,0:T(8,128)(2,1)S(1)} %get-tuple-element.100), channel_id=1, source_target_pairs={{0,12},{4,8},{8,4},{12,0},{1,13},{5,9},{9,5},{13,1},{2,14},{6,10},... | collective-permute-start | bytes 393224 | tf_op jit(solution)/shard_map/ppermute | solution.py:19
  63.9 1.3 collective-permute-done.28
  65.5 2.0 %collective-permute-start.30 = (bf16[256,256]{1,0:T(8,128)(2,1)S(1)}, bf16[256,256]{1,0:T(8,128)(2,1)S(1)}, u32[]{:S(2)}, u32[]{:S(2)}) collective-permute-start(bf16[256,256]{1,0:T(8,128)(2,1)S(1)} %add_convert_fusion.4), channel_id=1, source_target_pairs={{0,12},{4,8},{8,4},{12,0},{1,13},{5,9},{9,5},{13,1},{2,14},{6,10},... | collective-permute-start | bytes 393224 | tf_op jit(solution)/shard_map/ppermute | solution.py:19
  67.5 2.0 %collective-permute-start.29 = (bf16[256,256]{1,0:T(8,128)(2,1)S(1)}, bf16[256,256]{1,0:T(8,128)(2,1)S(1)}, u32[]{:S(2)}, u32[]{:S(2)}) collective-permute-start(bf16[256,256]{1,0:T(8,128)(2,1)S(1)} %get-tuple-element.99), channel_id=1, source_target_pairs={{0,2},{1,3},{2,0},{3,1},{4,6},{5,7},{6,4},{7,5},{8,10},{9,11},{10,... | collective-permute-start | bytes 393224 | tf_op jit(solution)/shard_map/ppermute | solution.py:19
  70.6 4.5 %collective-permute-done.29 = bf16[256,256]{1,0:T(8,128)(2,1)S(1)} collective-permute-done((bf16[256,256]{1,0:T(8,128)(2,1)S(1)}, bf16[256,256]{1,0:T(8,128)(2,1)S(1)}, u32[]{:S(2)}, u32[]{:S(2)}) %collective-permute-start.29) | collective-permute-done | bytes 131104 | tf_op jit(solution)/shard_map/ppermute | solution.py:19
  75.2 1.8 %collective-permute-done.31 = bf16[256,256]{1,0:T(8,128)(2,1)S(1)} collective-permute-done((bf16[256,256]{1,0:T(8,128)(2,1)S(1)}, bf16[256,256]{1,0:T(8,128)(2,1)S(1)}, u32[]{:S(2)}, u32[]{:S(2)}) %collective-permute-start.31) | collective-permute-done | bytes 131104 | tf_op jit(solution)/shard_map/ppermute | solution.py:19
  78.0 1.9 %collective-permute-start.34 = (bf16[256,256]{1,0:T(8,128)(2,1)S(1)}, bf16[256,256]{1,0:T(8,128)(2,1)S(1)}, u32[]{:S(2)}, u32[]{:S(2)}) collective-permute-start(bf16[256,256]{1,0:T(8,128)(2,1)S(1)} %get-tuple-element.68), channel_id=1, source_target_pairs={{0,12},{4,8},{8,4},{12,0},{1,13},{5,9},{9,5},{13,1},{2,14},{6,10},... | collective-permute-start | bytes 393224 | tf_op jit(solution)/shard_map/ppermute | solution.py:19
  79.9 1.2 collective-permute-start.32
  82.2 1.3 collective-permute-done.36
  83.7 2.3 %collective-permute-start.37 = (bf16[256,256]{1,0:T(8,128)(2,1)S(1)}, bf16[256,256]{1,0:T(8,128)(2,1)S(1)}, u32[]{:S(2)}, u32[]{:S(2)}) collective-permute-start(bf16[256,256]{1,0:T(8,128)(2,1)S(1)} %collective-permute-done.36), channel_id=1, source_target_pairs={{0,1},{1,0},{2,3},{3,2},{4,5},{5,4},{6,7},{7,6},{8,9},{9,8},{10,11... | collective-permute-start | bytes 393224 | tf_op jit(solution)/shard_map/ppermute | solution.py:19
  86.1 2.3 %collective-permute-start.40 = (bf16[256,512]{1,0:T(8,128)(2,1)S(1)}, bf16[256,512]{1,0:T(8,128)(2,1)S(1)}, u32[]{:S(2)}, u32[]{:S(2)}) collective-permute-start(bf16[256,512]{1,0:T(8,128)(2,1)S(1)} %constant_dynamic-update-slice_fusion.20), channel_id=1, source_target_pairs={{0,8},{4,12},{8,0},{12,4},{1,9},{5,13},{9,1},{13,5},{2,10},{6,14},... | collective-permute-start | bytes 786440 | tf_op jit(solution)/shard_map/ppermute | solution.py:19
  88.4 2.5 %collective-permute-done.38 = bf16[256,256]{1,0:T(8,128)(2,1)S(1)} collective-permute-done((bf16[256,256]{1,0:T(8,128)(2,1)S(1)}, bf16[256,256]{1,0:T(8,128)(2,1)S(1)}, u32[]{:S(2)}, u32[]{:S(2)}) %collective-permute-start.38) | collective-permute-done | bytes 131104 | tf_op jit(solution)/shard_map/ppermute | solution.py:19
  91.3 2.9 %collective-permute-start.41 = (bf16[256,512]{1,0:T(8,128)(2,1)S(1)}, bf16[256,512]{1,0:T(8,128)(2,1)S(1)}, u32[]{:S(2)}, u32[]{:S(2)}) collective-permute-start(bf16[256,512]{1,0:T(8,128)(2,1)S(1)} %pad_maximum_fusion.1), channel_id=1, source_target_pairs={{0,1},{1,0},{2,3},{3,2},{4,5},{5,4},{6,7},{7,6},{8,9},{9,8},{10,11... | collective-permute-start | bytes 786440 | tf_op jit(solution)/shard_map/ppermute | solution.py:19
  96.0 1.2 collective-permute-done.39
  98.5 1.6 %collective-permute-done.42 = bf16[256,256]{1,0:T(8,128)(2,1)S(1)} collective-permute-done((bf16[256,256]{1,0:T(8,128)(2,1)S(1)}, bf16[256,256]{1,0:T(8,128)(2,1)S(1)}, u32[]{:S(2)}, u32[]{:S(2)}) %collective-permute-start.42) | collective-permute-done | bytes 131104 | tf_op jit(solution)/shard_map/ppermute | solution.py:19
  101.0 1.5 %collective-permute-start.44 = (f32[256]{0:T(256)S(1)}, f32[256]{0:T(256)S(1)}, u32[]{:S(2)}, u32[]{:S(2)}) collective-permute-start(f32[256]{0:T(256)S(1)} %get-tuple-element.106), channel_id=1, source_target_pairs={{0,12},{4,8},{8,4},{12,0},{1,13},{5,9},{9,5},{13,1},{2,14},{6,10},... | collective-permute-start | bytes 3080 | tf_op jit(solution)/shard_map/ppermute | solution.py:19
  102.5 2.0 %collective-permute-start.45 = (f32[256]{0:T(256)S(1)}, f32[256]{0:T(256)S(1)}, u32[]{:S(2)}, u32[]{:S(2)}) collective-permute-start(f32[256]{0:T(256)S(1)} %get-tuple-element.106), channel_id=1, source_target_pairs={{0,8},{4,12},{8,0},{12,4},{1,9},{5,13},{9,1},{13,5},{2,10},{6,14},... | collective-permute-start | bytes 3080 | tf_op jit(solution)/shard_map/ppermute | solution.py:19
  106.0 2.0 %collective-permute-done.46 = f32[256]{0:T(256)S(1)} collective-permute-done((f32[256]{0:T(256)S(1)}, f32[256]{0:T(256)S(1)}, u32[]{:S(2)}, u32[]{:S(2)}) %collective-permute-start.46) | collective-permute-done | bytes 1056 | tf_op jit(solution)/shard_map/ppermute | solution.py:19
  108.1 2.0 %collective-permute-start.47 = (f32[256]{0:T(256)S(1)}, f32[256]{0:T(256)S(1)}, u32[]{:S(2)}, u32[]{:S(2)}) collective-permute-start(f32[256]{0:T(256)S(1)} %add.172), channel_id=1, source_target_pairs={{0,3},{1,2},{2,1},{3,0},{4,7},{5,6},{6,5},{7,4},{8,11},{9,10},{10,... | collective-permute-start | bytes 3080 | tf_op jit(solution)/shard_map/ppermute | solution.py:19
  110.1 2.3 %collective-permute-start.49 = (f32[256]{0:T(256)S(1)}, f32[256]{0:T(256)S(1)}, u32[]{:S(2)}, u32[]{:S(2)}) collective-permute-start(f32[256]{0:T(256)S(1)} %add.172), channel_id=1, source_target_pairs={{0,1},{1,0},{2,3},{3,2},{4,5},{5,4},{6,7},{7,6},{8,9},{9,8},{10,11... | collective-permute-start | bytes 3080 | tf_op jit(solution)/shard_map/ppermute | solution.py:19
  116.5 1.6 %collective-permute-start.56 = (bf16[256,512]{1,0:T(8,128)(2,1)S(1)}, bf16[256,512]{1,0:T(8,128)(2,1)S(1)}, u32[]{:S(2)}, u32[]{:S(2)}) collective-permute-start(bf16[256,512]{1,0:T(8,128)(2,1)S(1)} %slice.290), channel_id=1, source_target_pairs={{0,1},{1,0},{2,3},{3,2},{4,5},{5,4},{6,7},{7,6},{8,9},{9,8},{10,11... | collective-permute-start | bytes 786440 | tf_op jit(solution)/shard_map/ppermute | solution.py:19
  119.8 1.3 collective-permute-start.54
  121.1 2.0 %collective-permute-start.55 = (bf16[256,512]{1,0:T(8,128)(2,1)S(1)}, bf16[256,512]{1,0:T(8,128)(2,1)S(1)}, u32[]{:S(2)}, u32[]{:S(2)}) collective-permute-start(bf16[256,512]{1,0:T(8,128)(2,1)S(1)} %get-tuple-element.105), channel_id=1, source_target_pairs={{0,8},{4,12},{8,0},{12,4},{1,9},{5,13},{9,1},{13,5},{2,10},{6,14},... | collective-permute-start | bytes 786440 | tf_op jit(solution)/shard_map/ppermute | solution.py:19
  125.7 1.4 collective-permute-start.60
  127.0 1.3 collective-permute-start.52
  128.4 1.6 %collective-permute-done.54 = bf16[256,512]{1,0:T(8,128)(2,1)S(1)} collective-permute-done((bf16[256,512]{1,0:T(8,128)(2,1)S(1)}, bf16[256,512]{1,0:T(8,128)(2,1)S(1)}, u32[]{:S(2)}, u32[]{:S(2)}) %collective-permute-start.54) | collective-permute-done | bytes 262176 | tf_op jit(solution)/shard_map/ppermute | solution.py:19
  132.7 1.6 %collective-permute-start.62 = (bf16[256,256]{1,0:T(8,128)(2,1)S(1)}, bf16[256,256]{1,0:T(8,128)(2,1)S(1)}, u32[]{:S(2)}, u32[]{:S(2)}) collective-permute-start(bf16[256,256]{1,0:T(8,128)(2,1)S(1)} %add_convert_fusion.1), channel_id=1, source_target_pairs={{0,12},{4,8},{8,4},{12,0},{1,13},{5,9},{9,5},{13,1},{2,14},{6,10},... | collective-permute-start | bytes 393224 | tf_op jit(solution)/shard_map/ppermute | solution.py:19
  134.2 1.2 collective-permute-start.61
  135.5 2.1 %collective-permute-start.63 = (bf16[256,256]{1,0:T(8,128)(2,1)S(1)}, bf16[256,256]{1,0:T(8,128)(2,1)S(1)}, u32[]{:S(2)}, u32[]{:S(2)}) collective-permute-start(bf16[256,256]{1,0:T(8,128)(2,1)S(1)} %add_convert_fusion), channel_id=1, source_target_pairs={{0,1},{1,0},{2,3},{3,2},{4,5},{5,4},{6,7},{7,6},{8,9},{9,8},{10,11... | collective-permute-start | bytes 393224 | tf_op jit(solution)/shard_map/ppermute | solution.py:19
  137.5 4.0 %collective-permute-done.61 = bf16[256,256]{1,0:T(8,128)(2,1)S(1)} collective-permute-done((bf16[256,256]{1,0:T(8,128)(2,1)S(1)}, bf16[256,256]{1,0:T(8,128)(2,1)S(1)}, u32[]{:S(2)}, u32[]{:S(2)}) %collective-permute-start.61) | collective-permute-done | bytes 131104 | tf_op jit(solution)/shard_map/ppermute | solution.py:19
  (169 shorter events, 41.6 us)
Async XLA Ops:
  1.7 12.2 %collective-permute-start.4 = (bf16[256,256]{1,0:T(8,128)(2,1)S(1)}, bf16[256,256]{1,0:T(8,128)(2,1)S(1)}, u32[]{:S(2)}, u32[]{:S(2)}) collective-permute-start(bf16[256,256]{1,0:T(8,128)(2,1)S(1)} %fusion.28), channel_id=1, source_target_pairs={{0,2},{1,3},{2,0},{3,1},{4,6},{5,7},{6,4},{7,5},{8,10},{9,11},{10,... | collective-permute-start | bytes 393224 | tf_op jit(solution)/shard_map/ppermute | solution.py:19
  5.8 8.1 %collective-permute-start.3 = (bf16[256,256]{1,0:T(8,128)(2,1)S(1)}, bf16[256,256]{1,0:T(8,128)(2,1)S(1)}, u32[]{:S(2)}, u32[]{:S(2)}) collective-permute-start(bf16[256,256]{1,0:T(8,128)(2,1)S(1)} %fusion.28), channel_id=1, source_target_pairs={{0,1},{1,0},{2,3},{3,2},{4,5},{5,4},{6,7},{7,6},{8,9},{9,8},{10,11... | collective-permute-start | bytes 393224 | tf_op jit(solution)/shard_map/ppermute | solution.py:19
  7.4 8.6 %collective-permute-start.2 = (bf16[256,256]{1,0:T(8,128)(2,1)S(1)}, bf16[256,256]{1,0:T(8,128)(2,1)S(1)}, u32[]{:S(2)}, u32[]{:S(2)}) collective-permute-start(bf16[256,256]{1,0:T(8,128)(2,1)S(1)} %fusion.28), channel_id=1, source_target_pairs={{0,12},{4,8},{8,4},{12,0},{1,13},{5,9},{9,5},{13,1},{2,14},{6,10},... | collective-permute-start | bytes 393224 | tf_op jit(solution)/shard_map/ppermute | solution.py:19
  9.9 7.7 %collective-permute-start = (bf16[256,256]{1,0:T(8,128)(2,1)S(1)}, bf16[256,256]{1,0:T(8,128)(2,1)S(1)}, u32[]{:S(2)}, u32[]{:S(2)}) collective-permute-start(bf16[256,256]{1,0:T(8,128)(2,1)S(1)} %fusion.28), channel_id=1, source_target_pairs={{0,4},{4,0},{8,12},{12,8},{1,5},{5,1},{9,13},{13,9},{2,6},{6,2},{1... | collective-permute-start | bytes 393224 | tf_op jit(solution)/shard_map/ppermute | solution.py:19
  10.4 7.6 %collective-permute-start.1 = (bf16[256,256]{1,0:T(8,128)(2,1)S(1)}, bf16[256,256]{1,0:T(8,128)(2,1)S(1)}, u32[]{:S(2)}, u32[]{:S(2)}) collective-permute-start(bf16[256,256]{1,0:T(8,128)(2,1)S(1)} %fusion.28), channel_id=1, source_target_pairs={{0,8},{4,12},{8,0},{12,4},{1,9},{5,13},{9,1},{13,5},{2,10},{6,14},... | collective-permute-start | bytes 393224 | tf_op jit(solution)/shard_map/ppermute | solution.py:19
  14.5 15.6 %collective-permute-start.8 = (bf16[256,512]{1,0:T(8,128)(2,1)S(1)}, bf16[256,512]{1,0:T(8,128)(2,1)S(1)}, u32[]{:S(2)}, u32[]{:S(2)}) collective-permute-start(bf16[256,512]{1,0:T(8,128)(2,1)S(1)} %constant_dynamic-update-slice_fusion.6), channel_id=1, source_target_pairs={{0,8},{4,12},{8,0},{12,4},{1,9},{5,13},{9,1},{13,5},{2,10},{6,14},... | collective-permute-start | bytes 786440 | tf_op jit(solution)/shard_map/ppermute | solution.py:19
  16.1 14.0 %collective-permute-start.7 = (bf16[256,512]{1,0:T(8,128)(2,1)S(1)}, bf16[256,512]{1,0:T(8,128)(2,1)S(1)}, u32[]{:S(2)}, u32[]{:S(2)}) collective-permute-start(bf16[256,512]{1,0:T(8,128)(2,1)S(1)} %constant_dynamic-update-slice_fusion.6), channel_id=1, source_target_pairs={{0,4},{4,0},{8,12},{12,8},{1,5},{5,1},{9,13},{13,9},{2,6},{6,2},{1... | collective-permute-start | bytes 786440 | tf_op jit(solution)/shard_map/ppermute | solution.py:19
  17.6 7.4 %collective-permute-start.6 = (bf16[256,256]{1,0:T(8,128)(2,1)S(1)}, bf16[256,256]{1,0:T(8,128)(2,1)S(1)}, u32[]{:S(2)}, u32[]{:S(2)}) collective-permute-start(bf16[256,256]{1,0:T(8,128)(2,1)S(1)} %collective-permute-done.4), channel_id=1, source_target_pairs={{0,12},{4,8},{8,4},{12,0},{1,13},{5,9},{9,5},{13,1},{2,14},{6,10},... | collective-permute-start | bytes 393224 | tf_op jit(solution)/shard_map/ppermute | solution.py:19
  24.9 6.4 %collective-permute-start.9 = (bf16[256,512]{1,0:T(8,128)(2,1)S(1)}, bf16[256,512]{1,0:T(8,128)(2,1)S(1)}, u32[]{:S(2)}, u32[]{:S(2)}) collective-permute-start(bf16[256,512]{1,0:T(8,128)(2,1)S(1)} %pad_maximum_fusion), channel_id=1, source_target_pairs={{0,1},{1,0},{2,3},{3,2},{4,5},{5,4},{6,7},{7,6},{8,9},{9,8},{10,11... | collective-permute-start | bytes 786440 | tf_op jit(solution)/shard_map/ppermute | solution.py:19
  33.7 14.7 %collective-permute-start.18 = (bf16[256,768]{1,0:T(8,128)(2,1)S(1)}, bf16[256,768]{1,0:T(8,128)(2,1)S(1)}, u32[]{:S(2)}, u32[]{:S(2)}) collective-permute-start(bf16[256,768]{1,0:T(8,128)(2,1)S(1)} %get-tuple-element.113), channel_id=1, source_target_pairs={{0,16},{16,0},{1,17},{17,1},{2,18},{18,2},{3,19},{19,3},{4,20},{20... | collective-permute-start | bytes 1179656 | tf_op jit(solution)/shard_map/ppermute | solution.py:19
  39.5 5.4 %collective-permute-start.15 = (f32[256]{0:T(256)S(1)}, f32[256]{0:T(256)S(1)}, u32[]{:S(2)}, u32[]{:S(2)}) collective-permute-start(f32[256]{0:T(256)S(1)} %add.148), channel_id=1, source_target_pairs={{0,3},{1,2},{2,1},{3,0},{4,7},{5,6},{6,5},{7,4},{8,11},{9,10},{10,... | collective-permute-start | bytes 3080 | tf_op jit(solution)/shard_map/ppermute | solution.py:19
  49.1 8.5 %collective-permute-start.24 = (bf16[256,512]{1,0:T(8,128)(2,1)S(1)}, bf16[256,512]{1,0:T(8,128)(2,1)S(1)}, u32[]{:S(2)}, u32[]{:S(2)}) collective-permute-start(bf16[256,512]{1,0:T(8,128)(2,1)S(1)} %slice.265), channel_id=1, source_target_pairs={{0,1},{1,0},{2,3},{3,2},{4,5},{5,4},{6,7},{7,6},{8,9},{9,8},{10,11... | collective-permute-start | bytes 786440 | tf_op jit(solution)/shard_map/ppermute | solution.py:19
  49.4 10.7 %collective-permute-start.26 = (bf16[256,256]{1,0:T(8,128)(2,1)S(1)}, bf16[256,256]{1,0:T(8,128)(2,1)S(1)}, u32[]{:S(2)}, u32[]{:S(2)}) collective-permute-start(bf16[256,256]{1,0:T(8,128)(2,1)S(1)} %get-tuple-element.116), channel_id=1, source_target_pairs={{0,4},{4,0},{8,12},{12,8},{1,5},{5,1},{9,13},{13,9},{2,6},{6,2},{1... | collective-permute-start | bytes 393224 | tf_op jit(solution)/shard_map/ppermute | solution.py:19
  50.9 9.3 %collective-permute-start.27 = (bf16[256,256]{1,0:T(8,128)(2,1)S(1)}, bf16[256,256]{1,0:T(8,128)(2,1)S(1)}, u32[]{:S(2)}, u32[]{:S(2)}) collective-permute-start(bf16[256,256]{1,0:T(8,128)(2,1)S(1)} %get-tuple-element.117), channel_id=1, source_target_pairs={{0,8},{4,12},{8,0},{12,4},{1,9},{5,13},{9,1},{13,5},{2,10},{6,14},... | collective-permute-start | bytes 393224 | tf_op jit(solution)/shard_map/ppermute | solution.py:19
  53.7 8.3 %collective-permute-start.22 = (bf16[256,512]{1,0:T(8,128)(2,1)S(1)}, bf16[256,512]{1,0:T(8,128)(2,1)S(1)}, u32[]{:S(2)}, u32[]{:S(2)}) collective-permute-start(bf16[256,512]{1,0:T(8,128)(2,1)S(1)} %get-tuple-element.110), channel_id=1, source_target_pairs={{0,4},{4,0},{8,12},{12,8},{1,5},{5,1},{9,13},{13,9},{2,6},{6,2},{1... | collective-permute-start | bytes 786440 | tf_op jit(solution)/shard_map/ppermute | solution.py:19
  54.3 9.6 %collective-permute-start.23 = (bf16[256,512]{1,0:T(8,128)(2,1)S(1)}, bf16[256,512]{1,0:T(8,128)(2,1)S(1)}, u32[]{:S(2)}, u32[]{:S(2)}) collective-permute-start(bf16[256,512]{1,0:T(8,128)(2,1)S(1)} %get-tuple-element.111), channel_id=1, source_target_pairs={{0,8},{4,12},{8,0},{12,4},{1,9},{5,13},{9,1},{13,5},{2,10},{6,14},... | collective-permute-start | bytes 786440 | tf_op jit(solution)/shard_map/ppermute | solution.py:19
  57.6 7.7 %collective-permute-start.25 = (bf16[256,256]{1,0:T(8,128)(2,1)S(1)}, bf16[256,256]{1,0:T(8,128)(2,1)S(1)}, u32[]{:S(2)}, u32[]{:S(2)}) collective-permute-start(bf16[256,256]{1,0:T(8,128)(2,1)S(1)} %get-tuple-element.100), channel_id=1, source_target_pairs={{0,12},{4,8},{8,4},{12,0},{1,13},{5,9},{9,5},{13,1},{2,14},{6,10},... | collective-permute-start | bytes 393224 | tf_op jit(solution)/shard_map/ppermute | solution.py:19
  60.2 5.0 %collective-permute-start.28 = (bf16[256,256]{1,0:T(8,128)(2,1)S(1)}, bf16[256,256]{1,0:T(8,128)(2,1)S(1)}, u32[]{:S(2)}, u32[]{:S(2)}) collective-permute-start(bf16[256,256]{1,0:T(8,128)(2,1)S(1)} %add_convert_fusion.5), channel_id=1, source_target_pairs={{0,1},{1,0},{2,3},{3,2},{4,5},{5,4},{6,7},{7,6},{8,9},{9,8},{10,11... | collective-permute-start | bytes 393224 | tf_op jit(solution)/shard_map/ppermute | solution.py:19
  60.9 9.7 %collective-permute-start.20 = (bf16[256,256]{1,0:T(8,128)(2,1)S(1)}, bf16[256,256]{1,0:T(8,128)(2,1)S(1)}, u32[]{:S(2)}, u32[]{:S(2)}) collective-permute-start(bf16[256,256]{1,0:T(8,128)(2,1)S(1)} %get-tuple-element.108), channel_id=1, source_target_pairs={{0,4},{4,0},{8,12},{12,8},{1,5},{5,1},{9,13},{13,9},{2,6},{6,2},{1... | collective-permute-start | bytes 393224 | tf_op jit(solution)/shard_map/ppermute | solution.py:19
  62.1 8.5 %collective-permute-start.21 = (bf16[256,256]{1,0:T(8,128)(2,1)S(1)}, bf16[256,256]{1,0:T(8,128)(2,1)S(1)}, u32[]{:S(2)}, u32[]{:S(2)}) collective-permute-start(bf16[256,256]{1,0:T(8,128)(2,1)S(1)} %get-tuple-element.109), channel_id=1, source_target_pairs={{0,8},{4,12},{8,0},{12,4},{1,9},{5,13},{9,1},{13,5},{2,10},{6,14},... | collective-permute-start | bytes 393224 | tf_op jit(solution)/shard_map/ppermute | solution.py:19
  65.5 9.7 %collective-permute-start.30 = (bf16[256,256]{1,0:T(8,128)(2,1)S(1)}, bf16[256,256]{1,0:T(8,128)(2,1)S(1)}, u32[]{:S(2)}, u32[]{:S(2)}) collective-permute-start(bf16[256,256]{1,0:T(8,128)(2,1)S(1)} %add_convert_fusion.4), channel_id=1, source_target_pairs={{0,12},{4,8},{8,4},{12,0},{1,13},{5,9},{9,5},{13,1},{2,14},{6,10},... | collective-permute-start | bytes 393224 | tf_op jit(solution)/shard_map/ppermute | solution.py:19
  67.5 7.6 %collective-permute-start.29 = (bf16[256,256]{1,0:T(8,128)(2,1)S(1)}, bf16[256,256]{1,0:T(8,128)(2,1)S(1)}, u32[]{:S(2)}, u32[]{:S(2)}) collective-permute-start(bf16[256,256]{1,0:T(8,128)(2,1)S(1)} %get-tuple-element.99), channel_id=1, source_target_pairs={{0,2},{1,3},{2,0},{3,1},{4,6},{5,7},{6,4},{7,5},{8,10},{9,11},{10,... | collective-permute-start | bytes 393224 | tf_op jit(solution)/shard_map/ppermute | solution.py:19
  69.6 7.4 %collective-permute-start.31 = (bf16[256,256]{1,0:T(8,128)(2,1)S(1)}, bf16[256,256]{1,0:T(8,128)(2,1)S(1)}, u32[]{:S(2)}, u32[]{:S(2)}) collective-permute-start(bf16[256,256]{1,0:T(8,128)(2,1)S(1)} %add_convert_fusion.3), channel_id=1, source_target_pairs={{0,1},{1,0},{2,3},{3,2},{4,5},{5,4},{6,7},{7,6},{8,9},{9,8},{10,11... | collective-permute-start | bytes 393224 | tf_op jit(solution)/shard_map/ppermute | solution.py:19
  77.1 6.4 %collective-permute-start.36 = (bf16[256,256]{1,0:T(8,128)(2,1)S(1)}, bf16[256,256]{1,0:T(8,128)(2,1)S(1)}, u32[]{:S(2)}, u32[]{:S(2)}) collective-permute-start(bf16[256,256]{1,0:T(8,128)(2,1)S(1)} %get-tuple-element.68), channel_id=1, source_target_pairs={{0,2},{1,3},{2,0},{3,1},{4,6},{5,7},{6,4},{7,5},{8,10},{9,11},{10,... | collective-permute-start | bytes 393224 | tf_op jit(solution)/shard_map/ppermute | solution.py:19
  77.2 6.5 %collective-permute-start.35 = (bf16[256,256]{1,0:T(8,128)(2,1)S(1)}, bf16[256,256]{1,0:T(8,128)(2,1)S(1)}, u32[]{:S(2)}, u32[]{:S(2)}) collective-permute-start(bf16[256,256]{1,0:T(8,128)(2,1)S(1)} %get-tuple-element.68), channel_id=1, source_target_pairs={{0,1},{1,0},{2,3},{3,2},{4,5},{5,4},{6,7},{7,6},{8,9},{9,8},{10,11... | collective-permute-start | bytes 393224 | tf_op jit(solution)/shard_map/ppermute | solution.py:19
  78.0 8.1 %collective-permute-start.34 = (bf16[256,256]{1,0:T(8,128)(2,1)S(1)}, bf16[256,256]{1,0:T(8,128)(2,1)S(1)}, u32[]{:S(2)}, u32[]{:S(2)}) collective-permute-start(bf16[256,256]{1,0:T(8,128)(2,1)S(1)} %get-tuple-element.68), channel_id=1, source_target_pairs={{0,12},{4,8},{8,4},{12,0},{1,13},{5,9},{9,5},{13,1},{2,14},{6,10},... | collective-permute-start | bytes 393224 | tf_op jit(solution)/shard_map/ppermute | solution.py:19
  79.9 11.4 %collective-permute-start.32 = (bf16[256,256]{1,0:T(8,128)(2,1)S(1)}, bf16[256,256]{1,0:T(8,128)(2,1)S(1)}, u32[]{:S(2)}, u32[]{:S(2)}) collective-permute-start(bf16[256,256]{1,0:T(8,128)(2,1)S(1)} %get-tuple-element.68), channel_id=1, source_target_pairs={{0,4},{4,0},{8,12},{12,8},{1,5},{5,1},{9,13},{13,9},{2,6},{6,2},{1... | collective-permute-start | bytes 393224 | tf_op jit(solution)/shard_map/ppermute | solution.py:19
  81.2 13.0 %collective-permute-start.33 = (bf16[256,256]{1,0:T(8,128)(2,1)S(1)}, bf16[256,256]{1,0:T(8,128)(2,1)S(1)}, u32[]{:S(2)}, u32[]{:S(2)}) collective-permute-start(bf16[256,256]{1,0:T(8,128)(2,1)S(1)} %get-tuple-element.68), channel_id=1, source_target_pairs={{0,8},{4,12},{8,0},{12,4},{1,9},{5,13},{9,1},{13,5},{2,10},{6,14},... | collective-permute-start | bytes 393224 | tf_op jit(solution)/shard_map/ppermute | solution.py:19
  83.6 7.3 %collective-permute-start.38 = (bf16[256,256]{1,0:T(8,128)(2,1)S(1)}, bf16[256,256]{1,0:T(8,128)(2,1)S(1)}, u32[]{:S(2)}, u32[]{:S(2)}) collective-permute-start(bf16[256,256]{1,0:T(8,128)(2,1)S(1)} %collective-permute-done.36), channel_id=1, source_target_pairs={{0,12},{4,8},{8,4},{12,0},{1,13},{5,9},{9,5},{13,1},{2,14},{6,10},... | collective-permute-start | bytes 393224 | tf_op jit(solution)/shard_map/ppermute | solution.py:19
  83.7 10.5 %collective-permute-start.37 = (bf16[256,256]{1,0:T(8,128)(2,1)S(1)}, bf16[256,256]{1,0:T(8,128)(2,1)S(1)}, u32[]{:S(2)}, u32[]{:S(2)}) collective-permute-start(bf16[256,256]{1,0:T(8,128)(2,1)S(1)} %collective-permute-done.36), channel_id=1, source_target_pairs={{0,1},{1,0},{2,3},{3,2},{4,5},{5,4},{6,7},{7,6},{8,9},{9,8},{10,11... | collective-permute-start | bytes 393224 | tf_op jit(solution)/shard_map/ppermute | solution.py:19
  86.1 9.9 %collective-permute-start.40 = (bf16[256,512]{1,0:T(8,128)(2,1)S(1)}, bf16[256,512]{1,0:T(8,128)(2,1)S(1)}, u32[]{:S(2)}, u32[]{:S(2)}) collective-permute-start(bf16[256,512]{1,0:T(8,128)(2,1)S(1)} %constant_dynamic-update-slice_fusion.20), channel_id=1, source_target_pairs={{0,8},{4,12},{8,0},{12,4},{1,9},{5,13},{9,1},{13,5},{2,10},{6,14},... | collective-permute-start | bytes 786440 | tf_op jit(solution)/shard_map/ppermute | solution.py:19
  90.9 6.4 %collective-permute-start.39 = (bf16[256,512]{1,0:T(8,128)(2,1)S(1)}, bf16[256,512]{1,0:T(8,128)(2,1)S(1)}, u32[]{:S(2)}, u32[]{:S(2)}) collective-permute-start(bf16[256,512]{1,0:T(8,128)(2,1)S(1)} %constant_dynamic-update-slice_fusion.20), channel_id=1, source_target_pairs={{0,4},{4,0},{8,12},{12,8},{1,5},{5,1},{9,13},{13,9},{2,6},{6,2},{1... | collective-permute-start | bytes 786440 | tf_op jit(solution)/shard_map/ppermute | solution.py:19
  91.3 7.2 %collective-permute-start.41 = (bf16[256,512]{1,0:T(8,128)(2,1)S(1)}, bf16[256,512]{1,0:T(8,128)(2,1)S(1)}, u32[]{:S(2)}, u32[]{:S(2)}) collective-permute-start(bf16[256,512]{1,0:T(8,128)(2,1)S(1)} %pad_maximum_fusion.1), channel_id=1, source_target_pairs={{0,1},{1,0},{2,3},{3,2},{4,5},{5,4},{6,7},{7,6},{8,9},{9,8},{10,11... | collective-permute-start | bytes 786440 | tf_op jit(solution)/shard_map/ppermute | solution.py:19
  95.2 5.0 %collective-permute-start.43 = (bf16[256,256]{1,0:T(8,128)(2,1)S(1)}, bf16[256,256]{1,0:T(8,128)(2,1)S(1)}, u32[]{:S(2)}, u32[]{:S(2)}) collective-permute-start(bf16[256,256]{1,0:T(8,128)(2,1)S(1)} %collective-permute-done.37), channel_id=1, source_target_pairs={{0,8},{4,12},{8,0},{12,4},{1,9},{5,13},{9,1},{13,5},{2,10},{6,14},... | collective-permute-start | bytes 393224 | tf_op jit(solution)/shard_map/ppermute | solution.py:19
  100.9 14.8 %collective-permute-start.50 = (bf16[256,768]{1,0:T(8,128)(2,1)S(1)}, bf16[256,768]{1,0:T(8,128)(2,1)S(1)}, u32[]{:S(2)}, u32[]{:S(2)}) collective-permute-start(bf16[256,768]{1,0:T(8,128)(2,1)S(1)} %get-tuple-element.107.proj_ref), channel_id=1, source_target_pairs={{0,16},{16,0},{1,17},{17,1},{2,18},{18,2},{3,19},{19,3},{4,20},{20... | collective-permute-start | bytes 1179656 | tf_op jit(solution)/shard_map/ppermute | solution.py:19
  108.1 5.4 %collective-permute-start.47 = (f32[256]{0:T(256)S(1)}, f32[256]{0:T(256)S(1)}, u32[]{:S(2)}, u32[]{:S(2)}) collective-permute-start(f32[256]{0:T(256)S(1)} %add.172), channel_id=1, source_target_pairs={{0,3},{1,2},{2,1},{3,0},{4,7},{5,6},{6,5},{7,4},{8,11},{9,10},{10,... | collective-permute-start | bytes 3080 | tf_op jit(solution)/shard_map/ppermute | solution.py:19
  116.5 8.6 %collective-permute-start.56 = (bf16[256,512]{1,0:T(8,128)(2,1)S(1)}, bf16[256,512]{1,0:T(8,128)(2,1)S(1)}, u32[]{:S(2)}, u32[]{:S(2)}) collective-permute-start(bf16[256,512]{1,0:T(8,128)(2,1)S(1)} %slice.290), channel_id=1, source_target_pairs={{0,1},{1,0},{2,3},{3,2},{4,5},{5,4},{6,7},{7,6},{8,9},{9,8},{10,11... | collective-permute-start | bytes 786440 | tf_op jit(solution)/shard_map/ppermute | solution.py:19
  118.0 7.6 %collective-permute-start.58 = (bf16[256,256]{1,0:T(8,128)(2,1)S(1)}, bf16[256,256]{1,0:T(8,128)(2,1)S(1)}, u32[]{:S(2)}, u32[]{:S(2)}) collective-permute-start(bf16[256,256]{1,0:T(8,128)(2,1)S(1)} %get-tuple-element.114), channel_id=1, source_target_pairs={{0,4},{4,0},{8,12},{12,8},{1,5},{5,1},{9,13},{13,9},{2,6},{6,2},{1... | collective-permute-start | bytes 393224 | tf_op jit(solution)/shard_map/ppermute | solution.py:19
  118.1 7.5 %collective-permute-start.59 = (bf16[256,256]{1,0:T(8,128)(2,1)S(1)}, bf16[256,256]{1,0:T(8,128)(2,1)S(1)}, u32[]{:S(2)}, u32[]{:S(2)}) collective-permute-start(bf16[256,256]{1,0:T(8,128)(2,1)S(1)} %get-tuple-element.115), channel_id=1, source_target_pairs={{0,8},{4,12},{8,0},{12,4},{1,9},{5,13},{9,1},{13,5},{2,10},{6,14},... | collective-permute-start | bytes 393224 | tf_op jit(solution)/shard_map/ppermute | solution.py:19
  119.8 10.2 %collective-permute-start.54 = (bf16[256,512]{1,0:T(8,128)(2,1)S(1)}, bf16[256,512]{1,0:T(8,128)(2,1)S(1)}, u32[]{:S(2)}, u32[]{:S(2)}) collective-permute-start(bf16[256,512]{1,0:T(8,128)(2,1)S(1)} %get-tuple-element.104), channel_id=1, source_target_pairs={{0,4},{4,0},{8,12},{12,8},{1,5},{5,1},{9,13},{13,9},{2,6},{6,2},{1... | collective-permute-start | bytes 786440 | tf_op jit(solution)/shard_map/ppermute | solution.py:19
  121.1 10.3 %collective-permute-start.55 = (bf16[256,512]{1,0:T(8,128)(2,1)S(1)}, bf16[256,512]{1,0:T(8,128)(2,1)S(1)}, u32[]{:S(2)}, u32[]{:S(2)}) collective-permute-start(bf16[256,512]{1,0:T(8,128)(2,1)S(1)} %get-tuple-element.105), channel_id=1, source_target_pairs={{0,8},{4,12},{8,0},{12,4},{1,9},{5,13},{9,1},{13,5},{2,10},{6,14},... | collective-permute-start | bytes 786440 | tf_op jit(solution)/shard_map/ppermute | solution.py:19
  125.1 7.4 %collective-permute-start.57 = (bf16[256,256]{1,0:T(8,128)(2,1)S(1)}, bf16[256,256]{1,0:T(8,128)(2,1)S(1)}, u32[]{:S(2)}, u32[]{:S(2)}) collective-permute-start(bf16[256,256]{1,0:T(8,128)(2,1)S(1)} %get-tuple-element.95), channel_id=1, source_target_pairs={{0,12},{4,8},{8,4},{12,0},{1,13},{5,9},{9,5},{13,1},{2,14},{6,10},... | collective-permute-start | bytes 393224 | tf_op jit(solution)/shard_map/ppermute | solution.py:19
  125.7 5.8 %collective-permute-start.60 = (bf16[256,256]{1,0:T(8,128)(2,1)S(1)}, bf16[256,256]{1,0:T(8,128)(2,1)S(1)}, u32[]{:S(2)}, u32[]{:S(2)}) collective-permute-start(bf16[256,256]{1,0:T(8,128)(2,1)S(1)} %add_convert_fusion.2), channel_id=1, source_target_pairs={{0,1},{1,0},{2,3},{3,2},{4,5},{5,4},{6,7},{7,6},{8,9},{9,8},{10,11... | collective-permute-start | bytes 393224 | tf_op jit(solution)/shard_map/ppermute | solution.py:19
  127.0 10.5 %collective-permute-start.52 = (bf16[256,256]{1,0:T(8,128)(2,1)S(1)}, bf16[256,256]{1,0:T(8,128)(2,1)S(1)}, u32[]{:S(2)}, u32[]{:S(2)}) collective-permute-start(bf16[256,256]{1,0:T(8,128)(2,1)S(1)} %get-tuple-element.102), channel_id=1, source_target_pairs={{0,4},{4,0},{8,12},{12,8},{1,5},{5,1},{9,13},{13,9},{2,6},{6,2},{1... | collective-permute-start | bytes 393224 | tf_op jit(solution)/shard_map/ppermute | solution.py:19
  130.0 7.5 %collective-permute-start.53 = (bf16[256,256]{1,0:T(8,128)(2,1)S(1)}, bf16[256,256]{1,0:T(8,128)(2,1)S(1)}, u32[]{:S(2)}, u32[]{:S(2)}) collective-permute-start(bf16[256,256]{1,0:T(8,128)(2,1)S(1)} %get-tuple-element.103), channel_id=1, source_target_pairs={{0,8},{4,12},{8,0},{12,4},{1,9},{5,13},{9,1},{13,5},{2,10},{6,14},... | collective-permute-start | bytes 393224 | tf_op jit(solution)/shard_map/ppermute | solution.py:19
  132.7 8.9 %collective-permute-start.62 = (bf16[256,256]{1,0:T(8,128)(2,1)S(1)}, bf16[256,256]{1,0:T(8,128)(2,1)S(1)}, u32[]{:S(2)}, u32[]{:S(2)}) collective-permute-start(bf16[256,256]{1,0:T(8,128)(2,1)S(1)} %add_convert_fusion.1), channel_id=1, source_target_pairs={{0,12},{4,8},{8,4},{12,0},{1,13},{5,9},{9,5},{13,1},{2,14},{6,10},... | collective-permute-start | bytes 393224 | tf_op jit(solution)/shard_map/ppermute | solution.py:19
  134.2 7.3 %collective-permute-start.61 = (bf16[256,256]{1,0:T(8,128)(2,1)S(1)}, bf16[256,256]{1,0:T(8,128)(2,1)S(1)}, u32[]{:S(2)}, u32[]{:S(2)}) collective-permute-start(bf16[256,256]{1,0:T(8,128)(2,1)S(1)} %get-tuple-element.94), channel_id=1, source_target_pairs={{0,2},{1,3},{2,0},{3,1},{4,6},{5,7},{6,4},{7,5},{8,10},{9,11},{10,... | collective-permute-start | bytes 393224 | tf_op jit(solution)/shard_map/ppermute | solution.py:19
  135.5 6.1 %collective-permute-start.63 = (bf16[256,256]{1,0:T(8,128)(2,1)S(1)}, bf16[256,256]{1,0:T(8,128)(2,1)S(1)}, u32[]{:S(2)}, u32[]{:S(2)}) collective-permute-start(bf16[256,256]{1,0:T(8,128)(2,1)S(1)} %add_convert_fusion), channel_id=1, source_target_pairs={{0,1},{1,0},{2,3},{3,2},{4,5},{5,4},{6,7},{7,6},{8,9},{9,8},{10,11... | collective-permute-start | bytes 393224 | tf_op jit(solution)/shard_map/ppermute | solution.py:19
  (16 other events, 63.6 us)

commit v9 on v8

--- a/solution.py
+++ b/solution.py
@@ -78,9 +78,9 @@
     ones, twos = zip(*[send("row", r, b[r, 1], b[r, 2]) for r in (1, 2)])
     far_across = summed(b[3, 2], far_across)
     three = summed(after(b[0, 3], far_across), left, right)
-    near_across = summed(after(b[3, 0], three), near_across)
     (far_across,), (three,) = send("row", 3, far_across), send("feat", 1, three)
     two = summed(b[0, 2], *twos, far_across, three)
+    near_across = summed(after(b[3, 0], two), near_across)
     one = summed(after(b[0, 1], two), *ones)
     (two,), (near_across,), (one,) = (
         send("feat", 2, two),
@@ -189,7 +189,7 @@
         summed_proj = 0.0
         for g, places in enumerate(ARRIVALS):
             blocks = [dirs[p] for p in places]
-            blocks = lax.optimization_barrier(blocks + [dirs[0, 3]])[: len(places)]
+            blocks = lax.optimization_barrier(blocks + [dirs[3, 2], dirs[0, 3]])[: len(places)]
             part = lax.dot_general(
                 join(*blocks),
                 groups[g],

time: 143 us -> 138 us (0.965)
  waiting for transfers between devices: 47.8 us -> 42.6 us
    ppermute x64, waiting for transfers between devices: 47.8 us -> 42.6 us  [xor_move(): return lax.ppermute(block, axis, [(i, i ^ mask) for i in range(count)])]
  transfers between devices with their start and end apart: 64 -> 64, of which waited for: 36 -> 35; matrix products, arithmetic and copies ran while one was open for 6% -> 6% of each run, Pallas kernels for 3% -> 3%
where the time goes in v9:
time: 138 us
  starting transfers between devices  77.3 us (56%)
  waiting for transfers between devices  42.6 us (31%)
  matrix products  9.39 us (7%)
  Pallas kernels  3.92 us (3%)
  local copies, waits for them, and re-layouts  2.51 us (2%)
    ppermute x64, starting transfers between devices, xor_move(): return lax.ppermute(block, axis, [(i, i ^ mask) for i in range(count)])  77.3 us
    ppermute x64, waiting for transfers between devices, xor_move(): return lax.ppermute(block, axis, [(i, i ^ mask) for i in range(count)])  42.6 us
    dot_general x6, matrix products, on_device(): lax.dot_general(residue, groups[g], (((1,), (0,)), ((), ())), preferred_e...  4.77 us
    dot_general x6, matrix products, on_device(): lax.dot_general(join(*blocks), groups[g], (((1,), (1,)), ((), ())), prefe...  4.62 us
    pallas_call x1, Pallas kernels, regroup(): pl.pallas_call(kernel, out_shape=[jax.ShapeDtypeStruct((rows_here, len(pl...  3 us
  transfers between devices with their start and end apart: 64, of which 35 were waited for; matrix products, arithmetic and copies ran while one was open for 6% of the time, Pallas kernels for 3%

profile of v9, /device:TPU:0, one launch (start us, length us, event | category | flops | bytes accessed | tf_op | source)
XLA Modules:
  0.0 138.0 jit_solution(2251818791057245323)
XLA Ops:
  1.7 4.1 %collective-permute-start.4 = (bf16[256,256]{1,0:T(8,128)(2,1)S(1)}, bf16[256,256]{1,0:T(8,128)(2,1)S(1)}, u32[]{:S(2)}, u32[]{:S(2)}) collective-permute-start(bf16[256,256]{1,0:T(8,128)(2,1)S(1)} %fusion.28), channel_id=1, source_target_pairs={{0,2},{1,3},{2,0},{3,1},{4,6},{5,7},{6,4},{7,5},{8,10},{9,11},{10,... | collective-permute-start | bytes 393224 | tf_op jit(solution)/shard_map/ppermute | solution.py:19
  5.8 1.6 %collective-permute-start.3 = (bf16[256,256]{1,0:T(8,128)(2,1)S(1)}, bf16[256,256]{1,0:T(8,128)(2,1)S(1)}, u32[]{:S(2)}, u32[]{:S(2)}) collective-permute-start(bf16[256,256]{1,0:T(8,128)(2,1)S(1)} %fusion.28), channel_id=1, source_target_pairs={{0,1},{1,0},{2,3},{3,2},{4,5},{5,4},{6,7},{7,6},{8,9},{9,8},{10,11... | collective-permute-start | bytes 393224 | tf_op jit(solution)/shard_map/ppermute | solution.py:19
  7.4 2.4 %collective-permute-start.2 = (bf16[256,256]{1,0:T(8,128)(2,1)S(1)}, bf16[256,256]{1,0:T(8,128)(2,1)S(1)}, u32[]{:S(2)}, u32[]{:S(2)}) collective-permute-start(bf16[256,256]{1,0:T(8,128)(2,1)S(1)} %fusion.28), channel_id=1, source_target_pairs={{0,12},{4,8},{8,4},{12,0},{1,13},{5,9},{9,5},{13,1},{2,14},{6,10},... | collective-permute-start | bytes 393224 | tf_op jit(solution)/shard_map/ppermute | solution.py:19
  10.9 3.0 %regroup.1 = (bf16[768,1536]{1,0:T(8,128)(2,1)S(1)}, bf16[768,1536]{1,0:T(8,128)(2,1)S(1)}, bf16[768,1024]{1,0:T(8,128)(2,1)S(1)}) custom-call(bf16[768,4096]{1,0:T(8,128)(2,1)} %bitcast.37), custom_call_target="tpu_custom_call" | custom-call | bytes 12582912 | tf_op jit(solution)/shard_map/regroup/pallas_call | solution.py:140
  14.4 2.4 %collective-permute-start.5 = (bf16[256,256]{1,0:T(8,128)(2,1)S(1)}, bf16[256,256]{1,0:T(8,128)(2,1)S(1)}, u32[]{:S(2)}, u32[]{:S(2)}) collective-permute-start(bf16[256,256]{1,0:T(8,128)(2,1)S(1)} %collective-permute-done.4), channel_id=1, source_target_pairs={{0,12},{4,8},{8,4},{12,0},{1,13},{5,9},{9,5},{13,1},{2,14},{6,10},... | collective-permute-start | bytes 393224 | tf_op jit(solution)/shard_map/ppermute | solution.py:19
  19.0 2.8 %collective-permute-done.5 = bf16[256,256]{1,0:T(8,128)(2,1)S(1)} collective-permute-done((bf16[256,256]{1,0:T(8,128)(2,1)S(1)}, bf16[256,256]{1,0:T(8,128)(2,1)S(1)}, u32[]{:S(2)}, u32[]{:S(2)}) %collective-permute-start.5) | collective-permute-done | bytes 131104 | tf_op jit(solution)/shard_map/ppermute | solution.py:19
  22.7 1.6 %collective-permute-start.9 = (bf16[256,512]{1,0:T(8,128)(2,1)S(1)}, bf16[256,512]{1,0:T(8,128)(2,1)S(1)}, u32[]{:S(2)}, u32[]{:S(2)}) collective-permute-start(bf16[256,512]{1,0:T(8,128)(2,1)S(1)} %pad_maximum_fusion), channel_id=1, source_target_pairs={{0,1},{1,0},{2,3},{3,2},{4,5},{5,4},{6,7},{7,6},{8,9},{9,8},{10,11... | collective-permute-start | bytes 786440 | tf_op jit(solution)/shard_map/ppermute | solution.py:19
  24.3 1.5 %collective-permute-start.10 = (bf16[256,256]{1,0:T(8,128)(2,1)S(1)}, bf16[256,256]{1,0:T(8,128)(2,1)S(1)}, u32[]{:S(2)}, u32[]{:S(2)}) collective-permute-start(bf16[256,256]{1,0:T(8,128)(2,1)S(1)} %collective-permute-done.6), channel_id=1, source_target_pairs={{0,4},{4,0},{8,12},{12,8},{1,5},{5,1},{9,13},{13,9},{2,6},{6,2},{1... | collective-permute-start | bytes 393224 | tf_op jit(solution)/shard_map/ppermute | solution.py:19
  25.8 1.6 %collective-permute-start.11 = (bf16[256,256]{1,0:T(8,128)(2,1)S(1)}, bf16[256,256]{1,0:T(8,128)(2,1)S(1)}, u32[]{:S(2)}, u32[]{:S(2)}) collective-permute-start(bf16[256,256]{1,0:T(8,128)(2,1)S(1)} %collective-permute-done.6), channel_id=1, source_target_pairs={{0,8},{4,12},{8,0},{12,4},{1,9},{5,13},{9,1},{13,5},{2,10},{6,14},... | collective-permute-start | bytes 393224 | tf_op jit(solution)/shard_map/ppermute | solution.py:19
  29.3 1.5 %collective-permute-done.11 = bf16[256,256]{1,0:T(8,128)(2,1)S(1)} collective-permute-done((bf16[256,256]{1,0:T(8,128)(2,1)S(1)}, bf16[256,256]{1,0:T(8,128)(2,1)S(1)}, u32[]{:S(2)}, u32[]{:S(2)}) %collective-permute-start.11) | collective-permute-done | bytes 131104 | tf_op jit(solution)/shard_map/ppermute | solution.py:19
  31.6 1.6 %collective-permute-start.12 = (f32[256]{0:T(256)S(1)}, f32[256]{0:T(256)S(1)}, u32[]{:S(2)}, u32[]{:S(2)}) collective-permute-start(f32[256]{0:T(256)S(1)} %get-tuple-element.112), channel_id=1, source_target_pairs={{0,12},{4,8},{8,4},{12,0},{1,13},{5,9},{9,5},{13,1},{2,14},{6,10},... | collective-permute-start | bytes 3080 | tf_op jit(solution)/shard_map/ppermute | solution.py:19
  33.6 1.5 %collective-permute-start.14 = (f32[256]{0:T(256)S(1)}, f32[256]{0:T(256)S(1)}, u32[]{:S(2)}, u32[]{:S(2)}) collective-permute-start(f32[256]{0:T(256)S(1)} %get-tuple-element.112), channel_id=1, source_target_pairs={{0,4},{4,0},{8,12},{12,8},{1,5},{5,1},{9,13},{13,9},{2,6},{6,2},{1... | collective-permute-start | bytes 3080 | tf_op jit(solution)/shard_map/ppermute | solution.py:19
  37.2 1.3 collective-permute-start.15
  39.6 2.0 %collective-permute-start.17 = (f32[256]{0:T(256)S(1)}, f32[256]{0:T(256)S(1)}, u32[]{:S(2)}, u32[]{:S(2)}) collective-permute-start(f32[256]{0:T(256)S(1)} %add.148), channel_id=1, source_target_pairs={{0,1},{1,0},{2,3},{3,2},{4,5},{5,4},{6,7},{7,6},{8,9},{9,8},{10,11... | collective-permute-start | bytes 3080 | tf_op jit(solution)/shard_map/ppermute | solution.py:19
  43.2 1.1 collective-permute-done.19
  45.0 2.0 %collective-permute-start.24 = (bf16[256,512]{1,0:T(8,128)(2,1)S(1)}, bf16[256,512]{1,0:T(8,128)(2,1)S(1)}, u32[]{:S(2)}, u32[]{:S(2)}) collective-permute-start(bf16[256,512]{1,0:T(8,128)(2,1)S(1)} %slice.265), channel_id=1, source_target_pairs={{0,1},{1,0},{2,3},{3,2},{4,5},{5,4},{6,7},{7,6},{8,9},{9,8},{10,11... | collective-permute-start | bytes 786440 | tf_op jit(solution)/shard_map/ppermute | solution.py:19
  47.1 1.5 %collective-permute-start.26 = (bf16[256,256]{1,0:T(8,128)(2,1)S(1)}, bf16[256,256]{1,0:T(8,128)(2,1)S(1)}, u32[]{:S(2)}, u32[]{:S(2)}) collective-permute-start(bf16[256,256]{1,0:T(8,128)(2,1)S(1)} %get-tuple-element.116), channel_id=1, source_target_pairs={{0,4},{4,0},{8,12},{12,8},{1,5},{5,1},{9,13},{13,9},{2,6},{6,2},{1... | collective-permute-start | bytes 393224 | tf_op jit(solution)/shard_map/ppermute | solution.py:19
  48.6 1.6 %collective-permute-start.27 = (bf16[256,256]{1,0:T(8,128)(2,1)S(1)}, bf16[256,256]{1,0:T(8,128)(2,1)S(1)}, u32[]{:S(2)}, u32[]{:S(2)}) collective-permute-start(bf16[256,256]{1,0:T(8,128)(2,1)S(1)} %get-tuple-element.117), channel_id=1, source_target_pairs={{0,8},{4,12},{8,0},{12,4},{1,9},{5,13},{9,1},{13,5},{2,10},{6,14},... | collective-permute-start | bytes 393224 | tf_op jit(solution)/shard_map/ppermute | solution.py:19
  53.8 2.6 %collective-permute-start.25 = (bf16[256,256]{1,0:T(8,128)(2,1)S(1)}, bf16[256,256]{1,0:T(8,128)(2,1)S(1)}, u32[]{:S(2)}, u32[]{:S(2)}) collective-permute-start(bf16[256,256]{1,0:T(8,128)(2,1)S(1)} %get-tuple-element.100), channel_id=1, source_target_pairs={{0,12},{4,8},{8,4},{12,0},{1,13},{5,9},{9,5},{13,1},{2,14},{6,10},... | collective-permute-start | bytes 393224 | tf_op jit(solution)/shard_map/ppermute | solution.py:19
  56.4 1.8 %collective-permute-start.28 = (bf16[256,256]{1,0:T(8,128)(2,1)S(1)}, bf16[256,256]{1,0:T(8,128)(2,1)S(1)}, u32[]{:S(2)}, u32[]{:S(2)}) collective-permute-start(bf16[256,256]{1,0:T(8,128)(2,1)S(1)} %add_convert_fusion.5), channel_id=1, source_target_pairs={{0,1},{1,0},{2,3},{3,2},{4,5},{5,4},{6,7},{7,6},{8,9},{9,8},{10,11... | collective-permute-start | bytes 393224 | tf_op jit(solution)/shard_map/ppermute | solution.py:19
  58.8 1.6 %collective-permute-done.22 = bf16[256,512]{1,0:T(8,128)(2,1)S(1)} collective-permute-done((bf16[256,512]{1,0:T(8,128)(2,1)S(1)}, bf16[256,512]{1,0:T(8,128)(2,1)S(1)}, u32[]{:S(2)}, u32[]{:S(2)}) %collective-permute-start.22) | collective-permute-done | bytes 262176 | tf_op jit(solution)/shard_map/ppermute | solution.py:19
  61.7 1.4 collective-permute-done.25
  64.3 1.6 %collective-permute-start.30 = (bf16[256,256]{1,0:T(8,128)(2,1)S(1)}, bf16[256,256]{1,0:T(8,128)(2,1)S(1)}, u32[]{:S(2)}, u32[]{:S(2)}) collective-permute-start(bf16[256,256]{1,0:T(8,128)(2,1)S(1)} %add_convert_fusion.4), channel_id=1, source_target_pairs={{0,12},{4,8},{8,4},{12,0},{1,13},{5,9},{9,5},{13,1},{2,14},{6,10},... | collective-permute-start | bytes 393224 | tf_op jit(solution)/shard_map/ppermute | solution.py:19
  66.8 3.5 %collective-permute-done.29 = bf16[256,256]{1,0:T(8,128)(2,1)S(1)} collective-permute-done((bf16[256,256]{1,0:T(8,128)(2,1)S(1)}, bf16[256,256]{1,0:T(8,128)(2,1)S(1)}, u32[]{:S(2)}, u32[]{:S(2)}) %collective-permute-start.29) | collective-permute-done | bytes 131104 | tf_op jit(solution)/shard_map/ppermute | solution.py:19
  71.6 1.2 collective-permute-start.36
  72.8 1.4 %collective-permute-start.35 = (bf16[256,256]{1,0:T(8,128)(2,1)S(1)}, bf16[256,256]{1,0:T(8,128)(2,1)S(1)}, u32[]{:S(2)}, u32[]{:S(2)}) collective-permute-start(bf16[256,256]{1,0:T(8,128)(2,1)S(1)} %get-tuple-element.68), channel_id=1, source_target_pairs={{0,1},{1,0},{2,3},{3,2},{4,5},{5,4},{6,7},{7,6},{8,9},{9,8},{10,11... | collective-permute-start | bytes 393224 | tf_op jit(solution)/shard_map/ppermute | solution.py:19
  75.0 1.5 %collective-permute-start.32 = (bf16[256,256]{1,0:T(8,128)(2,1)S(1)}, bf16[256,256]{1,0:T(8,128)(2,1)S(1)}, u32[]{:S(2)}, u32[]{:S(2)}) collective-permute-start(bf16[256,256]{1,0:T(8,128)(2,1)S(1)} %get-tuple-element.68), channel_id=1, source_target_pairs={{0,4},{4,0},{8,12},{12,8},{1,5},{5,1},{9,13},{13,9},{2,6},{6,2},{1... | collective-permute-start | bytes 393224 | tf_op jit(solution)/shard_map/ppermute | solution.py:19
  76.6 1.2 collective-permute-start.33
  79.2 1.5 %collective-permute-start.37 = (bf16[256,256]{1,0:T(8,128)(2,1)S(1)}, bf16[256,256]{1,0:T(8,128)(2,1)S(1)}, u32[]{:S(2)}, u32[]{:S(2)}) collective-permute-start(bf16[256,256]{1,0:T(8,128)(2,1)S(1)} %collective-permute-done.36), channel_id=1, source_target_pairs={{0,12},{4,8},{8,4},{12,0},{1,13},{5,9},{9,5},{13,1},{2,14},{6,10},... | collective-permute-start | bytes 393224 | tf_op jit(solution)/shard_map/ppermute | solution.py:19
  81.0 3.5 %collective-permute-start.40 = (bf16[256,512]{1,0:T(8,128)(2,1)S(1)}, bf16[256,512]{1,0:T(8,128)(2,1)S(1)}, u32[]{:S(2)}, u32[]{:S(2)}) collective-permute-start(bf16[256,512]{1,0:T(8,128)(2,1)S(1)} %constant_dynamic-update-slice_fusion.20), channel_id=1, source_target_pairs={{0,8},{4,12},{8,0},{12,4},{1,9},{5,13},{9,1},{13,5},{2,10},{6,14},... | collective-permute-start | bytes 786440 | tf_op jit(solution)/shard_map/ppermute | solution.py:19
  84.6 1.1 collective-permute-done.37
  85.7 4.5 %collective-permute-start.39 = (bf16[256,512]{1,0:T(8,128)(2,1)S(1)}, bf16[256,512]{1,0:T(8,128)(2,1)S(1)}, u32[]{:S(2)}, u32[]{:S(2)}) collective-permute-start(bf16[256,512]{1,0:T(8,128)(2,1)S(1)} %constant_dynamic-update-slice_fusion.20), channel_id=1, source_target_pairs={{0,4},{4,0},{8,12},{12,8},{1,5},{5,1},{9,13},{13,9},{2,6},{6,2},{1... | collective-permute-start | bytes 786440 | tf_op jit(solution)/shard_map/ppermute | solution.py:19
  92.0 2.6 %collective-permute-done.39 = bf16[256,512]{1,0:T(8,128)(2,1)S(1)} collective-permute-done((bf16[256,512]{1,0:T(8,128)(2,1)S(1)}, bf16[256,512]{1,0:T(8,128)(2,1)S(1)}, u32[]{:S(2)}, u32[]{:S(2)}) %collective-permute-start.39) | collective-permute-done | bytes 262176 | tf_op jit(solution)/shard_map/ppermute | solution.py:19
  95.5 1.2 collective-permute-done.41
  97.6 1.1 collective-permute-start.44
  98.7 2.0 %collective-permute-start.45 = (f32[256]{0:T(256)S(1)}, f32[256]{0:T(256)S(1)}, u32[]{:S(2)}, u32[]{:S(2)}) collective-permute-start(f32[256]{0:T(256)S(1)} %get-tuple-element.106), channel_id=1, source_target_pairs={{0,8},{4,12},{8,0},{12,4},{1,9},{5,13},{9,1},{13,5},{2,10},{6,14},... | collective-permute-start | bytes 3080 | tf_op jit(solution)/shard_map/ppermute | solution.py:19
  102.2 2.0 %collective-permute-done.46 = f32[256]{0:T(256)S(1)} collective-permute-done((f32[256]{0:T(256)S(1)}, f32[256]{0:T(256)S(1)}, u32[]{:S(2)}, u32[]{:S(2)}) %collective-permute-start.46) | collective-permute-done | bytes 1056 | tf_op jit(solution)/shard_map/ppermute | solution.py:19
  104.7 3.0 %collective-permute-start.48 = (f32[256]{0:T(256)S(1)}, f32[256]{0:T(256)S(1)}, u32[]{:S(2)}, u32[]{:S(2)}) collective-permute-start(f32[256]{0:T(256)S(1)} %add.172), channel_id=1, source_target_pairs={{0,2},{1,3},{2,0},{3,1},{4,6},{5,7},{6,4},{7,5},{8,10},{9,11},{10,... | collective-permute-start | bytes 3080 | tf_op jit(solution)/shard_map/ppermute | solution.py:19
  109.6 1.6 %collective-permute-done.49 = f32[256]{0:T(256)S(1)} collective-permute-done((f32[256]{0:T(256)S(1)}, f32[256]{0:T(256)S(1)}, u32[]{:S(2)}, u32[]{:S(2)}) %collective-permute-start.49) | collective-permute-done | bytes 1056 | tf_op jit(solution)/shard_map/ppermute | solution.py:19
  115.8 1.5 %collective-permute-start.54 = (bf16[256,512]{1,0:T(8,128)(2,1)S(1)}, bf16[256,512]{1,0:T(8,128)(2,1)S(1)}, u32[]{:S(2)}, u32[]{:S(2)}) collective-permute-start(bf16[256,512]{1,0:T(8,128)(2,1)S(1)} %get-tuple-element.104), channel_id=1, source_target_pairs={{0,4},{4,0},{8,12},{12,8},{1,5},{5,1},{9,13},{13,9},{2,6},{6,2},{1... | collective-permute-start | bytes 786440 | tf_op jit(solution)/shard_map/ppermute | solution.py:19
  117.3 2.0 %collective-permute-start.55 = (bf16[256,512]{1,0:T(8,128)(2,1)S(1)}, bf16[256,512]{1,0:T(8,128)(2,1)S(1)}, u32[]{:S(2)}, u32[]{:S(2)}) collective-permute-start(bf16[256,512]{1,0:T(8,128)(2,1)S(1)} %get-tuple-element.105), channel_id=1, source_target_pairs={{0,8},{4,12},{8,0},{12,4},{1,9},{5,13},{9,1},{13,5},{2,10},{6,14},... | collective-permute-start | bytes 786440 | tf_op jit(solution)/shard_map/ppermute | solution.py:19
  120.1 1.6 %collective-permute-done.56 = bf16[256,512]{1,0:T(8,128)(2,1)S(1)} collective-permute-done((bf16[256,512]{1,0:T(8,128)(2,1)S(1)}, bf16[256,512]{1,0:T(8,128)(2,1)S(1)}, u32[]{:S(2)}, u32[]{:S(2)}) %collective-permute-start.56) | collective-permute-done | bytes 262176 | tf_op jit(solution)/shard_map/ppermute | solution.py:19
  123.1 1.5 %collective-permute-start.52 = (bf16[256,256]{1,0:T(8,128)(2,1)S(1)}, bf16[256,256]{1,0:T(8,128)(2,1)S(1)}, u32[]{:S(2)}, u32[]{:S(2)}) collective-permute-start(bf16[256,256]{1,0:T(8,128)(2,1)S(1)} %get-tuple-element.102), channel_id=1, source_target_pairs={{0,4},{4,0},{8,12},{12,8},{1,5},{5,1},{9,13},{13,9},{2,6},{6,2},{1... | collective-permute-start | bytes 393224 | tf_op jit(solution)/shard_map/ppermute | solution.py:19
  124.6 1.6 %collective-permute-done.54 = bf16[256,512]{1,0:T(8,128)(2,1)S(1)} collective-permute-done((bf16[256,512]{1,0:T(8,128)(2,1)S(1)}, bf16[256,512]{1,0:T(8,128)(2,1)S(1)}, u32[]{:S(2)}, u32[]{:S(2)}) %collective-permute-start.54) | collective-permute-done | bytes 262176 | tf_op jit(solution)/shard_map/ppermute | solution.py:19
  127.1 2.0 %collective-permute-done.57 = bf16[256,256]{1,0:T(8,128)(2,1)S(1)} collective-permute-done((bf16[256,256]{1,0:T(8,128)(2,1)S(1)}, bf16[256,256]{1,0:T(8,128)(2,1)S(1)}, u32[]{:S(2)}, u32[]{:S(2)}) %collective-permute-start.57) | collective-permute-done | bytes 131104 | tf_op jit(solution)/shard_map/ppermute | solution.py:19
  130.3 1.2 collective-permute-start.62
  131.5 1.1 collective-permute-start.63
  132.6 4.1 %collective-permute-done.61 = bf16[256,256]{1,0:T(8,128)(2,1)S(1)} collective-permute-done((bf16[256,256]{1,0:T(8,128)(2,1)S(1)}, bf16[256,256]{1,0:T(8,128)(2,1)S(1)}, u32[]{:S(2)}, u32[]{:S(2)}) %collective-permute-start.61) | collective-permute-done | bytes 131104 | tf_op jit(solution)/shard_map/ppermute | solution.py:19
  (169 shorter events, 42.8 us)
Async XLA Ops:
  1.7 12.2 %collective-permute-start.4 = (bf16[256,256]{1,0:T(8,128)(2,1)S(1)}, bf16[256,256]{1,0:T(8,128)(2,1)S(1)}, u32[]{:S(2)}, u32[]{:S(2)}) collective-permute-start(bf16[256,256]{1,0:T(8,128)(2,1)S(1)} %fusion.28), channel_id=1, source_target_pairs={{0,2},{1,3},{2,0},{3,1},{4,6},{5,7},{6,4},{7,5},{8,10},{9,11},{10,... | collective-permute-start | bytes 393224 | tf_op jit(solution)/shard_map/ppermute | solution.py:19
  5.8 8.1 %collective-permute-start.3 = (bf16[256,256]{1,0:T(8,128)(2,1)S(1)}, bf16[256,256]{1,0:T(8,128)(2,1)S(1)}, u32[]{:S(2)}, u32[]{:S(2)}) collective-permute-start(bf16[256,256]{1,0:T(8,128)(2,1)S(1)} %fusion.28), channel_id=1, source_target_pairs={{0,1},{1,0},{2,3},{3,2},{4,5},{5,4},{6,7},{7,6},{8,9},{9,8},{10,11... | collective-permute-start | bytes 393224 | tf_op jit(solution)/shard_map/ppermute | solution.py:19
  7.4 9.5 %collective-permute-start.2 = (bf16[256,256]{1,0:T(8,128)(2,1)S(1)}, bf16[256,256]{1,0:T(8,128)(2,1)S(1)}, u32[]{:S(2)}, u32[]{:S(2)}) collective-permute-start(bf16[256,256]{1,0:T(8,128)(2,1)S(1)} %fusion.28), channel_id=1, source_target_pairs={{0,12},{4,8},{8,4},{12,0},{1,13},{5,9},{9,5},{13,1},{2,14},{6,10},... | collective-permute-start | bytes 393224 | tf_op jit(solution)/shard_map/ppermute | solution.py:19
  9.9 7.6 %collective-permute-start = (bf16[256,256]{1,0:T(8,128)(2,1)S(1)}, bf16[256,256]{1,0:T(8,128)(2,1)S(1)}, u32[]{:S(2)}, u32[]{:S(2)}) collective-permute-start(bf16[256,256]{1,0:T(8,128)(2,1)S(1)} %fusion.28), channel_id=1, source_target_pairs={{0,4},{4,0},{8,12},{12,8},{1,5},{5,1},{9,13},{13,9},{2,6},{6,2},{1... | collective-permute-start | bytes 393224 | tf_op jit(solution)/shard_map/ppermute | solution.py:19
  10.4 7.7 %collective-permute-start.1 = (bf16[256,256]{1,0:T(8,128)(2,1)S(1)}, bf16[256,256]{1,0:T(8,128)(2,1)S(1)}, u32[]{:S(2)}, u32[]{:S(2)}) collective-permute-start(bf16[256,256]{1,0:T(8,128)(2,1)S(1)} %fusion.28), channel_id=1, source_target_pairs={{0,8},{4,12},{8,0},{12,4},{1,9},{5,13},{9,1},{13,5},{2,10},{6,14},... | collective-permute-start | bytes 393224 | tf_op jit(solution)/shard_map/ppermute | solution.py:19
  14.4 7.3 %collective-permute-start.5 = (bf16[256,256]{1,0:T(8,128)(2,1)S(1)}, bf16[256,256]{1,0:T(8,128)(2,1)S(1)}, u32[]{:S(2)}, u32[]{:S(2)}) collective-permute-start(bf16[256,256]{1,0:T(8,128)(2,1)S(1)} %collective-permute-done.4), channel_id=1, source_target_pairs={{0,12},{4,8},{8,4},{12,0},{1,13},{5,9},{9,5},{13,1},{2,14},{6,10},... | collective-permute-start | bytes 393224 | tf_op jit(solution)/shard_map/ppermute | solution.py:19
  16.9 10.4 %collective-permute-start.8 = (bf16[256,512]{1,0:T(8,128)(2,1)S(1)}, bf16[256,512]{1,0:T(8,128)(2,1)S(1)}, u32[]{:S(2)}, u32[]{:S(2)}) collective-permute-start(bf16[256,512]{1,0:T(8,128)(2,1)S(1)} %constant_dynamic-update-slice_fusion.6), channel_id=1, source_target_pairs={{0,8},{4,12},{8,0},{12,4},{1,9},{5,13},{9,1},{13,5},{2,10},{6,14},... | collective-permute-start | bytes 786440 | tf_op jit(solution)/shard_map/ppermute | solution.py:19
  17.5 9.9 %collective-permute-start.7 = (bf16[256,512]{1,0:T(8,128)(2,1)S(1)}, bf16[256,512]{1,0:T(8,128)(2,1)S(1)}, u32[]{:S(2)}, u32[]{:S(2)}) collective-permute-start(bf16[256,512]{1,0:T(8,128)(2,1)S(1)} %constant_dynamic-update-slice_fusion.6), channel_id=1, source_target_pairs={{0,4},{4,0},{8,12},{12,8},{1,5},{5,1},{9,13},{13,9},{2,6},{6,2},{1... | collective-permute-start | bytes 786440 | tf_op jit(solution)/shard_map/ppermute | solution.py:19
  22.7 6.4 %collective-permute-start.9 = (bf16[256,512]{1,0:T(8,128)(2,1)S(1)}, bf16[256,512]{1,0:T(8,128)(2,1)S(1)}, u32[]{:S(2)}, u32[]{:S(2)}) collective-permute-start(bf16[256,512]{1,0:T(8,128)(2,1)S(1)} %pad_maximum_fusion), channel_id=1, source_target_pairs={{0,1},{1,0},{2,3},{3,2},{4,5},{5,4},{6,7},{7,6},{8,9},{9,8},{10,11... | collective-permute-start | bytes 786440 | tf_op jit(solution)/shard_map/ppermute | solution.py:19
  31.5 12.9 %collective-permute-start.18 = (bf16[256,768]{1,0:T(8,128)(2,1)S(1)}, bf16[256,768]{1,0:T(8,128)(2,1)S(1)}, u32[]{:S(2)}, u32[]{:S(2)}) collective-permute-start(bf16[256,768]{1,0:T(8,128)(2,1)S(1)} %get-tuple-element.113), channel_id=1, source_target_pairs={{0,16},{16,0},{1,17},{17,1},{2,18},{18,2},{3,19},{19,3},{4,20},{20... | collective-permute-start | bytes 1179656 | tf_op jit(solution)/shard_map/ppermute | solution.py:19
  37.2 5.4 %collective-permute-start.15 = (f32[256]{0:T(256)S(1)}, f32[256]{0:T(256)S(1)}, u32[]{:S(2)}, u32[]{:S(2)}) collective-permute-start(f32[256]{0:T(256)S(1)} %add.148), channel_id=1, source_target_pairs={{0,3},{1,2},{2,1},{3,0},{4,7},{5,6},{6,5},{7,4},{8,11},{9,10},{10,... | collective-permute-start | bytes 3080 | tf_op jit(solution)/shard_map/ppermute | solution.py:19
  45.0 8.7 %collective-permute-start.24 = (bf16[256,512]{1,0:T(8,128)(2,1)S(1)}, bf16[256,512]{1,0:T(8,128)(2,1)S(1)}, u32[]{:S(2)}, u32[]{:S(2)}) collective-permute-start(bf16[256,512]{1,0:T(8,128)(2,1)S(1)} %slice.265), channel_id=1, source_target_pairs={{0,1},{1,0},{2,3},{3,2},{4,5},{5,4},{6,7},{7,6},{8,9},{9,8},{10,11... | collective-permute-start | bytes 786440 | tf_op jit(solution)/shard_map/ppermute | solution.py:19
  47.1 9.3 %collective-permute-start.26 = (bf16[256,256]{1,0:T(8,128)(2,1)S(1)}, bf16[256,256]{1,0:T(8,128)(2,1)S(1)}, u32[]{:S(2)}, u32[]{:S(2)}) collective-permute-start(bf16[256,256]{1,0:T(8,128)(2,1)S(1)} %get-tuple-element.116), channel_id=1, source_target_pairs={{0,4},{4,0},{8,12},{12,8},{1,5},{5,1},{9,13},{13,9},{2,6},{6,2},{1... | collective-permute-start | bytes 393224 | tf_op jit(solution)/shard_map/ppermute | solution.py:19
  48.6 7.8 %collective-permute-start.27 = (bf16[256,256]{1,0:T(8,128)(2,1)S(1)}, bf16[256,256]{1,0:T(8,128)(2,1)S(1)}, u32[]{:S(2)}, u32[]{:S(2)}) collective-permute-start(bf16[256,256]{1,0:T(8,128)(2,1)S(1)} %get-tuple-element.117), channel_id=1, source_target_pairs={{0,8},{4,12},{8,0},{12,4},{1,9},{5,13},{9,1},{13,5},{2,10},{6,14},... | collective-permute-start | bytes 393224 | tf_op jit(solution)/shard_map/ppermute | solution.py:19
  51.1 9.3 %collective-permute-start.22 = (bf16[256,512]{1,0:T(8,128)(2,1)S(1)}, bf16[256,512]{1,0:T(8,128)(2,1)S(1)}, u32[]{:S(2)}, u32[]{:S(2)}) collective-permute-start(bf16[256,512]{1,0:T(8,128)(2,1)S(1)} %get-tuple-element.110), channel_id=1, source_target_pairs={{0,4},{4,0},{8,12},{12,8},{1,5},{5,1},{9,13},{13,9},{2,6},{6,2},{1... | collective-permute-start | bytes 786440 | tf_op jit(solution)/shard_map/ppermute | solution.py:19
  51.6 10.1 %collective-permute-start.23 = (bf16[256,512]{1,0:T(8,128)(2,1)S(1)}, bf16[256,512]{1,0:T(8,128)(2,1)S(1)}, u32[]{:S(2)}, u32[]{:S(2)}) collective-permute-start(bf16[256,512]{1,0:T(8,128)(2,1)S(1)} %get-tuple-element.111), channel_id=1, source_target_pairs={{0,8},{4,12},{8,0},{12,4},{1,9},{5,13},{9,1},{13,5},{2,10},{6,14},... | collective-permute-start | bytes 786440 | tf_op jit(solution)/shard_map/ppermute | solution.py:19
  53.8 9.3 %collective-permute-start.25 = (bf16[256,256]{1,0:T(8,128)(2,1)S(1)}, bf16[256,256]{1,0:T(8,128)(2,1)S(1)}, u32[]{:S(2)}, u32[]{:S(2)}) collective-permute-start(bf16[256,256]{1,0:T(8,128)(2,1)S(1)} %get-tuple-element.100), channel_id=1, source_target_pairs={{0,12},{4,8},{8,4},{12,0},{1,13},{5,9},{9,5},{13,1},{2,14},{6,10},... | collective-permute-start | bytes 393224 | tf_op jit(solution)/shard_map/ppermute | solution.py:19
  56.4 5.3 %collective-permute-start.28 = (bf16[256,256]{1,0:T(8,128)(2,1)S(1)}, bf16[256,256]{1,0:T(8,128)(2,1)S(1)}, u32[]{:S(2)}, u32[]{:S(2)}) collective-permute-start(bf16[256,256]{1,0:T(8,128)(2,1)S(1)} %add_convert_fusion.5), channel_id=1, source_target_pairs={{0,1},{1,0},{2,3},{3,2},{4,5},{5,4},{6,7},{7,6},{8,9},{9,8},{10,11... | collective-permute-start | bytes 393224 | tf_op jit(solution)/shard_map/ppermute | solution.py:19
  58.3 8.6 %collective-permute-start.20 = (bf16[256,256]{1,0:T(8,128)(2,1)S(1)}, bf16[256,256]{1,0:T(8,128)(2,1)S(1)}, u32[]{:S(2)}, u32[]{:S(2)}) collective-permute-start(bf16[256,256]{1,0:T(8,128)(2,1)S(1)} %get-tuple-element.108), channel_id=1, source_target_pairs={{0,4},{4,0},{8,12},{12,8},{1,5},{5,1},{9,13},{13,9},{2,6},{6,2},{1... | collective-permute-start | bytes 393224 | tf_op jit(solution)/shard_map/ppermute | solution.py:19
  60.4 6.4 %collective-permute-start.21 = (bf16[256,256]{1,0:T(8,128)(2,1)S(1)}, bf16[256,256]{1,0:T(8,128)(2,1)S(1)}, u32[]{:S(2)}, u32[]{:S(2)}) collective-permute-start(bf16[256,256]{1,0:T(8,128)(2,1)S(1)} %get-tuple-element.109), channel_id=1, source_target_pairs={{0,8},{4,12},{8,0},{12,4},{1,9},{5,13},{9,1},{13,5},{2,10},{6,14},... | collective-permute-start | bytes 393224 | tf_op jit(solution)/shard_map/ppermute | solution.py:19
  63.2 7.1 %collective-permute-start.29 = (bf16[256,256]{1,0:T(8,128)(2,1)S(1)}, bf16[256,256]{1,0:T(8,128)(2,1)S(1)}, u32[]{:S(2)}, u32[]{:S(2)}) collective-permute-start(bf16[256,256]{1,0:T(8,128)(2,1)S(1)} %get-tuple-element.99), channel_id=1, source_target_pairs={{0,2},{1,3},{2,0},{3,1},{4,6},{5,7},{6,4},{7,5},{8,10},{9,11},{10,... | collective-permute-start | bytes 393224 | tf_op jit(solution)/shard_map/ppermute | solution.py:19
  64.3 6.2 %collective-permute-start.30 = (bf16[256,256]{1,0:T(8,128)(2,1)S(1)}, bf16[256,256]{1,0:T(8,128)(2,1)S(1)}, u32[]{:S(2)}, u32[]{:S(2)}) collective-permute-start(bf16[256,256]{1,0:T(8,128)(2,1)S(1)} %add_convert_fusion.4), channel_id=1, source_target_pairs={{0,12},{4,8},{8,4},{12,0},{1,13},{5,9},{9,5},{13,1},{2,14},{6,10},... | collective-permute-start | bytes 393224 | tf_op jit(solution)/shard_map/ppermute | solution.py:19
  66.0 5.5 %collective-permute-start.31 = (bf16[256,256]{1,0:T(8,128)(2,1)S(1)}, bf16[256,256]{1,0:T(8,128)(2,1)S(1)}, u32[]{:S(2)}, u32[]{:S(2)}) collective-permute-start(bf16[256,256]{1,0:T(8,128)(2,1)S(1)} %add_convert_fusion.3), channel_id=1, source_target_pairs={{0,1},{1,0},{2,3},{3,2},{4,5},{5,4},{6,7},{7,6},{8,9},{9,8},{10,11... | collective-permute-start | bytes 393224 | tf_op jit(solution)/shard_map/ppermute | solution.py:19
  71.6 7.2 %collective-permute-start.36 = (bf16[256,256]{1,0:T(8,128)(2,1)S(1)}, bf16[256,256]{1,0:T(8,128)(2,1)S(1)}, u32[]{:S(2)}, u32[]{:S(2)}) collective-permute-start(bf16[256,256]{1,0:T(8,128)(2,1)S(1)} %get-tuple-element.68), channel_id=1, source_target_pairs={{0,2},{1,3},{2,0},{3,1},{4,6},{5,7},{6,4},{7,5},{8,10},{9,11},{10,... | collective-permute-start | bytes 393224 | tf_op jit(solution)/shard_map/ppermute | solution.py:19
  72.8 6.4 %collective-permute-start.35 = (bf16[256,256]{1,0:T(8,128)(2,1)S(1)}, bf16[256,256]{1,0:T(8,128)(2,1)S(1)}, u32[]{:S(2)}, u32[]{:S(2)}) collective-permute-start(bf16[256,256]{1,0:T(8,128)(2,1)S(1)} %get-tuple-element.68), channel_id=1, source_target_pairs={{0,1},{1,0},{2,3},{3,2},{4,5},{5,4},{6,7},{7,6},{8,9},{9,8},{10,11... | collective-permute-start | bytes 393224 | tf_op jit(solution)/shard_map/ppermute | solution.py:19
  74.2 6.8 %collective-permute-start.34 = (bf16[256,256]{1,0:T(8,128)(2,1)S(1)}, bf16[256,256]{1,0:T(8,128)(2,1)S(1)}, u32[]{:S(2)}, u32[]{:S(2)}) collective-permute-start(bf16[256,256]{1,0:T(8,128)(2,1)S(1)} %get-tuple-element.68), channel_id=1, source_target_pairs={{0,12},{4,8},{8,4},{12,0},{1,13},{5,9},{9,5},{13,1},{2,14},{6,10},... | collective-permute-start | bytes 393224 | tf_op jit(solution)/shard_map/ppermute | solution.py:19
  75.0 15.2 %collective-permute-start.32 = (bf16[256,256]{1,0:T(8,128)(2,1)S(1)}, bf16[256,256]{1,0:T(8,128)(2,1)S(1)}, u32[]{:S(2)}, u32[]{:S(2)}) collective-permute-start(bf16[256,256]{1,0:T(8,128)(2,1)S(1)} %get-tuple-element.68), channel_id=1, source_target_pairs={{0,4},{4,0},{8,12},{12,8},{1,5},{5,1},{9,13},{13,9},{2,6},{6,2},{1... | collective-permute-start | bytes 393224 | tf_op jit(solution)/shard_map/ppermute | solution.py:19
  76.6 13.8 %collective-permute-start.33 = (bf16[256,256]{1,0:T(8,128)(2,1)S(1)}, bf16[256,256]{1,0:T(8,128)(2,1)S(1)}, u32[]{:S(2)}, u32[]{:S(2)}) collective-permute-start(bf16[256,256]{1,0:T(8,128)(2,1)S(1)} %get-tuple-element.68), channel_id=1, source_target_pairs={{0,8},{4,12},{8,0},{12,4},{1,9},{5,13},{9,1},{13,5},{2,10},{6,14},... | collective-permute-start | bytes 393224 | tf_op jit(solution)/shard_map/ppermute | solution.py:19
  79.2 6.5 %collective-permute-start.37 = (bf16[256,256]{1,0:T(8,128)(2,1)S(1)}, bf16[256,256]{1,0:T(8,128)(2,1)S(1)}, u32[]{:S(2)}, u32[]{:S(2)}) collective-permute-start(bf16[256,256]{1,0:T(8,128)(2,1)S(1)} %collective-permute-done.36), channel_id=1, source_target_pairs={{0,12},{4,8},{8,4},{12,0},{1,13},{5,9},{9,5},{13,1},{2,14},{6,10},... | collective-permute-start | bytes 393224 | tf_op jit(solution)/shard_map/ppermute | solution.py:19
  80.7 9.6 %collective-permute-start.38 = (bf16[256,256]{1,0:T(8,128)(2,1)S(1)}, bf16[256,256]{1,0:T(8,128)(2,1)S(1)}, u32[]{:S(2)}, u32[]{:S(2)}) collective-permute-start(bf16[256,256]{1,0:T(8,128)(2,1)S(1)} %collective-permute-done.36), channel_id=1, source_target_pairs={{0,1},{1,0},{2,3},{3,2},{4,5},{5,4},{6,7},{7,6},{8,9},{9,8},{10,11... | collective-permute-start | bytes 393224 | tf_op jit(solution)/shard_map/ppermute | solution.py:19
  81.0 10.9 %collective-permute-start.40 = (bf16[256,512]{1,0:T(8,128)(2,1)S(1)}, bf16[256,512]{1,0:T(8,128)(2,1)S(1)}, u32[]{:S(2)}, u32[]{:S(2)}) collective-permute-start(bf16[256,512]{1,0:T(8,128)(2,1)S(1)} %constant_dynamic-update-slice_fusion.20), channel_id=1, source_target_pairs={{0,8},{4,12},{8,0},{12,4},{1,9},{5,13},{9,1},{13,5},{2,10},{6,14},... | collective-permute-start | bytes 786440 | tf_op jit(solution)/shard_map/ppermute | solution.py:19
  85.7 8.9 %collective-permute-start.39 = (bf16[256,512]{1,0:T(8,128)(2,1)S(1)}, bf16[256,512]{1,0:T(8,128)(2,1)S(1)}, u32[]{:S(2)}, u32[]{:S(2)}) collective-permute-start(bf16[256,512]{1,0:T(8,128)(2,1)S(1)} %constant_dynamic-update-slice_fusion.20), channel_id=1, source_target_pairs={{0,4},{4,0},{8,12},{12,8},{1,5},{5,1},{9,13},{13,9},{2,6},{6,2},{1... | collective-permute-start | bytes 786440 | tf_op jit(solution)/shard_map/ppermute | solution.py:19
  90.3 6.4 %collective-permute-start.41 = (bf16[256,512]{1,0:T(8,128)(2,1)S(1)}, bf16[256,512]{1,0:T(8,128)(2,1)S(1)}, u32[]{:S(2)}, u32[]{:S(2)}) collective-permute-start(bf16[256,512]{1,0:T(8,128)(2,1)S(1)} %pad_maximum_fusion.1), channel_id=1, source_target_pairs={{0,1},{1,0},{2,3},{3,2},{4,5},{5,4},{6,7},{7,6},{8,9},{9,8},{10,11... | collective-permute-start | bytes 786440 | tf_op jit(solution)/shard_map/ppermute | solution.py:19
  91.3 5.4 %collective-permute-start.42 = (bf16[256,256]{1,0:T(8,128)(2,1)S(1)}, bf16[256,256]{1,0:T(8,128)(2,1)S(1)}, u32[]{:S(2)}, u32[]{:S(2)}) collective-permute-start(bf16[256,256]{1,0:T(8,128)(2,1)S(1)} %collective-permute-done.38), channel_id=1, source_target_pairs={{0,4},{4,0},{8,12},{12,8},{1,5},{5,1},{9,13},{13,9},{2,6},{6,2},{1... | collective-permute-start | bytes 393224 | tf_op jit(solution)/shard_map/ppermute | solution.py:19
  91.4 5.4 %collective-permute-start.43 = (bf16[256,256]{1,0:T(8,128)(2,1)S(1)}, bf16[256,256]{1,0:T(8,128)(2,1)S(1)}, u32[]{:S(2)}, u32[]{:S(2)}) collective-permute-start(bf16[256,256]{1,0:T(8,128)(2,1)S(1)} %collective-permute-done.38), channel_id=1, source_target_pairs={{0,8},{4,12},{8,0},{12,4},{1,9},{5,13},{9,1},{13,5},{2,10},{6,14},... | collective-permute-start | bytes 393224 | tf_op jit(solution)/shard_map/ppermute | solution.py:19
  97.5 15.0 %collective-permute-start.50 = (bf16[256,768]{1,0:T(8,128)(2,1)S(1)}, bf16[256,768]{1,0:T(8,128)(2,1)S(1)}, u32[]{:S(2)}, u32[]{:S(2)}) collective-permute-start(bf16[256,768]{1,0:T(8,128)(2,1)S(1)} %get-tuple-element.107.proj_ref), channel_id=1, source_target_pairs={{0,16},{16,0},{1,17},{17,1},{2,18},{18,2},{3,19},{19,3},{4,20},{20... | collective-permute-start | bytes 1179656 | tf_op jit(solution)/shard_map/ppermute | solution.py:19
  104.3 5.4 %collective-permute-start.47 = (f32[256]{0:T(256)S(1)}, f32[256]{0:T(256)S(1)}, u32[]{:S(2)}, u32[]{:S(2)}) collective-permute-start(f32[256]{0:T(256)S(1)} %add.172), channel_id=1, source_target_pairs={{0,3},{1,2},{2,1},{3,0},{4,7},{5,6},{6,5},{7,4},{8,11},{9,10},{10,... | collective-permute-start | bytes 3080 | tf_op jit(solution)/shard_map/ppermute | solution.py:19
  113.2 8.6 %collective-permute-start.56 = (bf16[256,512]{1,0:T(8,128)(2,1)S(1)}, bf16[256,512]{1,0:T(8,128)(2,1)S(1)}, u32[]{:S(2)}, u32[]{:S(2)}) collective-permute-start(bf16[256,512]{1,0:T(8,128)(2,1)S(1)} %slice.290), channel_id=1, source_target_pairs={{0,1},{1,0},{2,3},{3,2},{4,5},{5,4},{6,7},{7,6},{8,9},{9,8},{10,11... | collective-permute-start | bytes 786440 | tf_op jit(solution)/shard_map/ppermute | solution.py:19
  114.2 7.8 %collective-permute-start.58 = (bf16[256,256]{1,0:T(8,128)(2,1)S(1)}, bf16[256,256]{1,0:T(8,128)(2,1)S(1)}, u32[]{:S(2)}, u32[]{:S(2)}) collective-permute-start(bf16[256,256]{1,0:T(8,128)(2,1)S(1)} %get-tuple-element.114), channel_id=1, source_target_pairs={{0,4},{4,0},{8,12},{12,8},{1,5},{5,1},{9,13},{13,9},{2,6},{6,2},{1... | collective-permute-start | bytes 393224 | tf_op jit(solution)/shard_map/ppermute | solution.py:19
  114.6 7.4 %collective-permute-start.59 = (bf16[256,256]{1,0:T(8,128)(2,1)S(1)}, bf16[256,256]{1,0:T(8,128)(2,1)S(1)}, u32[]{:S(2)}, u32[]{:S(2)}) collective-permute-start(bf16[256,256]{1,0:T(8,128)(2,1)S(1)} %get-tuple-element.115), channel_id=1, source_target_pairs={{0,8},{4,12},{8,0},{12,4},{1,9},{5,13},{9,1},{13,5},{2,10},{6,14},... | collective-permute-start | bytes 393224 | tf_op jit(solution)/shard_map/ppermute | solution.py:19
  115.8 10.4 %collective-permute-start.54 = (bf16[256,512]{1,0:T(8,128)(2,1)S(1)}, bf16[256,512]{1,0:T(8,128)(2,1)S(1)}, u32[]{:S(2)}, u32[]{:S(2)}) collective-permute-start(bf16[256,512]{1,0:T(8,128)(2,1)S(1)} %get-tuple-element.104), channel_id=1, source_target_pairs={{0,4},{4,0},{8,12},{12,8},{1,5},{5,1},{9,13},{13,9},{2,6},{6,2},{1... | collective-permute-start | bytes 786440 | tf_op jit(solution)/shard_map/ppermute | solution.py:19
  117.3 9.8 %collective-permute-start.55 = (bf16[256,512]{1,0:T(8,128)(2,1)S(1)}, bf16[256,512]{1,0:T(8,128)(2,1)S(1)}, u32[]{:S(2)}, u32[]{:S(2)}) collective-permute-start(bf16[256,512]{1,0:T(8,128)(2,1)S(1)} %get-tuple-element.105), channel_id=1, source_target_pairs={{0,8},{4,12},{8,0},{12,4},{1,9},{5,13},{9,1},{13,5},{2,10},{6,14},... | collective-permute-start | bytes 786440 | tf_op jit(solution)/shard_map/ppermute | solution.py:19
  121.8 7.3 %collective-permute-start.57 = (bf16[256,256]{1,0:T(8,128)(2,1)S(1)}, bf16[256,256]{1,0:T(8,128)(2,1)S(1)}, u32[]{:S(2)}, u32[]{:S(2)}) collective-permute-start(bf16[256,256]{1,0:T(8,128)(2,1)S(1)} %get-tuple-element.95), channel_id=1, source_target_pairs={{0,12},{4,8},{8,4},{12,0},{1,13},{5,9},{9,5},{13,1},{2,14},{6,10},... | collective-permute-start | bytes 393224 | tf_op jit(solution)/shard_map/ppermute | solution.py:19
  123.1 9.6 %collective-permute-start.52 = (bf16[256,256]{1,0:T(8,128)(2,1)S(1)}, bf16[256,256]{1,0:T(8,128)(2,1)S(1)}, u32[]{:S(2)}, u32[]{:S(2)}) collective-permute-start(bf16[256,256]{1,0:T(8,128)(2,1)S(1)} %get-tuple-element.102), channel_id=1, source_target_pairs={{0,4},{4,0},{8,12},{12,8},{1,5},{5,1},{9,13},{13,9},{2,6},{6,2},{1... | collective-permute-start | bytes 393224 | tf_op jit(solution)/shard_map/ppermute | solution.py:19
  126.2 6.4 %collective-permute-start.53 = (bf16[256,256]{1,0:T(8,128)(2,1)S(1)}, bf16[256,256]{1,0:T(8,128)(2,1)S(1)}, u32[]{:S(2)}, u32[]{:S(2)}) collective-permute-start(bf16[256,256]{1,0:T(8,128)(2,1)S(1)} %get-tuple-element.103), channel_id=1, source_target_pairs={{0,8},{4,12},{8,0},{12,4},{1,9},{5,13},{9,1},{13,5},{2,10},{6,14},... | collective-permute-start | bytes 393224 | tf_op jit(solution)/shard_map/ppermute | solution.py:19
  129.3 7.4 %collective-permute-start.61 = (bf16[256,256]{1,0:T(8,128)(2,1)S(1)}, bf16[256,256]{1,0:T(8,128)(2,1)S(1)}, u32[]{:S(2)}, u32[]{:S(2)}) collective-permute-start(bf16[256,256]{1,0:T(8,128)(2,1)S(1)} %get-tuple-element.94), channel_id=1, source_target_pairs={{0,2},{1,3},{2,0},{3,1},{4,6},{5,7},{6,4},{7,5},{8,10},{9,11},{10,... | collective-permute-start | bytes 393224 | tf_op jit(solution)/shard_map/ppermute | solution.py:19
  130.3 6.5 %collective-permute-start.62 = (bf16[256,256]{1,0:T(8,128)(2,1)S(1)}, bf16[256,256]{1,0:T(8,128)(2,1)S(1)}, u32[]{:S(2)}, u32[]{:S(2)}) collective-permute-start(bf16[256,256]{1,0:T(8,128)(2,1)S(1)} %add_convert_fusion.1), channel_id=1, source_target_pairs={{0,12},{4,8},{8,4},{12,0},{1,13},{5,9},{9,5},{13,1},{2,14},{6,10},... | collective-permute-start | bytes 393224 | tf_op jit(solution)/shard_map/ppermute | solution.py:19
  131.5 5.6 %collective-permute-start.63 = (bf16[256,256]{1,0:T(8,128)(2,1)S(1)}, bf16[256,256]{1,0:T(8,128)(2,1)S(1)}, u32[]{:S(2)}, u32[]{:S(2)}) collective-permute-start(bf16[256,256]{1,0:T(8,128)(2,1)S(1)} %add_convert_fusion), channel_id=1, source_target_pairs={{0,1},{1,0},{2,3},{3,2},{4,5},{5,4},{6,7},{7,6},{8,9},{9,8},{10,11... | collective-permute-start | bytes 393224 | tf_op jit(solution)/shard_map/ppermute | solution.py:19
  (16 other events, 62.3 us)

commit v10 on v9

--- a/solution.py
+++ b/solution.py
@@ -56,7 +56,7 @@
     b[3, 2] = xor_move(b[0, 2], "row", 3)
     b[0, 3] = xor_move(b[0, 2], "feat", 1)
     for r in (1, 2):
-        pair = join(after(b[0, 1], b[0, 2]), b[0, 2])
+        pair = join(after(b[0, 1], b[0, 2], b[1, 0]) if r == 1 else b[0, 1], b[0, 2])
         b[r, 1], b[r, 2] = split(xor_move(pair, "row", r))
     b[3, 1], b[3, 3] = split(xor_move(join(b[3, 0], b[3, 2]), "feat", 1))
     for r in (1, 2):

time: 138 us -> 136 us (0.986)
  transfers between devices with their start and end apart: 64 -> 64, of which waited for: 35 -> 37; matrix products, arithmetic and copies ran while one was open for 6% -> 6% of each run, Pallas kernels for 3% -> 3%
where the time goes in v10:
time: 136 us
  starting transfers between devices  76.5 us (56%)
  waiting for transfers between devices  41.5 us (31%)
  matrix products  9.38 us (7%)
  Pallas kernels  3.92 us (3%)
  local copies, waits for them, and re-layouts  2.47 us (2%)
    ppermute x64, starting transfers between devices, xor_move(): return lax.ppermute(block, axis, [(i, i ^ mask) for i in range(count)])  76.5 us
    ppermute x64, waiting for transfers between devices, xor_move(): return lax.ppermute(block, axis, [(i, i ^ mask) for i in range(count)])  41.5 us
    dot_general x6, matrix products, on_device(): lax.dot_general(residue, groups[g], (((1,), (0,)), ((), ())), preferred_e...  4.76 us
    dot_general x6, matrix products, on_device(): lax.dot_general(join(*blocks), groups[g], (((1,), (1,)), ((), ())), prefe...  4.62 us
    pallas_call x1, Pallas kernels, regroup(): pl.pallas_call(kernel, out_shape=[jax.ShapeDtypeStruct((rows_here, len(pl...  3 us
  transfers between devices with their start and end apart: 64, of which 37 were waited for; matrix products, arithmetic and copies ran while one was open for 6% of the time, Pallas kernels for 3%

profile of v10, /device:TPU:0, one launch (start us, length us, event | category | flops | bytes accessed | tf_op | source)
XLA Modules:
  0.0 136.2 jit_solution(795761016151032575)
XLA Ops:
  1.7 4.1 %collective-permute-start.4 = (bf16[256,256]{1,0:T(8,128)(2,1)S(1)}, bf16[256,256]{1,0:T(8,128)(2,1)S(1)}, u32[]{:S(2)}, u32[]{:S(2)}) collective-permute-start(bf16[256,256]{1,0:T(8,128)(2,1)S(1)} %fusion.28), channel_id=1, source_target_pairs={{0,2},{1,3},{2,0},{3,1},{4,6},{5,7},{6,4},{7,5},{8,10},{9,11},{10,... | collective-permute-start | bytes 393224 | tf_op jit(solution)/shard_map/ppermute | solution.py:19
  5.8 1.6 %collective-permute-start.3 = (bf16[256,256]{1,0:T(8,128)(2,1)S(1)}, bf16[256,256]{1,0:T(8,128)(2,1)S(1)}, u32[]{:S(2)}, u32[]{:S(2)}) collective-permute-start(bf16[256,256]{1,0:T(8,128)(2,1)S(1)} %fusion.28), channel_id=1, source_target_pairs={{0,1},{1,0},{2,3},{3,2},{4,5},{5,4},{6,7},{7,6},{8,9},{9,8},{10,11... | collective-permute-start | bytes 393224 | tf_op jit(solution)/shard_map/ppermute | solution.py:19
  7.4 1.5 %collective-permute-start = (bf16[256,256]{1,0:T(8,128)(2,1)S(1)}, bf16[256,256]{1,0:T(8,128)(2,1)S(1)}, u32[]{:S(2)}, u32[]{:S(2)}) collective-permute-start(bf16[256,256]{1,0:T(8,128)(2,1)S(1)} %fusion.28), channel_id=1, source_target_pairs={{0,4},{4,0},{8,12},{12,8},{1,5},{5,1},{9,13},{13,9},{2,6},{6,2},{1... | collective-permute-start | bytes 393224 | tf_op jit(solution)/shard_map/ppermute | solution.py:19
  8.9 1.5 %collective-permute-start.2 = (bf16[256,256]{1,0:T(8,128)(2,1)S(1)}, bf16[256,256]{1,0:T(8,128)(2,1)S(1)}, u32[]{:S(2)}, u32[]{:S(2)}) collective-permute-start(bf16[256,256]{1,0:T(8,128)(2,1)S(1)} %fusion.28), channel_id=1, source_target_pairs={{0,12},{4,8},{8,4},{12,0},{1,13},{5,9},{9,5},{13,1},{2,14},{6,10},... | collective-permute-start | bytes 393224 | tf_op jit(solution)/shard_map/ppermute | solution.py:19
  10.9 1.3 collective-permute-done.4
  12.9 2.4 %collective-permute-start.5 = (bf16[256,256]{1,0:T(8,128)(2,1)S(1)}, bf16[256,256]{1,0:T(8,128)(2,1)S(1)}, u32[]{:S(2)}, u32[]{:S(2)}) collective-permute-start(bf16[256,256]{1,0:T(8,128)(2,1)S(1)} %collective-permute-done.4), channel_id=1, source_target_pairs={{0,12},{4,8},{8,4},{12,0},{1,13},{5,9},{9,5},{13,1},{2,14},{6,10},... | collective-permute-start | bytes 393224 | tf_op jit(solution)/shard_map/ppermute | solution.py:19
  15.3 3.0 %regroup.1 = (bf16[768,1536]{1,0:T(8,128)(2,1)S(1)}, bf16[768,1536]{1,0:T(8,128)(2,1)S(1)}, bf16[768,1024]{1,0:T(8,128)(2,1)S(1)}) custom-call(bf16[768,4096]{1,0:T(8,128)(2,1)} %bitcast.37), custom_call_target="tpu_custom_call" | custom-call | bytes 12582912 | tf_op jit(solution)/shard_map/regroup/pallas_call | solution.py:140
  21.9 1.5 %collective-permute-start.10 = (bf16[256,256]{1,0:T(8,128)(2,1)S(1)}, bf16[256,256]{1,0:T(8,128)(2,1)S(1)}, u32[]{:S(2)}, u32[]{:S(2)}) collective-permute-start(bf16[256,256]{1,0:T(8,128)(2,1)S(1)} %collective-permute-done.6), channel_id=1, source_target_pairs={{0,4},{4,0},{8,12},{12,8},{1,5},{5,1},{9,13},{13,9},{2,6},{6,2},{1... | collective-permute-start | bytes 393224 | tf_op jit(solution)/shard_map/ppermute | solution.py:19
  23.5 1.5 %collective-permute-start.11 = (bf16[256,256]{1,0:T(8,128)(2,1)S(1)}, bf16[256,256]{1,0:T(8,128)(2,1)S(1)}, u32[]{:S(2)}, u32[]{:S(2)}) collective-permute-start(bf16[256,256]{1,0:T(8,128)(2,1)S(1)} %collective-permute-done.6), channel_id=1, source_target_pairs={{0,8},{4,12},{8,0},{12,4},{1,9},{5,13},{9,1},{13,5},{2,10},{6,14},... | collective-permute-start | bytes 393224 | tf_op jit(solution)/shard_map/ppermute | solution.py:19
  25.0 2.5 %collective-permute-done.8 = bf16[256,512]{1,0:T(8,128)(2,1)S(1)} collective-permute-done((bf16[256,512]{1,0:T(8,128)(2,1)S(1)}, bf16[256,512]{1,0:T(8,128)(2,1)S(1)}, u32[]{:S(2)}, u32[]{:S(2)}) %collective-permute-start.8) | collective-permute-done | bytes 262176 | tf_op jit(solution)/shard_map/ppermute | solution.py:19
  29.9 1.6 %collective-permute-start.12 = (f32[256]{0:T(256)S(1)}, f32[256]{0:T(256)S(1)}, u32[]{:S(2)}, u32[]{:S(2)}) collective-permute-start(f32[256]{0:T(256)S(1)} %get-tuple-element.112), channel_id=1, source_target_pairs={{0,12},{4,8},{8,4},{12,0},{1,13},{5,9},{9,5},{13,1},{2,14},{6,10},... | collective-permute-start | bytes 3080 | tf_op jit(solution)/shard_map/ppermute | solution.py:19
  32.3 1.2 collective-permute-start.14
  35.9 2.8 %collective-permute-start.15 = (f32[256]{0:T(256)S(1)}, f32[256]{0:T(256)S(1)}, u32[]{:S(2)}, u32[]{:S(2)}) collective-permute-start(f32[256]{0:T(256)S(1)} %add.148), channel_id=1, source_target_pairs={{0,3},{1,2},{2,1},{3,0},{4,7},{5,6},{6,5},{7,4},{8,11},{9,10},{10,... | collective-permute-start | bytes 3080 | tf_op jit(solution)/shard_map/ppermute | solution.py:19
  38.9 1.3 collective-permute-start.17
  41.2 1.9 %collective-permute-done.16 = f32[256]{0:T(256)S(1)} collective-permute-done((f32[256]{0:T(256)S(1)}, f32[256]{0:T(256)S(1)}, u32[]{:S(2)}, u32[]{:S(2)}) %collective-permute-start.16) | collective-permute-done | bytes 1056 | tf_op jit(solution)/shard_map/ppermute | solution.py:19
  46.0 1.5 %collective-permute-start.26 = (bf16[256,256]{1,0:T(8,128)(2,1)S(1)}, bf16[256,256]{1,0:T(8,128)(2,1)S(1)}, u32[]{:S(2)}, u32[]{:S(2)}) collective-permute-start(bf16[256,256]{1,0:T(8,128)(2,1)S(1)} %get-tuple-element.116), channel_id=1, source_target_pairs={{0,4},{4,0},{8,12},{12,8},{1,5},{5,1},{9,13},{13,9},{2,6},{6,2},{1... | collective-permute-start | bytes 393224 | tf_op jit(solution)/shard_map/ppermute | solution.py:19
  47.4 1.5 %collective-permute-start.27 = (bf16[256,256]{1,0:T(8,128)(2,1)S(1)}, bf16[256,256]{1,0:T(8,128)(2,1)S(1)}, u32[]{:S(2)}, u32[]{:S(2)}) collective-permute-start(bf16[256,256]{1,0:T(8,128)(2,1)S(1)} %get-tuple-element.117), channel_id=1, source_target_pairs={{0,8},{4,12},{8,0},{12,4},{1,9},{5,13},{9,1},{13,5},{2,10},{6,14},... | collective-permute-start | bytes 393224 | tf_op jit(solution)/shard_map/ppermute | solution.py:19
  51.9 1.6 %collective-permute-done.24 = bf16[256,512]{1,0:T(8,128)(2,1)S(1)} collective-permute-done((bf16[256,512]{1,0:T(8,128)(2,1)S(1)}, bf16[256,512]{1,0:T(8,128)(2,1)S(1)}, u32[]{:S(2)}, u32[]{:S(2)}) %collective-permute-start.24) | collective-permute-done | bytes 262176 | tf_op jit(solution)/shard_map/ppermute | solution.py:19
  53.6 2.5 %collective-permute-start.25 = (bf16[256,256]{1,0:T(8,128)(2,1)S(1)}, bf16[256,256]{1,0:T(8,128)(2,1)S(1)}, u32[]{:S(2)}, u32[]{:S(2)}) collective-permute-start(bf16[256,256]{1,0:T(8,128)(2,1)S(1)} %get-tuple-element.100), channel_id=1, source_target_pairs={{0,12},{4,8},{8,4},{12,0},{1,13},{5,9},{9,5},{13,1},{2,14},{6,10},... | collective-permute-start | bytes 393224 | tf_op jit(solution)/shard_map/ppermute | solution.py:19
  58.4 1.3 collective-permute-start.21
  62.1 2.1 %collective-permute-start.29 = (bf16[256,256]{1,0:T(8,128)(2,1)S(1)}, bf16[256,256]{1,0:T(8,128)(2,1)S(1)}, u32[]{:S(2)}, u32[]{:S(2)}) collective-permute-start(bf16[256,256]{1,0:T(8,128)(2,1)S(1)} %get-tuple-element.99), channel_id=1, source_target_pairs={{0,2},{1,3},{2,0},{3,1},{4,6},{5,7},{6,4},{7,5},{8,10},{9,11},{10,... | collective-permute-start | bytes 393224 | tf_op jit(solution)/shard_map/ppermute | solution.py:19
  64.2 1.5 %collective-permute-start.30 = (bf16[256,256]{1,0:T(8,128)(2,1)S(1)}, bf16[256,256]{1,0:T(8,128)(2,1)S(1)}, u32[]{:S(2)}, u32[]{:S(2)}) collective-permute-start(bf16[256,256]{1,0:T(8,128)(2,1)S(1)} %add_convert_fusion.4), channel_id=1, source_target_pairs={{0,12},{4,8},{8,4},{12,0},{1,13},{5,9},{9,5},{13,1},{2,14},{6,10},... | collective-permute-start | bytes 393224 | tf_op jit(solution)/shard_map/ppermute | solution.py:19
  66.7 2.7 %collective-permute-done.29 = bf16[256,256]{1,0:T(8,128)(2,1)S(1)} collective-permute-done((bf16[256,256]{1,0:T(8,128)(2,1)S(1)}, bf16[256,256]{1,0:T(8,128)(2,1)S(1)}, u32[]{:S(2)}, u32[]{:S(2)}) %collective-permute-start.29) | collective-permute-done | bytes 131104 | tf_op jit(solution)/shard_map/ppermute | solution.py:19
  73.0 2.2 %collective-permute-start.35 = (bf16[256,256]{1,0:T(8,128)(2,1)S(1)}, bf16[256,256]{1,0:T(8,128)(2,1)S(1)}, u32[]{:S(2)}, u32[]{:S(2)}) collective-permute-start(bf16[256,256]{1,0:T(8,128)(2,1)S(1)} %get-tuple-element.68), channel_id=1, source_target_pairs={{0,1},{1,0},{2,3},{3,2},{4,5},{5,4},{6,7},{7,6},{8,9},{9,8},{10,11... | collective-permute-start | bytes 393224 | tf_op jit(solution)/shard_map/ppermute | solution.py:19
  75.2 1.2 collective-permute-start.34
  76.3 2.1 %collective-permute-done.36 = bf16[256,256]{1,0:T(8,128)(2,1)S(1)} collective-permute-done((bf16[256,256]{1,0:T(8,128)(2,1)S(1)}, bf16[256,256]{1,0:T(8,128)(2,1)S(1)}, u32[]{:S(2)}, u32[]{:S(2)}) %collective-permute-start.36) | collective-permute-done | bytes 131104 | tf_op jit(solution)/shard_map/ppermute | solution.py:19
  78.4 1.5 %collective-permute-start.37 = (bf16[256,256]{1,0:T(8,128)(2,1)S(1)}, bf16[256,256]{1,0:T(8,128)(2,1)S(1)}, u32[]{:S(2)}, u32[]{:S(2)}) collective-permute-start(bf16[256,256]{1,0:T(8,128)(2,1)S(1)} %collective-permute-done.36), channel_id=1, source_target_pairs={{0,12},{4,8},{8,4},{12,0},{1,13},{5,9},{9,5},{13,1},{2,14},{6,10},... | collective-permute-start | bytes 393224 | tf_op jit(solution)/shard_map/ppermute | solution.py:19
  79.9 1.2 collective-permute-start.33
  83.2 2.2 %collective-permute-done.37 = bf16[256,256]{1,0:T(8,128)(2,1)S(1)} collective-permute-done((bf16[256,256]{1,0:T(8,128)(2,1)S(1)}, bf16[256,256]{1,0:T(8,128)(2,1)S(1)}, u32[]{:S(2)}, u32[]{:S(2)}) %collective-permute-start.37) | collective-permute-done | bytes 131104 | tf_op jit(solution)/shard_map/ppermute | solution.py:19
  85.6 1.9 %collective-permute-done.33 = bf16[256,256]{1,0:T(8,128)(2,1)S(1)} collective-permute-done((bf16[256,256]{1,0:T(8,128)(2,1)S(1)}, bf16[256,256]{1,0:T(8,128)(2,1)S(1)}, u32[]{:S(2)}, u32[]{:S(2)}) %collective-permute-start.33) | collective-permute-done | bytes 131104 | tf_op jit(solution)/shard_map/ppermute | solution.py:19
  88.4 1.3 collective-permute-start.42
  90.5 1.7 %collective-permute-done.40 = bf16[256,512]{1,0:T(8,128)(2,1)S(1)} collective-permute-done((bf16[256,512]{1,0:T(8,128)(2,1)S(1)}, bf16[256,512]{1,0:T(8,128)(2,1)S(1)}, u32[]{:S(2)}, u32[]{:S(2)}) %collective-permute-start.40) | collective-permute-done | bytes 262176 | tf_op jit(solution)/shard_map/ppermute | solution.py:19
  93.4 1.2 collective-permute-done.43
  95.4 1.5 %collective-permute-start.44 = (f32[256]{0:T(256)S(1)}, f32[256]{0:T(256)S(1)}, u32[]{:S(2)}, u32[]{:S(2)}) collective-permute-start(f32[256]{0:T(256)S(1)} %get-tuple-element.106), channel_id=1, source_target_pairs={{0,12},{4,8},{8,4},{12,0},{1,13},{5,9},{9,5},{13,1},{2,14},{6,10},... | collective-permute-start | bytes 3080 | tf_op jit(solution)/shard_map/ppermute | solution.py:19
  97.7 1.2 collective-permute-start.46
  101.3 1.7 %collective-permute-start.47 = (f32[256]{0:T(256)S(1)}, f32[256]{0:T(256)S(1)}, u32[]{:S(2)}, u32[]{:S(2)}) collective-permute-start(f32[256]{0:T(256)S(1)} %add.172), channel_id=1, source_target_pairs={{0,3},{1,2},{2,1},{3,0},{4,7},{5,6},{6,5},{7,4},{8,11},{9,10},{10,... | collective-permute-start | bytes 3080 | tf_op jit(solution)/shard_map/ppermute | solution.py:19
  103.1 2.6 %collective-permute-start.49 = (f32[256]{0:T(256)S(1)}, f32[256]{0:T(256)S(1)}, u32[]{:S(2)}, u32[]{:S(2)}) collective-permute-start(f32[256]{0:T(256)S(1)} %add.172), channel_id=1, source_target_pairs={{0,1},{1,0},{2,3},{3,2},{4,5},{5,4},{6,7},{7,6},{8,9},{9,8},{10,11... | collective-permute-start | bytes 3080 | tf_op jit(solution)/shard_map/ppermute | solution.py:19
  109.5 1.8 %collective-permute-start.56 = (bf16[256,512]{1,0:T(8,128)(2,1)S(1)}, bf16[256,512]{1,0:T(8,128)(2,1)S(1)}, u32[]{:S(2)}, u32[]{:S(2)}) collective-permute-start(bf16[256,512]{1,0:T(8,128)(2,1)S(1)} %slice.290), channel_id=1, source_target_pairs={{0,1},{1,0},{2,3},{3,2},{4,5},{5,4},{6,7},{7,6},{8,9},{9,8},{10,11... | collective-permute-start | bytes 786440 | tf_op jit(solution)/shard_map/ppermute | solution.py:19
  111.3 1.2 collective-permute-start.58
  114.2 1.3 collective-permute-start.54
  118.1 1.8 %collective-permute-start.57 = (bf16[256,256]{1,0:T(8,128)(2,1)S(1)}, bf16[256,256]{1,0:T(8,128)(2,1)S(1)}, u32[]{:S(2)}, u32[]{:S(2)}) collective-permute-start(bf16[256,256]{1,0:T(8,128)(2,1)S(1)} %get-tuple-element.95), channel_id=1, source_target_pairs={{0,12},{4,8},{8,4},{12,0},{1,13},{5,9},{9,5},{13,1},{2,14},{6,10},... | collective-permute-start | bytes 393224 | tf_op jit(solution)/shard_map/ppermute | solution.py:19
  119.9 1.5 %collective-permute-start.60 = (bf16[256,256]{1,0:T(8,128)(2,1)S(1)}, bf16[256,256]{1,0:T(8,128)(2,1)S(1)}, u32[]{:S(2)}, u32[]{:S(2)}) collective-permute-start(bf16[256,256]{1,0:T(8,128)(2,1)S(1)} %add_convert_fusion.2), channel_id=1, source_target_pairs={{0,1},{1,0},{2,3},{3,2},{4,5},{5,4},{6,7},{7,6},{8,9},{9,8},{10,11... | collective-permute-start | bytes 393224 | tf_op jit(solution)/shard_map/ppermute | solution.py:19
  121.5 1.3 collective-permute-start.52
  123.5 1.2 collective-permute-start.53
  125.7 1.3 collective-permute-done.57
  127.8 1.8 %collective-permute-start.62 = (bf16[256,256]{1,0:T(8,128)(2,1)S(1)}, bf16[256,256]{1,0:T(8,128)(2,1)S(1)}, u32[]{:S(2)}, u32[]{:S(2)}) collective-permute-start(bf16[256,256]{1,0:T(8,128)(2,1)S(1)} %add_convert_fusion.1), channel_id=1, source_target_pairs={{0,12},{4,8},{8,4},{12,0},{1,13},{5,9},{9,5},{13,1},{2,14},{6,10},... | collective-permute-start | bytes 393224 | tf_op jit(solution)/shard_map/ppermute | solution.py:19
  129.6 1.7 %collective-permute-start.63 = (bf16[256,256]{1,0:T(8,128)(2,1)S(1)}, bf16[256,256]{1,0:T(8,128)(2,1)S(1)}, u32[]{:S(2)}, u32[]{:S(2)}) collective-permute-start(bf16[256,256]{1,0:T(8,128)(2,1)S(1)} %add_convert_fusion), channel_id=1, source_target_pairs={{0,1},{1,0},{2,3},{3,2},{4,5},{5,4},{6,7},{7,6},{8,9},{9,8},{10,11... | collective-permute-start | bytes 393224 | tf_op jit(solution)/shard_map/ppermute | solution.py:19
  131.3 3.0 %collective-permute-done.61 = bf16[256,256]{1,0:T(8,128)(2,1)S(1)} collective-permute-done((bf16[256,256]{1,0:T(8,128)(2,1)S(1)}, bf16[256,256]{1,0:T(8,128)(2,1)S(1)}, u32[]{:S(2)}, u32[]{:S(2)}) %collective-permute-start.61) | collective-permute-done | bytes 131104 | tf_op jit(solution)/shard_map/ppermute | solution.py:19
  (167 shorter events, 49.2 us)
Async XLA Ops:
  1.7 10.5 %collective-permute-start.4 = (bf16[256,256]{1,0:T(8,128)(2,1)S(1)}, bf16[256,256]{1,0:T(8,128)(2,1)S(1)}, u32[]{:S(2)}, u32[]{:S(2)}) collective-permute-start(bf16[256,256]{1,0:T(8,128)(2,1)S(1)} %fusion.28), channel_id=1, source_target_pairs={{0,2},{1,3},{2,0},{3,1},{4,6},{5,7},{6,4},{7,5},{8,10},{9,11},{10,... | collective-permute-start | bytes 393224 | tf_op jit(solution)/shard_map/ppermute | solution.py:19
  5.8 7.0 %collective-permute-start.3 = (bf16[256,256]{1,0:T(8,128)(2,1)S(1)}, bf16[256,256]{1,0:T(8,128)(2,1)S(1)}, u32[]{:S(2)}, u32[]{:S(2)}) collective-permute-start(bf16[256,256]{1,0:T(8,128)(2,1)S(1)} %fusion.28), channel_id=1, source_target_pairs={{0,1},{1,0},{2,3},{3,2},{4,5},{5,4},{6,7},{7,6},{8,9},{9,8},{10,11... | collective-permute-start | bytes 393224 | tf_op jit(solution)/shard_map/ppermute | solution.py:19
  7.4 10.9 %collective-permute-start = (bf16[256,256]{1,0:T(8,128)(2,1)S(1)}, bf16[256,256]{1,0:T(8,128)(2,1)S(1)}, u32[]{:S(2)}, u32[]{:S(2)}) collective-permute-start(bf16[256,256]{1,0:T(8,128)(2,1)S(1)} %fusion.28), channel_id=1, source_target_pairs={{0,4},{4,0},{8,12},{12,8},{1,5},{5,1},{9,13},{13,9},{2,6},{6,2},{1... | collective-permute-start | bytes 393224 | tf_op jit(solution)/shard_map/ppermute | solution.py:19
  8.9 10.0 %collective-permute-start.2 = (bf16[256,256]{1,0:T(8,128)(2,1)S(1)}, bf16[256,256]{1,0:T(8,128)(2,1)S(1)}, u32[]{:S(2)}, u32[]{:S(2)}) collective-permute-start(bf16[256,256]{1,0:T(8,128)(2,1)S(1)} %fusion.28), channel_id=1, source_target_pairs={{0,12},{4,8},{8,4},{12,0},{1,13},{5,9},{9,5},{13,1},{2,14},{6,10},... | collective-permute-start | bytes 393224 | tf_op jit(solution)/shard_map/ppermute | solution.py:19
  10.4 9.7 %collective-permute-start.1 = (bf16[256,256]{1,0:T(8,128)(2,1)S(1)}, bf16[256,256]{1,0:T(8,128)(2,1)S(1)}, u32[]{:S(2)}, u32[]{:S(2)}) collective-permute-start(bf16[256,256]{1,0:T(8,128)(2,1)S(1)} %fusion.28), channel_id=1, source_target_pairs={{0,8},{4,12},{8,0},{12,4},{1,9},{5,13},{9,1},{13,5},{2,10},{6,14},... | collective-permute-start | bytes 393224 | tf_op jit(solution)/shard_map/ppermute | solution.py:19
  12.3 7.8 %collective-permute-start.6 = (bf16[256,256]{1,0:T(8,128)(2,1)S(1)}, bf16[256,256]{1,0:T(8,128)(2,1)S(1)}, u32[]{:S(2)}, u32[]{:S(2)}) collective-permute-start(bf16[256,256]{1,0:T(8,128)(2,1)S(1)} %collective-permute-done.4), channel_id=1, source_target_pairs={{0,1},{1,0},{2,3},{3,2},{4,5},{5,4},{6,7},{7,6},{8,9},{9,8},{10,11... | collective-permute-start | bytes 393224 | tf_op jit(solution)/shard_map/ppermute | solution.py:19
  12.9 7.2 %collective-permute-start.5 = (bf16[256,256]{1,0:T(8,128)(2,1)S(1)}, bf16[256,256]{1,0:T(8,128)(2,1)S(1)}, u32[]{:S(2)}, u32[]{:S(2)}) collective-permute-start(bf16[256,256]{1,0:T(8,128)(2,1)S(1)} %collective-permute-done.4), channel_id=1, source_target_pairs={{0,12},{4,8},{8,4},{12,0},{1,13},{5,9},{9,5},{13,1},{2,14},{6,10},... | collective-permute-start | bytes 393224 | tf_op jit(solution)/shard_map/ppermute | solution.py:19
  18.4 9.1 %collective-permute-start.8 = (bf16[256,512]{1,0:T(8,128)(2,1)S(1)}, bf16[256,512]{1,0:T(8,128)(2,1)S(1)}, u32[]{:S(2)}, u32[]{:S(2)}) collective-permute-start(bf16[256,512]{1,0:T(8,128)(2,1)S(1)} %get-tuple-element.132), channel_id=1, source_target_pairs={{0,8},{4,12},{8,0},{12,4},{1,9},{5,13},{9,1},{13,5},{2,10},{6,14},... | collective-permute-start | bytes 786440 | tf_op jit(solution)/shard_map/ppermute | solution.py:19
  19.0 8.8 %collective-permute-start.7 = (bf16[256,512]{1,0:T(8,128)(2,1)S(1)}, bf16[256,512]{1,0:T(8,128)(2,1)S(1)}, u32[]{:S(2)}, u32[]{:S(2)}) collective-permute-start(bf16[256,512]{1,0:T(8,128)(2,1)S(1)} %get-tuple-element.133), channel_id=1, source_target_pairs={{0,4},{4,0},{8,12},{12,8},{1,5},{5,1},{9,13},{13,9},{2,6},{6,2},{1... | collective-permute-start | bytes 786440 | tf_op jit(solution)/shard_map/ppermute | solution.py:19
  21.0 7.7 %collective-permute-start.9 = (bf16[256,512]{1,0:T(8,128)(2,1)S(1)}, bf16[256,512]{1,0:T(8,128)(2,1)S(1)}, u32[]{:S(2)}, u32[]{:S(2)}) collective-permute-start(bf16[256,512]{1,0:T(8,128)(2,1)S(1)} %pad_maximum_fusion.4), channel_id=1, source_target_pairs={{0,1},{1,0},{2,3},{3,2},{4,5},{5,4},{6,7},{7,6},{8,9},{9,8},{10,11... | collective-permute-start | bytes 786440 | tf_op jit(solution)/shard_map/ppermute | solution.py:19
  21.9 7.2 %collective-permute-start.10 = (bf16[256,256]{1,0:T(8,128)(2,1)S(1)}, bf16[256,256]{1,0:T(8,128)(2,1)S(1)}, u32[]{:S(2)}, u32[]{:S(2)}) collective-permute-start(bf16[256,256]{1,0:T(8,128)(2,1)S(1)} %collective-permute-done.6), channel_id=1, source_target_pairs={{0,4},{4,0},{8,12},{12,8},{1,5},{5,1},{9,13},{13,9},{2,6},{6,2},{1... | collective-permute-start | bytes 393224 | tf_op jit(solution)/shard_map/ppermute | solution.py:19
  23.5 5.7 %collective-permute-start.11 = (bf16[256,256]{1,0:T(8,128)(2,1)S(1)}, bf16[256,256]{1,0:T(8,128)(2,1)S(1)}, u32[]{:S(2)}, u32[]{:S(2)}) collective-permute-start(bf16[256,256]{1,0:T(8,128)(2,1)S(1)} %collective-permute-done.6), channel_id=1, source_target_pairs={{0,8},{4,12},{8,0},{12,4},{1,9},{5,13},{9,1},{13,5},{2,10},{6,14},... | collective-permute-start | bytes 393224 | tf_op jit(solution)/shard_map/ppermute | solution.py:19
  29.8 14.5 %collective-permute-start.18 = (bf16[256,768]{1,0:T(8,128)(2,1)S(1)}, bf16[256,768]{1,0:T(8,128)(2,1)S(1)}, u32[]{:S(2)}, u32[]{:S(2)}) collective-permute-start(bf16[256,768]{1,0:T(8,128)(2,1)S(1)} %get-tuple-element.113), channel_id=1, source_target_pairs={{0,16},{16,0},{1,17},{17,1},{2,18},{18,2},{3,19},{19,3},{4,20},{20... | collective-permute-start | bytes 1179656 | tf_op jit(solution)/shard_map/ppermute | solution.py:19
  35.9 5.4 %collective-permute-start.15 = (f32[256]{0:T(256)S(1)}, f32[256]{0:T(256)S(1)}, u32[]{:S(2)}, u32[]{:S(2)}) collective-permute-start(f32[256]{0:T(256)S(1)} %add.148), channel_id=1, source_target_pairs={{0,3},{1,2},{2,1},{3,0},{4,7},{5,6},{6,5},{7,4},{8,11},{9,10},{10,... | collective-permute-start | bytes 3080 | tf_op jit(solution)/shard_map/ppermute | solution.py:19
  45.0 8.5 %collective-permute-start.24 = (bf16[256,512]{1,0:T(8,128)(2,1)S(1)}, bf16[256,512]{1,0:T(8,128)(2,1)S(1)}, u32[]{:S(2)}, u32[]{:S(2)}) collective-permute-start(bf16[256,512]{1,0:T(8,128)(2,1)S(1)} %slice.265), channel_id=1, source_target_pairs={{0,1},{1,0},{2,3},{3,2},{4,5},{5,4},{6,7},{7,6},{8,9},{9,8},{10,11... | collective-permute-start | bytes 786440 | tf_op jit(solution)/shard_map/ppermute | solution.py:19
  46.0 10.1 %collective-permute-start.26 = (bf16[256,256]{1,0:T(8,128)(2,1)S(1)}, bf16[256,256]{1,0:T(8,128)(2,1)S(1)}, u32[]{:S(2)}, u32[]{:S(2)}) collective-permute-start(bf16[256,256]{1,0:T(8,128)(2,1)S(1)} %get-tuple-element.116), channel_id=1, source_target_pairs={{0,4},{4,0},{8,12},{12,8},{1,5},{5,1},{9,13},{13,9},{2,6},{6,2},{1... | collective-permute-start | bytes 393224 | tf_op jit(solution)/shard_map/ppermute | solution.py:19
  47.4 8.6 %collective-permute-start.27 = (bf16[256,256]{1,0:T(8,128)(2,1)S(1)}, bf16[256,256]{1,0:T(8,128)(2,1)S(1)}, u32[]{:S(2)}, u32[]{:S(2)}) collective-permute-start(bf16[256,256]{1,0:T(8,128)(2,1)S(1)} %get-tuple-element.117), channel_id=1, source_target_pairs={{0,8},{4,12},{8,0},{12,4},{1,9},{5,13},{9,1},{13,5},{2,10},{6,14},... | collective-permute-start | bytes 393224 | tf_op jit(solution)/shard_map/ppermute | solution.py:19
  49.9 8.5 %collective-permute-start.22 = (bf16[256,512]{1,0:T(8,128)(2,1)S(1)}, bf16[256,512]{1,0:T(8,128)(2,1)S(1)}, u32[]{:S(2)}, u32[]{:S(2)}) collective-permute-start(bf16[256,512]{1,0:T(8,128)(2,1)S(1)} %get-tuple-element.110), channel_id=1, source_target_pairs={{0,4},{4,0},{8,12},{12,8},{1,5},{5,1},{9,13},{13,9},{2,6},{6,2},{1... | collective-permute-start | bytes 786440 | tf_op jit(solution)/shard_map/ppermute | solution.py:19
  50.5 10.1 %collective-permute-start.23 = (bf16[256,512]{1,0:T(8,128)(2,1)S(1)}, bf16[256,512]{1,0:T(8,128)(2,1)S(1)}, u32[]{:S(2)}, u32[]{:S(2)}) collective-permute-start(bf16[256,512]{1,0:T(8,128)(2,1)S(1)} %get-tuple-element.111), channel_id=1, source_target_pairs={{0,8},{4,12},{8,0},{12,4},{1,9},{5,13},{9,1},{13,5},{2,10},{6,14},... | collective-permute-start | bytes 786440 | tf_op jit(solution)/shard_map/ppermute | solution.py:19
  53.6 8.4 %collective-permute-start.25 = (bf16[256,256]{1,0:T(8,128)(2,1)S(1)}, bf16[256,256]{1,0:T(8,128)(2,1)S(1)}, u32[]{:S(2)}, u32[]{:S(2)}) collective-permute-start(bf16[256,256]{1,0:T(8,128)(2,1)S(1)} %get-tuple-element.100), channel_id=1, source_target_pairs={{0,12},{4,8},{8,4},{12,0},{1,13},{5,9},{9,5},{13,1},{2,14},{6,10},... | collective-permute-start | bytes 393224 | tf_op jit(solution)/shard_map/ppermute | solution.py:19
  57.1 9.6 %collective-permute-start.20 = (bf16[256,256]{1,0:T(8,128)(2,1)S(1)}, bf16[256,256]{1,0:T(8,128)(2,1)S(1)}, u32[]{:S(2)}, u32[]{:S(2)}) collective-permute-start(bf16[256,256]{1,0:T(8,128)(2,1)S(1)} %get-tuple-element.108), channel_id=1, source_target_pairs={{0,4},{4,0},{8,12},{12,8},{1,5},{5,1},{9,13},{13,9},{2,6},{6,2},{1... | collective-permute-start | bytes 393224 | tf_op jit(solution)/shard_map/ppermute | solution.py:19
  58.4 8.3 %collective-permute-start.21 = (bf16[256,256]{1,0:T(8,128)(2,1)S(1)}, bf16[256,256]{1,0:T(8,128)(2,1)S(1)}, u32[]{:S(2)}, u32[]{:S(2)}) collective-permute-start(bf16[256,256]{1,0:T(8,128)(2,1)S(1)} %get-tuple-element.109), channel_id=1, source_target_pairs={{0,8},{4,12},{8,0},{12,4},{1,9},{5,13},{9,1},{13,5},{2,10},{6,14},... | collective-permute-start | bytes 393224 | tf_op jit(solution)/shard_map/ppermute | solution.py:19
  62.1 7.3 %collective-permute-start.29 = (bf16[256,256]{1,0:T(8,128)(2,1)S(1)}, bf16[256,256]{1,0:T(8,128)(2,1)S(1)}, u32[]{:S(2)}, u32[]{:S(2)}) collective-permute-start(bf16[256,256]{1,0:T(8,128)(2,1)S(1)} %get-tuple-element.99), channel_id=1, source_target_pairs={{0,2},{1,3},{2,0},{3,1},{4,6},{5,7},{6,4},{7,5},{8,10},{9,11},{10,... | collective-permute-start | bytes 393224 | tf_op jit(solution)/shard_map/ppermute | solution.py:19
  64.2 5.9 %collective-permute-start.30 = (bf16[256,256]{1,0:T(8,128)(2,1)S(1)}, bf16[256,256]{1,0:T(8,128)(2,1)S(1)}, u32[]{:S(2)}, u32[]{:S(2)}) collective-permute-start(bf16[256,256]{1,0:T(8,128)(2,1)S(1)} %add_convert_fusion.4), channel_id=1, source_target_pairs={{0,12},{4,8},{8,4},{12,0},{1,13},{5,9},{9,5},{13,1},{2,14},{6,10},... | collective-permute-start | bytes 393224 | tf_op jit(solution)/shard_map/ppermute | solution.py:19
  70.9 7.4 %collective-permute-start.36 = (bf16[256,256]{1,0:T(8,128)(2,1)S(1)}, bf16[256,256]{1,0:T(8,128)(2,1)S(1)}, u32[]{:S(2)}, u32[]{:S(2)}) collective-permute-start(bf16[256,256]{1,0:T(8,128)(2,1)S(1)} %get-tuple-element.68), channel_id=1, source_target_pairs={{0,2},{1,3},{2,0},{3,1},{4,6},{5,7},{6,4},{7,5},{8,10},{9,11},{10,... | collective-permute-start | bytes 393224 | tf_op jit(solution)/shard_map/ppermute | solution.py:19
  71.9 9.2 %collective-permute-start.32 = (bf16[256,256]{1,0:T(8,128)(2,1)S(1)}, bf16[256,256]{1,0:T(8,128)(2,1)S(1)}, u32[]{:S(2)}, u32[]{:S(2)}) collective-permute-start(bf16[256,256]{1,0:T(8,128)(2,1)S(1)} %get-tuple-element.68), channel_id=1, source_target_pairs={{0,4},{4,0},{8,12},{12,8},{1,5},{5,1},{9,13},{13,9},{2,6},{6,2},{1... | collective-permute-start | bytes 393224 | tf_op jit(solution)/shard_map/ppermute | solution.py:19
  73.0 8.1 %collective-permute-start.35 = (bf16[256,256]{1,0:T(8,128)(2,1)S(1)}, bf16[256,256]{1,0:T(8,128)(2,1)S(1)}, u32[]{:S(2)}, u32[]{:S(2)}) collective-permute-start(bf16[256,256]{1,0:T(8,128)(2,1)S(1)} %get-tuple-element.68), channel_id=1, source_target_pairs={{0,1},{1,0},{2,3},{3,2},{4,5},{5,4},{6,7},{7,6},{8,9},{9,8},{10,11... | collective-permute-start | bytes 393224 | tf_op jit(solution)/shard_map/ppermute | solution.py:19
  75.2 7.0 %collective-permute-start.34 = (bf16[256,256]{1,0:T(8,128)(2,1)S(1)}, bf16[256,256]{1,0:T(8,128)(2,1)S(1)}, u32[]{:S(2)}, u32[]{:S(2)}) collective-permute-start(bf16[256,256]{1,0:T(8,128)(2,1)S(1)} %get-tuple-element.68), channel_id=1, source_target_pairs={{0,12},{4,8},{8,4},{12,0},{1,13},{5,9},{9,5},{13,1},{2,14},{6,10},... | collective-permute-start | bytes 393224 | tf_op jit(solution)/shard_map/ppermute | solution.py:19
  78.4 7.0 %collective-permute-start.37 = (bf16[256,256]{1,0:T(8,128)(2,1)S(1)}, bf16[256,256]{1,0:T(8,128)(2,1)S(1)}, u32[]{:S(2)}, u32[]{:S(2)}) collective-permute-start(bf16[256,256]{1,0:T(8,128)(2,1)S(1)} %collective-permute-done.36), channel_id=1, source_target_pairs={{0,12},{4,8},{8,4},{12,0},{1,13},{5,9},{9,5},{13,1},{2,14},{6,10},... | collective-permute-start | bytes 393224 | tf_op jit(solution)/shard_map/ppermute | solution.py:19
  79.9 7.6 %collective-permute-start.33 = (bf16[256,256]{1,0:T(8,128)(2,1)S(1)}, bf16[256,256]{1,0:T(8,128)(2,1)S(1)}, u32[]{:S(2)}, u32[]{:S(2)}) collective-permute-start(bf16[256,256]{1,0:T(8,128)(2,1)S(1)} %get-tuple-element.68), channel_id=1, source_target_pairs={{0,8},{4,12},{8,0},{12,4},{1,9},{5,13},{9,1},{13,5},{2,10},{6,14},... | collective-permute-start | bytes 393224 | tf_op jit(solution)/shard_map/ppermute | solution.py:19
  81.1 6.4 %collective-permute-start.38 = (bf16[256,256]{1,0:T(8,128)(2,1)S(1)}, bf16[256,256]{1,0:T(8,128)(2,1)S(1)}, u32[]{:S(2)}, u32[]{:S(2)}) collective-permute-start(bf16[256,256]{1,0:T(8,128)(2,1)S(1)} %collective-permute-done.36), channel_id=1, source_target_pairs={{0,1},{1,0},{2,3},{3,2},{4,5},{5,4},{6,7},{7,6},{8,9},{9,8},{10,11... | collective-permute-start | bytes 393224 | tf_op jit(solution)/shard_map/ppermute | solution.py:19
  81.1 11.0 %collective-permute-start.40 = (bf16[256,512]{1,0:T(8,128)(2,1)S(1)}, bf16[256,512]{1,0:T(8,128)(2,1)S(1)}, u32[]{:S(2)}, u32[]{:S(2)}) collective-permute-start(bf16[256,512]{1,0:T(8,128)(2,1)S(1)} %get-tuple-element.130), channel_id=1, source_target_pairs={{0,8},{4,12},{8,0},{12,4},{1,9},{5,13},{9,1},{13,5},{2,10},{6,14},... | collective-permute-start | bytes 786440 | tf_op jit(solution)/shard_map/ppermute | solution.py:19
  82.2 10.0 %collective-permute-start.39 = (bf16[256,512]{1,0:T(8,128)(2,1)S(1)}, bf16[256,512]{1,0:T(8,128)(2,1)S(1)}, u32[]{:S(2)}, u32[]{:S(2)}) collective-permute-start(bf16[256,512]{1,0:T(8,128)(2,1)S(1)} %get-tuple-element.131), channel_id=1, source_target_pairs={{0,4},{4,0},{8,12},{12,8},{1,5},{5,1},{9,13},{13,9},{2,6},{6,2},{1... | collective-permute-start | bytes 786440 | tf_op jit(solution)/shard_map/ppermute | solution.py:19
  85.4 7.7 %collective-permute-start.41 = (bf16[256,512]{1,0:T(8,128)(2,1)S(1)}, bf16[256,512]{1,0:T(8,128)(2,1)S(1)}, u32[]{:S(2)}, u32[]{:S(2)}) collective-permute-start(bf16[256,512]{1,0:T(8,128)(2,1)S(1)} %pad_maximum_fusion.5), channel_id=1, source_target_pairs={{0,1},{1,0},{2,3},{3,2},{4,5},{5,4},{6,7},{7,6},{8,9},{9,8},{10,11... | collective-permute-start | bytes 786440 | tf_op jit(solution)/shard_map/ppermute | solution.py:19
  95.3 13.4 %collective-permute-start.50 = (bf16[256,768]{1,0:T(8,128)(2,1)S(1)}, bf16[256,768]{1,0:T(8,128)(2,1)S(1)}, u32[]{:S(2)}, u32[]{:S(2)}) collective-permute-start(bf16[256,768]{1,0:T(8,128)(2,1)S(1)} %get-tuple-element.107.proj_ref), channel_id=1, source_target_pairs={{0,16},{16,0},{1,17},{17,1},{2,18},{18,2},{3,19},{19,3},{4,20},{20... | collective-permute-start | bytes 1179656 | tf_op jit(solution)/shard_map/ppermute | solution.py:19
  101.3 5.4 %collective-permute-start.47 = (f32[256]{0:T(256)S(1)}, f32[256]{0:T(256)S(1)}, u32[]{:S(2)}, u32[]{:S(2)}) collective-permute-start(f32[256]{0:T(256)S(1)} %add.172), channel_id=1, source_target_pairs={{0,3},{1,2},{2,1},{3,0},{4,7},{5,6},{6,5},{7,4},{8,11},{9,10},{10,... | collective-permute-start | bytes 3080 | tf_op jit(solution)/shard_map/ppermute | solution.py:19
  109.5 8.6 %collective-permute-start.56 = (bf16[256,512]{1,0:T(8,128)(2,1)S(1)}, bf16[256,512]{1,0:T(8,128)(2,1)S(1)}, u32[]{:S(2)}, u32[]{:S(2)}) collective-permute-start(bf16[256,512]{1,0:T(8,128)(2,1)S(1)} %slice.290), channel_id=1, source_target_pairs={{0,1},{1,0},{2,3},{3,2},{4,5},{5,4},{6,7},{7,6},{8,9},{9,8},{10,11... | collective-permute-start | bytes 786440 | tf_op jit(solution)/shard_map/ppermute | solution.py:19
  111.3 8.6 %collective-permute-start.58 = (bf16[256,256]{1,0:T(8,128)(2,1)S(1)}, bf16[256,256]{1,0:T(8,128)(2,1)S(1)}, u32[]{:S(2)}, u32[]{:S(2)}) collective-permute-start(bf16[256,256]{1,0:T(8,128)(2,1)S(1)} %get-tuple-element.114), channel_id=1, source_target_pairs={{0,4},{4,0},{8,12},{12,8},{1,5},{5,1},{9,13},{13,9},{2,6},{6,2},{1... | collective-permute-start | bytes 393224 | tf_op jit(solution)/shard_map/ppermute | solution.py:19
  112.5 7.4 %collective-permute-start.59 = (bf16[256,256]{1,0:T(8,128)(2,1)S(1)}, bf16[256,256]{1,0:T(8,128)(2,1)S(1)}, u32[]{:S(2)}, u32[]{:S(2)}) collective-permute-start(bf16[256,256]{1,0:T(8,128)(2,1)S(1)} %get-tuple-element.115), channel_id=1, source_target_pairs={{0,8},{4,12},{8,0},{12,4},{1,9},{5,13},{9,1},{13,5},{2,10},{6,14},... | collective-permute-start | bytes 393224 | tf_op jit(solution)/shard_map/ppermute | solution.py:19
  114.2 9.3 %collective-permute-start.54 = (bf16[256,512]{1,0:T(8,128)(2,1)S(1)}, bf16[256,512]{1,0:T(8,128)(2,1)S(1)}, u32[]{:S(2)}, u32[]{:S(2)}) collective-permute-start(bf16[256,512]{1,0:T(8,128)(2,1)S(1)} %get-tuple-element.104), channel_id=1, source_target_pairs={{0,4},{4,0},{8,12},{12,8},{1,5},{5,1},{9,13},{13,9},{2,6},{6,2},{1... | collective-permute-start | bytes 786440 | tf_op jit(solution)/shard_map/ppermute | solution.py:19
  115.5 10.2 %collective-permute-start.55 = (bf16[256,512]{1,0:T(8,128)(2,1)S(1)}, bf16[256,512]{1,0:T(8,128)(2,1)S(1)}, u32[]{:S(2)}, u32[]{:S(2)}) collective-permute-start(bf16[256,512]{1,0:T(8,128)(2,1)S(1)} %get-tuple-element.105), channel_id=1, source_target_pairs={{0,8},{4,12},{8,0},{12,4},{1,9},{5,13},{9,1},{13,5},{2,10},{6,14},... | collective-permute-start | bytes 786440 | tf_op jit(solution)/shard_map/ppermute | solution.py:19
  118.1 8.9 %collective-permute-start.57 = (bf16[256,256]{1,0:T(8,128)(2,1)S(1)}, bf16[256,256]{1,0:T(8,128)(2,1)S(1)}, u32[]{:S(2)}, u32[]{:S(2)}) collective-permute-start(bf16[256,256]{1,0:T(8,128)(2,1)S(1)} %get-tuple-element.95), channel_id=1, source_target_pairs={{0,12},{4,8},{8,4},{12,0},{1,13},{5,9},{9,5},{13,1},{2,14},{6,10},... | collective-permute-start | bytes 393224 | tf_op jit(solution)/shard_map/ppermute | solution.py:19
  119.9 5.8 %collective-permute-start.60 = (bf16[256,256]{1,0:T(8,128)(2,1)S(1)}, bf16[256,256]{1,0:T(8,128)(2,1)S(1)}, u32[]{:S(2)}, u32[]{:S(2)}) collective-permute-start(bf16[256,256]{1,0:T(8,128)(2,1)S(1)} %add_convert_fusion.2), channel_id=1, source_target_pairs={{0,1},{1,0},{2,3},{3,2},{4,5},{5,4},{6,7},{7,6},{8,9},{9,8},{10,11... | collective-permute-start | bytes 393224 | tf_op jit(solution)/shard_map/ppermute | solution.py:19
  121.5 9.8 %collective-permute-start.52 = (bf16[256,256]{1,0:T(8,128)(2,1)S(1)}, bf16[256,256]{1,0:T(8,128)(2,1)S(1)}, u32[]{:S(2)}, u32[]{:S(2)}) collective-permute-start(bf16[256,256]{1,0:T(8,128)(2,1)S(1)} %get-tuple-element.102), channel_id=1, source_target_pairs={{0,4},{4,0},{8,12},{12,8},{1,5},{5,1},{9,13},{13,9},{2,6},{6,2},{1... | collective-permute-start | bytes 393224 | tf_op jit(solution)/shard_map/ppermute | solution.py:19
  123.5 7.7 %collective-permute-start.53 = (bf16[256,256]{1,0:T(8,128)(2,1)S(1)}, bf16[256,256]{1,0:T(8,128)(2,1)S(1)}, u32[]{:S(2)}, u32[]{:S(2)}) collective-permute-start(bf16[256,256]{1,0:T(8,128)(2,1)S(1)} %get-tuple-element.103), channel_id=1, source_target_pairs={{0,8},{4,12},{8,0},{12,4},{1,9},{5,13},{9,1},{13,5},{2,10},{6,14},... | collective-permute-start | bytes 393224 | tf_op jit(solution)/shard_map/ppermute | solution.py:19
  127.1 7.2 %collective-permute-start.61 = (bf16[256,256]{1,0:T(8,128)(2,1)S(1)}, bf16[256,256]{1,0:T(8,128)(2,1)S(1)}, u32[]{:S(2)}, u32[]{:S(2)}) collective-permute-start(bf16[256,256]{1,0:T(8,128)(2,1)S(1)} %get-tuple-element.94), channel_id=1, source_target_pairs={{0,2},{1,3},{2,0},{3,1},{4,6},{5,7},{6,4},{7,5},{8,10},{9,11},{10,... | collective-permute-start | bytes 393224 | tf_op jit(solution)/shard_map/ppermute | solution.py:19
  127.8 6.6 %collective-permute-start.62 = (bf16[256,256]{1,0:T(8,128)(2,1)S(1)}, bf16[256,256]{1,0:T(8,128)(2,1)S(1)}, u32[]{:S(2)}, u32[]{:S(2)}) collective-permute-start(bf16[256,256]{1,0:T(8,128)(2,1)S(1)} %add_convert_fusion.1), channel_id=1, source_target_pairs={{0,12},{4,8},{8,4},{12,0},{1,13},{5,9},{9,5},{13,1},{2,14},{6,10},... | collective-permute-start | bytes 393224 | tf_op jit(solution)/shard_map/ppermute | solution.py:19
  129.6 5.6 %collective-permute-start.63 = (bf16[256,256]{1,0:T(8,128)(2,1)S(1)}, bf16[256,256]{1,0:T(8,128)(2,1)S(1)}, u32[]{:S(2)}, u32[]{:S(2)}) collective-permute-start(bf16[256,256]{1,0:T(8,128)(2,1)S(1)} %add_convert_fusion), channel_id=1, source_target_pairs={{0,1},{1,0},{2,3},{3,2},{4,5},{5,4},{6,7},{7,6},{8,9},{9,8},{10,11... | collective-permute-start | bytes 393224 | tf_op jit(solution)/shard_map/ppermute | solution.py:19
  (16 other events, 63.4 us)

commit v11 on v10

--- a/solution.py
+++ b/solution.py
@@ -41,8 +41,8 @@
 
 
 ARRIVALS = (
-    ((0, 0), (1, 0), (2, 0), (3, 0), (0, 1), (0, 2)),
-    ((0, 3), (3, 2), (1, 1), (1, 2), (2, 1), (2, 2)),
+    ((0, 0), (1, 0), (3, 0), (0, 1), (0, 2)),
+    ((2, 0), (0, 3), (3, 2), (1, 1), (1, 2), (2, 1), (2, 2)),
     ((3, 1), (3, 3), (1, 3), (2, 3)),
 )
 

time: 136 us -> 143 us (1.051)
  waiting for transfers between devices: 41.5 us -> 46.5 us
  starting transfers between devices: 76.5 us -> 78.2 us
    ppermute x64, waiting for transfers between devices: 41.5 us -> 46.5 us  [xor_move(): return lax.ppermute(block, axis, [(i, i ^ mask) for i in range(count)])]
    ppermute x64, starting transfers between devices: 76.5 us -> 78.2 us  [xor_move(): return lax.ppermute(block, axis, [(i, i ^ mask) for i in range(count)])]
  transfers between devices with their start and end apart: 64 -> 64, of which waited for: 37 -> 29; matrix products, arithmetic and copies ran while one was open for 6% -> 6% of each run, Pallas kernels for 3% -> 3%
where the time goes in v11:
time: 143 us
  starting transfers between devices  78.2 us (55%)
  waiting for transfers between devices  46.5 us (33%)
  matrix products  9.59 us (7%)
  Pallas kernels  3.92 us (3%)
  local copies, waits for them, and re-layouts  2.49 us (2%)
    ppermute x64, starting transfers between devices, xor_move(): return lax.ppermute(block, axis, [(i, i ^ mask) for i in range(count)])  78.2 us
    ppermute x64, waiting for transfers between devices, xor_move(): return lax.ppermute(block, axis, [(i, i ^ mask) for i in range(count)])  46.5 us
    dot_general x6, matrix products, on_device(): lax.dot_general(residue, groups[g], (((1,), (0,)), ((), ())), preferred_e...  4.92 us
    dot_general x6, matrix products, on_device(): lax.dot_general(join(*blocks), groups[g], (((1,), (1,)), ((), ())), prefe...  4.67 us
    pallas_call x1, Pallas kernels, regroup(): pl.pallas_call(kernel, out_shape=[jax.ShapeDtypeStruct((rows_here, len(pl...  3 us
  transfers between devices with their start and end apart: 64, of which 29 were waited for; matrix products, arithmetic and copies ran while one was open for 6% of the time, Pallas kernels for 3%

profile of v11, /device:TPU:0, one launch (start us, length us, event | category | flops | bytes accessed | tf_op | source)
XLA Modules:
  0.0 143.0 jit_solution(17892490103327963200)
XLA Ops:
  1.7 4.1 %collective-permute-start.3 = (bf16[256,256]{1,0:T(8,128)(2,1)S(1)}, bf16[256,256]{1,0:T(8,128)(2,1)S(1)}, u32[]{:S(2)}, u32[]{:S(2)}) collective-permute-start(bf16[256,256]{1,0:T(8,128)(2,1)S(1)} %fusion.28), channel_id=1, source_target_pairs={{0,2},{1,3},{2,0},{3,1},{4,6},{5,7},{6,4},{7,5},{8,10},{9,11},{10,... | collective-permute-start | bytes 393224 | tf_op jit(solution)/shard_map/ppermute | solution.py:19
  5.8 1.6 %collective-permute-start.2 = (bf16[256,256]{1,0:T(8,128)(2,1)S(1)}, bf16[256,256]{1,0:T(8,128)(2,1)S(1)}, u32[]{:S(2)}, u32[]{:S(2)}) collective-permute-start(bf16[256,256]{1,0:T(8,128)(2,1)S(1)} %fusion.28), channel_id=1, source_target_pairs={{0,1},{1,0},{2,3},{3,2},{4,5},{5,4},{6,7},{7,6},{8,9},{9,8},{10,11... | collective-permute-start | bytes 393224 | tf_op jit(solution)/shard_map/ppermute | solution.py:19
  7.4 1.5 %collective-permute-start = (bf16[256,256]{1,0:T(8,128)(2,1)S(1)}, bf16[256,256]{1,0:T(8,128)(2,1)S(1)}, u32[]{:S(2)}, u32[]{:S(2)}) collective-permute-start(bf16[256,256]{1,0:T(8,128)(2,1)S(1)} %fusion.28), channel_id=1, source_target_pairs={{0,4},{4,0},{8,12},{12,8},{1,5},{5,1},{9,13},{13,9},{2,6},{6,2},{1... | collective-permute-start | bytes 393224 | tf_op jit(solution)/shard_map/ppermute | solution.py:19
  8.9 1.5 %collective-permute-start.1 = (bf16[256,256]{1,0:T(8,128)(2,1)S(1)}, bf16[256,256]{1,0:T(8,128)(2,1)S(1)}, u32[]{:S(2)}, u32[]{:S(2)}) collective-permute-start(bf16[256,256]{1,0:T(8,128)(2,1)S(1)} %fusion.28), channel_id=1, source_target_pairs={{0,12},{4,8},{8,4},{12,0},{1,13},{5,9},{9,5},{13,1},{2,14},{6,10},... | collective-permute-start | bytes 393224 | tf_op jit(solution)/shard_map/ppermute | solution.py:19
  10.4 1.9 %collective-permute-done.3 = bf16[256,256]{1,0:T(8,128)(2,1)S(1)} collective-permute-done((bf16[256,256]{1,0:T(8,128)(2,1)S(1)}, bf16[256,256]{1,0:T(8,128)(2,1)S(1)}, u32[]{:S(2)}, u32[]{:S(2)}) %collective-permute-start.3) | collective-permute-done | bytes 131104 | tf_op jit(solution)/shard_map/ppermute | solution.py:19
  12.9 2.4 %collective-permute-start.4 = (bf16[256,256]{1,0:T(8,128)(2,1)S(1)}, bf16[256,256]{1,0:T(8,128)(2,1)S(1)}, u32[]{:S(2)}, u32[]{:S(2)}) collective-permute-start(bf16[256,256]{1,0:T(8,128)(2,1)S(1)} %collective-permute-done.3), channel_id=1, source_target_pairs={{0,12},{4,8},{8,4},{12,0},{1,13},{5,9},{9,5},{13,1},{2,14},{6,10},... | collective-permute-start | bytes 393224 | tf_op jit(solution)/shard_map/ppermute | solution.py:19
  15.3 3.0 %regroup.1 = (bf16[768,1280]{1,0:T(8,128)(2,1)S(1)}, bf16[768,1792]{1,0:T(8,128)(2,1)S(1)}, bf16[768,1024]{1,0:T(8,128)(2,1)S(1)}) custom-call(bf16[768,4096]{1,0:T(8,128)(2,1)} %bitcast.37), custom_call_target="tpu_custom_call" | custom-call | bytes 12582912 | tf_op jit(solution)/shard_map/regroup/pallas_call | solution.py:140
  18.9 1.6 %collective-permute-start.8 = (bf16[256,512]{1,0:T(8,128)(2,1)S(1)}, bf16[256,512]{1,0:T(8,128)(2,1)S(1)}, u32[]{:S(2)}, u32[]{:S(2)}) collective-permute-start(bf16[256,512]{1,0:T(8,128)(2,1)S(1)} %get-tuple-element.128), channel_id=1, source_target_pairs={{0,8},{4,12},{8,0},{12,4},{1,9},{5,13},{9,1},{13,5},{2,10},{6,14},... | collective-permute-start | bytes 786440 | tf_op jit(solution)/shard_map/ppermute | solution.py:19
  21.9 1.5 %collective-permute-start.9 = (bf16[256,512]{1,0:T(8,128)(2,1)S(1)}, bf16[256,512]{1,0:T(8,128)(2,1)S(1)}, u32[]{:S(2)}, u32[]{:S(2)}) collective-permute-start(bf16[256,512]{1,0:T(8,128)(2,1)S(1)} %pad_maximum_fusion.4), channel_id=1, source_target_pairs={{0,1},{1,0},{2,3},{3,2},{4,5},{5,4},{6,7},{7,6},{8,9},{9,8},{10,11... | collective-permute-start | bytes 786440 | tf_op jit(solution)/shard_map/ppermute | solution.py:19
  23.4 1.5 %collective-permute-start.10 = (bf16[256,256]{1,0:T(8,128)(2,1)S(1)}, bf16[256,256]{1,0:T(8,128)(2,1)S(1)}, u32[]{:S(2)}, u32[]{:S(2)}) collective-permute-start(bf16[256,256]{1,0:T(8,128)(2,1)S(1)} %collective-permute-done.5), channel_id=1, source_target_pairs={{0,4},{4,0},{8,12},{12,8},{1,5},{5,1},{9,13},{13,9},{2,6},{6,2},{1... | collective-permute-start | bytes 393224 | tf_op jit(solution)/shard_map/ppermute | solution.py:19
  24.9 3.9 %collective-permute-done.8 = bf16[256,512]{1,0:T(8,128)(2,1)S(1)} collective-permute-done((bf16[256,512]{1,0:T(8,128)(2,1)S(1)}, bf16[256,512]{1,0:T(8,128)(2,1)S(1)}, u32[]{:S(2)}, u32[]{:S(2)}) %collective-permute-start.8) | collective-permute-done | bytes 262176 | tf_op jit(solution)/shard_map/ppermute | solution.py:19
  30.6 3.3 %collective-permute-done.11 = bf16[256,256]{1,0:T(8,128)(2,1)S(1)} collective-permute-done((bf16[256,256]{1,0:T(8,128)(2,1)S(1)}, bf16[256,256]{1,0:T(8,128)(2,1)S(1)}, u32[]{:S(2)}, u32[]{:S(2)}) %collective-permute-start.11) | collective-permute-done | bytes 131104 | tf_op jit(solution)/shard_map/ppermute | solution.py:19
  36.7 1.5 %collective-permute-start.14 = (f32[256]{0:T(256)S(1)}, f32[256]{0:T(256)S(1)}, u32[]{:S(2)}, u32[]{:S(2)}) collective-permute-start(f32[256]{0:T(256)S(1)} %get-tuple-element.108), channel_id=1, source_target_pairs={{0,4},{4,0},{8,12},{12,8},{1,5},{5,1},{9,13},{13,9},{2,6},{6,2},{1... | collective-permute-start | bytes 3080 | tf_op jit(solution)/shard_map/ppermute | solution.py:19
  40.2 3.1 %collective-permute-start.15 = (f32[256]{0:T(256)S(1)}, f32[256]{0:T(256)S(1)}, u32[]{:S(2)}, u32[]{:S(2)}) collective-permute-start(f32[256]{0:T(256)S(1)} %add.148), channel_id=1, source_target_pairs={{0,3},{1,2},{2,1},{3,0},{4,7},{5,6},{6,5},{7,4},{8,11},{9,10},{10,... | collective-permute-start | bytes 3080 | tf_op jit(solution)/shard_map/ppermute | solution.py:19
  45.6 2.2 %collective-permute-done.16 = f32[256]{0:T(256)S(1)} collective-permute-done((f32[256]{0:T(256)S(1)}, f32[256]{0:T(256)S(1)}, u32[]{:S(2)}, u32[]{:S(2)}) %collective-permute-start.16) | collective-permute-done | bytes 1056 | tf_op jit(solution)/shard_map/ppermute | solution.py:19
  47.9 1.1 collective-permute-done.19
  50.6 1.5 %collective-permute-start.26 = (bf16[256,256]{1,0:T(8,128)(2,1)S(1)}, bf16[256,256]{1,0:T(8,128)(2,1)S(1)}, u32[]{:S(2)}, u32[]{:S(2)}) collective-permute-start(bf16[256,256]{1,0:T(8,128)(2,1)S(1)} %get-tuple-element.112), channel_id=1, source_target_pairs={{0,4},{4,0},{8,12},{12,8},{1,5},{5,1},{9,13},{13,9},{2,6},{6,2},{1... | collective-permute-start | bytes 393224 | tf_op jit(solution)/shard_map/ppermute | solution.py:19
  55.8 2.4 %collective-permute-done.24 = bf16[256,512]{1,0:T(8,128)(2,1)S(1)} collective-permute-done((bf16[256,512]{1,0:T(8,128)(2,1)S(1)}, bf16[256,512]{1,0:T(8,128)(2,1)S(1)}, u32[]{:S(2)}, u32[]{:S(2)}) %collective-permute-start.24) | collective-permute-done | bytes 262176 | tf_op jit(solution)/shard_map/ppermute | solution.py:19
  59.2 2.1 %collective-permute-start.25 = (bf16[256,256]{1,0:T(8,128)(2,1)S(1)}, bf16[256,256]{1,0:T(8,128)(2,1)S(1)}, u32[]{:S(2)}, u32[]{:S(2)}) collective-permute-start(bf16[256,256]{1,0:T(8,128)(2,1)S(1)} %get-tuple-element.94), channel_id=1, source_target_pairs={{0,12},{4,8},{8,4},{12,0},{1,13},{5,9},{9,5},{13,1},{2,14},{6,10},... | collective-permute-start | bytes 393224 | tf_op jit(solution)/shard_map/ppermute | solution.py:19
  63.6 3.1 %collective-permute-done.23 = bf16[256,512]{1,0:T(8,128)(2,1)S(1)} collective-permute-done((bf16[256,512]{1,0:T(8,128)(2,1)S(1)}, bf16[256,512]{1,0:T(8,128)(2,1)S(1)}, u32[]{:S(2)}, u32[]{:S(2)}) %collective-permute-start.23) | collective-permute-done | bytes 262176 | tf_op jit(solution)/shard_map/ppermute | solution.py:19
  66.9 2.1 %collective-permute-start.29 = (bf16[256,256]{1,0:T(8,128)(2,1)S(1)}, bf16[256,256]{1,0:T(8,128)(2,1)S(1)}, u32[]{:S(2)}, u32[]{:S(2)}) collective-permute-start(bf16[256,256]{1,0:T(8,128)(2,1)S(1)} %get-tuple-element.101), channel_id=1, source_target_pairs={{0,2},{1,3},{2,0},{3,1},{4,6},{5,7},{6,4},{7,5},{8,10},{9,11},{10,... | collective-permute-start | bytes 393224 | tf_op jit(solution)/shard_map/ppermute | solution.py:19
  69.0 1.8 %collective-permute-start.30 = (bf16[256,256]{1,0:T(8,128)(2,1)S(1)}, bf16[256,256]{1,0:T(8,128)(2,1)S(1)}, u32[]{:S(2)}, u32[]{:S(2)}) collective-permute-start(bf16[256,256]{1,0:T(8,128)(2,1)S(1)} %add_convert_fusion.4), channel_id=1, source_target_pairs={{0,12},{4,8},{8,4},{12,0},{1,13},{5,9},{9,5},{13,1},{2,14},{6,10},... | collective-permute-start | bytes 393224 | tf_op jit(solution)/shard_map/ppermute | solution.py:19
  71.8 2.4 %collective-permute-done.29 = bf16[256,256]{1,0:T(8,128)(2,1)S(1)} collective-permute-done((bf16[256,256]{1,0:T(8,128)(2,1)S(1)}, bf16[256,256]{1,0:T(8,128)(2,1)S(1)}, u32[]{:S(2)}, u32[]{:S(2)}) %collective-permute-start.29) | collective-permute-done | bytes 131104 | tf_op jit(solution)/shard_map/ppermute | solution.py:19
  76.0 2.7 %collective-permute-start.35 = (bf16[256,256]{1,0:T(8,128)(2,1)S(1)}, bf16[256,256]{1,0:T(8,128)(2,1)S(1)}, u32[]{:S(2)}, u32[]{:S(2)}) collective-permute-start(bf16[256,256]{1,0:T(8,128)(2,1)S(1)} %get-tuple-element.68), channel_id=1, source_target_pairs={{0,2},{1,3},{2,0},{3,1},{4,6},{5,7},{6,4},{7,5},{8,10},{9,11},{10,... | collective-permute-start | bytes 393224 | tf_op jit(solution)/shard_map/ppermute | solution.py:19
  78.9 2.5 %collective-permute-start.34 = (bf16[256,256]{1,0:T(8,128)(2,1)S(1)}, bf16[256,256]{1,0:T(8,128)(2,1)S(1)}, u32[]{:S(2)}, u32[]{:S(2)}) collective-permute-start(bf16[256,256]{1,0:T(8,128)(2,1)S(1)} %get-tuple-element.68), channel_id=1, source_target_pairs={{0,1},{1,0},{2,3},{3,2},{4,5},{5,4},{6,7},{7,6},{8,9},{9,8},{10,11... | collective-permute-start | bytes 393224 | tf_op jit(solution)/shard_map/ppermute | solution.py:19
  81.4 2.1 %collective-permute-start.33 = (bf16[256,256]{1,0:T(8,128)(2,1)S(1)}, bf16[256,256]{1,0:T(8,128)(2,1)S(1)}, u32[]{:S(2)}, u32[]{:S(2)}) collective-permute-start(bf16[256,256]{1,0:T(8,128)(2,1)S(1)} %get-tuple-element.68), channel_id=1, source_target_pairs={{0,12},{4,8},{8,4},{12,0},{1,13},{5,9},{9,5},{13,1},{2,14},{6,10},... | collective-permute-start | bytes 393224 | tf_op jit(solution)/shard_map/ppermute | solution.py:19
  85.7 1.3 collective-permute-start.37
  87.1 1.9 %collective-permute-start.40 = (bf16[256,512]{1,0:T(8,128)(2,1)S(1)}, bf16[256,512]{1,0:T(8,128)(2,1)S(1)}, u32[]{:S(2)}, u32[]{:S(2)}) collective-permute-start(bf16[256,512]{1,0:T(8,128)(2,1)S(1)} %get-tuple-element.126), channel_id=1, source_target_pairs={{0,8},{4,12},{8,0},{12,4},{1,9},{5,13},{9,1},{13,5},{2,10},{6,14},... | collective-permute-start | bytes 786440 | tf_op jit(solution)/shard_map/ppermute | solution.py:19
  89.9 1.6 %collective-permute-done.36 = bf16[256,256]{1,0:T(8,128)(2,1)S(1)} collective-permute-done((bf16[256,256]{1,0:T(8,128)(2,1)S(1)}, bf16[256,256]{1,0:T(8,128)(2,1)S(1)}, u32[]{:S(2)}, u32[]{:S(2)}) %collective-permute-start.36) | collective-permute-done | bytes 131104 | tf_op jit(solution)/shard_map/ppermute | solution.py:19
  94.2 1.8 %collective-permute-done.40 = bf16[256,512]{1,0:T(8,128)(2,1)S(1)} collective-permute-done((bf16[256,512]{1,0:T(8,128)(2,1)S(1)}, bf16[256,512]{1,0:T(8,128)(2,1)S(1)}, u32[]{:S(2)}, u32[]{:S(2)}) %collective-permute-start.40) | collective-permute-done | bytes 262176 | tf_op jit(solution)/shard_map/ppermute | solution.py:19
  98.5 2.5 %collective-permute-done.43 = bf16[256,256]{1,0:T(8,128)(2,1)S(1)} collective-permute-done((bf16[256,256]{1,0:T(8,128)(2,1)S(1)}, bf16[256,256]{1,0:T(8,128)(2,1)S(1)}, u32[]{:S(2)}, u32[]{:S(2)}) %collective-permute-start.43) | collective-permute-done | bytes 131104 | tf_op jit(solution)/shard_map/ppermute | solution.py:19
  101.7 1.4 %collective-permute-start.44 = (f32[256]{0:T(256)S(1)}, f32[256]{0:T(256)S(1)}, u32[]{:S(2)}, u32[]{:S(2)}) collective-permute-start(f32[256]{0:T(256)S(1)} %get-tuple-element.106), channel_id=1, source_target_pairs={{0,12},{4,8},{8,4},{12,0},{1,13},{5,9},{9,5},{13,1},{2,14},{6,10},... | collective-permute-start | bytes 3080 | tf_op jit(solution)/shard_map/ppermute | solution.py:19
  103.2 1.1 collective-permute-start.45
  106.8 1.1 collective-permute-done.46
  107.9 2.2 %collective-permute-start.47 = (f32[256]{0:T(256)S(1)}, f32[256]{0:T(256)S(1)}, u32[]{:S(2)}, u32[]{:S(2)}) collective-permute-start(f32[256]{0:T(256)S(1)} %add.172), channel_id=1, source_target_pairs={{0,3},{1,2},{2,1},{3,0},{4,7},{5,6},{6,5},{7,4},{8,11},{9,10},{10,... | collective-permute-start | bytes 3080 | tf_op jit(solution)/shard_map/ppermute | solution.py:19
  110.1 2.2 %collective-permute-start.49 = (f32[256]{0:T(256)S(1)}, f32[256]{0:T(256)S(1)}, u32[]{:S(2)}, u32[]{:S(2)}) collective-permute-start(f32[256]{0:T(256)S(1)} %add.172), channel_id=1, source_target_pairs={{0,1},{1,0},{2,3},{3,2},{4,5},{5,4},{6,7},{7,6},{8,9},{9,8},{10,11... | collective-permute-start | bytes 3080 | tf_op jit(solution)/shard_map/ppermute | solution.py:19
  113.2 1.3 collective-permute-done.48
  116.4 1.4 collective-permute-start.56
  118.9 1.2 fusion.44
  120.1 1.9 %collective-permute-start.54 = (bf16[256,512]{1,0:T(8,128)(2,1)S(1)}, bf16[256,512]{1,0:T(8,128)(2,1)S(1)}, u32[]{:S(2)}, u32[]{:S(2)}) collective-permute-start(bf16[256,512]{1,0:T(8,128)(2,1)S(1)} %get-tuple-element.102), channel_id=1, source_target_pairs={{0,4},{4,0},{8,12},{12,8},{1,5},{5,1},{9,13},{13,9},{2,6},{6,2},{1... | collective-permute-start | bytes 786440 | tf_op jit(solution)/shard_map/ppermute | solution.py:19
  122.0 1.1 collective-permute-start.55
  123.2 1.9 %collective-permute-done.56 = bf16[256,512]{1,0:T(8,128)(2,1)S(1)} collective-permute-done((bf16[256,512]{1,0:T(8,128)(2,1)S(1)}, bf16[256,512]{1,0:T(8,128)(2,1)S(1)}, u32[]{:S(2)}, u32[]{:S(2)}) %collective-permute-start.56) | collective-permute-done | bytes 262176 | tf_op jit(solution)/shard_map/ppermute | solution.py:19
  125.9 1.3 collective-permute-start.57
  127.2 1.8 %collective-permute-start.60 = (bf16[256,256]{1,0:T(8,128)(2,1)S(1)}, bf16[256,256]{1,0:T(8,128)(2,1)S(1)}, u32[]{:S(2)}, u32[]{:S(2)}) collective-permute-start(bf16[256,256]{1,0:T(8,128)(2,1)S(1)} %add_convert_fusion.2), channel_id=1, source_target_pairs={{0,1},{1,0},{2,3},{3,2},{4,5},{5,4},{6,7},{7,6},{8,9},{9,8},{10,11... | collective-permute-start | bytes 393224 | tf_op jit(solution)/shard_map/ppermute | solution.py:19
  130.9 2.9 %collective-permute-done.55 = bf16[256,512]{1,0:T(8,128)(2,1)S(1)} collective-permute-done((bf16[256,512]{1,0:T(8,128)(2,1)S(1)}, bf16[256,512]{1,0:T(8,128)(2,1)S(1)}, u32[]{:S(2)}, u32[]{:S(2)}) %collective-permute-start.55) | collective-permute-done | bytes 262176 | tf_op jit(solution)/shard_map/ppermute | solution.py:19
  134.9 1.3 collective-permute-start.62
  136.3 1.9 %collective-permute-start.63 = (bf16[256,256]{1,0:T(8,128)(2,1)S(1)}, bf16[256,256]{1,0:T(8,128)(2,1)S(1)}, u32[]{:S(2)}, u32[]{:S(2)}) collective-permute-start(bf16[256,256]{1,0:T(8,128)(2,1)S(1)} %add_convert_fusion), channel_id=1, source_target_pairs={{0,1},{1,0},{2,3},{3,2},{4,5},{5,4},{6,7},{7,6},{8,9},{9,8},{10,11... | collective-permute-start | bytes 393224 | tf_op jit(solution)/shard_map/ppermute | solution.py:19
  138.1 3.1 %collective-permute-done.61 = bf16[256,256]{1,0:T(8,128)(2,1)S(1)} collective-permute-done((bf16[256,256]{1,0:T(8,128)(2,1)S(1)}, bf16[256,256]{1,0:T(8,128)(2,1)S(1)}, u32[]{:S(2)}, u32[]{:S(2)}) %collective-permute-start.61) | collective-permute-done | bytes 131104 | tf_op jit(solution)/shard_map/ppermute | solution.py:19
  (169 shorter events, 45.3 us)
Async XLA Ops:
  1.7 10.5 %collective-permute-start.3 = (bf16[256,256]{1,0:T(8,128)(2,1)S(1)}, bf16[256,256]{1,0:T(8,128)(2,1)S(1)}, u32[]{:S(2)}, u32[]{:S(2)}) collective-permute-start(bf16[256,256]{1,0:T(8,128)(2,1)S(1)} %fusion.28), channel_id=1, source_target_pairs={{0,2},{1,3},{2,0},{3,1},{4,6},{5,7},{6,4},{7,5},{8,10},{9,11},{10,... | collective-permute-start | bytes 393224 | tf_op jit(solution)/shard_map/ppermute | solution.py:19
  5.8 12.5 %collective-permute-start.2 = (bf16[256,256]{1,0:T(8,128)(2,1)S(1)}, bf16[256,256]{1,0:T(8,128)(2,1)S(1)}, u32[]{:S(2)}, u32[]{:S(2)}) collective-permute-start(bf16[256,256]{1,0:T(8,128)(2,1)S(1)} %fusion.28), channel_id=1, source_target_pairs={{0,1},{1,0},{2,3},{3,2},{4,5},{5,4},{6,7},{7,6},{8,9},{9,8},{10,11... | collective-permute-start | bytes 393224 | tf_op jit(solution)/shard_map/ppermute | solution.py:19
  7.4 11.5 %collective-permute-start = (bf16[256,256]{1,0:T(8,128)(2,1)S(1)}, bf16[256,256]{1,0:T(8,128)(2,1)S(1)}, u32[]{:S(2)}, u32[]{:S(2)}) collective-permute-start(bf16[256,256]{1,0:T(8,128)(2,1)S(1)} %fusion.28), channel_id=1, source_target_pairs={{0,4},{4,0},{8,12},{12,8},{1,5},{5,1},{9,13},{13,9},{2,6},{6,2},{1... | collective-permute-start | bytes 393224 | tf_op jit(solution)/shard_map/ppermute | solution.py:19
  8.9 11.6 %collective-permute-start.1 = (bf16[256,256]{1,0:T(8,128)(2,1)S(1)}, bf16[256,256]{1,0:T(8,128)(2,1)S(1)}, u32[]{:S(2)}, u32[]{:S(2)}) collective-permute-start(bf16[256,256]{1,0:T(8,128)(2,1)S(1)} %fusion.28), channel_id=1, source_target_pairs={{0,12},{4,8},{8,4},{12,0},{1,13},{5,9},{9,5},{13,1},{2,14},{6,10},... | collective-permute-start | bytes 393224 | tf_op jit(solution)/shard_map/ppermute | solution.py:19
  12.3 8.8 %collective-permute-start.5 = (bf16[256,256]{1,0:T(8,128)(2,1)S(1)}, bf16[256,256]{1,0:T(8,128)(2,1)S(1)}, u32[]{:S(2)}, u32[]{:S(2)}) collective-permute-start(bf16[256,256]{1,0:T(8,128)(2,1)S(1)} %collective-permute-done.3), channel_id=1, source_target_pairs={{0,1},{1,0},{2,3},{3,2},{4,5},{5,4},{6,7},{7,6},{8,9},{9,8},{10,11... | collective-permute-start | bytes 393224 | tf_op jit(solution)/shard_map/ppermute | solution.py:19
  12.9 8.2 %collective-permute-start.4 = (bf16[256,256]{1,0:T(8,128)(2,1)S(1)}, bf16[256,256]{1,0:T(8,128)(2,1)S(1)}, u32[]{:S(2)}, u32[]{:S(2)}) collective-permute-start(bf16[256,256]{1,0:T(8,128)(2,1)S(1)} %collective-permute-done.3), channel_id=1, source_target_pairs={{0,12},{4,8},{8,4},{12,0},{1,13},{5,9},{9,5},{13,1},{2,14},{6,10},... | collective-permute-start | bytes 393224 | tf_op jit(solution)/shard_map/ppermute | solution.py:19
  18.3 11.1 %collective-permute-start.6 = (bf16[256,256]{1,0:T(8,128)(2,1)S(1)}, bf16[256,256]{1,0:T(8,128)(2,1)S(1)}, u32[]{:S(2)}, u32[]{:S(2)}) collective-permute-start(bf16[256,256]{1,0:T(8,128)(2,1)S(1)} %fusion.28), channel_id=1, source_target_pairs={{0,8},{4,12},{8,0},{12,4},{1,9},{5,13},{9,1},{13,5},{2,10},{6,14},... | collective-permute-start | bytes 393224 | tf_op jit(solution)/shard_map/ppermute | solution.py:19
  18.9 9.9 %collective-permute-start.8 = (bf16[256,512]{1,0:T(8,128)(2,1)S(1)}, bf16[256,512]{1,0:T(8,128)(2,1)S(1)}, u32[]{:S(2)}, u32[]{:S(2)}) collective-permute-start(bf16[256,512]{1,0:T(8,128)(2,1)S(1)} %get-tuple-element.128), channel_id=1, source_target_pairs={{0,8},{4,12},{8,0},{12,4},{1,9},{5,13},{9,1},{13,5},{2,10},{6,14},... | collective-permute-start | bytes 786440 | tf_op jit(solution)/shard_map/ppermute | solution.py:19
  20.5 8.9 %collective-permute-start.7 = (bf16[256,512]{1,0:T(8,128)(2,1)S(1)}, bf16[256,512]{1,0:T(8,128)(2,1)S(1)}, u32[]{:S(2)}, u32[]{:S(2)}) collective-permute-start(bf16[256,512]{1,0:T(8,128)(2,1)S(1)} %get-tuple-element.129), channel_id=1, source_target_pairs={{0,4},{4,0},{8,12},{12,8},{1,5},{5,1},{9,13},{13,9},{2,6},{6,2},{1... | collective-permute-start | bytes 786440 | tf_op jit(solution)/shard_map/ppermute | solution.py:19
  21.9 8.6 %collective-permute-start.9 = (bf16[256,512]{1,0:T(8,128)(2,1)S(1)}, bf16[256,512]{1,0:T(8,128)(2,1)S(1)}, u32[]{:S(2)}, u32[]{:S(2)}) collective-permute-start(bf16[256,512]{1,0:T(8,128)(2,1)S(1)} %pad_maximum_fusion.4), channel_id=1, source_target_pairs={{0,1},{1,0},{2,3},{3,2},{4,5},{5,4},{6,7},{7,6},{8,9},{9,8},{10,11... | collective-permute-start | bytes 786440 | tf_op jit(solution)/shard_map/ppermute | solution.py:19
  23.4 7.1 %collective-permute-start.10 = (bf16[256,256]{1,0:T(8,128)(2,1)S(1)}, bf16[256,256]{1,0:T(8,128)(2,1)S(1)}, u32[]{:S(2)}, u32[]{:S(2)}) collective-permute-start(bf16[256,256]{1,0:T(8,128)(2,1)S(1)} %collective-permute-done.5), channel_id=1, source_target_pairs={{0,4},{4,0},{8,12},{12,8},{1,5},{5,1},{9,13},{13,9},{2,6},{6,2},{1... | collective-permute-start | bytes 393224 | tf_op jit(solution)/shard_map/ppermute | solution.py:19
  34.5 14.5 %collective-permute-start.18 = (bf16[256,768]{1,0:T(8,128)(2,1)S(1)}, bf16[256,768]{1,0:T(8,128)(2,1)S(1)}, u32[]{:S(2)}, u32[]{:S(2)}) collective-permute-start(bf16[256,768]{1,0:T(8,128)(2,1)S(1)} %get-tuple-element.109), channel_id=1, source_target_pairs={{0,16},{16,0},{1,17},{17,1},{2,18},{18,2},{3,19},{19,3},{4,20},{20... | collective-permute-start | bytes 1179656 | tf_op jit(solution)/shard_map/ppermute | solution.py:19
  40.2 5.4 %collective-permute-start.15 = (f32[256]{0:T(256)S(1)}, f32[256]{0:T(256)S(1)}, u32[]{:S(2)}, u32[]{:S(2)}) collective-permute-start(f32[256]{0:T(256)S(1)} %add.148), channel_id=1, source_target_pairs={{0,3},{1,2},{2,1},{3,0},{4,7},{5,6},{6,5},{7,4},{8,11},{9,10},{10,... | collective-permute-start | bytes 3080 | tf_op jit(solution)/shard_map/ppermute | solution.py:19
  49.7 8.5 %collective-permute-start.24 = (bf16[256,512]{1,0:T(8,128)(2,1)S(1)}, bf16[256,512]{1,0:T(8,128)(2,1)S(1)}, u32[]{:S(2)}, u32[]{:S(2)}) collective-permute-start(bf16[256,512]{1,0:T(8,128)(2,1)S(1)} %slice.265), channel_id=1, source_target_pairs={{0,1},{1,0},{2,3},{3,2},{4,5},{5,4},{6,7},{7,6},{8,9},{9,8},{10,11... | collective-permute-start | bytes 786440 | tf_op jit(solution)/shard_map/ppermute | solution.py:19
  50.6 8.6 %collective-permute-start.26 = (bf16[256,256]{1,0:T(8,128)(2,1)S(1)}, bf16[256,256]{1,0:T(8,128)(2,1)S(1)}, u32[]{:S(2)}, u32[]{:S(2)}) collective-permute-start(bf16[256,256]{1,0:T(8,128)(2,1)S(1)} %get-tuple-element.112), channel_id=1, source_target_pairs={{0,4},{4,0},{8,12},{12,8},{1,5},{5,1},{9,13},{13,9},{2,6},{6,2},{1... | collective-permute-start | bytes 393224 | tf_op jit(solution)/shard_map/ppermute | solution.py:19
  52.1 9.2 %collective-permute-start.27 = (bf16[256,256]{1,0:T(8,128)(2,1)S(1)}, bf16[256,256]{1,0:T(8,128)(2,1)S(1)}, u32[]{:S(2)}, u32[]{:S(2)}) collective-permute-start(bf16[256,256]{1,0:T(8,128)(2,1)S(1)} %get-tuple-element.113), channel_id=1, source_target_pairs={{0,8},{4,12},{8,0},{12,4},{1,9},{5,13},{9,1},{13,5},{2,10},{6,14},... | collective-permute-start | bytes 393224 | tf_op jit(solution)/shard_map/ppermute | solution.py:19
  53.7 9.4 %collective-permute-start.22 = (bf16[256,512]{1,0:T(8,128)(2,1)S(1)}, bf16[256,512]{1,0:T(8,128)(2,1)S(1)}, u32[]{:S(2)}, u32[]{:S(2)}) collective-permute-start(bf16[256,512]{1,0:T(8,128)(2,1)S(1)} %get-tuple-element.104), channel_id=1, source_target_pairs={{0,4},{4,0},{8,12},{12,8},{1,5},{5,1},{9,13},{13,9},{2,6},{6,2},{1... | collective-permute-start | bytes 786440 | tf_op jit(solution)/shard_map/ppermute | solution.py:19
  54.7 12.1 %collective-permute-start.23 = (bf16[256,512]{1,0:T(8,128)(2,1)S(1)}, bf16[256,512]{1,0:T(8,128)(2,1)S(1)}, u32[]{:S(2)}, u32[]{:S(2)}) collective-permute-start(bf16[256,512]{1,0:T(8,128)(2,1)S(1)} %get-tuple-element.105), channel_id=1, source_target_pairs={{0,8},{4,12},{8,0},{12,4},{1,9},{5,13},{9,1},{13,5},{2,10},{6,14},... | collective-permute-start | bytes 786440 | tf_op jit(solution)/shard_map/ppermute | solution.py:19
  58.2 13.6 %collective-permute-start.21 = (bf16[256,256]{1,0:T(8,128)(2,1)S(1)}, bf16[256,256]{1,0:T(8,128)(2,1)S(1)}, u32[]{:S(2)}, u32[]{:S(2)}) collective-permute-start(bf16[256,256]{1,0:T(8,128)(2,1)S(1)} %slice.258), channel_id=1, source_target_pairs={{0,8},{4,12},{8,0},{12,4},{1,9},{5,13},{9,1},{13,5},{2,10},{6,14},... | collective-permute-start | bytes 393224 | tf_op jit(solution)/shard_map/ppermute | solution.py:19
  59.2 7.6 %collective-permute-start.25 = (bf16[256,256]{1,0:T(8,128)(2,1)S(1)}, bf16[256,256]{1,0:T(8,128)(2,1)S(1)}, u32[]{:S(2)}, u32[]{:S(2)}) collective-permute-start(bf16[256,256]{1,0:T(8,128)(2,1)S(1)} %get-tuple-element.94), channel_id=1, source_target_pairs={{0,12},{4,8},{8,4},{12,0},{1,13},{5,9},{9,5},{13,1},{2,14},{6,10},... | collective-permute-start | bytes 393224 | tf_op jit(solution)/shard_map/ppermute | solution.py:19
  61.3 5.4 %collective-permute-start.28 = (bf16[256,256]{1,0:T(8,128)(2,1)S(1)}, bf16[256,256]{1,0:T(8,128)(2,1)S(1)}, u32[]{:S(2)}, u32[]{:S(2)}) collective-permute-start(bf16[256,256]{1,0:T(8,128)(2,1)S(1)} %add_convert_fusion.5), channel_id=1, source_target_pairs={{0,1},{1,0},{2,3},{3,2},{4,5},{5,4},{6,7},{7,6},{8,9},{9,8},{10,11... | collective-permute-start | bytes 393224 | tf_op jit(solution)/shard_map/ppermute | solution.py:19
  63.1 8.7 %collective-permute-start.20 = (bf16[256,256]{1,0:T(8,128)(2,1)S(1)}, bf16[256,256]{1,0:T(8,128)(2,1)S(1)}, u32[]{:S(2)}, u32[]{:S(2)}) collective-permute-start(bf16[256,256]{1,0:T(8,128)(2,1)S(1)} %slice.349), channel_id=1, source_target_pairs={{0,4},{4,0},{8,12},{12,8},{1,5},{5,1},{9,13},{13,9},{2,6},{6,2},{1... | collective-permute-start | bytes 393224 | tf_op jit(solution)/shard_map/ppermute | solution.py:19
  66.9 7.3 %collective-permute-start.29 = (bf16[256,256]{1,0:T(8,128)(2,1)S(1)}, bf16[256,256]{1,0:T(8,128)(2,1)S(1)}, u32[]{:S(2)}, u32[]{:S(2)}) collective-permute-start(bf16[256,256]{1,0:T(8,128)(2,1)S(1)} %get-tuple-element.101), channel_id=1, source_target_pairs={{0,2},{1,3},{2,0},{3,1},{4,6},{5,7},{6,4},{7,5},{8,10},{9,11},{10,... | collective-permute-start | bytes 393224 | tf_op jit(solution)/shard_map/ppermute | solution.py:19
  69.0 5.9 %collective-permute-start.30 = (bf16[256,256]{1,0:T(8,128)(2,1)S(1)}, bf16[256,256]{1,0:T(8,128)(2,1)S(1)}, u32[]{:S(2)}, u32[]{:S(2)}) collective-permute-start(bf16[256,256]{1,0:T(8,128)(2,1)S(1)} %add_convert_fusion.4), channel_id=1, source_target_pairs={{0,12},{4,8},{8,4},{12,0},{1,13},{5,9},{9,5},{13,1},{2,14},{6,10},... | collective-permute-start | bytes 393224 | tf_op jit(solution)/shard_map/ppermute | solution.py:19
  76.0 7.5 %collective-permute-start.35 = (bf16[256,256]{1,0:T(8,128)(2,1)S(1)}, bf16[256,256]{1,0:T(8,128)(2,1)S(1)}, u32[]{:S(2)}, u32[]{:S(2)}) collective-permute-start(bf16[256,256]{1,0:T(8,128)(2,1)S(1)} %get-tuple-element.68), channel_id=1, source_target_pairs={{0,2},{1,3},{2,0},{3,1},{4,6},{5,7},{6,4},{7,5},{8,10},{9,11},{10,... | collective-permute-start | bytes 393224 | tf_op jit(solution)/shard_map/ppermute | solution.py:19
  78.7 6.3 %collective-permute-start.32 = (bf16[256,256]{1,0:T(8,128)(2,1)S(1)}, bf16[256,256]{1,0:T(8,128)(2,1)S(1)}, u32[]{:S(2)}, u32[]{:S(2)}) collective-permute-start(bf16[256,256]{1,0:T(8,128)(2,1)S(1)} %get-tuple-element.68), channel_id=1, source_target_pairs={{0,4},{4,0},{8,12},{12,8},{1,5},{5,1},{9,13},{13,9},{2,6},{6,2},{1... | collective-permute-start | bytes 393224 | tf_op jit(solution)/shard_map/ppermute | solution.py:19
  78.9 6.8 %collective-permute-start.34 = (bf16[256,256]{1,0:T(8,128)(2,1)S(1)}, bf16[256,256]{1,0:T(8,128)(2,1)S(1)}, u32[]{:S(2)}, u32[]{:S(2)}) collective-permute-start(bf16[256,256]{1,0:T(8,128)(2,1)S(1)} %get-tuple-element.68), channel_id=1, source_target_pairs={{0,1},{1,0},{2,3},{3,2},{4,5},{5,4},{6,7},{7,6},{8,9},{9,8},{10,11... | collective-permute-start | bytes 393224 | tf_op jit(solution)/shard_map/ppermute | solution.py:19
  81.4 7.5 %collective-permute-start.33 = (bf16[256,256]{1,0:T(8,128)(2,1)S(1)}, bf16[256,256]{1,0:T(8,128)(2,1)S(1)}, u32[]{:S(2)}, u32[]{:S(2)}) collective-permute-start(bf16[256,256]{1,0:T(8,128)(2,1)S(1)} %get-tuple-element.68), channel_id=1, source_target_pairs={{0,12},{4,8},{8,4},{12,0},{1,13},{5,9},{9,5},{13,1},{2,14},{6,10},... | collective-permute-start | bytes 393224 | tf_op jit(solution)/shard_map/ppermute | solution.py:19
  83.5 8.1 %collective-permute-start.36 = (bf16[256,256]{1,0:T(8,128)(2,1)S(1)}, bf16[256,256]{1,0:T(8,128)(2,1)S(1)}, u32[]{:S(2)}, u32[]{:S(2)}) collective-permute-start(bf16[256,256]{1,0:T(8,128)(2,1)S(1)} %collective-permute-done.35), channel_id=1, source_target_pairs={{0,12},{4,8},{8,4},{12,0},{1,13},{5,9},{9,5},{13,1},{2,14},{6,10},... | collective-permute-start | bytes 393224 | tf_op jit(solution)/shard_map/ppermute | solution.py:19
  84.3 11.8 %collective-permute-start.38 = (bf16[256,256]{1,0:T(8,128)(2,1)S(1)}, bf16[256,256]{1,0:T(8,128)(2,1)S(1)}, u32[]{:S(2)}, u32[]{:S(2)}) collective-permute-start(bf16[256,256]{1,0:T(8,128)(2,1)S(1)} %get-tuple-element.68), channel_id=1, source_target_pairs={{0,8},{4,12},{8,0},{12,4},{1,9},{5,13},{9,1},{13,5},{2,10},{6,14},... | collective-permute-start | bytes 393224 | tf_op jit(solution)/shard_map/ppermute | solution.py:19
  85.7 6.9 %collective-permute-start.37 = (bf16[256,256]{1,0:T(8,128)(2,1)S(1)}, bf16[256,256]{1,0:T(8,128)(2,1)S(1)}, u32[]{:S(2)}, u32[]{:S(2)}) collective-permute-start(bf16[256,256]{1,0:T(8,128)(2,1)S(1)} %collective-permute-done.35), channel_id=1, source_target_pairs={{0,1},{1,0},{2,3},{3,2},{4,5},{5,4},{6,7},{7,6},{8,9},{9,8},{10,11... | collective-permute-start | bytes 393224 | tf_op jit(solution)/shard_map/ppermute | solution.py:19
  87.1 8.9 %collective-permute-start.40 = (bf16[256,512]{1,0:T(8,128)(2,1)S(1)}, bf16[256,512]{1,0:T(8,128)(2,1)S(1)}, u32[]{:S(2)}, u32[]{:S(2)}) collective-permute-start(bf16[256,512]{1,0:T(8,128)(2,1)S(1)} %get-tuple-element.126), channel_id=1, source_target_pairs={{0,8},{4,12},{8,0},{12,4},{1,9},{5,13},{9,1},{13,5},{2,10},{6,14},... | collective-permute-start | bytes 786440 | tf_op jit(solution)/shard_map/ppermute | solution.py:19
  88.9 7.2 %collective-permute-start.39 = (bf16[256,512]{1,0:T(8,128)(2,1)S(1)}, bf16[256,512]{1,0:T(8,128)(2,1)S(1)}, u32[]{:S(2)}, u32[]{:S(2)}) collective-permute-start(bf16[256,512]{1,0:T(8,128)(2,1)S(1)} %get-tuple-element.127), channel_id=1, source_target_pairs={{0,4},{4,0},{8,12},{12,8},{1,5},{5,1},{9,13},{13,9},{2,6},{6,2},{1... | collective-permute-start | bytes 786440 | tf_op jit(solution)/shard_map/ppermute | solution.py:19
  91.6 6.4 %collective-permute-start.41 = (bf16[256,512]{1,0:T(8,128)(2,1)S(1)}, bf16[256,512]{1,0:T(8,128)(2,1)S(1)}, u32[]{:S(2)}, u32[]{:S(2)}) collective-permute-start(bf16[256,512]{1,0:T(8,128)(2,1)S(1)} %pad_maximum_fusion.5), channel_id=1, source_target_pairs={{0,1},{1,0},{2,3},{3,2},{4,5},{5,4},{6,7},{7,6},{8,9},{9,8},{10,11... | collective-permute-start | bytes 786440 | tf_op jit(solution)/shard_map/ppermute | solution.py:19
  101.7 14.1 %collective-permute-start.50 = (bf16[256,768]{1,0:T(8,128)(2,1)S(1)}, bf16[256,768]{1,0:T(8,128)(2,1)S(1)}, u32[]{:S(2)}, u32[]{:S(2)}) collective-permute-start(bf16[256,768]{1,0:T(8,128)(2,1)S(1)} %get-tuple-element.107.proj_ref), channel_id=1, source_target_pairs={{0,16},{16,0},{1,17},{17,1},{2,18},{18,2},{3,19},{19,3},{4,20},{20... | collective-permute-start | bytes 1179656 | tf_op jit(solution)/shard_map/ppermute | solution.py:19
  107.9 5.4 %collective-permute-start.47 = (f32[256]{0:T(256)S(1)}, f32[256]{0:T(256)S(1)}, u32[]{:S(2)}, u32[]{:S(2)}) collective-permute-start(f32[256]{0:T(256)S(1)} %add.172), channel_id=1, source_target_pairs={{0,3},{1,2},{2,1},{3,0},{4,7},{5,6},{6,5},{7,4},{8,11},{9,10},{10,... | collective-permute-start | bytes 3080 | tf_op jit(solution)/shard_map/ppermute | solution.py:19
  116.4 8.6 %collective-permute-start.56 = (bf16[256,512]{1,0:T(8,128)(2,1)S(1)}, bf16[256,512]{1,0:T(8,128)(2,1)S(1)}, u32[]{:S(2)}, u32[]{:S(2)}) collective-permute-start(bf16[256,512]{1,0:T(8,128)(2,1)S(1)} %slice.290), channel_id=1, source_target_pairs={{0,1},{1,0},{2,3},{3,2},{4,5},{5,4},{6,7},{7,6},{8,9},{9,8},{10,11... | collective-permute-start | bytes 786440 | tf_op jit(solution)/shard_map/ppermute | solution.py:19
  117.8 8.0 %collective-permute-start.58 = (bf16[256,256]{1,0:T(8,128)(2,1)S(1)}, bf16[256,256]{1,0:T(8,128)(2,1)S(1)}, u32[]{:S(2)}, u32[]{:S(2)}) collective-permute-start(bf16[256,256]{1,0:T(8,128)(2,1)S(1)} %get-tuple-element.110), channel_id=1, source_target_pairs={{0,4},{4,0},{8,12},{12,8},{1,5},{5,1},{9,13},{13,9},{2,6},{6,2},{1... | collective-permute-start | bytes 393224 | tf_op jit(solution)/shard_map/ppermute | solution.py:19
  118.8 8.4 %collective-permute-start.59 = (bf16[256,256]{1,0:T(8,128)(2,1)S(1)}, bf16[256,256]{1,0:T(8,128)(2,1)S(1)}, u32[]{:S(2)}, u32[]{:S(2)}) collective-permute-start(bf16[256,256]{1,0:T(8,128)(2,1)S(1)} %get-tuple-element.111), channel_id=1, source_target_pairs={{0,8},{4,12},{8,0},{12,4},{1,9},{5,13},{9,1},{13,5},{2,10},{6,14},... | collective-permute-start | bytes 393224 | tf_op jit(solution)/shard_map/ppermute | solution.py:19
  120.1 9.7 %collective-permute-start.54 = (bf16[256,512]{1,0:T(8,128)(2,1)S(1)}, bf16[256,512]{1,0:T(8,128)(2,1)S(1)}, u32[]{:S(2)}, u32[]{:S(2)}) collective-permute-start(bf16[256,512]{1,0:T(8,128)(2,1)S(1)} %get-tuple-element.102), channel_id=1, source_target_pairs={{0,4},{4,0},{8,12},{12,8},{1,5},{5,1},{9,13},{13,9},{2,6},{6,2},{1... | collective-permute-start | bytes 786440 | tf_op jit(solution)/shard_map/ppermute | solution.py:19
  122.0 11.7 %collective-permute-start.55 = (bf16[256,512]{1,0:T(8,128)(2,1)S(1)}, bf16[256,512]{1,0:T(8,128)(2,1)S(1)}, u32[]{:S(2)}, u32[]{:S(2)}) collective-permute-start(bf16[256,512]{1,0:T(8,128)(2,1)S(1)} %get-tuple-element.103), channel_id=1, source_target_pairs={{0,8},{4,12},{8,0},{12,4},{1,9},{5,13},{9,1},{13,5},{2,10},{6,14},... | collective-permute-start | bytes 786440 | tf_op jit(solution)/shard_map/ppermute | solution.py:19
  125.0 13.1 %collective-permute-start.53 = (bf16[256,256]{1,0:T(8,128)(2,1)S(1)}, bf16[256,256]{1,0:T(8,128)(2,1)S(1)}, u32[]{:S(2)}, u32[]{:S(2)}) collective-permute-start(bf16[256,256]{1,0:T(8,128)(2,1)S(1)} %slice.283), channel_id=1, source_target_pairs={{0,8},{4,12},{8,0},{12,4},{1,9},{5,13},{9,1},{13,5},{2,10},{6,14},... | collective-permute-start | bytes 393224 | tf_op jit(solution)/shard_map/ppermute | solution.py:19
  125.9 7.9 %collective-permute-start.57 = (bf16[256,256]{1,0:T(8,128)(2,1)S(1)}, bf16[256,256]{1,0:T(8,128)(2,1)S(1)}, u32[]{:S(2)}, u32[]{:S(2)}) collective-permute-start(bf16[256,256]{1,0:T(8,128)(2,1)S(1)} %get-tuple-element.92), channel_id=1, source_target_pairs={{0,12},{4,8},{8,4},{12,0},{1,13},{5,9},{9,5},{13,1},{2,14},{6,10},... | collective-permute-start | bytes 393224 | tf_op jit(solution)/shard_map/ppermute | solution.py:19
  127.2 6.6 %collective-permute-start.60 = (bf16[256,256]{1,0:T(8,128)(2,1)S(1)}, bf16[256,256]{1,0:T(8,128)(2,1)S(1)}, u32[]{:S(2)}, u32[]{:S(2)}) collective-permute-start(bf16[256,256]{1,0:T(8,128)(2,1)S(1)} %add_convert_fusion.2), channel_id=1, source_target_pairs={{0,1},{1,0},{2,3},{3,2},{4,5},{5,4},{6,7},{7,6},{8,9},{9,8},{10,11... | collective-permute-start | bytes 393224 | tf_op jit(solution)/shard_map/ppermute | solution.py:19
  129.8 8.3 %collective-permute-start.52 = (bf16[256,256]{1,0:T(8,128)(2,1)S(1)}, bf16[256,256]{1,0:T(8,128)(2,1)S(1)}, u32[]{:S(2)}, u32[]{:S(2)}) collective-permute-start(bf16[256,256]{1,0:T(8,128)(2,1)S(1)} %slice.348), channel_id=1, source_target_pairs={{0,4},{4,0},{8,12},{12,8},{1,5},{5,1},{9,13},{13,9},{2,6},{6,2},{1... | collective-permute-start | bytes 393224 | tf_op jit(solution)/shard_map/ppermute | solution.py:19
  133.9 7.4 %collective-permute-start.61 = (bf16[256,256]{1,0:T(8,128)(2,1)S(1)}, bf16[256,256]{1,0:T(8,128)(2,1)S(1)}, u32[]{:S(2)}, u32[]{:S(2)}) collective-permute-start(bf16[256,256]{1,0:T(8,128)(2,1)S(1)} %get-tuple-element.98), channel_id=1, source_target_pairs={{0,2},{1,3},{2,0},{3,1},{4,6},{5,7},{6,4},{7,5},{8,10},{9,11},{10,... | collective-permute-start | bytes 393224 | tf_op jit(solution)/shard_map/ppermute | solution.py:19
  134.9 6.4 %collective-permute-start.62 = (bf16[256,256]{1,0:T(8,128)(2,1)S(1)}, bf16[256,256]{1,0:T(8,128)(2,1)S(1)}, u32[]{:S(2)}, u32[]{:S(2)}) collective-permute-start(bf16[256,256]{1,0:T(8,128)(2,1)S(1)} %add_convert_fusion.1), channel_id=1, source_target_pairs={{0,12},{4,8},{8,4},{12,0},{1,13},{5,9},{9,5},{13,1},{2,14},{6,10},... | collective-permute-start | bytes 393224 | tf_op jit(solution)/shard_map/ppermute | solution.py:19
  136.3 5.8 %collective-permute-start.63 = (bf16[256,256]{1,0:T(8,128)(2,1)S(1)}, bf16[256,256]{1,0:T(8,128)(2,1)S(1)}, u32[]{:S(2)}, u32[]{:S(2)}) collective-permute-start(bf16[256,256]{1,0:T(8,128)(2,1)S(1)} %add_convert_fusion), channel_id=1, source_target_pairs={{0,1},{1,0},{2,3},{3,2},{4,5},{5,4},{6,7},{7,6},{8,9},{9,8},{10,11... | collective-permute-start | bytes 393224 | tf_op jit(solution)/shard_map/ppermute | solution.py:19
  (16 other events, 63.3 us)

commit v12 on v10

--- a/solution.py
+++ b/solution.py
@@ -81,7 +81,7 @@
     (far_across,), (three,) = send("row", 3, far_across), send("feat", 1, three)
     two = summed(b[0, 2], *twos, far_across, three)
     near_across = summed(after(b[3, 0], two), near_across)
-    one = summed(after(b[0, 1], two), *ones)
+    one = summed(after(b[0, 1], three), *ones)
     (two,), (near_across,), (one,) = (
         send("feat", 2, two),
         send("row", 3, near_across),

time: 136 us -> 136 us (level)
  no operation moved by 1% of the time
where the time goes in v12:
time: 136 us
  starting transfers between devices  76.5 us (56%)
  waiting for transfers between devices  41.5 us (31%)
  matrix products  9.38 us (7%)
  Pallas kernels  3.92 us (3%)
  local copies, waits for them, and re-layouts  2.47 us (2%)
    ppermute x64, starting transfers between devices, xor_move(): return lax.ppermute(block, axis, [(i, i ^ mask) for i in range(count)])  76.5 us
    ppermute x64, waiting for transfers between devices, xor_move(): return lax.ppermute(block, axis, [(i, i ^ mask) for i in range(count)])  41.5 us
    dot_general x6, matrix products, on_device(): lax.dot_general(residue, groups[g], (((1,), (0,)), ((), ())), preferred_e...  4.76 us
    dot_general x6, matrix products, on_device(): lax.dot_general(join(*blocks), groups[g], (((1,), (1,)), ((), ())), prefe...  4.62 us
    pallas_call x1, Pallas kernels, regroup(): pl.pallas_call(kernel, out_shape=[jax.ShapeDtypeStruct((rows_here, len(pl...  3 us
  transfers between devices with their start and end apart: 64, of which 37 were waited for; matrix products, arithmetic and copies ran while one was open for 6% of the time, Pallas kernels for 3%

profile of v12, /device:TPU:0, one launch (start us, length us, event | category | flops | bytes accessed | tf_op | source)
XLA Modules:
  0.0 136.2 jit_solution(9867886437225755565)
XLA Ops:
  1.7 4.1 %collective-permute-start.4 = (bf16[256,256]{1,0:T(8,128)(2,1)S(1)}, bf16[256,256]{1,0:T(8,128)(2,1)S(1)}, u32[]{:S(2)}, u32[]{:S(2)}) collective-permute-start(bf16[256,256]{1,0:T(8,128)(2,1)S(1)} %fusion.28), channel_id=1, source_target_pairs={{0,2},{1,3},{2,0},{3,1},{4,6},{5,7},{6,4},{7,5},{8,10},{9,11},{10,... | collective-permute-start | bytes 393224 | tf_op jit(solution)/shard_map/ppermute | solution.py:19
  5.8 1.6 %collective-permute-start.3 = (bf16[256,256]{1,0:T(8,128)(2,1)S(1)}, bf16[256,256]{1,0:T(8,128)(2,1)S(1)}, u32[]{:S(2)}, u32[]{:S(2)}) collective-permute-start(bf16[256,256]{1,0:T(8,128)(2,1)S(1)} %fusion.28), channel_id=1, source_target_pairs={{0,1},{1,0},{2,3},{3,2},{4,5},{5,4},{6,7},{7,6},{8,9},{9,8},{10,11... | collective-permute-start | bytes 393224 | tf_op jit(solution)/shard_map/ppermute | solution.py:19
  7.4 1.5 %collective-permute-start = (bf16[256,256]{1,0:T(8,128)(2,1)S(1)}, bf16[256,256]{1,0:T(8,128)(2,1)S(1)}, u32[]{:S(2)}, u32[]{:S(2)}) collective-permute-start(bf16[256,256]{1,0:T(8,128)(2,1)S(1)} %fusion.28), channel_id=1, source_target_pairs={{0,4},{4,0},{8,12},{12,8},{1,5},{5,1},{9,13},{13,9},{2,6},{6,2},{1... | collective-permute-start | bytes 393224 | tf_op jit(solution)/shard_map/ppermute | solution.py:19
  8.9 1.5 %collective-permute-start.2 = (bf16[256,256]{1,0:T(8,128)(2,1)S(1)}, bf16[256,256]{1,0:T(8,128)(2,1)S(1)}, u32[]{:S(2)}, u32[]{:S(2)}) collective-permute-start(bf16[256,256]{1,0:T(8,128)(2,1)S(1)} %fusion.28), channel_id=1, source_target_pairs={{0,12},{4,8},{8,4},{12,0},{1,13},{5,9},{9,5},{13,1},{2,14},{6,10},... | collective-permute-start | bytes 393224 | tf_op jit(solution)/shard_map/ppermute | solution.py:19
  10.9 1.3 collective-permute-done.4
  12.9 2.4 %collective-permute-start.5 = (bf16[256,256]{1,0:T(8,128)(2,1)S(1)}, bf16[256,256]{1,0:T(8,128)(2,1)S(1)}, u32[]{:S(2)}, u32[]{:S(2)}) collective-permute-start(bf16[256,256]{1,0:T(8,128)(2,1)S(1)} %collective-permute-done.4), channel_id=1, source_target_pairs={{0,12},{4,8},{8,4},{12,0},{1,13},{5,9},{9,5},{13,1},{2,14},{6,10},... | collective-permute-start | bytes 393224 | tf_op jit(solution)/shard_map/ppermute | solution.py:19
  15.3 3.0 %regroup.1 = (bf16[768,1536]{1,0:T(8,128)(2,1)S(1)}, bf16[768,1536]{1,0:T(8,128)(2,1)S(1)}, bf16[768,1024]{1,0:T(8,128)(2,1)S(1)}) custom-call(bf16[768,4096]{1,0:T(8,128)(2,1)} %bitcast.37), custom_call_target="tpu_custom_call" | custom-call | bytes 12582912 | tf_op jit(solution)/shard_map/regroup/pallas_call | solution.py:140
  21.9 1.5 %collective-permute-start.10 = (bf16[256,256]{1,0:T(8,128)(2,1)S(1)}, bf16[256,256]{1,0:T(8,128)(2,1)S(1)}, u32[]{:S(2)}, u32[]{:S(2)}) collective-permute-start(bf16[256,256]{1,0:T(8,128)(2,1)S(1)} %collective-permute-done.6), channel_id=1, source_target_pairs={{0,4},{4,0},{8,12},{12,8},{1,5},{5,1},{9,13},{13,9},{2,6},{6,2},{1... | collective-permute-start | bytes 393224 | tf_op jit(solution)/shard_map/ppermute | solution.py:19
  23.5 1.5 %collective-permute-start.11 = (bf16[256,256]{1,0:T(8,128)(2,1)S(1)}, bf16[256,256]{1,0:T(8,128)(2,1)S(1)}, u32[]{:S(2)}, u32[]{:S(2)}) collective-permute-start(bf16[256,256]{1,0:T(8,128)(2,1)S(1)} %collective-permute-done.6), channel_id=1, source_target_pairs={{0,8},{4,12},{8,0},{12,4},{1,9},{5,13},{9,1},{13,5},{2,10},{6,14},... | collective-permute-start | bytes 393224 | tf_op jit(solution)/shard_map/ppermute | solution.py:19
  25.0 2.5 %collective-permute-done.8 = bf16[256,512]{1,0:T(8,128)(2,1)S(1)} collective-permute-done((bf16[256,512]{1,0:T(8,128)(2,1)S(1)}, bf16[256,512]{1,0:T(8,128)(2,1)S(1)}, u32[]{:S(2)}, u32[]{:S(2)}) %collective-permute-start.8) | collective-permute-done | bytes 262176 | tf_op jit(solution)/shard_map/ppermute | solution.py:19
  29.9 1.6 %collective-permute-start.12 = (f32[256]{0:T(256)S(1)}, f32[256]{0:T(256)S(1)}, u32[]{:S(2)}, u32[]{:S(2)}) collective-permute-start(f32[256]{0:T(256)S(1)} %get-tuple-element.112), channel_id=1, source_target_pairs={{0,12},{4,8},{8,4},{12,0},{1,13},{5,9},{9,5},{13,1},{2,14},{6,10},... | collective-permute-start | bytes 3080 | tf_op jit(solution)/shard_map/ppermute | solution.py:19
  32.3 1.2 collective-permute-start.14
  35.9 2.8 %collective-permute-start.15 = (f32[256]{0:T(256)S(1)}, f32[256]{0:T(256)S(1)}, u32[]{:S(2)}, u32[]{:S(2)}) collective-permute-start(f32[256]{0:T(256)S(1)} %add.148), channel_id=1, source_target_pairs={{0,3},{1,2},{2,1},{3,0},{4,7},{5,6},{6,5},{7,4},{8,11},{9,10},{10,... | collective-permute-start | bytes 3080 | tf_op jit(solution)/shard_map/ppermute | solution.py:19
  38.9 1.3 collective-permute-start.17
  41.2 1.9 %collective-permute-done.16 = f32[256]{0:T(256)S(1)} collective-permute-done((f32[256]{0:T(256)S(1)}, f32[256]{0:T(256)S(1)}, u32[]{:S(2)}, u32[]{:S(2)}) %collective-permute-start.16) | collective-permute-done | bytes 1056 | tf_op jit(solution)/shard_map/ppermute | solution.py:19
  46.0 1.5 %collective-permute-start.26 = (bf16[256,256]{1,0:T(8,128)(2,1)S(1)}, bf16[256,256]{1,0:T(8,128)(2,1)S(1)}, u32[]{:S(2)}, u32[]{:S(2)}) collective-permute-start(bf16[256,256]{1,0:T(8,128)(2,1)S(1)} %get-tuple-element.116), channel_id=1, source_target_pairs={{0,4},{4,0},{8,12},{12,8},{1,5},{5,1},{9,13},{13,9},{2,6},{6,2},{1... | collective-permute-start | bytes 393224 | tf_op jit(solution)/shard_map/ppermute | solution.py:19
  47.4 1.5 %collective-permute-start.27 = (bf16[256,256]{1,0:T(8,128)(2,1)S(1)}, bf16[256,256]{1,0:T(8,128)(2,1)S(1)}, u32[]{:S(2)}, u32[]{:S(2)}) collective-permute-start(bf16[256,256]{1,0:T(8,128)(2,1)S(1)} %get-tuple-element.117), channel_id=1, source_target_pairs={{0,8},{4,12},{8,0},{12,4},{1,9},{5,13},{9,1},{13,5},{2,10},{6,14},... | collective-permute-start | bytes 393224 | tf_op jit(solution)/shard_map/ppermute | solution.py:19
  51.9 1.6 %collective-permute-done.24 = bf16[256,512]{1,0:T(8,128)(2,1)S(1)} collective-permute-done((bf16[256,512]{1,0:T(8,128)(2,1)S(1)}, bf16[256,512]{1,0:T(8,128)(2,1)S(1)}, u32[]{:S(2)}, u32[]{:S(2)}) %collective-permute-start.24) | collective-permute-done | bytes 262176 | tf_op jit(solution)/shard_map/ppermute | solution.py:19
  53.6 2.5 %collective-permute-start.25 = (bf16[256,256]{1,0:T(8,128)(2,1)S(1)}, bf16[256,256]{1,0:T(8,128)(2,1)S(1)}, u32[]{:S(2)}, u32[]{:S(2)}) collective-permute-start(bf16[256,256]{1,0:T(8,128)(2,1)S(1)} %get-tuple-element.101), channel_id=1, source_target_pairs={{0,12},{4,8},{8,4},{12,0},{1,13},{5,9},{9,5},{13,1},{2,14},{6,10},... | collective-permute-start | bytes 393224 | tf_op jit(solution)/shard_map/ppermute | solution.py:19
  58.4 1.3 collective-permute-start.21
  62.1 2.1 %collective-permute-start.29 = (bf16[256,256]{1,0:T(8,128)(2,1)S(1)}, bf16[256,256]{1,0:T(8,128)(2,1)S(1)}, u32[]{:S(2)}, u32[]{:S(2)}) collective-permute-start(bf16[256,256]{1,0:T(8,128)(2,1)S(1)} %get-tuple-element.99), channel_id=1, source_target_pairs={{0,2},{1,3},{2,0},{3,1},{4,6},{5,7},{6,4},{7,5},{8,10},{9,11},{10,... | collective-permute-start | bytes 393224 | tf_op jit(solution)/shard_map/ppermute | solution.py:19
  64.2 1.5 %collective-permute-start.30 = (bf16[256,256]{1,0:T(8,128)(2,1)S(1)}, bf16[256,256]{1,0:T(8,128)(2,1)S(1)}, u32[]{:S(2)}, u32[]{:S(2)}) collective-permute-start(bf16[256,256]{1,0:T(8,128)(2,1)S(1)} %add_convert_fusion.4), channel_id=1, source_target_pairs={{0,12},{4,8},{8,4},{12,0},{1,13},{5,9},{9,5},{13,1},{2,14},{6,10},... | collective-permute-start | bytes 393224 | tf_op jit(solution)/shard_map/ppermute | solution.py:19
  66.7 2.7 %collective-permute-done.29 = bf16[256,256]{1,0:T(8,128)(2,1)S(1)} collective-permute-done((bf16[256,256]{1,0:T(8,128)(2,1)S(1)}, bf16[256,256]{1,0:T(8,128)(2,1)S(1)}, u32[]{:S(2)}, u32[]{:S(2)}) %collective-permute-start.29) | collective-permute-done | bytes 131104 | tf_op jit(solution)/shard_map/ppermute | solution.py:19
  73.0 2.2 %collective-permute-start.35 = (bf16[256,256]{1,0:T(8,128)(2,1)S(1)}, bf16[256,256]{1,0:T(8,128)(2,1)S(1)}, u32[]{:S(2)}, u32[]{:S(2)}) collective-permute-start(bf16[256,256]{1,0:T(8,128)(2,1)S(1)} %get-tuple-element.68), channel_id=1, source_target_pairs={{0,1},{1,0},{2,3},{3,2},{4,5},{5,4},{6,7},{7,6},{8,9},{9,8},{10,11... | collective-permute-start | bytes 393224 | tf_op jit(solution)/shard_map/ppermute | solution.py:19
  75.2 1.2 collective-permute-start.34
  76.3 2.1 %collective-permute-done.36 = bf16[256,256]{1,0:T(8,128)(2,1)S(1)} collective-permute-done((bf16[256,256]{1,0:T(8,128)(2,1)S(1)}, bf16[256,256]{1,0:T(8,128)(2,1)S(1)}, u32[]{:S(2)}, u32[]{:S(2)}) %collective-permute-start.36) | collective-permute-done | bytes 131104 | tf_op jit(solution)/shard_map/ppermute | solution.py:19
  78.4 1.5 %collective-permute-start.37 = (bf16[256,256]{1,0:T(8,128)(2,1)S(1)}, bf16[256,256]{1,0:T(8,128)(2,1)S(1)}, u32[]{:S(2)}, u32[]{:S(2)}) collective-permute-start(bf16[256,256]{1,0:T(8,128)(2,1)S(1)} %collective-permute-done.36), channel_id=1, source_target_pairs={{0,12},{4,8},{8,4},{12,0},{1,13},{5,9},{9,5},{13,1},{2,14},{6,10},... | collective-permute-start | bytes 393224 | tf_op jit(solution)/shard_map/ppermute | solution.py:19
  79.9 1.2 collective-permute-start.33
  83.2 2.2 %collective-permute-done.37 = bf16[256,256]{1,0:T(8,128)(2,1)S(1)} collective-permute-done((bf16[256,256]{1,0:T(8,128)(2,1)S(1)}, bf16[256,256]{1,0:T(8,128)(2,1)S(1)}, u32[]{:S(2)}, u32[]{:S(2)}) %collective-permute-start.37) | collective-permute-done | bytes 131104 | tf_op jit(solution)/shard_map/ppermute | solution.py:19
  85.6 1.9 %collective-permute-done.33 = bf16[256,256]{1,0:T(8,128)(2,1)S(1)} collective-permute-done((bf16[256,256]{1,0:T(8,128)(2,1)S(1)}, bf16[256,256]{1,0:T(8,128)(2,1)S(1)}, u32[]{:S(2)}, u32[]{:S(2)}) %collective-permute-start.33) | collective-permute-done | bytes 131104 | tf_op jit(solution)/shard_map/ppermute | solution.py:19
  88.4 1.3 collective-permute-start.42
  90.5 1.7 %collective-permute-done.40 = bf16[256,512]{1,0:T(8,128)(2,1)S(1)} collective-permute-done((bf16[256,512]{1,0:T(8,128)(2,1)S(1)}, bf16[256,512]{1,0:T(8,128)(2,1)S(1)}, u32[]{:S(2)}, u32[]{:S(2)}) %collective-permute-start.40) | collective-permute-done | bytes 262176 | tf_op jit(solution)/shard_map/ppermute | solution.py:19
  93.4 1.2 collective-permute-done.43
  95.4 1.5 %collective-permute-start.44 = (f32[256]{0:T(256)S(1)}, f32[256]{0:T(256)S(1)}, u32[]{:S(2)}, u32[]{:S(2)}) collective-permute-start(f32[256]{0:T(256)S(1)} %get-tuple-element.106), channel_id=1, source_target_pairs={{0,12},{4,8},{8,4},{12,0},{1,13},{5,9},{9,5},{13,1},{2,14},{6,10},... | collective-permute-start | bytes 3080 | tf_op jit(solution)/shard_map/ppermute | solution.py:19
  97.7 1.2 collective-permute-start.46
  101.3 1.7 %collective-permute-start.47 = (f32[256]{0:T(256)S(1)}, f32[256]{0:T(256)S(1)}, u32[]{:S(2)}, u32[]{:S(2)}) collective-permute-start(f32[256]{0:T(256)S(1)} %add.172), channel_id=1, source_target_pairs={{0,3},{1,2},{2,1},{3,0},{4,7},{5,6},{6,5},{7,4},{8,11},{9,10},{10,... | collective-permute-start | bytes 3080 | tf_op jit(solution)/shard_map/ppermute | solution.py:19
  103.1 2.6 %collective-permute-start.49 = (f32[256]{0:T(256)S(1)}, f32[256]{0:T(256)S(1)}, u32[]{:S(2)}, u32[]{:S(2)}) collective-permute-start(f32[256]{0:T(256)S(1)} %add.172), channel_id=1, source_target_pairs={{0,1},{1,0},{2,3},{3,2},{4,5},{5,4},{6,7},{7,6},{8,9},{9,8},{10,11... | collective-permute-start | bytes 3080 | tf_op jit(solution)/shard_map/ppermute | solution.py:19
  109.5 1.8 %collective-permute-start.56 = (bf16[256,512]{1,0:T(8,128)(2,1)S(1)}, bf16[256,512]{1,0:T(8,128)(2,1)S(1)}, u32[]{:S(2)}, u32[]{:S(2)}) collective-permute-start(bf16[256,512]{1,0:T(8,128)(2,1)S(1)} %slice.290), channel_id=1, source_target_pairs={{0,1},{1,0},{2,3},{3,2},{4,5},{5,4},{6,7},{7,6},{8,9},{9,8},{10,11... | collective-permute-start | bytes 786440 | tf_op jit(solution)/shard_map/ppermute | solution.py:19
  111.3 1.2 collective-permute-start.58
  114.2 1.3 collective-permute-start.54
  118.1 1.8 %collective-permute-start.57 = (bf16[256,256]{1,0:T(8,128)(2,1)S(1)}, bf16[256,256]{1,0:T(8,128)(2,1)S(1)}, u32[]{:S(2)}, u32[]{:S(2)}) collective-permute-start(bf16[256,256]{1,0:T(8,128)(2,1)S(1)} %get-tuple-element.96), channel_id=1, source_target_pairs={{0,12},{4,8},{8,4},{12,0},{1,13},{5,9},{9,5},{13,1},{2,14},{6,10},... | collective-permute-start | bytes 393224 | tf_op jit(solution)/shard_map/ppermute | solution.py:19
  119.9 1.5 %collective-permute-start.60 = (bf16[256,256]{1,0:T(8,128)(2,1)S(1)}, bf16[256,256]{1,0:T(8,128)(2,1)S(1)}, u32[]{:S(2)}, u32[]{:S(2)}) collective-permute-start(bf16[256,256]{1,0:T(8,128)(2,1)S(1)} %add_convert_fusion.2), channel_id=1, source_target_pairs={{0,1},{1,0},{2,3},{3,2},{4,5},{5,4},{6,7},{7,6},{8,9},{9,8},{10,11... | collective-permute-start | bytes 393224 | tf_op jit(solution)/shard_map/ppermute | solution.py:19
  121.5 1.3 collective-permute-start.52
  123.5 1.2 collective-permute-start.53
  125.7 1.3 collective-permute-done.57
  127.8 1.8 %collective-permute-start.62 = (bf16[256,256]{1,0:T(8,128)(2,1)S(1)}, bf16[256,256]{1,0:T(8,128)(2,1)S(1)}, u32[]{:S(2)}, u32[]{:S(2)}) collective-permute-start(bf16[256,256]{1,0:T(8,128)(2,1)S(1)} %add_convert_fusion.1), channel_id=1, source_target_pairs={{0,12},{4,8},{8,4},{12,0},{1,13},{5,9},{9,5},{13,1},{2,14},{6,10},... | collective-permute-start | bytes 393224 | tf_op jit(solution)/shard_map/ppermute | solution.py:19
  129.6 1.7 %collective-permute-start.63 = (bf16[256,256]{1,0:T(8,128)(2,1)S(1)}, bf16[256,256]{1,0:T(8,128)(2,1)S(1)}, u32[]{:S(2)}, u32[]{:S(2)}) collective-permute-start(bf16[256,256]{1,0:T(8,128)(2,1)S(1)} %add_convert_fusion), channel_id=1, source_target_pairs={{0,1},{1,0},{2,3},{3,2},{4,5},{5,4},{6,7},{7,6},{8,9},{9,8},{10,11... | collective-permute-start | bytes 393224 | tf_op jit(solution)/shard_map/ppermute | solution.py:19
  131.3 3.0 %collective-permute-done.61 = bf16[256,256]{1,0:T(8,128)(2,1)S(1)} collective-permute-done((bf16[256,256]{1,0:T(8,128)(2,1)S(1)}, bf16[256,256]{1,0:T(8,128)(2,1)S(1)}, u32[]{:S(2)}, u32[]{:S(2)}) %collective-permute-start.61) | collective-permute-done | bytes 131104 | tf_op jit(solution)/shard_map/ppermute | solution.py:19
  (167 shorter events, 49.2 us)
Async XLA Ops:
  1.7 10.5 %collective-permute-start.4 = (bf16[256,256]{1,0:T(8,128)(2,1)S(1)}, bf16[256,256]{1,0:T(8,128)(2,1)S(1)}, u32[]{:S(2)}, u32[]{:S(2)}) collective-permute-start(bf16[256,256]{1,0:T(8,128)(2,1)S(1)} %fusion.28), channel_id=1, source_target_pairs={{0,2},{1,3},{2,0},{3,1},{4,6},{5,7},{6,4},{7,5},{8,10},{9,11},{10,... | collective-permute-start | bytes 393224 | tf_op jit(solution)/shard_map/ppermute | solution.py:19
  5.8 7.0 %collective-permute-start.3 = (bf16[256,256]{1,0:T(8,128)(2,1)S(1)}, bf16[256,256]{1,0:T(8,128)(2,1)S(1)}, u32[]{:S(2)}, u32[]{:S(2)}) collective-permute-start(bf16[256,256]{1,0:T(8,128)(2,1)S(1)} %fusion.28), channel_id=1, source_target_pairs={{0,1},{1,0},{2,3},{3,2},{4,5},{5,4},{6,7},{7,6},{8,9},{9,8},{10,11... | collective-permute-start | bytes 393224 | tf_op jit(solution)/shard_map/ppermute | solution.py:19
  7.4 10.9 %collective-permute-start = (bf16[256,256]{1,0:T(8,128)(2,1)S(1)}, bf16[256,256]{1,0:T(8,128)(2,1)S(1)}, u32[]{:S(2)}, u32[]{:S(2)}) collective-permute-start(bf16[256,256]{1,0:T(8,128)(2,1)S(1)} %fusion.28), channel_id=1, source_target_pairs={{0,4},{4,0},{8,12},{12,8},{1,5},{5,1},{9,13},{13,9},{2,6},{6,2},{1... | collective-permute-start | bytes 393224 | tf_op jit(solution)/shard_map/ppermute | solution.py:19
  8.9 10.0 %collective-permute-start.2 = (bf16[256,256]{1,0:T(8,128)(2,1)S(1)}, bf16[256,256]{1,0:T(8,128)(2,1)S(1)}, u32[]{:S(2)}, u32[]{:S(2)}) collective-permute-start(bf16[256,256]{1,0:T(8,128)(2,1)S(1)} %fusion.28), channel_id=1, source_target_pairs={{0,12},{4,8},{8,4},{12,0},{1,13},{5,9},{9,5},{13,1},{2,14},{6,10},... | collective-permute-start | bytes 393224 | tf_op jit(solution)/shard_map/ppermute | solution.py:19
  10.4 9.7 %collective-permute-start.1 = (bf16[256,256]{1,0:T(8,128)(2,1)S(1)}, bf16[256,256]{1,0:T(8,128)(2,1)S(1)}, u32[]{:S(2)}, u32[]{:S(2)}) collective-permute-start(bf16[256,256]{1,0:T(8,128)(2,1)S(1)} %fusion.28), channel_id=1, source_target_pairs={{0,8},{4,12},{8,0},{12,4},{1,9},{5,13},{9,1},{13,5},{2,10},{6,14},... | collective-permute-start | bytes 393224 | tf_op jit(solution)/shard_map/ppermute | solution.py:19
  12.3 7.8 %collective-permute-start.6 = (bf16[256,256]{1,0:T(8,128)(2,1)S(1)}, bf16[256,256]{1,0:T(8,128)(2,1)S(1)}, u32[]{:S(2)}, u32[]{:S(2)}) collective-permute-start(bf16[256,256]{1,0:T(8,128)(2,1)S(1)} %collective-permute-done.4), channel_id=1, source_target_pairs={{0,1},{1,0},{2,3},{3,2},{4,5},{5,4},{6,7},{7,6},{8,9},{9,8},{10,11... | collective-permute-start | bytes 393224 | tf_op jit(solution)/shard_map/ppermute | solution.py:19
  12.9 7.2 %collective-permute-start.5 = (bf16[256,256]{1,0:T(8,128)(2,1)S(1)}, bf16[256,256]{1,0:T(8,128)(2,1)S(1)}, u32[]{:S(2)}, u32[]{:S(2)}) collective-permute-start(bf16[256,256]{1,0:T(8,128)(2,1)S(1)} %collective-permute-done.4), channel_id=1, source_target_pairs={{0,12},{4,8},{8,4},{12,0},{1,13},{5,9},{9,5},{13,1},{2,14},{6,10},... | collective-permute-start | bytes 393224 | tf_op jit(solution)/shard_map/ppermute | solution.py:19
  18.4 9.1 %collective-permute-start.8 = (bf16[256,512]{1,0:T(8,128)(2,1)S(1)}, bf16[256,512]{1,0:T(8,128)(2,1)S(1)}, u32[]{:S(2)}, u32[]{:S(2)}) collective-permute-start(bf16[256,512]{1,0:T(8,128)(2,1)S(1)} %get-tuple-element.132), channel_id=1, source_target_pairs={{0,8},{4,12},{8,0},{12,4},{1,9},{5,13},{9,1},{13,5},{2,10},{6,14},... | collective-permute-start | bytes 786440 | tf_op jit(solution)/shard_map/ppermute | solution.py:19
  19.0 8.8 %collective-permute-start.7 = (bf16[256,512]{1,0:T(8,128)(2,1)S(1)}, bf16[256,512]{1,0:T(8,128)(2,1)S(1)}, u32[]{:S(2)}, u32[]{:S(2)}) collective-permute-start(bf16[256,512]{1,0:T(8,128)(2,1)S(1)} %get-tuple-element.133), channel_id=1, source_target_pairs={{0,4},{4,0},{8,12},{12,8},{1,5},{5,1},{9,13},{13,9},{2,6},{6,2},{1... | collective-permute-start | bytes 786440 | tf_op jit(solution)/shard_map/ppermute | solution.py:19
  21.0 7.7 %collective-permute-start.9 = (bf16[256,512]{1,0:T(8,128)(2,1)S(1)}, bf16[256,512]{1,0:T(8,128)(2,1)S(1)}, u32[]{:S(2)}, u32[]{:S(2)}) collective-permute-start(bf16[256,512]{1,0:T(8,128)(2,1)S(1)} %pad_maximum_fusion.4), channel_id=1, source_target_pairs={{0,1},{1,0},{2,3},{3,2},{4,5},{5,4},{6,7},{7,6},{8,9},{9,8},{10,11... | collective-permute-start | bytes 786440 | tf_op jit(solution)/shard_map/ppermute | solution.py:19
  21.9 7.2 %collective-permute-start.10 = (bf16[256,256]{1,0:T(8,128)(2,1)S(1)}, bf16[256,256]{1,0:T(8,128)(2,1)S(1)}, u32[]{:S(2)}, u32[]{:S(2)}) collective-permute-start(bf16[256,256]{1,0:T(8,128)(2,1)S(1)} %collective-permute-done.6), channel_id=1, source_target_pairs={{0,4},{4,0},{8,12},{12,8},{1,5},{5,1},{9,13},{13,9},{2,6},{6,2},{1... | collective-permute-start | bytes 393224 | tf_op jit(solution)/shard_map/ppermute | solution.py:19
  23.5 5.7 %collective-permute-start.11 = (bf16[256,256]{1,0:T(8,128)(2,1)S(1)}, bf16[256,256]{1,0:T(8,128)(2,1)S(1)}, u32[]{:S(2)}, u32[]{:S(2)}) collective-permute-start(bf16[256,256]{1,0:T(8,128)(2,1)S(1)} %collective-permute-done.6), channel_id=1, source_target_pairs={{0,8},{4,12},{8,0},{12,4},{1,9},{5,13},{9,1},{13,5},{2,10},{6,14},... | collective-permute-start | bytes 393224 | tf_op jit(solution)/shard_map/ppermute | solution.py:19
  29.8 14.5 %collective-permute-start.18 = (bf16[256,768]{1,0:T(8,128)(2,1)S(1)}, bf16[256,768]{1,0:T(8,128)(2,1)S(1)}, u32[]{:S(2)}, u32[]{:S(2)}) collective-permute-start(bf16[256,768]{1,0:T(8,128)(2,1)S(1)} %get-tuple-element.113), channel_id=1, source_target_pairs={{0,16},{16,0},{1,17},{17,1},{2,18},{18,2},{3,19},{19,3},{4,20},{20... | collective-permute-start | bytes 1179656 | tf_op jit(solution)/shard_map/ppermute | solution.py:19
  35.9 5.4 %collective-permute-start.15 = (f32[256]{0:T(256)S(1)}, f32[256]{0:T(256)S(1)}, u32[]{:S(2)}, u32[]{:S(2)}) collective-permute-start(f32[256]{0:T(256)S(1)} %add.148), channel_id=1, source_target_pairs={{0,3},{1,2},{2,1},{3,0},{4,7},{5,6},{6,5},{7,4},{8,11},{9,10},{10,... | collective-permute-start | bytes 3080 | tf_op jit(solution)/shard_map/ppermute | solution.py:19
  45.0 8.5 %collective-permute-start.24 = (bf16[256,512]{1,0:T(8,128)(2,1)S(1)}, bf16[256,512]{1,0:T(8,128)(2,1)S(1)}, u32[]{:S(2)}, u32[]{:S(2)}) collective-permute-start(bf16[256,512]{1,0:T(8,128)(2,1)S(1)} %slice.265), channel_id=1, source_target_pairs={{0,1},{1,0},{2,3},{3,2},{4,5},{5,4},{6,7},{7,6},{8,9},{9,8},{10,11... | collective-permute-start | bytes 786440 | tf_op jit(solution)/shard_map/ppermute | solution.py:19
  46.0 10.1 %collective-permute-start.26 = (bf16[256,256]{1,0:T(8,128)(2,1)S(1)}, bf16[256,256]{1,0:T(8,128)(2,1)S(1)}, u32[]{:S(2)}, u32[]{:S(2)}) collective-permute-start(bf16[256,256]{1,0:T(8,128)(2,1)S(1)} %get-tuple-element.116), channel_id=1, source_target_pairs={{0,4},{4,0},{8,12},{12,8},{1,5},{5,1},{9,13},{13,9},{2,6},{6,2},{1... | collective-permute-start | bytes 393224 | tf_op jit(solution)/shard_map/ppermute | solution.py:19
  47.4 8.6 %collective-permute-start.27 = (bf16[256,256]{1,0:T(8,128)(2,1)S(1)}, bf16[256,256]{1,0:T(8,128)(2,1)S(1)}, u32[]{:S(2)}, u32[]{:S(2)}) collective-permute-start(bf16[256,256]{1,0:T(8,128)(2,1)S(1)} %get-tuple-element.117), channel_id=1, source_target_pairs={{0,8},{4,12},{8,0},{12,4},{1,9},{5,13},{9,1},{13,5},{2,10},{6,14},... | collective-permute-start | bytes 393224 | tf_op jit(solution)/shard_map/ppermute | solution.py:19
  49.9 8.5 %collective-permute-start.22 = (bf16[256,512]{1,0:T(8,128)(2,1)S(1)}, bf16[256,512]{1,0:T(8,128)(2,1)S(1)}, u32[]{:S(2)}, u32[]{:S(2)}) collective-permute-start(bf16[256,512]{1,0:T(8,128)(2,1)S(1)} %get-tuple-element.110), channel_id=1, source_target_pairs={{0,4},{4,0},{8,12},{12,8},{1,5},{5,1},{9,13},{13,9},{2,6},{6,2},{1... | collective-permute-start | bytes 786440 | tf_op jit(solution)/shard_map/ppermute | solution.py:19
  50.5 10.1 %collective-permute-start.23 = (bf16[256,512]{1,0:T(8,128)(2,1)S(1)}, bf16[256,512]{1,0:T(8,128)(2,1)S(1)}, u32[]{:S(2)}, u32[]{:S(2)}) collective-permute-start(bf16[256,512]{1,0:T(8,128)(2,1)S(1)} %get-tuple-element.111), channel_id=1, source_target_pairs={{0,8},{4,12},{8,0},{12,4},{1,9},{5,13},{9,1},{13,5},{2,10},{6,14},... | collective-permute-start | bytes 786440 | tf_op jit(solution)/shard_map/ppermute | solution.py:19
  53.6 8.4 %collective-permute-start.25 = (bf16[256,256]{1,0:T(8,128)(2,1)S(1)}, bf16[256,256]{1,0:T(8,128)(2,1)S(1)}, u32[]{:S(2)}, u32[]{:S(2)}) collective-permute-start(bf16[256,256]{1,0:T(8,128)(2,1)S(1)} %get-tuple-element.101), channel_id=1, source_target_pairs={{0,12},{4,8},{8,4},{12,0},{1,13},{5,9},{9,5},{13,1},{2,14},{6,10},... | collective-permute-start | bytes 393224 | tf_op jit(solution)/shard_map/ppermute | solution.py:19
  57.1 9.6 %collective-permute-start.20 = (bf16[256,256]{1,0:T(8,128)(2,1)S(1)}, bf16[256,256]{1,0:T(8,128)(2,1)S(1)}, u32[]{:S(2)}, u32[]{:S(2)}) collective-permute-start(bf16[256,256]{1,0:T(8,128)(2,1)S(1)} %get-tuple-element.108), channel_id=1, source_target_pairs={{0,4},{4,0},{8,12},{12,8},{1,5},{5,1},{9,13},{13,9},{2,6},{6,2},{1... | collective-permute-start | bytes 393224 | tf_op jit(solution)/shard_map/ppermute | solution.py:19
  58.4 8.3 %collective-permute-start.21 = (bf16[256,256]{1,0:T(8,128)(2,1)S(1)}, bf16[256,256]{1,0:T(8,128)(2,1)S(1)}, u32[]{:S(2)}, u32[]{:S(2)}) collective-permute-start(bf16[256,256]{1,0:T(8,128)(2,1)S(1)} %get-tuple-element.109), channel_id=1, source_target_pairs={{0,8},{4,12},{8,0},{12,4},{1,9},{5,13},{9,1},{13,5},{2,10},{6,14},... | collective-permute-start | bytes 393224 | tf_op jit(solution)/shard_map/ppermute | solution.py:19
  62.1 7.3 %collective-permute-start.29 = (bf16[256,256]{1,0:T(8,128)(2,1)S(1)}, bf16[256,256]{1,0:T(8,128)(2,1)S(1)}, u32[]{:S(2)}, u32[]{:S(2)}) collective-permute-start(bf16[256,256]{1,0:T(8,128)(2,1)S(1)} %get-tuple-element.99), channel_id=1, source_target_pairs={{0,2},{1,3},{2,0},{3,1},{4,6},{5,7},{6,4},{7,5},{8,10},{9,11},{10,... | collective-permute-start | bytes 393224 | tf_op jit(solution)/shard_map/ppermute | solution.py:19
  64.2 5.9 %collective-permute-start.30 = (bf16[256,256]{1,0:T(8,128)(2,1)S(1)}, bf16[256,256]{1,0:T(8,128)(2,1)S(1)}, u32[]{:S(2)}, u32[]{:S(2)}) collective-permute-start(bf16[256,256]{1,0:T(8,128)(2,1)S(1)} %add_convert_fusion.4), channel_id=1, source_target_pairs={{0,12},{4,8},{8,4},{12,0},{1,13},{5,9},{9,5},{13,1},{2,14},{6,10},... | collective-permute-start | bytes 393224 | tf_op jit(solution)/shard_map/ppermute | solution.py:19
  70.9 7.4 %collective-permute-start.36 = (bf16[256,256]{1,0:T(8,128)(2,1)S(1)}, bf16[256,256]{1,0:T(8,128)(2,1)S(1)}, u32[]{:S(2)}, u32[]{:S(2)}) collective-permute-start(bf16[256,256]{1,0:T(8,128)(2,1)S(1)} %get-tuple-element.68), channel_id=1, source_target_pairs={{0,2},{1,3},{2,0},{3,1},{4,6},{5,7},{6,4},{7,5},{8,10},{9,11},{10,... | collective-permute-start | bytes 393224 | tf_op jit(solution)/shard_map/ppermute | solution.py:19
  71.9 9.2 %collective-permute-start.32 = (bf16[256,256]{1,0:T(8,128)(2,1)S(1)}, bf16[256,256]{1,0:T(8,128)(2,1)S(1)}, u32[]{:S(2)}, u32[]{:S(2)}) collective-permute-start(bf16[256,256]{1,0:T(8,128)(2,1)S(1)} %get-tuple-element.68), channel_id=1, source_target_pairs={{0,4},{4,0},{8,12},{12,8},{1,5},{5,1},{9,13},{13,9},{2,6},{6,2},{1... | collective-permute-start | bytes 393224 | tf_op jit(solution)/shard_map/ppermute | solution.py:19
  73.0 8.1 %collective-permute-start.35 = (bf16[256,256]{1,0:T(8,128)(2,1)S(1)}, bf16[256,256]{1,0:T(8,128)(2,1)S(1)}, u32[]{:S(2)}, u32[]{:S(2)}) collective-permute-start(bf16[256,256]{1,0:T(8,128)(2,1)S(1)} %get-tuple-element.68), channel_id=1, source_target_pairs={{0,1},{1,0},{2,3},{3,2},{4,5},{5,4},{6,7},{7,6},{8,9},{9,8},{10,11... | collective-permute-start | bytes 393224 | tf_op jit(solution)/shard_map/ppermute | solution.py:19
  75.2 7.0 %collective-permute-start.34 = (bf16[256,256]{1,0:T(8,128)(2,1)S(1)}, bf16[256,256]{1,0:T(8,128)(2,1)S(1)}, u32[]{:S(2)}, u32[]{:S(2)}) collective-permute-start(bf16[256,256]{1,0:T(8,128)(2,1)S(1)} %get-tuple-element.68), channel_id=1, source_target_pairs={{0,12},{4,8},{8,4},{12,0},{1,13},{5,9},{9,5},{13,1},{2,14},{6,10},... | collective-permute-start | bytes 393224 | tf_op jit(solution)/shard_map/ppermute | solution.py:19
  78.4 7.0 %collective-permute-start.37 = (bf16[256,256]{1,0:T(8,128)(2,1)S(1)}, bf16[256,256]{1,0:T(8,128)(2,1)S(1)}, u32[]{:S(2)}, u32[]{:S(2)}) collective-permute-start(bf16[256,256]{1,0:T(8,128)(2,1)S(1)} %collective-permute-done.36), channel_id=1, source_target_pairs={{0,12},{4,8},{8,4},{12,0},{1,13},{5,9},{9,5},{13,1},{2,14},{6,10},... | collective-permute-start | bytes 393224 | tf_op jit(solution)/shard_map/ppermute | solution.py:19
  79.9 7.6 %collective-permute-start.33 = (bf16[256,256]{1,0:T(8,128)(2,1)S(1)}, bf16[256,256]{1,0:T(8,128)(2,1)S(1)}, u32[]{:S(2)}, u32[]{:S(2)}) collective-permute-start(bf16[256,256]{1,0:T(8,128)(2,1)S(1)} %get-tuple-element.68), channel_id=1, source_target_pairs={{0,8},{4,12},{8,0},{12,4},{1,9},{5,13},{9,1},{13,5},{2,10},{6,14},... | collective-permute-start | bytes 393224 | tf_op jit(solution)/shard_map/ppermute | solution.py:19
  81.1 6.4 %collective-permute-start.38 = (bf16[256,256]{1,0:T(8,128)(2,1)S(1)}, bf16[256,256]{1,0:T(8,128)(2,1)S(1)}, u32[]{:S(2)}, u32[]{:S(2)}) collective-permute-start(bf16[256,256]{1,0:T(8,128)(2,1)S(1)} %collective-permute-done.36), channel_id=1, source_target_pairs={{0,1},{1,0},{2,3},{3,2},{4,5},{5,4},{6,7},{7,6},{8,9},{9,8},{10,11... | collective-permute-start | bytes 393224 | tf_op jit(solution)/shard_map/ppermute | solution.py:19
  81.1 11.0 %collective-permute-start.40 = (bf16[256,512]{1,0:T(8,128)(2,1)S(1)}, bf16[256,512]{1,0:T(8,128)(2,1)S(1)}, u32[]{:S(2)}, u32[]{:S(2)}) collective-permute-start(bf16[256,512]{1,0:T(8,128)(2,1)S(1)} %get-tuple-element.130), channel_id=1, source_target_pairs={{0,8},{4,12},{8,0},{12,4},{1,9},{5,13},{9,1},{13,5},{2,10},{6,14},... | collective-permute-start | bytes 786440 | tf_op jit(solution)/shard_map/ppermute | solution.py:19
  82.2 10.0 %collective-permute-start.39 = (bf16[256,512]{1,0:T(8,128)(2,1)S(1)}, bf16[256,512]{1,0:T(8,128)(2,1)S(1)}, u32[]{:S(2)}, u32[]{:S(2)}) collective-permute-start(bf16[256,512]{1,0:T(8,128)(2,1)S(1)} %get-tuple-element.131), channel_id=1, source_target_pairs={{0,4},{4,0},{8,12},{12,8},{1,5},{5,1},{9,13},{13,9},{2,6},{6,2},{1... | collective-permute-start | bytes 786440 | tf_op jit(solution)/shard_map/ppermute | solution.py:19
  85.4 7.7 %collective-permute-start.41 = (bf16[256,512]{1,0:T(8,128)(2,1)S(1)}, bf16[256,512]{1,0:T(8,128)(2,1)S(1)}, u32[]{:S(2)}, u32[]{:S(2)}) collective-permute-start(bf16[256,512]{1,0:T(8,128)(2,1)S(1)} %pad_maximum_fusion.5), channel_id=1, source_target_pairs={{0,1},{1,0},{2,3},{3,2},{4,5},{5,4},{6,7},{7,6},{8,9},{9,8},{10,11... | collective-permute-start | bytes 786440 | tf_op jit(solution)/shard_map/ppermute | solution.py:19
  95.3 13.4 %collective-permute-start.50 = (bf16[256,768]{1,0:T(8,128)(2,1)S(1)}, bf16[256,768]{1,0:T(8,128)(2,1)S(1)}, u32[]{:S(2)}, u32[]{:S(2)}) collective-permute-start(bf16[256,768]{1,0:T(8,128)(2,1)S(1)} %get-tuple-element.107.proj_ref), channel_id=1, source_target_pairs={{0,16},{16,0},{1,17},{17,1},{2,18},{18,2},{3,19},{19,3},{4,20},{20... | collective-permute-start | bytes 1179656 | tf_op jit(solution)/shard_map/ppermute | solution.py:19
  101.3 5.4 %collective-permute-start.47 = (f32[256]{0:T(256)S(1)}, f32[256]{0:T(256)S(1)}, u32[]{:S(2)}, u32[]{:S(2)}) collective-permute-start(f32[256]{0:T(256)S(1)} %add.172), channel_id=1, source_target_pairs={{0,3},{1,2},{2,1},{3,0},{4,7},{5,6},{6,5},{7,4},{8,11},{9,10},{10,... | collective-permute-start | bytes 3080 | tf_op jit(solution)/shard_map/ppermute | solution.py:19
  109.5 8.6 %collective-permute-start.56 = (bf16[256,512]{1,0:T(8,128)(2,1)S(1)}, bf16[256,512]{1,0:T(8,128)(2,1)S(1)}, u32[]{:S(2)}, u32[]{:S(2)}) collective-permute-start(bf16[256,512]{1,0:T(8,128)(2,1)S(1)} %slice.290), channel_id=1, source_target_pairs={{0,1},{1,0},{2,3},{3,2},{4,5},{5,4},{6,7},{7,6},{8,9},{9,8},{10,11... | collective-permute-start | bytes 786440 | tf_op jit(solution)/shard_map/ppermute | solution.py:19
  111.3 8.6 %collective-permute-start.58 = (bf16[256,256]{1,0:T(8,128)(2,1)S(1)}, bf16[256,256]{1,0:T(8,128)(2,1)S(1)}, u32[]{:S(2)}, u32[]{:S(2)}) collective-permute-start(bf16[256,256]{1,0:T(8,128)(2,1)S(1)} %get-tuple-element.114), channel_id=1, source_target_pairs={{0,4},{4,0},{8,12},{12,8},{1,5},{5,1},{9,13},{13,9},{2,6},{6,2},{1... | collective-permute-start | bytes 393224 | tf_op jit(solution)/shard_map/ppermute | solution.py:19
  112.5 7.4 %collective-permute-start.59 = (bf16[256,256]{1,0:T(8,128)(2,1)S(1)}, bf16[256,256]{1,0:T(8,128)(2,1)S(1)}, u32[]{:S(2)}, u32[]{:S(2)}) collective-permute-start(bf16[256,256]{1,0:T(8,128)(2,1)S(1)} %get-tuple-element.115), channel_id=1, source_target_pairs={{0,8},{4,12},{8,0},{12,4},{1,9},{5,13},{9,1},{13,5},{2,10},{6,14},... | collective-permute-start | bytes 393224 | tf_op jit(solution)/shard_map/ppermute | solution.py:19
  114.2 9.3 %collective-permute-start.54 = (bf16[256,512]{1,0:T(8,128)(2,1)S(1)}, bf16[256,512]{1,0:T(8,128)(2,1)S(1)}, u32[]{:S(2)}, u32[]{:S(2)}) collective-permute-start(bf16[256,512]{1,0:T(8,128)(2,1)S(1)} %get-tuple-element.104), channel_id=1, source_target_pairs={{0,4},{4,0},{8,12},{12,8},{1,5},{5,1},{9,13},{13,9},{2,6},{6,2},{1... | collective-permute-start | bytes 786440 | tf_op jit(solution)/shard_map/ppermute | solution.py:19
  115.5 10.2 %collective-permute-start.55 = (bf16[256,512]{1,0:T(8,128)(2,1)S(1)}, bf16[256,512]{1,0:T(8,128)(2,1)S(1)}, u32[]{:S(2)}, u32[]{:S(2)}) collective-permute-start(bf16[256,512]{1,0:T(8,128)(2,1)S(1)} %get-tuple-element.105), channel_id=1, source_target_pairs={{0,8},{4,12},{8,0},{12,4},{1,9},{5,13},{9,1},{13,5},{2,10},{6,14},... | collective-permute-start | bytes 786440 | tf_op jit(solution)/shard_map/ppermute | solution.py:19
  118.1 8.9 %collective-permute-start.57 = (bf16[256,256]{1,0:T(8,128)(2,1)S(1)}, bf16[256,256]{1,0:T(8,128)(2,1)S(1)}, u32[]{:S(2)}, u32[]{:S(2)}) collective-permute-start(bf16[256,256]{1,0:T(8,128)(2,1)S(1)} %get-tuple-element.96), channel_id=1, source_target_pairs={{0,12},{4,8},{8,4},{12,0},{1,13},{5,9},{9,5},{13,1},{2,14},{6,10},... | collective-permute-start | bytes 393224 | tf_op jit(solution)/shard_map/ppermute | solution.py:19
  119.9 5.8 %collective-permute-start.60 = (bf16[256,256]{1,0:T(8,128)(2,1)S(1)}, bf16[256,256]{1,0:T(8,128)(2,1)S(1)}, u32[]{:S(2)}, u32[]{:S(2)}) collective-permute-start(bf16[256,256]{1,0:T(8,128)(2,1)S(1)} %add_convert_fusion.2), channel_id=1, source_target_pairs={{0,1},{1,0},{2,3},{3,2},{4,5},{5,4},{6,7},{7,6},{8,9},{9,8},{10,11... | collective-permute-start | bytes 393224 | tf_op jit(solution)/shard_map/ppermute | solution.py:19
  121.5 9.8 %collective-permute-start.52 = (bf16[256,256]{1,0:T(8,128)(2,1)S(1)}, bf16[256,256]{1,0:T(8,128)(2,1)S(1)}, u32[]{:S(2)}, u32[]{:S(2)}) collective-permute-start(bf16[256,256]{1,0:T(8,128)(2,1)S(1)} %get-tuple-element.102), channel_id=1, source_target_pairs={{0,4},{4,0},{8,12},{12,8},{1,5},{5,1},{9,13},{13,9},{2,6},{6,2},{1... | collective-permute-start | bytes 393224 | tf_op jit(solution)/shard_map/ppermute | solution.py:19
  123.5 7.7 %collective-permute-start.53 = (bf16[256,256]{1,0:T(8,128)(2,1)S(1)}, bf16[256,256]{1,0:T(8,128)(2,1)S(1)}, u32[]{:S(2)}, u32[]{:S(2)}) collective-permute-start(bf16[256,256]{1,0:T(8,128)(2,1)S(1)} %get-tuple-element.103), channel_id=1, source_target_pairs={{0,8},{4,12},{8,0},{12,4},{1,9},{5,13},{9,1},{13,5},{2,10},{6,14},... | collective-permute-start | bytes 393224 | tf_op jit(solution)/shard_map/ppermute | solution.py:19
  127.1 7.2 %collective-permute-start.61 = (bf16[256,256]{1,0:T(8,128)(2,1)S(1)}, bf16[256,256]{1,0:T(8,128)(2,1)S(1)}, u32[]{:S(2)}, u32[]{:S(2)}) collective-permute-start(bf16[256,256]{1,0:T(8,128)(2,1)S(1)} %get-tuple-element.94), channel_id=1, source_target_pairs={{0,2},{1,3},{2,0},{3,1},{4,6},{5,7},{6,4},{7,5},{8,10},{9,11},{10,... | collective-permute-start | bytes 393224 | tf_op jit(solution)/shard_map/ppermute | solution.py:19
  127.8 6.6 %collective-permute-start.62 = (bf16[256,256]{1,0:T(8,128)(2,1)S(1)}, bf16[256,256]{1,0:T(8,128)(2,1)S(1)}, u32[]{:S(2)}, u32[]{:S(2)}) collective-permute-start(bf16[256,256]{1,0:T(8,128)(2,1)S(1)} %add_convert_fusion.1), channel_id=1, source_target_pairs={{0,12},{4,8},{8,4},{12,0},{1,13},{5,9},{9,5},{13,1},{2,14},{6,10},... | collective-permute-start | bytes 393224 | tf_op jit(solution)/shard_map/ppermute | solution.py:19
  129.6 5.6 %collective-permute-start.63 = (bf16[256,256]{1,0:T(8,128)(2,1)S(1)}, bf16[256,256]{1,0:T(8,128)(2,1)S(1)}, u32[]{:S(2)}, u32[]{:S(2)}) collective-permute-start(bf16[256,256]{1,0:T(8,128)(2,1)S(1)} %add_convert_fusion), channel_id=1, source_target_pairs={{0,1},{1,0},{2,3},{3,2},{4,5},{5,4},{6,7},{7,6},{8,9},{9,8},{10,11... | collective-permute-start | bytes 393224 | tf_op jit(solution)/shard_map/ppermute | solution.py:19
  (16 other events, 63.4 us)

commit v13 on v10

--- a/solution.py
+++ b/solution.py
@@ -26,7 +26,10 @@
 def total(values):
     for axis in ("row", "feat"):
         own = values
-        for mask in reversed(range(1, lax.axis_size(axis))):
+        masks = sorted(range(1, lax.axis_size(axis)), reverse=True)
+        if axis == "feat":
+            masks.sort(key=lambda mask: mask != lax.axis_size(axis) // 2)
+        for mask in masks:
             values = lax.optimization_barrier(values + xor_move(own, axis, mask))
     return values
 

time: 136 us -> 137 us (level)
  waiting for transfers between devices: 41.5 us -> 46.6 us
  starting transfers between devices: 76.5 us -> 71.8 us
    ppermute x64, waiting for transfers between devices: 41.5 us -> 46.6 us  [xor_move(): return lax.ppermute(block, axis, [(i, i ^ mask) for i in range(count)])]
    ppermute x64, starting transfers between devices: 76.5 us -> 71.8 us  [xor_move(): return lax.ppermute(block, axis, [(i, i ^ mask) for i in range(count)])]
  transfers between devices with their start and end apart: 64 -> 64, of which waited for: 37 -> 38; matrix products, arithmetic and copies ran while one was open for 6% -> 6% of each run, Pallas kernels for 3% -> 3%
where the time goes in v13:
time: 137 us; the launch traced here: 136 us
  starting transfers between devices  71.8 us (52%)
  waiting for transfers between devices  46.6 us (34%)
  matrix products  9.39 us (7%)
  Pallas kernels  3.92 us (3%)
  local copies, waits for them, and re-layouts  2.47 us (2%)
    ppermute x64, starting transfers between devices, xor_move(): return lax.ppermute(block, axis, [(i, i ^ mask) for i in range(count)])  71.8 us
    ppermute x64, waiting for transfers between devices, xor_move(): return lax.ppermute(block, axis, [(i, i ^ mask) for i in range(count)])  46.6 us
    dot_general x6, matrix products, on_device(): lax.dot_general(residue, groups[g], (((1,), (0,)), ((), ())), preferred_e...  4.76 us
    dot_general x6, matrix products, on_device(): lax.dot_general(join(*blocks), groups[g], (((1,), (1,)), ((), ())), prefe...  4.63 us
    pallas_call x1, Pallas kernels, regroup(): pl.pallas_call(kernel, out_shape=[jax.ShapeDtypeStruct((rows_here, len(pl...  3 us
  transfers between devices with their start and end apart: 64, of which 38 were waited for; matrix products, arithmetic and copies ran while one was open for 6% of the time, Pallas kernels for 3%

profile of v13, /device:TPU:0, one launch (start us, length us, event | category | flops | bytes accessed | tf_op | source)
XLA Modules:
  0.0 136.5 jit_solution(8326245294234105423)
XLA Ops:
  1.7 4.1 %collective-permute-start.4 = (bf16[256,256]{1,0:T(8,128)(2,1)S(1)}, bf16[256,256]{1,0:T(8,128)(2,1)S(1)}, u32[]{:S(2)}, u32[]{:S(2)}) collective-permute-start(bf16[256,256]{1,0:T(8,128)(2,1)S(1)} %fusion.28), channel_id=1, source_target_pairs={{0,2},{1,3},{2,0},{3,1},{4,6},{5,7},{6,4},{7,5},{8,10},{9,11},{10,... | collective-permute-start | bytes 393224 | tf_op jit(solution)/shard_map/ppermute | solution.py:19
  5.8 1.6 %collective-permute-start.3 = (bf16[256,256]{1,0:T(8,128)(2,1)S(1)}, bf16[256,256]{1,0:T(8,128)(2,1)S(1)}, u32[]{:S(2)}, u32[]{:S(2)}) collective-permute-start(bf16[256,256]{1,0:T(8,128)(2,1)S(1)} %fusion.28), channel_id=1, source_target_pairs={{0,1},{1,0},{2,3},{3,2},{4,5},{5,4},{6,7},{7,6},{8,9},{9,8},{10,11... | collective-permute-start | bytes 393224 | tf_op jit(solution)/shard_map/ppermute | solution.py:19
  7.4 1.5 %collective-permute-start = (bf16[256,256]{1,0:T(8,128)(2,1)S(1)}, bf16[256,256]{1,0:T(8,128)(2,1)S(1)}, u32[]{:S(2)}, u32[]{:S(2)}) collective-permute-start(bf16[256,256]{1,0:T(8,128)(2,1)S(1)} %fusion.28), channel_id=1, source_target_pairs={{0,4},{4,0},{8,12},{12,8},{1,5},{5,1},{9,13},{13,9},{2,6},{6,2},{1... | collective-permute-start | bytes 393224 | tf_op jit(solution)/shard_map/ppermute | solution.py:19
  8.9 1.5 %collective-permute-start.2 = (bf16[256,256]{1,0:T(8,128)(2,1)S(1)}, bf16[256,256]{1,0:T(8,128)(2,1)S(1)}, u32[]{:S(2)}, u32[]{:S(2)}) collective-permute-start(bf16[256,256]{1,0:T(8,128)(2,1)S(1)} %fusion.28), channel_id=1, source_target_pairs={{0,12},{4,8},{8,4},{12,0},{1,13},{5,9},{9,5},{13,1},{2,14},{6,10},... | collective-permute-start | bytes 393224 | tf_op jit(solution)/shard_map/ppermute | solution.py:19
  10.9 1.3 collective-permute-done.4
  12.9 2.4 %collective-permute-start.5 = (bf16[256,256]{1,0:T(8,128)(2,1)S(1)}, bf16[256,256]{1,0:T(8,128)(2,1)S(1)}, u32[]{:S(2)}, u32[]{:S(2)}) collective-permute-start(bf16[256,256]{1,0:T(8,128)(2,1)S(1)} %collective-permute-done.4), channel_id=1, source_target_pairs={{0,12},{4,8},{8,4},{12,0},{1,13},{5,9},{9,5},{13,1},{2,14},{6,10},... | collective-permute-start | bytes 393224 | tf_op jit(solution)/shard_map/ppermute | solution.py:19
  15.3 3.0 %regroup.1 = (bf16[768,1536]{1,0:T(8,128)(2,1)S(1)}, bf16[768,1536]{1,0:T(8,128)(2,1)S(1)}, bf16[768,1024]{1,0:T(8,128)(2,1)S(1)}) custom-call(bf16[768,4096]{1,0:T(8,128)(2,1)} %bitcast.37), custom_call_target="tpu_custom_call" | custom-call | bytes 12582912 | tf_op jit(solution)/shard_map/regroup/pallas_call | solution.py:143
  21.9 1.5 %collective-permute-start.10 = (bf16[256,256]{1,0:T(8,128)(2,1)S(1)}, bf16[256,256]{1,0:T(8,128)(2,1)S(1)}, u32[]{:S(2)}, u32[]{:S(2)}) collective-permute-start(bf16[256,256]{1,0:T(8,128)(2,1)S(1)} %collective-permute-done.6), channel_id=1, source_target_pairs={{0,4},{4,0},{8,12},{12,8},{1,5},{5,1},{9,13},{13,9},{2,6},{6,2},{1... | collective-permute-start | bytes 393224 | tf_op jit(solution)/shard_map/ppermute | solution.py:19
  23.5 1.5 %collective-permute-start.11 = (bf16[256,256]{1,0:T(8,128)(2,1)S(1)}, bf16[256,256]{1,0:T(8,128)(2,1)S(1)}, u32[]{:S(2)}, u32[]{:S(2)}) collective-permute-start(bf16[256,256]{1,0:T(8,128)(2,1)S(1)} %collective-permute-done.6), channel_id=1, source_target_pairs={{0,8},{4,12},{8,0},{12,4},{1,9},{5,13},{9,1},{13,5},{2,10},{6,14},... | collective-permute-start | bytes 393224 | tf_op jit(solution)/shard_map/ppermute | solution.py:19
  25.0 2.5 %collective-permute-done.8 = bf16[256,512]{1,0:T(8,128)(2,1)S(1)} collective-permute-done((bf16[256,512]{1,0:T(8,128)(2,1)S(1)}, bf16[256,512]{1,0:T(8,128)(2,1)S(1)}, u32[]{:S(2)}, u32[]{:S(2)}) %collective-permute-start.8) | collective-permute-done | bytes 262176 | tf_op jit(solution)/shard_map/ppermute | solution.py:19
  29.9 1.6 %collective-permute-start.12 = (f32[256]{0:T(256)S(1)}, f32[256]{0:T(256)S(1)}, u32[]{:S(2)}, u32[]{:S(2)}) collective-permute-start(f32[256]{0:T(256)S(1)} %get-tuple-element.112), channel_id=1, source_target_pairs={{0,12},{4,8},{8,4},{12,0},{1,13},{5,9},{9,5},{13,1},{2,14},{6,10},... | collective-permute-start | bytes 3080 | tf_op jit(solution)/shard_map/ppermute | solution.py:19
  32.3 1.2 collective-permute-start.14
  35.9 3.1 %collective-permute-start.15 = (f32[256]{0:T(256)S(1)}, f32[256]{0:T(256)S(1)}, u32[]{:S(2)}, u32[]{:S(2)}) collective-permute-start(f32[256]{0:T(256)S(1)} %add.148), channel_id=1, source_target_pairs={{0,2},{1,3},{2,0},{3,1},{4,6},{5,7},{6,4},{7,5},{8,10},{9,11},{10,... | collective-permute-start | bytes 3080 | tf_op jit(solution)/shard_map/ppermute | solution.py:19
  40.5 3.8 %collective-permute-done.16 = f32[256]{0:T(256)S(1)} collective-permute-done((f32[256]{0:T(256)S(1)}, f32[256]{0:T(256)S(1)}, u32[]{:S(2)}, u32[]{:S(2)}) %collective-permute-start.16) | collective-permute-done | bytes 1056 | tf_op jit(solution)/shard_map/ppermute | solution.py:19
  46.3 1.6 %collective-permute-start.26 = (bf16[256,256]{1,0:T(8,128)(2,1)S(1)}, bf16[256,256]{1,0:T(8,128)(2,1)S(1)}, u32[]{:S(2)}, u32[]{:S(2)}) collective-permute-start(bf16[256,256]{1,0:T(8,128)(2,1)S(1)} %get-tuple-element.116), channel_id=1, source_target_pairs={{0,4},{4,0},{8,12},{12,8},{1,5},{5,1},{9,13},{13,9},{2,6},{6,2},{1... | collective-permute-start | bytes 393224 | tf_op jit(solution)/shard_map/ppermute | solution.py:19
  47.9 1.5 %collective-permute-start.27 = (bf16[256,256]{1,0:T(8,128)(2,1)S(1)}, bf16[256,256]{1,0:T(8,128)(2,1)S(1)}, u32[]{:S(2)}, u32[]{:S(2)}) collective-permute-start(bf16[256,256]{1,0:T(8,128)(2,1)S(1)} %get-tuple-element.117), channel_id=1, source_target_pairs={{0,8},{4,12},{8,0},{12,4},{1,9},{5,13},{9,1},{13,5},{2,10},{6,14},... | collective-permute-start | bytes 393224 | tf_op jit(solution)/shard_map/ppermute | solution.py:19
  52.3 2.4 %collective-permute-done.24 = bf16[256,512]{1,0:T(8,128)(2,1)S(1)} collective-permute-done((bf16[256,512]{1,0:T(8,128)(2,1)S(1)}, bf16[256,512]{1,0:T(8,128)(2,1)S(1)}, u32[]{:S(2)}, u32[]{:S(2)}) %collective-permute-start.24) | collective-permute-done | bytes 262176 | tf_op jit(solution)/shard_map/ppermute | solution.py:19
  54.8 2.5 %collective-permute-start.25 = (bf16[256,256]{1,0:T(8,128)(2,1)S(1)}, bf16[256,256]{1,0:T(8,128)(2,1)S(1)}, u32[]{:S(2)}, u32[]{:S(2)}) collective-permute-start(bf16[256,256]{1,0:T(8,128)(2,1)S(1)} %get-tuple-element.100), channel_id=1, source_target_pairs={{0,12},{4,8},{8,4},{12,0},{1,13},{5,9},{9,5},{13,1},{2,14},{6,10},... | collective-permute-start | bytes 393224 | tf_op jit(solution)/shard_map/ppermute | solution.py:19
  58.6 1.3 collective-permute-start.21
  59.9 1.3 collective-permute-done.23
  61.2 1.1 collective-permute-done.28
  62.5 2.6 %collective-permute-start.29 = (bf16[256,256]{1,0:T(8,128)(2,1)S(1)}, bf16[256,256]{1,0:T(8,128)(2,1)S(1)}, u32[]{:S(2)}, u32[]{:S(2)}) collective-permute-start(bf16[256,256]{1,0:T(8,128)(2,1)S(1)} %get-tuple-element.99), channel_id=1, source_target_pairs={{0,2},{1,3},{2,0},{3,1},{4,6},{5,7},{6,4},{7,5},{8,10},{9,11},{10,... | collective-permute-start | bytes 393224 | tf_op jit(solution)/shard_map/ppermute | solution.py:19
  66.2 1.2 collective-permute-start.31
  67.4 2.7 %collective-permute-done.29 = bf16[256,256]{1,0:T(8,128)(2,1)S(1)} collective-permute-done((bf16[256,256]{1,0:T(8,128)(2,1)S(1)}, bf16[256,256]{1,0:T(8,128)(2,1)S(1)}, u32[]{:S(2)}, u32[]{:S(2)}) %collective-permute-start.29) | collective-permute-done | bytes 131104 | tf_op jit(solution)/shard_map/ppermute | solution.py:19
  71.5 1.4 collective-permute-start.36
  73.9 1.8 %collective-permute-start.35 = (bf16[256,256]{1,0:T(8,128)(2,1)S(1)}, bf16[256,256]{1,0:T(8,128)(2,1)S(1)}, u32[]{:S(2)}, u32[]{:S(2)}) collective-permute-start(bf16[256,256]{1,0:T(8,128)(2,1)S(1)} %get-tuple-element.68), channel_id=1, source_target_pairs={{0,1},{1,0},{2,3},{3,2},{4,5},{5,4},{6,7},{7,6},{8,9},{9,8},{10,11... | collective-permute-start | bytes 393224 | tf_op jit(solution)/shard_map/ppermute | solution.py:19
  75.7 1.4 %collective-permute-start.34 = (bf16[256,256]{1,0:T(8,128)(2,1)S(1)}, bf16[256,256]{1,0:T(8,128)(2,1)S(1)}, u32[]{:S(2)}, u32[]{:S(2)}) collective-permute-start(bf16[256,256]{1,0:T(8,128)(2,1)S(1)} %get-tuple-element.68), channel_id=1, source_target_pairs={{0,12},{4,8},{8,4},{12,0},{1,13},{5,9},{9,5},{13,1},{2,14},{6,10},... | collective-permute-start | bytes 393224 | tf_op jit(solution)/shard_map/ppermute | solution.py:19
  77.1 2.0 %collective-permute-done.36 = bf16[256,256]{1,0:T(8,128)(2,1)S(1)} collective-permute-done((bf16[256,256]{1,0:T(8,128)(2,1)S(1)}, bf16[256,256]{1,0:T(8,128)(2,1)S(1)}, u32[]{:S(2)}, u32[]{:S(2)}) %collective-permute-start.36) | collective-permute-done | bytes 131104 | tf_op jit(solution)/shard_map/ppermute | solution.py:19
  79.1 1.9 %collective-permute-start.37 = (bf16[256,256]{1,0:T(8,128)(2,1)S(1)}, bf16[256,256]{1,0:T(8,128)(2,1)S(1)}, u32[]{:S(2)}, u32[]{:S(2)}) collective-permute-start(bf16[256,256]{1,0:T(8,128)(2,1)S(1)} %collective-permute-done.36), channel_id=1, source_target_pairs={{0,12},{4,8},{8,4},{12,0},{1,13},{5,9},{9,5},{13,1},{2,14},{6,10},... | collective-permute-start | bytes 393224 | tf_op jit(solution)/shard_map/ppermute | solution.py:19
  81.8 2.0 %collective-permute-start.40 = (bf16[256,512]{1,0:T(8,128)(2,1)S(1)}, bf16[256,512]{1,0:T(8,128)(2,1)S(1)}, u32[]{:S(2)}, u32[]{:S(2)}) collective-permute-start(bf16[256,512]{1,0:T(8,128)(2,1)S(1)} %get-tuple-element.130), channel_id=1, source_target_pairs={{0,8},{4,12},{8,0},{12,4},{1,9},{5,13},{9,1},{13,5},{2,10},{6,14},... | collective-permute-start | bytes 786440 | tf_op jit(solution)/shard_map/ppermute | solution.py:19
  83.9 2.5 %collective-permute-done.37 = bf16[256,256]{1,0:T(8,128)(2,1)S(1)} collective-permute-done((bf16[256,256]{1,0:T(8,128)(2,1)S(1)}, bf16[256,256]{1,0:T(8,128)(2,1)S(1)}, u32[]{:S(2)}, u32[]{:S(2)}) %collective-permute-start.37) | collective-permute-done | bytes 131104 | tf_op jit(solution)/shard_map/ppermute | solution.py:19
  86.5 1.8 %collective-permute-done.33 = bf16[256,256]{1,0:T(8,128)(2,1)S(1)} collective-permute-done((bf16[256,256]{1,0:T(8,128)(2,1)S(1)}, bf16[256,256]{1,0:T(8,128)(2,1)S(1)}, u32[]{:S(2)}, u32[]{:S(2)}) %collective-permute-start.33) | collective-permute-done | bytes 131104 | tf_op jit(solution)/shard_map/ppermute | solution.py:19
  90.2 1.2 collective-permute-start.43
  91.4 1.6 %collective-permute-done.40 = bf16[256,512]{1,0:T(8,128)(2,1)S(1)} collective-permute-done((bf16[256,512]{1,0:T(8,128)(2,1)S(1)}, bf16[256,512]{1,0:T(8,128)(2,1)S(1)}, u32[]{:S(2)}, u32[]{:S(2)}) %collective-permute-start.40) | collective-permute-done | bytes 262176 | tf_op jit(solution)/shard_map/ppermute | solution.py:19
  95.9 1.6 %collective-permute-start.44 = (f32[256]{0:T(256)S(1)}, f32[256]{0:T(256)S(1)}, u32[]{:S(2)}, u32[]{:S(2)}) collective-permute-start(f32[256]{0:T(256)S(1)} %get-tuple-element.106), channel_id=1, source_target_pairs={{0,12},{4,8},{8,4},{12,0},{1,13},{5,9},{9,5},{13,1},{2,14},{6,10},... | collective-permute-start | bytes 3080 | tf_op jit(solution)/shard_map/ppermute | solution.py:19
  97.5 1.1 collective-permute-start.45
  101.1 1.1 collective-permute-done.46
  102.9 1.9 %collective-permute-start.48 = (f32[256]{0:T(256)S(1)}, f32[256]{0:T(256)S(1)}, u32[]{:S(2)}, u32[]{:S(2)}) collective-permute-start(f32[256]{0:T(256)S(1)} %add.172), channel_id=1, source_target_pairs={{0,3},{1,2},{2,1},{3,0},{4,7},{5,6},{6,5},{7,4},{8,11},{9,10},{10,... | collective-permute-start | bytes 3080 | tf_op jit(solution)/shard_map/ppermute | solution.py:19
  106.7 1.5 %collective-permute-done.48 = f32[256]{0:T(256)S(1)} collective-permute-done((f32[256]{0:T(256)S(1)}, f32[256]{0:T(256)S(1)}, u32[]{:S(2)}, u32[]{:S(2)}) %collective-permute-start.48) | collective-permute-done | bytes 1056 | tf_op jit(solution)/shard_map/ppermute | solution.py:19
  112.1 1.2 collective-permute-start.59
  115.2 1.1 collective-permute-start.55
  117.2 1.6 %collective-permute-done.56 = bf16[256,512]{1,0:T(8,128)(2,1)S(1)} collective-permute-done((bf16[256,512]{1,0:T(8,128)(2,1)S(1)}, bf16[256,512]{1,0:T(8,128)(2,1)S(1)}, u32[]{:S(2)}, u32[]{:S(2)}) %collective-permute-start.56) | collective-permute-done | bytes 262176 | tf_op jit(solution)/shard_map/ppermute | solution.py:19
  118.9 1.7 %collective-permute-start.57 = (bf16[256,256]{1,0:T(8,128)(2,1)S(1)}, bf16[256,256]{1,0:T(8,128)(2,1)S(1)}, u32[]{:S(2)}, u32[]{:S(2)}) collective-permute-start(bf16[256,256]{1,0:T(8,128)(2,1)S(1)} %get-tuple-element.95), channel_id=1, source_target_pairs={{0,12},{4,8},{8,4},{12,0},{1,13},{5,9},{9,5},{13,1},{2,14},{6,10},... | collective-permute-start | bytes 393224 | tf_op jit(solution)/shard_map/ppermute | solution.py:19
  123.9 1.3 collective-permute-done.55
  126.4 1.7 %collective-permute-start.61 = (bf16[256,256]{1,0:T(8,128)(2,1)S(1)}, bf16[256,256]{1,0:T(8,128)(2,1)S(1)}, u32[]{:S(2)}, u32[]{:S(2)}) collective-permute-start(bf16[256,256]{1,0:T(8,128)(2,1)S(1)} %get-tuple-element.94), channel_id=1, source_target_pairs={{0,2},{1,3},{2,0},{3,1},{4,6},{5,7},{6,4},{7,5},{8,10},{9,11},{10,... | collective-permute-start | bytes 393224 | tf_op jit(solution)/shard_map/ppermute | solution.py:19
  128.2 1.9 %collective-permute-start.62 = (bf16[256,256]{1,0:T(8,128)(2,1)S(1)}, bf16[256,256]{1,0:T(8,128)(2,1)S(1)}, u32[]{:S(2)}, u32[]{:S(2)}) collective-permute-start(bf16[256,256]{1,0:T(8,128)(2,1)S(1)} %add_convert_fusion.1), channel_id=1, source_target_pairs={{0,12},{4,8},{8,4},{12,0},{1,13},{5,9},{9,5},{13,1},{2,14},{6,10},... | collective-permute-start | bytes 393224 | tf_op jit(solution)/shard_map/ppermute | solution.py:19
  130.7 3.4 %collective-permute-done.61 = bf16[256,256]{1,0:T(8,128)(2,1)S(1)} collective-permute-done((bf16[256,256]{1,0:T(8,128)(2,1)S(1)}, bf16[256,256]{1,0:T(8,128)(2,1)S(1)}, u32[]{:S(2)}, u32[]{:S(2)}) %collective-permute-start.61) | collective-permute-done | bytes 131104 | tf_op jit(solution)/shard_map/ppermute | solution.py:19
  134.2 1.3 collective-permute-done.63
  (167 shorter events, 46.3 us)
Async XLA Ops:
  1.7 10.5 %collective-permute-start.4 = (bf16[256,256]{1,0:T(8,128)(2,1)S(1)}, bf16[256,256]{1,0:T(8,128)(2,1)S(1)}, u32[]{:S(2)}, u32[]{:S(2)}) collective-permute-start(bf16[256,256]{1,0:T(8,128)(2,1)S(1)} %fusion.28), channel_id=1, source_target_pairs={{0,2},{1,3},{2,0},{3,1},{4,6},{5,7},{6,4},{7,5},{8,10},{9,11},{10,... | collective-permute-start | bytes 393224 | tf_op jit(solution)/shard_map/ppermute | solution.py:19
  5.8 7.0 %collective-permute-start.3 = (bf16[256,256]{1,0:T(8,128)(2,1)S(1)}, bf16[256,256]{1,0:T(8,128)(2,1)S(1)}, u32[]{:S(2)}, u32[]{:S(2)}) collective-permute-start(bf16[256,256]{1,0:T(8,128)(2,1)S(1)} %fusion.28), channel_id=1, source_target_pairs={{0,1},{1,0},{2,3},{3,2},{4,5},{5,4},{6,7},{7,6},{8,9},{9,8},{10,11... | collective-permute-start | bytes 393224 | tf_op jit(solution)/shard_map/ppermute | solution.py:19
  7.4 10.9 %collective-permute-start = (bf16[256,256]{1,0:T(8,128)(2,1)S(1)}, bf16[256,256]{1,0:T(8,128)(2,1)S(1)}, u32[]{:S(2)}, u32[]{:S(2)}) collective-permute-start(bf16[256,256]{1,0:T(8,128)(2,1)S(1)} %fusion.28), channel_id=1, source_target_pairs={{0,4},{4,0},{8,12},{12,8},{1,5},{5,1},{9,13},{13,9},{2,6},{6,2},{1... | collective-permute-start | bytes 393224 | tf_op jit(solution)/shard_map/ppermute | solution.py:19
  8.9 10.0 %collective-permute-start.2 = (bf16[256,256]{1,0:T(8,128)(2,1)S(1)}, bf16[256,256]{1,0:T(8,128)(2,1)S(1)}, u32[]{:S(2)}, u32[]{:S(2)}) collective-permute-start(bf16[256,256]{1,0:T(8,128)(2,1)S(1)} %fusion.28), channel_id=1, source_target_pairs={{0,12},{4,8},{8,4},{12,0},{1,13},{5,9},{9,5},{13,1},{2,14},{6,10},... | collective-permute-start | bytes 393224 | tf_op jit(solution)/shard_map/ppermute | solution.py:19
  10.4 9.7 %collective-permute-start.1 = (bf16[256,256]{1,0:T(8,128)(2,1)S(1)}, bf16[256,256]{1,0:T(8,128)(2,1)S(1)}, u32[]{:S(2)}, u32[]{:S(2)}) collective-permute-start(bf16[256,256]{1,0:T(8,128)(2,1)S(1)} %fusion.28), channel_id=1, source_target_pairs={{0,8},{4,12},{8,0},{12,4},{1,9},{5,13},{9,1},{13,5},{2,10},{6,14},... | collective-permute-start | bytes 393224 | tf_op jit(solution)/shard_map/ppermute | solution.py:19
  12.3 7.8 %collective-permute-start.6 = (bf16[256,256]{1,0:T(8,128)(2,1)S(1)}, bf16[256,256]{1,0:T(8,128)(2,1)S(1)}, u32[]{:S(2)}, u32[]{:S(2)}) collective-permute-start(bf16[256,256]{1,0:T(8,128)(2,1)S(1)} %collective-permute-done.4), channel_id=1, source_target_pairs={{0,1},{1,0},{2,3},{3,2},{4,5},{5,4},{6,7},{7,6},{8,9},{9,8},{10,11... | collective-permute-start | bytes 393224 | tf_op jit(solution)/shard_map/ppermute | solution.py:19
  12.9 7.2 %collective-permute-start.5 = (bf16[256,256]{1,0:T(8,128)(2,1)S(1)}, bf16[256,256]{1,0:T(8,128)(2,1)S(1)}, u32[]{:S(2)}, u32[]{:S(2)}) collective-permute-start(bf16[256,256]{1,0:T(8,128)(2,1)S(1)} %collective-permute-done.4), channel_id=1, source_target_pairs={{0,12},{4,8},{8,4},{12,0},{1,13},{5,9},{9,5},{13,1},{2,14},{6,10},... | collective-permute-start | bytes 393224 | tf_op jit(solution)/shard_map/ppermute | solution.py:19
  18.4 9.1 %collective-permute-start.8 = (bf16[256,512]{1,0:T(8,128)(2,1)S(1)}, bf16[256,512]{1,0:T(8,128)(2,1)S(1)}, u32[]{:S(2)}, u32[]{:S(2)}) collective-permute-start(bf16[256,512]{1,0:T(8,128)(2,1)S(1)} %get-tuple-element.132), channel_id=1, source_target_pairs={{0,8},{4,12},{8,0},{12,4},{1,9},{5,13},{9,1},{13,5},{2,10},{6,14},... | collective-permute-start | bytes 786440 | tf_op jit(solution)/shard_map/ppermute | solution.py:19
  19.0 8.8 %collective-permute-start.7 = (bf16[256,512]{1,0:T(8,128)(2,1)S(1)}, bf16[256,512]{1,0:T(8,128)(2,1)S(1)}, u32[]{:S(2)}, u32[]{:S(2)}) collective-permute-start(bf16[256,512]{1,0:T(8,128)(2,1)S(1)} %get-tuple-element.133), channel_id=1, source_target_pairs={{0,4},{4,0},{8,12},{12,8},{1,5},{5,1},{9,13},{13,9},{2,6},{6,2},{1... | collective-permute-start | bytes 786440 | tf_op jit(solution)/shard_map/ppermute | solution.py:19
  21.0 7.7 %collective-permute-start.9 = (bf16[256,512]{1,0:T(8,128)(2,1)S(1)}, bf16[256,512]{1,0:T(8,128)(2,1)S(1)}, u32[]{:S(2)}, u32[]{:S(2)}) collective-permute-start(bf16[256,512]{1,0:T(8,128)(2,1)S(1)} %pad_maximum_fusion.4), channel_id=1, source_target_pairs={{0,1},{1,0},{2,3},{3,2},{4,5},{5,4},{6,7},{7,6},{8,9},{9,8},{10,11... | collective-permute-start | bytes 786440 | tf_op jit(solution)/shard_map/ppermute | solution.py:19
  21.9 7.2 %collective-permute-start.10 = (bf16[256,256]{1,0:T(8,128)(2,1)S(1)}, bf16[256,256]{1,0:T(8,128)(2,1)S(1)}, u32[]{:S(2)}, u32[]{:S(2)}) collective-permute-start(bf16[256,256]{1,0:T(8,128)(2,1)S(1)} %collective-permute-done.6), channel_id=1, source_target_pairs={{0,4},{4,0},{8,12},{12,8},{1,5},{5,1},{9,13},{13,9},{2,6},{6,2},{1... | collective-permute-start | bytes 393224 | tf_op jit(solution)/shard_map/ppermute | solution.py:19
  23.5 5.7 %collective-permute-start.11 = (bf16[256,256]{1,0:T(8,128)(2,1)S(1)}, bf16[256,256]{1,0:T(8,128)(2,1)S(1)}, u32[]{:S(2)}, u32[]{:S(2)}) collective-permute-start(bf16[256,256]{1,0:T(8,128)(2,1)S(1)} %collective-permute-done.6), channel_id=1, source_target_pairs={{0,8},{4,12},{8,0},{12,4},{1,9},{5,13},{9,1},{13,5},{2,10},{6,14},... | collective-permute-start | bytes 393224 | tf_op jit(solution)/shard_map/ppermute | solution.py:19
  29.8 15.7 %collective-permute-start.18 = (bf16[256,768]{1,0:T(8,128)(2,1)S(1)}, bf16[256,768]{1,0:T(8,128)(2,1)S(1)}, u32[]{:S(2)}, u32[]{:S(2)}) collective-permute-start(bf16[256,768]{1,0:T(8,128)(2,1)S(1)} %get-tuple-element.113), channel_id=1, source_target_pairs={{0,16},{16,0},{1,17},{17,1},{2,18},{18,2},{3,19},{19,3},{4,20},{20... | collective-permute-start | bytes 1179656 | tf_op jit(solution)/shard_map/ppermute | solution.py:19
  38.9 5.4 %collective-permute-start.16 = (f32[256]{0:T(256)S(1)}, f32[256]{0:T(256)S(1)}, u32[]{:S(2)}, u32[]{:S(2)}) collective-permute-start(f32[256]{0:T(256)S(1)} %add.148), channel_id=1, source_target_pairs={{0,3},{1,2},{2,1},{3,0},{4,7},{5,6},{6,5},{7,4},{8,11},{9,10},{10,... | collective-permute-start | bytes 3080 | tf_op jit(solution)/shard_map/ppermute | solution.py:19
  38.9 5.4 %collective-permute-start.17 = (f32[256]{0:T(256)S(1)}, f32[256]{0:T(256)S(1)}, u32[]{:S(2)}, u32[]{:S(2)}) collective-permute-start(f32[256]{0:T(256)S(1)} %add.148), channel_id=1, source_target_pairs={{0,1},{1,0},{2,3},{3,2},{4,5},{5,4},{6,7},{7,6},{8,9},{9,8},{10,11... | collective-permute-start | bytes 3080 | tf_op jit(solution)/shard_map/ppermute | solution.py:19
  46.2 8.5 %collective-permute-start.24 = (bf16[256,512]{1,0:T(8,128)(2,1)S(1)}, bf16[256,512]{1,0:T(8,128)(2,1)S(1)}, u32[]{:S(2)}, u32[]{:S(2)}) collective-permute-start(bf16[256,512]{1,0:T(8,128)(2,1)S(1)} %slice.265), channel_id=1, source_target_pairs={{0,1},{1,0},{2,3},{3,2},{4,5},{5,4},{6,7},{7,6},{8,9},{9,8},{10,11... | collective-permute-start | bytes 786440 | tf_op jit(solution)/shard_map/ppermute | solution.py:19
  46.3 11.0 %collective-permute-start.26 = (bf16[256,256]{1,0:T(8,128)(2,1)S(1)}, bf16[256,256]{1,0:T(8,128)(2,1)S(1)}, u32[]{:S(2)}, u32[]{:S(2)}) collective-permute-start(bf16[256,256]{1,0:T(8,128)(2,1)S(1)} %get-tuple-element.116), channel_id=1, source_target_pairs={{0,4},{4,0},{8,12},{12,8},{1,5},{5,1},{9,13},{13,9},{2,6},{6,2},{1... | collective-permute-start | bytes 393224 | tf_op jit(solution)/shard_map/ppermute | solution.py:19
  47.9 9.4 %collective-permute-start.27 = (bf16[256,256]{1,0:T(8,128)(2,1)S(1)}, bf16[256,256]{1,0:T(8,128)(2,1)S(1)}, u32[]{:S(2)}, u32[]{:S(2)}) collective-permute-start(bf16[256,256]{1,0:T(8,128)(2,1)S(1)} %get-tuple-element.117), channel_id=1, source_target_pairs={{0,8},{4,12},{8,0},{12,4},{1,9},{5,13},{9,1},{13,5},{2,10},{6,14},... | collective-permute-start | bytes 393224 | tf_op jit(solution)/shard_map/ppermute | solution.py:19
  50.3 8.3 %collective-permute-start.22 = (bf16[256,512]{1,0:T(8,128)(2,1)S(1)}, bf16[256,512]{1,0:T(8,128)(2,1)S(1)}, u32[]{:S(2)}, u32[]{:S(2)}) collective-permute-start(bf16[256,512]{1,0:T(8,128)(2,1)S(1)} %get-tuple-element.110), channel_id=1, source_target_pairs={{0,4},{4,0},{8,12},{12,8},{1,5},{5,1},{9,13},{13,9},{2,6},{6,2},{1... | collective-permute-start | bytes 786440 | tf_op jit(solution)/shard_map/ppermute | solution.py:19
  50.9 10.3 %collective-permute-start.23 = (bf16[256,512]{1,0:T(8,128)(2,1)S(1)}, bf16[256,512]{1,0:T(8,128)(2,1)S(1)}, u32[]{:S(2)}, u32[]{:S(2)}) collective-permute-start(bf16[256,512]{1,0:T(8,128)(2,1)S(1)} %get-tuple-element.111), channel_id=1, source_target_pairs={{0,8},{4,12},{8,0},{12,4},{1,9},{5,13},{9,1},{13,5},{2,10},{6,14},... | collective-permute-start | bytes 786440 | tf_op jit(solution)/shard_map/ppermute | solution.py:19
  54.8 7.6 %collective-permute-start.25 = (bf16[256,256]{1,0:T(8,128)(2,1)S(1)}, bf16[256,256]{1,0:T(8,128)(2,1)S(1)}, u32[]{:S(2)}, u32[]{:S(2)}) collective-permute-start(bf16[256,256]{1,0:T(8,128)(2,1)S(1)} %get-tuple-element.100), channel_id=1, source_target_pairs={{0,12},{4,8},{8,4},{12,0},{1,13},{5,9},{9,5},{13,1},{2,14},{6,10},... | collective-permute-start | bytes 393224 | tf_op jit(solution)/shard_map/ppermute | solution.py:19
  57.7 9.7 %collective-permute-start.20 = (bf16[256,256]{1,0:T(8,128)(2,1)S(1)}, bf16[256,256]{1,0:T(8,128)(2,1)S(1)}, u32[]{:S(2)}, u32[]{:S(2)}) collective-permute-start(bf16[256,256]{1,0:T(8,128)(2,1)S(1)} %get-tuple-element.108), channel_id=1, source_target_pairs={{0,4},{4,0},{8,12},{12,8},{1,5},{5,1},{9,13},{13,9},{2,6},{6,2},{1... | collective-permute-start | bytes 393224 | tf_op jit(solution)/shard_map/ppermute | solution.py:19
  58.6 8.8 %collective-permute-start.21 = (bf16[256,256]{1,0:T(8,128)(2,1)S(1)}, bf16[256,256]{1,0:T(8,128)(2,1)S(1)}, u32[]{:S(2)}, u32[]{:S(2)}) collective-permute-start(bf16[256,256]{1,0:T(8,128)(2,1)S(1)} %get-tuple-element.109), channel_id=1, source_target_pairs={{0,8},{4,12},{8,0},{12,4},{1,9},{5,13},{9,1},{13,5},{2,10},{6,14},... | collective-permute-start | bytes 393224 | tf_op jit(solution)/shard_map/ppermute | solution.py:19
  62.5 7.7 %collective-permute-start.29 = (bf16[256,256]{1,0:T(8,128)(2,1)S(1)}, bf16[256,256]{1,0:T(8,128)(2,1)S(1)}, u32[]{:S(2)}, u32[]{:S(2)}) collective-permute-start(bf16[256,256]{1,0:T(8,128)(2,1)S(1)} %get-tuple-element.99), channel_id=1, source_target_pairs={{0,2},{1,3},{2,0},{3,1},{4,6},{5,7},{6,4},{7,5},{8,10},{9,11},{10,... | collective-permute-start | bytes 393224 | tf_op jit(solution)/shard_map/ppermute | solution.py:19
  65.1 5.9 %collective-permute-start.30 = (bf16[256,256]{1,0:T(8,128)(2,1)S(1)}, bf16[256,256]{1,0:T(8,128)(2,1)S(1)}, u32[]{:S(2)}, u32[]{:S(2)}) collective-permute-start(bf16[256,256]{1,0:T(8,128)(2,1)S(1)} %add_convert_fusion.4), channel_id=1, source_target_pairs={{0,12},{4,8},{8,4},{12,0},{1,13},{5,9},{9,5},{13,1},{2,14},{6,10},... | collective-permute-start | bytes 393224 | tf_op jit(solution)/shard_map/ppermute | solution.py:19
  71.5 7.5 %collective-permute-start.36 = (bf16[256,256]{1,0:T(8,128)(2,1)S(1)}, bf16[256,256]{1,0:T(8,128)(2,1)S(1)}, u32[]{:S(2)}, u32[]{:S(2)}) collective-permute-start(bf16[256,256]{1,0:T(8,128)(2,1)S(1)} %get-tuple-element.68), channel_id=1, source_target_pairs={{0,2},{1,3},{2,0},{3,1},{4,6},{5,7},{6,4},{7,5},{8,10},{9,11},{10,... | collective-permute-start | bytes 393224 | tf_op jit(solution)/shard_map/ppermute | solution.py:19
  72.9 8.9 %collective-permute-start.32 = (bf16[256,256]{1,0:T(8,128)(2,1)S(1)}, bf16[256,256]{1,0:T(8,128)(2,1)S(1)}, u32[]{:S(2)}, u32[]{:S(2)}) collective-permute-start(bf16[256,256]{1,0:T(8,128)(2,1)S(1)} %get-tuple-element.68), channel_id=1, source_target_pairs={{0,4},{4,0},{8,12},{12,8},{1,5},{5,1},{9,13},{13,9},{2,6},{6,2},{1... | collective-permute-start | bytes 393224 | tf_op jit(solution)/shard_map/ppermute | solution.py:19
  73.9 7.9 %collective-permute-start.35 = (bf16[256,256]{1,0:T(8,128)(2,1)S(1)}, bf16[256,256]{1,0:T(8,128)(2,1)S(1)}, u32[]{:S(2)}, u32[]{:S(2)}) collective-permute-start(bf16[256,256]{1,0:T(8,128)(2,1)S(1)} %get-tuple-element.68), channel_id=1, source_target_pairs={{0,1},{1,0},{2,3},{3,2},{4,5},{5,4},{6,7},{7,6},{8,9},{9,8},{10,11... | collective-permute-start | bytes 393224 | tf_op jit(solution)/shard_map/ppermute | solution.py:19
  75.7 8.2 %collective-permute-start.34 = (bf16[256,256]{1,0:T(8,128)(2,1)S(1)}, bf16[256,256]{1,0:T(8,128)(2,1)S(1)}, u32[]{:S(2)}, u32[]{:S(2)}) collective-permute-start(bf16[256,256]{1,0:T(8,128)(2,1)S(1)} %get-tuple-element.68), channel_id=1, source_target_pairs={{0,12},{4,8},{8,4},{12,0},{1,13},{5,9},{9,5},{13,1},{2,14},{6,10},... | collective-permute-start | bytes 393224 | tf_op jit(solution)/shard_map/ppermute | solution.py:19
  79.1 7.3 %collective-permute-start.37 = (bf16[256,256]{1,0:T(8,128)(2,1)S(1)}, bf16[256,256]{1,0:T(8,128)(2,1)S(1)}, u32[]{:S(2)}, u32[]{:S(2)}) collective-permute-start(bf16[256,256]{1,0:T(8,128)(2,1)S(1)} %collective-permute-done.36), channel_id=1, source_target_pairs={{0,12},{4,8},{8,4},{12,0},{1,13},{5,9},{9,5},{13,1},{2,14},{6,10},... | collective-permute-start | bytes 393224 | tf_op jit(solution)/shard_map/ppermute | solution.py:19
  81.0 7.4 %collective-permute-start.33 = (bf16[256,256]{1,0:T(8,128)(2,1)S(1)}, bf16[256,256]{1,0:T(8,128)(2,1)S(1)}, u32[]{:S(2)}, u32[]{:S(2)}) collective-permute-start(bf16[256,256]{1,0:T(8,128)(2,1)S(1)} %get-tuple-element.68), channel_id=1, source_target_pairs={{0,8},{4,12},{8,0},{12,4},{1,9},{5,13},{9,1},{13,5},{2,10},{6,14},... | collective-permute-start | bytes 393224 | tf_op jit(solution)/shard_map/ppermute | solution.py:19
  81.8 6.6 %collective-permute-start.38 = (bf16[256,256]{1,0:T(8,128)(2,1)S(1)}, bf16[256,256]{1,0:T(8,128)(2,1)S(1)}, u32[]{:S(2)}, u32[]{:S(2)}) collective-permute-start(bf16[256,256]{1,0:T(8,128)(2,1)S(1)} %collective-permute-done.36), channel_id=1, source_target_pairs={{0,1},{1,0},{2,3},{3,2},{4,5},{5,4},{6,7},{7,6},{8,9},{9,8},{10,11... | collective-permute-start | bytes 393224 | tf_op jit(solution)/shard_map/ppermute | solution.py:19
  81.8 11.1 %collective-permute-start.40 = (bf16[256,512]{1,0:T(8,128)(2,1)S(1)}, bf16[256,512]{1,0:T(8,128)(2,1)S(1)}, u32[]{:S(2)}, u32[]{:S(2)}) collective-permute-start(bf16[256,512]{1,0:T(8,128)(2,1)S(1)} %get-tuple-element.130), channel_id=1, source_target_pairs={{0,8},{4,12},{8,0},{12,4},{1,9},{5,13},{9,1},{13,5},{2,10},{6,14},... | collective-permute-start | bytes 786440 | tf_op jit(solution)/shard_map/ppermute | solution.py:19
  83.9 9.1 %collective-permute-start.39 = (bf16[256,512]{1,0:T(8,128)(2,1)S(1)}, bf16[256,512]{1,0:T(8,128)(2,1)S(1)}, u32[]{:S(2)}, u32[]{:S(2)}) collective-permute-start(bf16[256,512]{1,0:T(8,128)(2,1)S(1)} %get-tuple-element.131), channel_id=1, source_target_pairs={{0,4},{4,0},{8,12},{12,8},{1,5},{5,1},{9,13},{13,9},{2,6},{6,2},{1... | collective-permute-start | bytes 786440 | tf_op jit(solution)/shard_map/ppermute | solution.py:19
  86.4 7.5 %collective-permute-start.41 = (bf16[256,512]{1,0:T(8,128)(2,1)S(1)}, bf16[256,512]{1,0:T(8,128)(2,1)S(1)}, u32[]{:S(2)}, u32[]{:S(2)}) collective-permute-start(bf16[256,512]{1,0:T(8,128)(2,1)S(1)} %pad_maximum_fusion.5), channel_id=1, source_target_pairs={{0,1},{1,0},{2,3},{3,2},{4,5},{5,4},{6,7},{7,6},{8,9},{9,8},{10,11... | collective-permute-start | bytes 786440 | tf_op jit(solution)/shard_map/ppermute | solution.py:19
  95.9 13.7 %collective-permute-start.50 = (bf16[256,768]{1,0:T(8,128)(2,1)S(1)}, bf16[256,768]{1,0:T(8,128)(2,1)S(1)}, u32[]{:S(2)}, u32[]{:S(2)}) collective-permute-start(bf16[256,768]{1,0:T(8,128)(2,1)S(1)} %get-tuple-element.107.proj_ref), channel_id=1, source_target_pairs={{0,16},{16,0},{1,17},{17,1},{2,18},{18,2},{3,19},{19,3},{4,20},{20... | collective-permute-start | bytes 1179656 | tf_op jit(solution)/shard_map/ppermute | solution.py:19
  102.9 5.4 %collective-permute-start.48 = (f32[256]{0:T(256)S(1)}, f32[256]{0:T(256)S(1)}, u32[]{:S(2)}, u32[]{:S(2)}) collective-permute-start(f32[256]{0:T(256)S(1)} %add.172), channel_id=1, source_target_pairs={{0,3},{1,2},{2,1},{3,0},{4,7},{5,6},{6,5},{7,4},{8,11},{9,10},{10,... | collective-permute-start | bytes 3080 | tf_op jit(solution)/shard_map/ppermute | solution.py:19
  110.3 8.6 %collective-permute-start.56 = (bf16[256,512]{1,0:T(8,128)(2,1)S(1)}, bf16[256,512]{1,0:T(8,128)(2,1)S(1)}, u32[]{:S(2)}, u32[]{:S(2)}) collective-permute-start(bf16[256,512]{1,0:T(8,128)(2,1)S(1)} %slice.290), channel_id=1, source_target_pairs={{0,1},{1,0},{2,3},{3,2},{4,5},{5,4},{6,7},{7,6},{8,9},{9,8},{10,11... | collective-permute-start | bytes 786440 | tf_op jit(solution)/shard_map/ppermute | solution.py:19
  111.3 9.3 %collective-permute-start.58 = (bf16[256,256]{1,0:T(8,128)(2,1)S(1)}, bf16[256,256]{1,0:T(8,128)(2,1)S(1)}, u32[]{:S(2)}, u32[]{:S(2)}) collective-permute-start(bf16[256,256]{1,0:T(8,128)(2,1)S(1)} %get-tuple-element.114), channel_id=1, source_target_pairs={{0,4},{4,0},{8,12},{12,8},{1,5},{5,1},{9,13},{13,9},{2,6},{6,2},{1... | collective-permute-start | bytes 393224 | tf_op jit(solution)/shard_map/ppermute | solution.py:19
  112.1 8.5 %collective-permute-start.59 = (bf16[256,256]{1,0:T(8,128)(2,1)S(1)}, bf16[256,256]{1,0:T(8,128)(2,1)S(1)}, u32[]{:S(2)}, u32[]{:S(2)}) collective-permute-start(bf16[256,256]{1,0:T(8,128)(2,1)S(1)} %get-tuple-element.115), channel_id=1, source_target_pairs={{0,8},{4,12},{8,0},{12,4},{1,9},{5,13},{9,1},{13,5},{2,10},{6,14},... | collective-permute-start | bytes 393224 | tf_op jit(solution)/shard_map/ppermute | solution.py:19
  114.2 8.8 %collective-permute-start.54 = (bf16[256,512]{1,0:T(8,128)(2,1)S(1)}, bf16[256,512]{1,0:T(8,128)(2,1)S(1)}, u32[]{:S(2)}, u32[]{:S(2)}) collective-permute-start(bf16[256,512]{1,0:T(8,128)(2,1)S(1)} %get-tuple-element.104), channel_id=1, source_target_pairs={{0,4},{4,0},{8,12},{12,8},{1,5},{5,1},{9,13},{13,9},{2,6},{6,2},{1... | collective-permute-start | bytes 786440 | tf_op jit(solution)/shard_map/ppermute | solution.py:19
  115.2 9.9 %collective-permute-start.55 = (bf16[256,512]{1,0:T(8,128)(2,1)S(1)}, bf16[256,512]{1,0:T(8,128)(2,1)S(1)}, u32[]{:S(2)}, u32[]{:S(2)}) collective-permute-start(bf16[256,512]{1,0:T(8,128)(2,1)S(1)} %get-tuple-element.105), channel_id=1, source_target_pairs={{0,8},{4,12},{8,0},{12,4},{1,9},{5,13},{9,1},{13,5},{2,10},{6,14},... | collective-permute-start | bytes 786440 | tf_op jit(solution)/shard_map/ppermute | solution.py:19
  118.9 7.4 %collective-permute-start.57 = (bf16[256,256]{1,0:T(8,128)(2,1)S(1)}, bf16[256,256]{1,0:T(8,128)(2,1)S(1)}, u32[]{:S(2)}, u32[]{:S(2)}) collective-permute-start(bf16[256,256]{1,0:T(8,128)(2,1)S(1)} %get-tuple-element.95), channel_id=1, source_target_pairs={{0,12},{4,8},{8,4},{12,0},{1,13},{5,9},{9,5},{13,1},{2,14},{6,10},... | collective-permute-start | bytes 393224 | tf_op jit(solution)/shard_map/ppermute | solution.py:19
  121.5 9.2 %collective-permute-start.52 = (bf16[256,256]{1,0:T(8,128)(2,1)S(1)}, bf16[256,256]{1,0:T(8,128)(2,1)S(1)}, u32[]{:S(2)}, u32[]{:S(2)}) collective-permute-start(bf16[256,256]{1,0:T(8,128)(2,1)S(1)} %get-tuple-element.102), channel_id=1, source_target_pairs={{0,4},{4,0},{8,12},{12,8},{1,5},{5,1},{9,13},{13,9},{2,6},{6,2},{1... | collective-permute-start | bytes 393224 | tf_op jit(solution)/shard_map/ppermute | solution.py:19
  123.0 7.7 %collective-permute-start.53 = (bf16[256,256]{1,0:T(8,128)(2,1)S(1)}, bf16[256,256]{1,0:T(8,128)(2,1)S(1)}, u32[]{:S(2)}, u32[]{:S(2)}) collective-permute-start(bf16[256,256]{1,0:T(8,128)(2,1)S(1)} %get-tuple-element.103), channel_id=1, source_target_pairs={{0,8},{4,12},{8,0},{12,4},{1,9},{5,13},{9,1},{13,5},{2,10},{6,14},... | collective-permute-start | bytes 393224 | tf_op jit(solution)/shard_map/ppermute | solution.py:19
  126.4 7.7 %collective-permute-start.61 = (bf16[256,256]{1,0:T(8,128)(2,1)S(1)}, bf16[256,256]{1,0:T(8,128)(2,1)S(1)}, u32[]{:S(2)}, u32[]{:S(2)}) collective-permute-start(bf16[256,256]{1,0:T(8,128)(2,1)S(1)} %get-tuple-element.94), channel_id=1, source_target_pairs={{0,2},{1,3},{2,0},{3,1},{4,6},{5,7},{6,4},{7,5},{8,10},{9,11},{10,... | collective-permute-start | bytes 393224 | tf_op jit(solution)/shard_map/ppermute | solution.py:19
  128.2 6.0 %collective-permute-start.62 = (bf16[256,256]{1,0:T(8,128)(2,1)S(1)}, bf16[256,256]{1,0:T(8,128)(2,1)S(1)}, u32[]{:S(2)}, u32[]{:S(2)}) collective-permute-start(bf16[256,256]{1,0:T(8,128)(2,1)S(1)} %add_convert_fusion.1), channel_id=1, source_target_pairs={{0,12},{4,8},{8,4},{12,0},{1,13},{5,9},{9,5},{13,1},{2,14},{6,10},... | collective-permute-start | bytes 393224 | tf_op jit(solution)/shard_map/ppermute | solution.py:19
  130.1 5.4 %collective-permute-start.63 = (bf16[256,256]{1,0:T(8,128)(2,1)S(1)}, bf16[256,256]{1,0:T(8,128)(2,1)S(1)}, u32[]{:S(2)}, u32[]{:S(2)}) collective-permute-start(bf16[256,256]{1,0:T(8,128)(2,1)S(1)} %add_convert_fusion), channel_id=1, source_target_pairs={{0,1},{1,0},{2,3},{3,2},{4,5},{5,4},{6,7},{7,6},{8,9},{9,8},{10,11... | collective-permute-start | bytes 393224 | tf_op jit(solution)/shard_map/ppermute | solution.py:19
  (16 other events, 63.7 us)
